TPU v7x, 32 devices: a whole 2x2x4 slice. The times are simulated.
32 devices in a mesh: grp: 2 (over x), wide: 16 (over z, y, core).
Axes of the slice: x: 2, y: 2, z: 4, core: 2. Of those that a mesh axis runs over, the one named last changes fastest.
Arguments:
- qkv: bfloat16 [4096, 3456], P(('grp', 'wide')), parts along dimension 0, may hold values from -51.854497 to 51.854497
- grid: int32 [4, 2], P('grp'), parts along dimension 0, may hold values from 2 to 512, as said below
- w_out: bfloat16 [1152, 1152], replicated, may hold values from -0.1875 to 0.1875
- ln_gain: float32 [4608], replicated, may hold values from 0.1 to 1.9
- ln_bias: float32 [4608], replicated, may hold values from -3 to 3
- w_merge: bfloat16 [4608, 2048], P('wide'), may hold values from -0.09375 to 0.09375
- w_router: bfloat16 [2048, 8], replicated, may hold values from -0.125 to 0.125
- expert_ids: int32 [1024, 6], P(('grp', 'wide')), parts along dimension 0, may hold values from 0 to 7, as said below
- slot_pos: int32 [1024, 6], P(('grp', 'wide')), parts along dimension 0, may hold values from 0 to 31, as said below
- w_gate: bfloat16 [16, 2048, 704], P('wide'), may hold values from -0.125 to 0.125
- w_up: bfloat16 [16, 2048, 704], P('wide'), may hold values from -0.125 to 0.125
- w_down: bfloat16 [16, 704, 2048], P('wide'), may hold values from -0.15625 to 0.15625
Outputs:
- moe_out: bfloat16 [1024, 2048], P(('grp', 'wide')), parts along dimension 0
There are 2 independent parts, one for each index of `grp`. A program takes and returns all parts, laid end to end along the dimension named above; an argument that names none is the same for every part. Nothing has to cross between parts.
Inputs may be any that keep to these rules, and one draw needn't show every extreme that they name: `expert_ids`: each row names 6 different experts. Among the rows of one device no expert is named more than 32 times, and one expert is named exactly 32 times by the rows of every device. `slot_pos`: among the rows of one device, the pairs naming expert e take the slots 0, 1, ... up to the number of such pairs minus one, each once. `grid`: both numbers are even; one clip's product equals 1024, and every other clip's product lies between 512 and 768.
All inputs are finite; a program needn't handle non-finite values.
Results may differ from a plain program's by a relative error of at most 0.023.
Values may be sent and summed in bfloat16 or wider, within the bound.
No kernel may reach another device: no remote copies, remote signals or barrier semaphores. Data moves between devices by JAX's collectives and lax.ppermute only.
A program may use at most 128 MiB of HBM per device.

v0:
```python
import jax
import jax.numpy as jnp
from jax import lax
from jax.sharding import PartitionSpec as P

HEADS = 16
CLIPS = 2


route_scale = 2.446
norm_eps = 1e-05


def swapped(value, axis, stride):
    mask = 2**stride
    pairs = [(source, source ^ mask) for source in range(lax.axis_size(axis))]
    return lax.ppermute(value, axis, pairs)


def ordered_pair(own_part, partner, upper_bit):
    return jnp.where(
        upper_bit == 1,
        jnp.concatenate([partner, own_part], 0),
        jnp.concatenate([own_part, partner], 0),
    )


def local(
    qkv,
    grid,
    w_out,
    ln_gain,
    ln_bias,
    w_merge,
    w_router,
    expert_ids,
    slot_pos,
    w_gate,
    w_up,
    w_down,
):
    devices = lax.axis_size("wide")
    position_self = lax.axis_index("wide")
    vit_width = w_out.shape[0]
    head_dim = vit_width // HEADS
    groups = devices // HEADS
    local_rows = qkv.shape[0]
    sub_rows = local_rows // groups
    per_clip = devices // CLIPS
    query_send = (
        qkv[:, :vit_width]
        .reshape(groups, sub_rows, HEADS, head_dim)
        .transpose(2, 0, 1, 3)
        .reshape(devices, sub_rows, head_dim)
    )
    key_value = jnp.concatenate(
        [
            qkv[:, vit_width : 2 * vit_width].reshape(local_rows, HEADS, head_dim),
            qkv[:, 2 * vit_width :].reshape(local_rows, HEADS, head_dim),
        ],
        axis=2,
    )
    spread_send = jnp.broadcast_to(
        key_value.transpose(1, 0, 2)[:, None], (HEADS, groups, local_rows, 2 * head_dim)
    ).reshape(devices, local_rows, 2 * head_dim)
    queries, key_rows = (
        lax.all_to_all(query_send, "wide", split_axis=0, concat_axis=0, tiled=True),
        lax.all_to_all(spread_send, "wide", split_axis=0, concat_axis=0, tiled=True),
    )
    key_rows = key_rows[None]
    key_groups = key_rows.shape[0]
    key_count = key_rows.shape[2]
    key_place = (
        jnp.arange(per_clip, dtype=jnp.int32)[None, :, None] * local_rows
        + jnp.arange(key_groups, dtype=jnp.int32)[:, None, None] * local_rows
        + jnp.arange(key_count, dtype=jnp.int32)[None, None, :]
    ).reshape(-1)
    patch_counts = grid[:, 0] * grid[:, 1]
    clip_queries = queries.reshape(CLIPS, per_clip * sub_rows, head_dim)
    query_block_rows = min(512, per_clip * sub_rows)
    score_scale = head_dim ** (-0.5)

    def attend(clip_index):
        key_block = lax.dynamic_slice_in_dim(key_rows, clip_index * per_clip, per_clip, 1).reshape(
            -1, 2 * head_dim
        )
        visible = key_place < lax.dynamic_index_in_dim(patch_counts, clip_index, 0, keepdims=False)
        query_all = lax.dynamic_index_in_dim(clip_queries, clip_index, 0, keepdims=False)

        def one_block(query_block):
            scores = (
                lax.dot_general(
                    query_block,
                    key_block[:, :head_dim],
                    (((1,), (1,)), ((), ())),
                    preferred_element_type=jnp.float32,
                )
                * score_scale
            )
            scores = jnp.where(visible[None, :], scores, -jnp.inf)
            highest = jnp.max(scores, axis=1, keepdims=True)
            weights = jnp.exp(scores - highest)
            running = jnp.sum(weights, axis=1, keepdims=True)
            mixture = jnp.dot(
                weights.astype(jnp.bfloat16),
                key_block[:, head_dim:],
                preferred_element_type=jnp.float32,
            )
            return (mixture / running).astype(jnp.bfloat16)

        return lax.map(one_block, query_all.reshape(-1, query_block_rows, head_dim)).reshape(
            -1, head_dim
        )

    attended = lax.map(attend, jnp.arange(CLIPS, dtype=jnp.int32))
    returned = lax.all_to_all(
        attended.reshape(devices, sub_rows, head_dim),
        "wide",
        split_axis=0,
        concat_axis=0,
        tiled=True,
    )
    attention = (
        returned.reshape(HEADS, groups, sub_rows, head_dim)
        .transpose(1, 2, 0, 3)
        .reshape(local_rows, vit_width)
    )
    projected = jnp.dot(attention, w_out, preferred_element_type=jnp.float32).astype(jnp.bfloat16)
    merged = projected.reshape(local_rows // 4, 4 * vit_width).astype(jnp.float32)
    centre = jnp.mean(merged, axis=1, keepdims=True)
    centered = merged - centre
    spread = jnp.mean(centered * centered, axis=1, keepdims=True)
    normed = (centered * lax.rsqrt(spread + norm_eps) * ln_gain + ln_bias).astype(jnp.bfloat16)
    tok_groups = min(8, devices)
    feat_groups = devices // tok_groups
    merge_rows = w_merge
    for bit_index in range(tok_groups.bit_length() - 1):
        partner = swapped(merge_rows, "wide", bit_index)
        upper_bit = position_self // (1 << bit_index) % 2
        merge_rows = ordered_pair(merge_rows, partner, upper_bit)
    token_count = normed.shape[0]
    part_rows = token_count // tok_groups
    feat_width = normed.shape[1] // feat_groups
    out_width = w_merge.shape[1]
    merge_send = (
        normed.reshape(tok_groups, part_rows, feat_groups, feat_width)
        .transpose(2, 0, 1, 3)
        .reshape(devices, part_rows, feat_width)
    )
    flat_rows = lax.all_to_all(merge_send, "wide", split_axis=0, concat_axis=0, tiled=True).reshape(
        -1, feat_width
    )
    partial_value = jnp.dot(flat_rows, merge_rows, preferred_element_type=jnp.float32).reshape(
        devices, -1, out_width
    )
    summed = lax.all_to_all(partial_value, "wide", split_axis=0, concat_axis=0, tiled=True)
    tokens = (
        jnp.sum(summed.reshape(feat_groups, tok_groups, part_rows, out_width), axis=0)
        .reshape(token_count, out_width)
        .astype(jnp.bfloat16)
    )
    logits = jnp.dot(tokens, w_router, preferred_element_type=jnp.float32)
    experts = w_router.shape[1]
    top_count = expert_ids.shape[1]
    matches = expert_ids[:, :, None] == jnp.arange(experts, dtype=jnp.int32)[None, None, :]
    chosen = jnp.sum(jnp.where(matches, logits[:, None, :], 0.0), axis=2)
    gate_values = jax.nn.sigmoid(chosen)
    route_weight = route_scale * gate_values / jnp.sum(gate_values, axis=1, keepdims=True)
    capacity = min(token_count, 2 * token_count * top_count // experts)
    slot_count = experts * capacity
    target = expert_ids * capacity + slot_pos
    one_hot = jnp.any(
        target[None, :, :] == jnp.arange(slot_count, dtype=jnp.int32)[:, None, None], axis=2
    ).astype(jnp.bfloat16)
    buffer = jnp.dot(one_hot, tokens, preferred_element_type=jnp.float32).astype(jnp.bfloat16)
    gate_half = w_gate[0]
    up_half = w_up[0]
    down_half = w_down[0]
    half_cap = capacity // 2
    dispatch = buffer.reshape(devices, half_cap, out_width)
    portion = lax.all_to_all(dispatch, "wide", split_axis=0, concat_axis=0, tiled=True)
    item_count = portion.shape[1]
    partner_rows = swapped(portion, "wide", 0)
    both_rows = jnp.concatenate([portion, partner_rows], axis=1)
    flat_rows = both_rows.reshape(-1, out_width)
    gate_part = jnp.dot(flat_rows, gate_half, preferred_element_type=jnp.float32)
    up_part = jnp.dot(flat_rows, up_half, preferred_element_type=jnp.float32)
    hidden = (jax.nn.silu(gate_part) * up_part).astype(jnp.bfloat16)
    product = (
        jnp.dot(hidden, down_half, preferred_element_type=jnp.float32)
        .astype(jnp.bfloat16)
        .reshape(devices, 2 * item_count, out_width)
    )
    from_partner = swapped(product[:, item_count:], "wide", 0)
    joined = (
        product[:, :item_count].astype(jnp.float32) + from_partner.astype(jnp.float32)
    ).astype(jnp.bfloat16)
    answers = lax.all_to_all(joined, "wide", split_axis=0, concat_axis=0, tiled=True)
    slot_result = answers.reshape(slot_count, out_width)
    slot_result = lax.optimization_barrier(slot_result)
    picked = jnp.take(slot_result, target.reshape(-1), axis=0).reshape(
        token_count, top_count, out_width
    )
    return jnp.sum(picked.astype(jnp.float32) * route_weight[:, :, None], axis=1).astype(
        jnp.bfloat16
    )


def solution(mesh):
    placed = (
        P(("grp", "wide"), None),
        P("grp", None),
        P(),
        P(),
        P(),
        P("wide", None),
        P(),
        P(("grp", "wide"), None),
        P(("grp", "wide"), None),
        P("wide", None, None),
        P("wide", None, None),
        P("wide", None, None),
    )
    return jax.shard_map(
        local, mesh=mesh, in_specs=placed, out_specs=P(("grp", "wide"), None), check_vma=False
    )
```

profile of v0, /device:TPU:0, one launch (start us, length us, event | category | flops | bytes accessed | tf_op | source)
XLA Modules:
  0.0 330.1 jit_solution(15057886115371229711)
XLA Ops:
  0.5 2.8 collective-permute-done
  3.3 4.2 %maximum_select_fusion.2 = bf16[576,2048]{1,0:T(8,128)(2,1)} fusion(bf16[288,2048]{1,0:T(8,128)(2,1)} %param.21, bf16[288,2048]{1,0:T(8,128)(2,1)} %collective-permute-done, pred[]{:T(512)S(6)} %eq.44), kind=kLoop, calls=%fused_computation.39 | loop fusion | flops 10616832 | bytes 4718593 | tf_op jit(solution)/shard_map/jit(_where)/select_n | solution.py:21
  7.4 2.9 collective-permute-start.1
  12.0 5.0 %all-to-all-start = ((bf16[16,128,72]{1,2,0:T(8,128)(2,1)}), bf16[16,128,72]{1,2,0:T(8,128)(2,1)S(1)}, u32[]{:S(2)}, u32[]{:S(2)}) async-start(bf16[16,128,72]{1,2,0:T(8,128)(2,1)} %bitcast.98), calls=%async_computation | async-start | bytes 589824 | tf_op jit(solution)/shard_map/all_to_all | solution.py:67
  21.6 43.4 %all-to-all-done = bf16[16,128,72]{1,2,0:T(8,128)(2,1)S(1)} async-done(((bf16[16,128,72]{1,2,0:T(8,128)(2,1)}), bf16[16,128,72]{1,2,0:T(8,128)(2,1)S(1)}, u32[]{:S(2)}, u32[]{:S(2)}) %all-to-all-start) | async-done | bytes 294944 | tf_op jit(solution)/shard_map/all_to_all | solution.py:67
  65.0 6.4 %all-to-all-start.1 = ((bf16[16,128,144]{1,2,0:T(8,128)(2,1)}), bf16[16,128,144]{1,2,0:T(8,128)(2,1)}, u32[]{:S(2)}, u32[]{:S(2)}) async-start(bf16[16,128,144]{1,2,0:T(8,128)(2,1)} %maximum_bitcast_fusion), calls=%async_computation.1 | async-start | bytes 1179648 | tf_op jit(solution)/shard_map/all_to_all | solution.py:68
  73.9 6.7 %maximum_select_fusion.1 = bf16[1152,2048]{1,0:T(8,128)(2,1)} fusion(bf16[576,2048]{1,0:T(8,128)(2,1)} %maximum_select_fusion.2, bf16[576,2048]{1,0:T(8,128)(2,1)} %collective-permute-done.1, pred[]{:T(512)S(6)} %eq.43), kind=kLoop, calls=%fused_computation.29 | loop fusion | flops 21233664 | bytes 9437185 | tf_op jit(solution)/shard_map/jit(_where)/select_n | solution.py:21
  82.5 4.7 %all-to-all-done.1 = bf16[16,128,144]{1,2,0:T(8,128)(2,1)} async-done(((bf16[16,128,144]{1,2,0:T(8,128)(2,1)}), bf16[16,128,144]{1,2,0:T(8,128)(2,1)}, u32[]{:S(2)}, u32[]{:S(2)}) %all-to-all-start.1) | async-done | bytes 589856 | tf_op jit(solution)/shard_map/all_to_all | solution.py:68
  87.7 36.0 %while.23 = (s32[]{:T(128)}, bf16[2,1024,72]{2,1,0:T(8,128)(2,1)}, s32[2]{0:T(128)}, bf16[2,1024,72]{2,1,0:T(8,128)(2,1)}, bf16[1,16,128,144]{2,3,1,0:T(8,128)(2...) while((s32[]{:T(128)}, bf16[2,1024,72]{2,1,0:T(8,128)(2,1)}, ...), condition=%wide.region_6.7_spmd.clone, body=%wide.region_1.6_spmd.clone.sunk | while | flops 156836864 | bytes 9226694 | solution.py:115
  99.3 5.5 %while.24 = (s32[]{:T(128)}, bf16[2,512,72]{1,2,0:T(8,128)(2,1)S(1)}, pred[1024]{0:T(1024)(128)(4,1)}, bf16[2,512,72]{2,1,0:T(8,128)(2,1)}, bf16[1024,144]{1,0:T(8,128)(2,1)S(1)}, /*index=5*/s32[]{:T(128)}) while((s32[]{:T(128)}, bf16[2,512,72]{1,2,0:T(8,128)(2,1)S(1)}, pred[1024]{0:T(1024)(128)(4,1)}, bf16[2,512,72]{2,1,0:T(8,128)(2,1)}, ...), condition=%wide.region_5.5_spmd, body=%wide.region_2.4_spmd.sunk | while | flops 156834816 | bytes 7038065 | solution.py:111
  117.3 5.5 %while.24 = (s32[]{:T(128)}, bf16[2,512,72]{1,2,0:T(8,128)(2,1)S(1)}, pred[1024]{0:T(1024)(128)(4,1)}, bf16[2,512,72]{2,1,0:T(8,128)(2,1)}, bf16[1024,144]{1,0:T(8,128)(2,1)S(1)}, /*index=5*/s32[]{:T(128)}) while((s32[]{:T(128)}, bf16[2,512,72]{1,2,0:T(8,128)(2,1)S(1)}, pred[1024]{0:T(1024)(128)(4,1)}, bf16[2,512,72]{2,1,0:T(8,128)(2,1)}, ...), condition=%wide.region_5.5_spmd, body=%wide.region_2.4_spmd.sunk | while | flops 156834816 | bytes 7038065 | solution.py:111
  125.6 4.4 %all-to-all-start.2 = ((bf16[16,128,72]{1,2,0:T(8,128)(2,1)}), bf16[16,128,72]{1,2,0:T(8,128)(2,1)S(1)}, u32[]{:S(2)}, u32[]{:S(2)}) async-start(bf16[16,128,72]{1,2,0:T(8,128)(2,1)} %copy.92), calls=%async_computation.2 | async-start | bytes 589824 | tf_op jit(solution)/shard_map/all_to_all | solution.py:116
  131.5 61.3 %all-to-all-done.2 = bf16[16,128,72]{1,2,0:T(8,128)(2,1)S(1)} async-done(((bf16[16,128,72]{1,2,0:T(8,128)(2,1)}), bf16[16,128,72]{1,2,0:T(8,128)(2,1)S(1)}, u32[]{:S(2)}, u32[]{:S(2)}) %all-to-all-start.2) | async-done | bytes 294944 | tf_op jit(solution)/shard_map/all_to_all | solution.py:116
  200.8 3.9 %all-to-all-start.3 = ((bf16[16,4,2304]{2,1,0:T(4,128)(2,1)}), bf16[16,4,2304]{2,1,0:T(4,128)(2,1)S(1)}, u32[]{:S(2)}, u32[]{:S(2)}) async-start(bf16[16,4,2304]{2,1,0:T(4,128)(2,1)} %bitcast.15), calls=%async_computation.3 | async-start | bytes 589824 | tf_op jit(solution)/shard_map/all_to_all | solution.py:150
  204.7 10.5 %all-to-all-done.3 = bf16[16,4,2304]{2,1,0:T(4,128)(2,1)S(1)} async-done(((bf16[16,4,2304]{2,1,0:T(4,128)(2,1)}), bf16[16,4,2304]{2,1,0:T(4,128)(2,1)S(1)}, u32[]{:S(2)}, u32[]{:S(2)}) %all-to-all-start.3) | async-done | bytes 294944 | tf_op jit(solution)/shard_map/all_to_all | solution.py:150
  215.2 7.9 %fusion.20 = f32[16,4,2048]{2,0,1:T(8,128)S(1)} fusion(bf16[1152,2048]{1,0:T(8,128)(2,1)} %maximum_select_fusion.1, bf16[1152,2048]{1,0:T(8,128)(2,1)} %collective-permute-done.2, pred[]{:T(512)S(6)} %eq.42, bf16[16,4,2304]{2,1,0:T(4,128)(2,1)S(1)} %all-to-all-done.3), kind=kOutput, calls=%fused_computation.27 | convolution fusion | flops 646447104 | bytes 10256385 | tf_op jit(solution)/shard_map/dot_general | solution.py:153
  224.2 3.6 %all-to-all-start.4 = ((f32[16,4,2048]{2,1,0:T(4,128)}), f32[16,4,2048]{2,1,0:T(4,128)S(1)}, u32[]{:S(2)}, u32[]{:S(2)}) async-start(f32[16,4,2048]{2,1,0:T(4,128)} %copy.95), calls=%async_computation.4 | async-start | bytes 1048576 | tf_op jit(solution)/shard_map/all_to_all | solution.py:156
  228.5 13.7 %all-to-all-done.4 = f32[16,4,2048]{2,1,0:T(4,128)S(1)} async-done(((f32[16,4,2048]{2,1,0:T(4,128)}), f32[16,4,2048]{2,1,0:T(4,128)S(1)}, u32[]{:S(2)}, u32[]{:S(2)}) %all-to-all-start.4) | async-done | bytes 524320 | tf_op jit(solution)/shard_map/all_to_all | solution.py:156
  243.1 28.7 %all_to_all.35 = bf16[16,16,2048]{2,1,0:T(8,128)(2,1)S(1)} all-to-all(bf16[16,16,2048]{2,1,0:T(8,128)(2,1)S(1)} %bitcast.92), channel_id=1, replica_groups=mesh['grp'=2,'wide'=16] {'wide'}, dimensions={0} | all-to-all | bytes 2097152 | tf_op jit(solution)/shard_map/all_to_all | solution.py:181
  279.3 7.7 %convolution_convert_fusion = bf16[512,2048]{1,0:T(8,128)(2,1)} fusion(bf16[1,704,2048]{2,1,0:T(8,128)(2,1)S(1)} %copy-done, f32[512,704]{0,1:T(8,128)} %fusion.24, bf16[512,2048]{1,0:T(8,128)(2,1)} %bitcast.96, bf16[1,2048,704]{1,2,0:T(8,128)(2,1)} %param.25), kind=kOutput, calls=%fused_computation.30 | convolution fusion | flops 2956001280 | bytes 11403264 | tf_op jit(solution)/shard_map/dot_general | solution.py:190
  292.6 4.6 %all-to-all-start.6 = ((bf16[16,16,2048]{2,1,0:T(8,128)(2,1)}), bf16[16,16,2048]{2,1,0:T(8,128)(2,1)}, u32[]{:S(2)}, u32[]{:S(2)}) async-start(bf16[16,16,2048]{2,1,0:T(8,128)(2,1)} %add_convert_fusion), calls=%async_computation.6 | async-start | bytes 2097152 | tf_op jit(solution)/shard_map/all_to_all | solution.py:198
  297.9 22.4 %all-to-all-done.6 = bf16[16,16,2048]{2,1,0:T(8,128)(2,1)} async-done(((bf16[16,16,2048]{2,1,0:T(8,128)(2,1)}), bf16[16,16,2048]{2,1,0:T(8,128)(2,1)}, u32[]{:S(2)}, u32[]{:S(2)}) %all-to-all-start.6) | async-done | bytes 1048608 | tf_op jit(solution)/shard_map/all_to_all | solution.py:198
  320.2 4.2 %gather_fusion = bf16[192,2048]{1,0:T(8,128)(2,1)} fusion(bf16[256,2048]{1,0:T(8,128)(2,1)} %bitcast.24, s32[1024]{0:T(1024)S(1)} %pad_clamp_fusion), kind=kCustom, calls=%fused_computation | custom fusion | bytes 1573632 | tf_op jit(solution)/shard_map/jit(_take)/gather | solution.py:201
  326.6 3.5 %multiply_reduce_fusion = bf16[32,2048]{1,0:T(8,128)(2,1)} fusion(f32[32,6]{1,0:T(8,128)S(1)} %copy.99, bf16[32,6,2048]{2,1,0:T(8,128)(2,1)} %gather.7, pred[32,6]{1,0:T(8,128)(4,1)S(1)} %copy.84), kind=kLoop, calls=%fused_computation.41 | loop fusion | flops 1507328 | bytes 918464 | tf_op jit(solution)/shard_map/reduce_sum | solution.py:204
  (121 shorter events, 72.0 us)
Async XLA Ops:
  0.0 279.3 %copy-start = (bf16[1,704,2048]{2,1,0:T(8,128)(2,1)S(1)}, bf16[1,704,2048]{2,1,0:T(8,128)(2,1)}, u32[]{:S(2)}) copy-start(bf16[1,704,2048]{2,1,0:T(8,128)(2,1)} %param.27) | copy-start | bytes 8650756
  0.0 3.3 collective-permute-start
  0.5 9.9 %copy-start.5 = (bf16[128,3456]{1,0:T(8,128)(2,1)S(1)}, bf16[128,3456]{1,0:T(8,128)(2,1)}, u32[]{:S(2)}) copy-start(bf16[128,3456]{1,0:T(8,128)(2,1)} %param.16) | copy-start | bytes 2654212
  7.4 66.5 %collective-permute-start.1 = (bf16[576,2048]{1,0:T(8,128)(2,1)}, bf16[576,2048]{1,0:T(8,128)(2,1)}, u32[]{:S(2)}, u32[]{:S(2)}) collective-permute-start(bf16[576,2048]{1,0:T(8,128)(2,1)} %maximum_select_fusion.2), channel_id=1, source_target_pairs={{0,2},{1,3},{2,0},{3,1},{4,6},{5,7},{6,4},{7,5},{8,10},{9,11},{10,... | collective-permute-start | bytes 7077896 | tf_op jit(solution)/shard_map/ppermute | solution.py:17
  11.1 61.0 %copy-start.8 = (s32[2,2]{1,0:T(2,128)S(1)}, s32[2,2]{1,0:T(2,128)}, u32[]{:S(2)}) copy-start(s32[2,2]{1,0:T(2,128)} %param.17) | copy-start | bytes 52
  12.0 53.0 %all-to-all-start = ((bf16[16,128,72]{1,2,0:T(8,128)(2,1)}), bf16[16,128,72]{1,2,0:T(8,128)(2,1)S(1)}, u32[]{:S(2)}, u32[]{:S(2)}) async-start(bf16[16,128,72]{1,2,0:T(8,128)(2,1)} %bitcast.98), calls=%async_computation | async-start | bytes 589824 | tf_op jit(solution)/shard_map/all_to_all | solution.py:67
  65.0 22.1 %all-to-all-start.1 = ((bf16[16,128,144]{1,2,0:T(8,128)(2,1)}), bf16[16,128,144]{1,2,0:T(8,128)(2,1)}, u32[]{:S(2)}, u32[]{:S(2)}) async-start(bf16[16,128,144]{1,2,0:T(8,128)(2,1)} %maximum_bitcast_fusion), calls=%async_computation.1 | async-start | bytes 1179648 | tf_op jit(solution)/shard_map/all_to_all | solution.py:68
  80.6 134.6 %collective-permute-start.2 = (bf16[1152,2048]{1,0:T(8,128)(2,1)}, bf16[1152,2048]{1,0:T(8,128)(2,1)}, u32[]{:S(2)}, u32[]{:S(2)}) collective-permute-start(bf16[1152,2048]{1,0:T(8,128)(2,1)} %maximum_select_fusion.1), channel_id=1, source_target_pairs={{0,4},{1,5},{2,6},{3,7},{4,0},{5,1},{6,2},{7,3},{8,12},{9,13},{10,... | collective-permute-start | bytes 14155784 | tf_op jit(solution)/shard_map/ppermute | solution.py:17
  99.3 1.4 copy-start.1
  102.0 1.4 copy-start.1
  117.3 1.4 copy-start.1
  120.0 1.4 copy-start.1
  125.6 67.2 %all-to-all-start.2 = ((bf16[16,128,72]{1,2,0:T(8,128)(2,1)}), bf16[16,128,72]{1,2,0:T(8,128)(2,1)S(1)}, u32[]{:S(2)}, u32[]{:S(2)}) async-start(bf16[16,128,72]{1,2,0:T(8,128)(2,1)} %copy.92), calls=%async_computation.2 | async-start | bytes 589824 | tf_op jit(solution)/shard_map/all_to_all | solution.py:116
  200.8 14.5 %all-to-all-start.3 = ((bf16[16,4,2304]{2,1,0:T(4,128)(2,1)}), bf16[16,4,2304]{2,1,0:T(4,128)(2,1)S(1)}, u32[]{:S(2)}, u32[]{:S(2)}) async-start(bf16[16,4,2304]{2,1,0:T(4,128)(2,1)} %bitcast.15), calls=%async_computation.3 | async-start | bytes 589824 | tf_op jit(solution)/shard_map/all_to_all | solution.py:150
  204.7 23.1 %copy-start.7 = (s32[32,6]{0,1:T(8,128)S(1)}, s32[32,6]{0,1:T(8,128)}, u32[]{:S(2)}) copy-start(s32[32,6]{0,1:T(8,128)} %param.23) | copy-start | bytes 2308
  204.7 23.1 %copy-start.9 = (s32[32,6]{0,1:T(8,128)S(1)}, s32[32,6]{0,1:T(8,128)}, u32[]{:S(2)}) copy-start(s32[32,6]{0,1:T(8,128)} %param.24) | copy-start | bytes 2308
  224.2 18.0 %all-to-all-start.4 = ((f32[16,4,2048]{2,1,0:T(4,128)}), f32[16,4,2048]{2,1,0:T(4,128)S(1)}, u32[]{:S(2)}, u32[]{:S(2)}) async-start(f32[16,4,2048]{2,1,0:T(4,128)} %copy.95), calls=%async_computation.4 | async-start | bytes 1048576 | tf_op jit(solution)/shard_map/all_to_all | solution.py:156
  271.8 4.7 %copy-start.11 = (bf16[1,2048,704]{1,2,0:T(8,128)(2,1)S(1)}, bf16[1,2048,704]{1,2,0:T(8,128)(2,1)}, u32[]{:S(2)}) copy-start(bf16[1,2048,704]{1,2,0:T(8,128)(2,1)} %param.26) | copy-start | bytes 8650756
  271.8 3.1 collective-permute-start.3
  286.9 4.2 %copy-start.2 = (bf16[512,2048]{1,0:T(8,128)(2,1)S(1)}, bf16[512,2048]{1,0:T(8,128)(2,1)}, u32[]{:S(2)}) copy-start(bf16[512,2048]{1,0:T(8,128)(2,1)} %convolution_convert_fusion) | copy-start | bytes 6291460
  288.4 8.9 %copy-start.10 = (pred[32,6]{0,1:T(8,128)(4,1)S(1)}, pred[32,6]{0,1:T(8,128)(4,1)}, u32[]{:S(2)}) copy-start(pred[32,6]{0,1:T(8,128)(4,1)} %get-tuple-element.147) | copy-start | bytes 580
  288.4 9.2 %copy-start.6 = (bf16[2048,8]{0,1:T(8,128)(2,1)S(1)}, bf16[2048,8]{0,1:T(8,128)(2,1)}, u32[]{:S(2)}) copy-start(bf16[2048,8]{0,1:T(8,128)(2,1)} %param.22) | copy-start | bytes 98308
  288.4 2.7 collective-permute-start.4
  292.6 27.6 %all-to-all-start.6 = ((bf16[16,16,2048]{2,1,0:T(8,128)(2,1)}), bf16[16,16,2048]{2,1,0:T(8,128)(2,1)}, u32[]{:S(2)}, u32[]{:S(2)}) async-start(bf16[16,16,2048]{2,1,0:T(8,128)(2,1)} %add_convert_fusion), calls=%async_computation.6 | async-start | bytes 2097152 | tf_op jit(solution)/shard_map/all_to_all | solution.py:198
  (2 other events, 2.1 us)
where the time goes:
time: 333 us; the launch traced here: 330 us
  waiting for transfers between devices  163 us (49%)
  local copies, waits for them, and re-layouts  40.9 us (12%)
  starting transfers between devices  34.3 us (10%)
  matrix products  30 us (9%)
  blocking collectives  28.7 us (9%)
  other arithmetic  27 us (8%)
  loops' own time  5.37 us (2%)
    all_to_all x1, waiting for transfers between devices, local(): lax.all_to_all(attended.reshape(devices, sub_rows, head_dim), 'wide', spl...  61.3 us
    all_to_all x1, waiting for transfers between devices, local(): lax.all_to_all(query_send, 'wide', split_axis=0, concat_axis=0, tiled=True)  43.4 us
    all_to_all x1, blocking collectives, local(): lax.all_to_all(dispatch, 'wide', split_axis=0, concat_axis=0, tiled=True)  28.7 us
    all_to_all x1, waiting for transfers between devices, local(): lax.all_to_all(joined, 'wide', split_axis=0, concat_axis=0, tiled=True)  22.4 us
    all_to_all x1, waiting for transfers between devices, local(): lax.all_to_all(partial_value, 'wide', split_axis=0, concat_axis=0, tiled=...  13.7 us
    select_n x2, other arithmetic, ordered_pair(): jnp.where(upper_bit == 1, jnp.concatenate([partner, own_part], 0), jnp.co...  10.9 us
    all_to_all x1, waiting for transfers between devices, local(): lax.all_to_all(merge_send, 'wide', split_axis=0, concat_axis=0, tiled=True)  10.5 us
    dot_general x1, matrix products, local(): jnp.dot(flat_rows, merge_rows, preferred_element_type=jnp.float32)  7.87 us
  transfers between devices with their start and end apart: 11, of which 9 were waited for; matrix products, arithmetic and copies ran while one was open for 18% of the time, Pallas kernels for 0%

commit v1 on v0

--- a/solution.py
+++ b/solution.py
@@ -1,6 +1,8 @@
 import jax
 import jax.numpy as jnp
 from jax import lax
+from jax.experimental import pallas as pl
+from jax.experimental.pallas import tpu as pltpu
 from jax.sharding import PartitionSpec as P
 
 HEADS = 16
@@ -25,7 +27,7 @@
     )
 
 
-def local(
+def general(
     qkv,
     grid,
     w_out,
@@ -206,6 +208,328 @@
     )
 
 
+BF = jnp.bfloat16
+F32 = jnp.float32
+VMEM = pl.BlockSpec(memory_space=pltpu.VMEM)
+SMEM = pl.BlockSpec(memory_space=pltpu.SMEM)
+HBM = pl.BlockSpec(memory_space=pl.ANY)
+LANES = 128
+MASKED = -1e30
+LOG2E = 1.4426950408889634
+
+
+def params(mib):
+    return pltpu.CompilerParams(vmem_limit_bytes=mib * 2**20)
+
+
+def pieces(value, count):
+    out = []
+    for _ in range(count):
+        piece = value.astype(BF).astype(F32)
+        out.append(piece)
+        value = value - piece
+    return out
+
+
+def pack_kernel(qkv_ref, out_ref):
+    rows, width = qkv_ref.shape
+    tokens = rows // 4
+    peers, parts, _ = out_ref.shape
+    source = lax.broadcasted_iota(jnp.int32, (rows, rows), 0)
+    place = lax.broadcasted_iota(jnp.int32, (rows, rows), 1)
+    order = jnp.where(source == 4 * (place % tokens) + place // tokens, 1.0, 0.0).astype(BF)
+    part = parts // 3
+    third = width // 3
+    for kind in range(3):
+        turned = lax.dot_general(
+            qkv_ref[:, kind * third : (kind + 1) * third],
+            order,
+            (((0,), (0,)), ((), ())),
+            preferred_element_type=F32,
+        ).astype(BF)
+        for peer in range(peers):
+            out_ref[peer, kind * part : (kind + 1) * part, :] = turned[peer * part : (peer + 1) * part]
+
+
+def attend_kernel(x_ref, grid_ref, out_ref):
+    peers, parts, lanes = x_ref.shape
+    part = parts // 3
+    dim = part // 2
+    quarters = 4
+    sides = peers // quarters
+    tokens = lanes // 4
+    clip = lax.axis_index("wide") // peers
+    count = grid_ref[clip, 0] * grid_ref[clip, 1]
+    factor = dim ** (-0.5) * LOG2E
+    keys = jnp.concatenate([x_ref[s, part : 2 * part, :] for s in range(peers)], 1)
+    lane = lax.broadcasted_iota(jnp.int32, (16, peers * lanes), 1)
+    row = lax.broadcasted_iota(jnp.int32, (16, peers * lanes), 0)
+    inner = lane % lanes
+    place = lane // lanes * lanes + 4 * (inner % tokens) + inner // tokens
+    hidden = jnp.where((row == 0) & (place >= count), MASKED, 0.0).astype(BF)
+    keys = jnp.concatenate([keys, hidden], 0).T
+    values = jnp.concatenate([x_ref[s, 2 * part :, :] for s in range(peers)], 1).astype(F32)
+    values = [values[:dim].astype(BF), values[dim:].astype(BF)]
+    ones = jnp.where(lax.broadcasted_iota(jnp.int32, (16, sides * lanes), 0) == 0, 1.0, 0.0).astype(BF)
+    head_row = lax.broadcasted_iota(jnp.int32, (part, sides * lanes), 0) // dim
+    group = lax.broadcasted_iota(jnp.int32, (dim, lanes), 1) // tokens
+    for quarter in range(quarters):
+        query = jnp.concatenate(
+            [x_ref[quarter + quarters * s, :part, :] for s in range(sides)], 1
+        ).astype(F32)
+        mixed = []
+        for head in range(2):
+            own = jnp.concatenate([jnp.where(head_row == head, query, 0.0).astype(BF), ones], 0)
+            scores = jnp.dot(keys, own, preferred_element_type=F32)
+            highest = jnp.max(scores, axis=0, keepdims=True)
+            weights = jnp.exp2(scores * factor - highest * factor)
+            total = jnp.sum(weights, axis=0, keepdims=True)
+            value = jnp.dot(values[head], weights.astype(BF), preferred_element_type=F32) / total
+            mixed += [value[:, s * lanes : (s + 1) * lanes] for s in range(sides)]
+        for position in range(4):
+            block = mixed[position]
+            for g in range(4):
+                if g != position:
+                    shift = (g - position) * tokens % lanes
+                    block = jnp.where(group == g, pltpu.roll(mixed[g], shift, 1), block)
+            out_ref[quarters * position + quarter] = block.astype(BF)
+
+
+def merge_kernel(
+    x_ref, w_out_ref, gain_ref, bias_ref, w0, w1, w2, w3, out_ref, att_ref, w_ref, sems
+):
+    me = lax.axis_index("wide")
+    position, quarter = me // 4, me % 4
+    blocks, dim, lanes = x_ref.shape
+    pairs = blocks // 2
+    depth = w0.shape[0]
+    out_width = w0.shape[1]
+    width = w_out_ref.shape[1]
+    copies = []
+    for k, source in enumerate((w0, w1, w2, w3)):
+        low = (quarter % 2 + k % 2) % 2
+        high = (quarter // 2 + k // 2) % 2
+        spot = pl.multiple_of((2 * high + low) * depth, depth)
+        copies.append(pltpu.make_async_copy(source, w_ref.at[pl.ds(spot, depth), :], sems.at[k]))
+        copies[-1].start()
+    left = lax.broadcasted_iota(jnp.int32, (dim, lanes), 1) < lanes // 2
+    for pair in range(pairs):
+        first, second = x_ref[pair].astype(F32), x_ref[pairs + pair].astype(F32)
+        upper = jnp.where(left, first, pltpu.roll(second, lanes // 2, 1))
+        lower = jnp.where(left, pltpu.roll(first, lanes // 2, 1), second)
+        att_ref[2 * dim * pair : 2 * dim * (pair + 1), :] = jnp.concatenate([upper, lower], 0).astype(BF)
+    mixed = lax.dot_general(
+        att_ref[...], w_out_ref[...], (((0,), (0,)), ((), ())), preferred_element_type=F32
+    )
+    mixed = mixed.astype(BF).astype(F32)
+    centre = jnp.sum(mixed, axis=1, keepdims=True) / width
+    centered = mixed - centre
+    square = jnp.sum(centered * centered, axis=1, keepdims=True)
+    gain, bias = gain_ref[position], bias_ref[position]
+    row = lax.broadcasted_iota(jnp.int32, (16, width), 0)
+    extra = jnp.zeros((16, width), F32)
+    for k, line in enumerate(pieces(gain, 2) + pieces(bias, 2)):
+        extra = jnp.where(row == k, line, extra)
+    left_side = jnp.concatenate([(centered * gain).astype(BF), extra.astype(BF)], 0)
+    lane = lax.broadcasted_iota(jnp.int32, (lanes, LANES), 1)
+    stats = jnp.zeros((lanes, LANES), F32)
+    for k, column in enumerate(pieces(centre, 3) + pieces(square, 3)):
+        stats = jnp.where(lane == k, column, stats)
+    stats = stats.astype(BF)
+    for copy in copies:
+        copy.wait()
+    planes, tokens, _ = out_ref.shape
+    half = tokens // 2
+    step = 2 * LANES
+    shared = [None] * tokens
+    for begin in range(0, out_width, step):
+        part = jnp.dot(left_side, w_ref[:, begin : begin + step], preferred_element_type=F32)
+        for plane in range(planes):
+            out_ref[plane, :, begin : begin + step] = part[plane * tokens : (plane + 1) * tokens].astype(BF)
+        scale = part[lanes : lanes + 1] + part[lanes + 1 : lanes + 2]
+        shift = part[lanes + 2 : lanes + 3] + part[lanes + 3 : lanes + 4]
+        for k in range(step // LANES):
+            shared[begin // LANES + k] = scale[:, k * LANES : (k + 1) * LANES]
+            shared[half + begin // LANES + k] = shift[:, k * LANES : (k + 1) * LANES]
+    shared = jnp.concatenate(shared, 0).astype(BF)
+    for plane in range(planes):
+        out_ref[plane, :, out_width : out_width + LANES] = shared
+        out_ref[plane, :, out_width + LANES :] = stats[plane * tokens : (plane + 1) * tokens]
+
+
+def route_kernel(x_ref, router_ref, ids_ref, out_ref, *, merge_width, experts):
+    planes, tokens, _ = x_ref.shape
+    out_width = out_ref.shape[1] - LANES
+    half = tokens // 2
+    stats = [x_ref[p, :, out_width + LANES :].astype(F32) for p in range(planes)]
+    shared = [x_ref[p, :, out_width : out_width + LANES].astype(F32) for p in range(planes)]
+    centres = [s[:, 0:1] + s[:, 1:2] + s[:, 2:3] for s in stats]
+    squares = [s[:, 3:4] + s[:, 4:5] + s[:, 5:6] for s in stats]
+    mean = sum(centres) / planes
+    offsets = [c - mean for c in centres]
+    spread = sum(q + (merge_width // planes) * (o * o) for q, o in zip(squares, offsets)) / merge_width
+    inverse = lax.rsqrt(spread + norm_eps)
+    bias = sum(shared)
+    for k in range(out_width // LANES):
+        cut = slice(k * LANES, (k + 1) * LANES)
+        total = sum(x_ref[p, :, cut].astype(F32) for p in range(planes))
+        total += sum(offsets[p] * shared[p][k : k + 1] for p in range(planes))
+        out_ref[:, cut] = (total * inverse + bias[half + k : half + k + 1]).astype(BF)
+    logits = jnp.dot(out_ref[:, :out_width], router_ref[...], preferred_element_type=F32)
+    lane = lax.broadcasted_iota(jnp.int32, (tokens, LANES), 1)
+    expert = lane % experts
+    chosen = lane < 0
+    for k in range(ids_ref.shape[1]):
+        chosen = chosen | (ids_ref[:, k : k + 1] == expert)
+    gates = jnp.where(chosen & (lane < 2 * experts), 1.0 / (1.0 + jnp.exp(-logits)), 0.0)
+    total = jnp.sum(jnp.where(lane < experts, gates, 0.0), axis=1, keepdims=True)
+    weight = route_scale * gates / total
+    high, low = pieces(weight, 2)
+    out_ref[:, out_width:] = jnp.where(lane < experts, high, low).astype(BF)
+
+
+def expert_kernel(x_ref, gate_ref, up_ref, down_ref, out_ref, *, experts):
+    blocks, tokens, width = out_ref.shape
+    expert = lax.axis_index("wide") // 2
+    rows = x_ref.shape[0]
+    inputs = x_ref[:, :width]
+    lane = lax.broadcasted_iota(jnp.int32, (rows, LANES), 1)
+    weight = jnp.where(
+        (lane == expert) | (lane == expert + experts), x_ref[:, width:].astype(F32), 0.0
+    )
+    weight = jnp.sum(weight, axis=1, keepdims=True)
+    gate = jnp.dot(inputs, gate_ref[0], preferred_element_type=F32)
+    up = jnp.dot(inputs, up_ref[0], preferred_element_type=F32)
+    hidden = (gate / (1.0 + jnp.exp(-gate)) * up).astype(BF)
+    step = 4 * LANES
+    for begin in range(0, width, step):
+        product = jnp.dot(hidden, down_ref[0, :, begin : begin + step], preferred_element_type=F32)
+        product = (product * weight).astype(BF)
+        for block in range(blocks):
+            out_ref[block, :, begin : begin + step] = product[block * tokens : (block + 1) * tokens]
+
+
+def crossed(value, mask):
+    pairs = [(source, source ^ mask) for source in range(lax.axis_size("wide"))]
+    return lax.ppermute(value, "wide", pairs)
+
+
+def local(
+    qkv, grid, w_out, ln_gain, ln_bias, w_merge, w_router, expert_ids, slot_pos, w_gate, w_up, w_down
+):
+    devices = lax.axis_size("wide")
+    rows = qkv.shape[0]
+    vit_width = w_out.shape[0]
+    experts = w_router.shape[1]
+    out_width = w_merge.shape[1]
+    tokens = rows // 4
+    peers = devices // CLIPS
+    suits = (
+        devices == HEADS
+        and peers == 8
+        and rows == LANES
+        and devices == 2 * experts
+        and 2 * out_width == tokens * LANES
+        and 4 * w_merge.shape[0] == vit_width
+    )
+    if not suits:
+        return general(
+            qkv, grid, w_out, ln_gain, ln_bias, w_merge, w_router, expert_ids, slot_pos, w_gate, w_up, w_down
+        )
+    part = vit_width // peers
+    dim = vit_width // HEADS
+    packed = pl.pallas_call(
+        pack_kernel,
+        out_shape=jax.ShapeDtypeStruct((peers, 3 * part, rows), BF),
+        in_specs=[VMEM],
+        out_specs=VMEM,
+        compiler_params=params(32),
+    )(qkv)
+    clips = [[c * peers + i for i in range(peers)] for c in range(CLIPS)]
+    gathered = lax.all_to_all(
+        packed, "wide", split_axis=0, concat_axis=0, tiled=True, axis_index_groups=clips
+    )
+    gathered, held = lax.optimization_barrier((gathered, w_merge))
+    held_y = crossed(held, 2)
+    held_c = crossed(held, 1)
+    held_yc = crossed(held_y, 1)
+    attended = pl.pallas_call(
+        attend_kernel,
+        out_shape=jax.ShapeDtypeStruct((devices, dim, rows), BF),
+        in_specs=[VMEM, SMEM],
+        out_specs=VMEM,
+        compiler_params=params(48),
+    )(gathered, grid)
+    returned = lax.all_to_all(attended, "wide", split_axis=0, concat_axis=0, tiled=True)
+    planes = devices // 4
+    message = out_width + 2 * LANES
+    partial = pl.pallas_call(
+        merge_kernel,
+        out_shape=jax.ShapeDtypeStruct((planes, tokens, message), BF),
+        in_specs=[VMEM, VMEM, VMEM, VMEM, HBM, HBM, HBM, HBM],
+        out_specs=VMEM,
+        scratch_shapes=[
+            pltpu.VMEM((vit_width, rows), BF),
+            pltpu.VMEM((vit_width, out_width), BF),
+            pltpu.SemaphoreType.DMA((4,)),
+        ],
+        compiler_params=params(48),
+    )(
+        returned,
+        w_out,
+        ln_gain.reshape(4, 1, vit_width),
+        ln_bias.reshape(4, 1, vit_width),
+        held,
+        held_c,
+        held_y,
+        held_yc,
+    )
+    columns = [[q + 4 * i for i in range(planes)] for q in range(4)]
+    summed = lax.all_to_all(
+        partial, "wide", split_axis=0, concat_axis=0, tiled=True, axis_index_groups=columns
+    )
+    router = jnp.concatenate(
+        [w_router, w_router, jnp.zeros((out_width, LANES - 2 * experts), BF)], 1
+    )
+    routed = pl.pallas_call(
+        lambda *refs: route_kernel(*refs, merge_width=4 * vit_width, experts=experts),
+        out_shape=jax.ShapeDtypeStruct((tokens, out_width + LANES), BF),
+        in_specs=[VMEM, VMEM, VMEM],
+        out_specs=VMEM,
+        compiler_params=params(32),
+    )(summed, router, expert_ids)
+    along = (4, 8, 12)
+    near = [routed] + [crossed(routed, mask) for mask in along]
+    far = [crossed(block, 2) for block in near]
+    own_plane = jnp.concatenate(near + far, 0)
+    other_plane = crossed(own_plane, 1)
+
+    def experts_of(block):
+        return pl.pallas_call(
+            lambda *refs: expert_kernel(*refs, experts=experts),
+            out_shape=jax.ShapeDtypeStruct((devices // 2, tokens, out_width), BF),
+            in_specs=[VMEM, VMEM, VMEM, VMEM],
+            out_specs=VMEM,
+            compiler_params=params(48),
+        )(block, w_gate, w_up, w_down)
+
+    own_out = experts_of(own_plane)
+    other_out = experts_of(other_plane)
+    total = (own_out.astype(F32) + crossed(other_out, 1).astype(F32)).astype(BF)
+    total = total.reshape(2, planes, tokens, out_width)
+    cut = out_width // 2
+    first, second = total[..., :cut], total[..., cut:]
+    first_y = crossed(first[1], 2)
+    second_z = [crossed(second[:, i], mask) for i, mask in enumerate(along, 1)]
+    first = (first[0].astype(F32) + first_y.astype(F32)).astype(BF)
+    second = second[:, 0].astype(F32) + sum(block.astype(F32) for block in second_z)
+    second_y = crossed(second[1].astype(BF), 2)
+    first_z = [crossed(first[i], mask) for i, mask in enumerate(along, 1)]
+    first = first[0].astype(F32) + sum(block.astype(F32) for block in first_z)
+    second = second[0] + second_y.astype(F32)
+    return jnp.concatenate([first, second], 1).astype(BF)
+
+
 def solution(mesh):
     placed = (
         P(("grp", "wide"), None),

time: 333 us -> 170 us (0.51)
  waiting for transfers between devices: 163 us -> 73.9 us
  matrix products: 30 us -> 0 us
  other arithmetic: 27 us -> 1.56 us
  Pallas kernels: 0 us -> 24.9 us
  local copies, waits for them, and re-layouts: 40.9 us -> 21.3 us
  blocking collectives: 28.7 us -> 18.7 us
  starting transfers between devices: 34.3 us -> 28.8 us
  loops' own time: 5.37 us -> 0 us
    all_to_all x6 -> x2, waiting for transfers between devices: 156 us -> 23.1 us  [the longest x1 15.2 us: local(): lax.all_to_all(partial, 'wide', split_axis=0, concat_axis=0, tiled=True,...]
    ppermute x5 -> x20, waiting for transfers between devices: 7.39 us -> 50.7 us  [crossed(): return lax.ppermute(value, 'wide', pairs)]
    dot_general x14 -> x0, matrix products: 30 us -> none  [the longest x1 7.87 us: local(): jnp.dot(flat_rows, merge_rows, preferred_element_type=jnp.float32)]
    pallas_call x0 -> x6, Pallas kernels: none -> 24.9 us  [the longest x2 11.6 us: experts_of(): pl.pallas_call(lambda *refs: expert_kernel(*refs, experts=experts), out_s...]
    all_to_all x6 -> x2, starting transfers between devices: 27.9 us -> 8.33 us  [the longest x1 4.67 us: local(): lax.all_to_all(attended, 'wide', split_axis=0, concat_axis=0, tiled=True)]
    ppermute x5 -> x20, starting transfers between devices: 6.4 us -> 20.5 us  [crossed(): return lax.ppermute(value, 'wide', pairs)]
    dynamic_slice x10 -> x0, local copies, waits for them, and re-layouts: 14 us -> none  [the longest x4 5.7 us: attend(): lax.dynamic_slice_in_dim(key_rows, clip_index * per_clip, per_clip, 1)]
    unnamed x27 -> x29, local copies, waits for them, and re-layouts: 6.84 us -> 17.8 us
  transfers between devices with their start and end apart: 11 -> 22, of which waited for: 9 -> 11; matrix products, arithmetic and copies ran while one was open for 18% -> 10% of each run, Pallas kernels for 0% -> 7%
where the time goes in v1:
time: 170 us; the launch traced here: 169 us
  waiting for transfers between devices  73.9 us (43%)
  starting transfers between devices  28.8 us (17%)
  Pallas kernels  24.9 us (15%)
  local copies, waits for them, and re-layouts  21.3 us (13%)
  blocking collectives  18.7 us (11%)
    ppermute x20, waiting for transfers between devices, crossed(): return lax.ppermute(value, 'wide', pairs)  50.7 us
    ppermute x20, starting transfers between devices, crossed(): return lax.ppermute(value, 'wide', pairs)  20.5 us
    all_to_all x1, blocking collectives, local(): lax.all_to_all(packed, 'wide', split_axis=0, concat_axis=0, tiled=True, a...  18.7 us
    unnamed x29, local copies, waits for them, and re-layouts  17.8 us
    all_to_all x1, waiting for transfers between devices, local(): lax.all_to_all(partial, 'wide', split_axis=0, concat_axis=0, tiled=True,...  15.2 us
    pallas_call x2, Pallas kernels, experts_of(): pl.pallas_call(lambda *refs: expert_kernel(*refs, experts=experts), out_s...  11.6 us
    all_to_all x1, waiting for transfers between devices, local(): lax.all_to_all(attended, 'wide', split_axis=0, concat_axis=0, tiled=True)  7.93 us
    pallas_call x1, Pallas kernels, local(): pl.pallas_call(attend_kernel, out_shape=jax.ShapeDtypeStruct((devices, di...  6.52 us
  transfers between devices with their start and end apart: 22, of which 11 were waited for; matrix products, arithmetic and copies ran while one was open for 10% of the time, Pallas kernels for 7%

profile of v1, /device:TPU:0, one launch (start us, length us, event | category | flops | bytes accessed | tf_op | source)
XLA Modules:
  0.0 169.4 jit_solution(12604909658419633035)
XLA Ops:
  1.6 18.7 %all_to_all.15.x_ref = bf16[8,432,128]{2,1,0:T(8,128)(2,1)S(1)} all-to-all(bf16[8,432,128]{2,1,0:T(8,128)(2,1)S(1)} %shard_map.109), channel_id=1, replica_groups={{0,1,2,3,4,5,6,7},{8,9,10,11,12,13,14,15},{16,17,18,19,20,21,22,23},{24..., dimensions={0} | all-to-all | bytes 1769472 | tf_op jit(solution)/shard_map/all_to_all | solution.py:449
  21.1 26.7 %collective-permute-done.1.w2 = bf16[288,2048]{1,0:T(8,128)(2,1)S(1)} collective-permute-done((bf16[288,2048]{1,0:T(8,128)(2,1)S(1)}, bf16[288,2048]{1,0:T(8,128)(2,1)S(1)}, u32[]{:S(2)}, u32[]{:S(2)}) %collective-permute-start.1) | collective-permute-done | bytes 1179680 | tf_op jit(solution)/shard_map/ppermute | solution.py:414
  47.9 6.5 %shard_map.110 = bf16[16,72,128]{2,1,0:T(8,128)(2,1)S(1)} custom-call(bf16[8,432,128]{2,1,0:T(8,128)(2,1)S(1)} %all_to_all.15.x_ref, s32[2,2]{1,0:T(2,128)S(1)} %copy-done.6), custom_call_target="tpu_custom_call" | custom-call | tf_op jit(solution)/shard_map/pallas_call | solution.py:456
  55.1 4.7 %all-to-all-start.1 = ((bf16[16,72,128]{2,1,0:T(8,128)(2,1)}), bf16[16,72,128]{2,1,0:T(8,128)(2,1)}, u32[]{:S(2)}, u32[]{:S(2)}) async-start(bf16[16,72,128]{2,1,0:T(8,128)(2,1)} %copy-done.2), calls=%async_computation.1 | async-start | bytes 589824 | tf_op jit(solution)/shard_map/all_to_all | solution.py:463
  62.5 7.9 %all-to-all-done.1.x_ref = bf16[16,72,128]{2,1,0:T(8,128)(2,1)} async-done(((bf16[16,72,128]{2,1,0:T(8,128)(2,1)}), bf16[16,72,128]{2,1,0:T(8,128)(2,1)}, u32[]{:S(2)}, u32[]{:S(2)}) %all-to-all-start.1) | async-done | bytes 294944 | tf_op jit(solution)/shard_map/all_to_all | solution.py:463
  71.9 5.9 %shard_map.111 = bf16[4,32,2304]{2,1,0:T(8,128)(2,1)} custom-call(bf16[16,72,128]{2,1,0:T(8,128)(2,1)} %all-to-all-done.1.x_ref, bf16[1152,1152]{1,0:T(8,128)(2,1)} %w_out_ref.1, f32[4,1,1152]{2,1,0:T(1,128)S(1)} %copy-done.4, f32[4,1,1152]{2,1,0:T(1,128)S(1)} %copy-done.5, bf16[288,2048]{1,0:T(8,128)(2,1)S(1)} %copy-done.1, ...), custom_call_target="tpu_custom_call" | custom-call | tf_op jit(solution)/shard_map/pallas_call | solution.py:466
  77.8 3.7 %all-to-all-start.2 = ((bf16[4,32,2304]{2,1,0:T(8,128)(2,1)}), bf16[4,32,2304]{2,1,0:T(8,128)(2,1)S(1)}, u32[]{:S(2)}, u32[]{:S(2)}) async-start(bf16[4,32,2304]{2,1,0:T(8,128)(2,1)} %shard_map.111), calls=%async_computation.2 | async-start | bytes 1179648 | tf_op jit(solution)/shard_map/all_to_all | solution.py:488
  82.2 15.2 %all-to-all-done.2.refs_0_ = bf16[4,32,2304]{2,1,0:T(8,128)(2,1)S(1)} async-done(((bf16[4,32,2304]{2,1,0:T(8,128)(2,1)}), bf16[4,32,2304]{2,1,0:T(8,128)(2,1)S(1)}, u32[]{:S(2)}, u32[]{:S(2)}) %all-to-all-start.2) | async-done | bytes 589856 | tf_op jit(solution)/shard_map/all_to_all | solution.py:488
  100.3 2.9 %collective-permute-start.3 = (bf16[32,2176]{1,0:T(8,128)(2,1)S(1)}, bf16[32,2176]{1,0:T(8,128)(2,1)S(1)}, u32[]{:S(2)}, u32[]{:S(2)}) collective-permute-start(bf16[32,2176]{1,0:T(8,128)(2,1)S(1)} %shard_map.112), channel_id=1, source_target_pairs={{0,4},{1,5},{2,6},{3,7},{4,0},{5,1},{6,2},{7,3},{8,12},{9,13},{10,... | collective-permute-start | bytes 417800 | tf_op jit(solution)/shard_map/ppermute | solution.py:414
  103.9 3.4 %collective-permute-done.5 = bf16[32,2176]{1,0:T(8,128)(2,1)S(1)} collective-permute-done((bf16[32,2176]{1,0:T(8,128)(2,1)S(1)}, bf16[32,2176]{1,0:T(8,128)(2,1)S(1)}, u32[]{:S(2)}, u32[]{:S(2)}) %collective-permute-start.5) | collective-permute-done | bytes 139296 | tf_op jit(solution)/shard_map/ppermute | solution.py:414
  108.6 3.1 %collective-permute-done.4 = bf16[32,2176]{1,0:T(8,128)(2,1)S(1)} collective-permute-done((bf16[32,2176]{1,0:T(8,128)(2,1)S(1)}, bf16[32,2176]{1,0:T(8,128)(2,1)S(1)}, u32[]{:S(2)}, u32[]{:S(2)}) %collective-permute-start.4) | collective-permute-done | bytes 139296 | tf_op jit(solution)/shard_map/ppermute | solution.py:414
  116.4 3.9 %collective-permute-done.7 = bf16[32,2176]{1,0:T(8,128)(2,1)S(1)} collective-permute-done((bf16[32,2176]{1,0:T(8,128)(2,1)S(1)}, bf16[32,2176]{1,0:T(8,128)(2,1)S(1)}, u32[]{:S(2)}, u32[]{:S(2)}) %collective-permute-start.7) | collective-permute-done | bytes 139296 | tf_op jit(solution)/shard_map/ppermute | solution.py:414
  122.3 4.6 %copy.15.refs_1_ = bf16[1,2048,704]{2,1,0:T(8,128)(2,1)} copy(bf16[1,2048,704]{1,2,0:T(8,128)(2,1)} %param.20) | data formatting | bytes 5767168 | tf_op args[9]
  126.9 4.8 %copy.16.refs_2_ = bf16[1,2048,704]{2,1,0:T(8,128)(2,1)} copy(bf16[1,2048,704]{1,2,0:T(8,128)(2,1)} %param.21) | data formatting | bytes 5767168 | tf_op args[10]
  131.7 5.8 %shard_map.114 = bf16[8,32,2048]{2,1,0:T(8,128)(2,1)S(1)} custom-call(bf16[256,2176]{1,0:T(8,128)(2,1)} %collective-permute-done.10.refs_0_, bf16[1,2048,704]{2,1,0:T(8,128)(2,1)} %copy.15.refs_1_, bf16[1,2048,704]{2,1,0:T(8,128)(2,1)} %copy.16.refs_2_, bf16[1,704,2048]{2,1,0:T(8,128)(2,1)S(1)} %copy-done), custom_call_target="tpu_custom_call" | custom-call | tf_op jit(solution)/shard_map/pallas_call | solution.py:508
  138.0 5.8 %shard_map.113 = bf16[8,32,2048]{2,1,0:T(8,128)(2,1)S(1)} custom-call(bf16[256,2176]{1,0:T(8,128)(2,1)} %constant_dynamic-update-slice_fusion.refs_0_, bf16[1,2048,704]{2,1,0:T(8,128)(2,1)} %copy.15.refs_1_, bf16[1,2048,704]{2,1,0:T(8,128)(2,1)} %copy.16.refs_2_, bf16[1,704,2048]{2,1,0:T(8,128)(2,1)S(1)} %copy-done), custom_call_target="tpu_custom_call" | custom-call | tf_op jit(solution)/shard_map/pallas_call | solution.py:508
  144.3 2.3 %collective-permute-start.17 = (bf16[2,32,1024]{2,1,0:T(8,128)(2,1)S(1)}, bf16[2,32,1024]{2,1,0:T(8,128)(2,1)S(1)}, u32[]{:S(2)}, u32[]{:S(2)}) collective-permute-start(bf16[2,32,1024]{2,1,0:T(8,128)(2,1)S(1)} %get-tuple-element.10), channel_id=1, source_target_pairs={{0,8},{1,9},{2,10},{3,11},{4,12},{5,13},{6,14},{7,15},{8,0},{9,1},... | collective-permute-start | bytes 393224 | tf_op jit(solution)/shard_map/ppermute | solution.py:414
  146.6 2.1 %collective-permute-start.18 = (bf16[2,32,1024]{2,1,0:T(8,128)(2,1)S(1)}, bf16[2,32,1024]{2,1,0:T(8,128)(2,1)S(1)}, u32[]{:S(2)}, u32[]{:S(2)}) collective-permute-start(bf16[2,32,1024]{2,1,0:T(8,128)(2,1)S(1)} %get-tuple-element.11), channel_id=1, source_target_pairs={{0,12},{1,13},{2,14},{3,15},{4,8},{5,9},{6,10},{7,11},{8,4},{9,5},... | collective-permute-start | bytes 393224 | tf_op jit(solution)/shard_map/ppermute | solution.py:414
  149.5 2.1 %collective-permute-done.16 = bf16[2,32,1024]{2,1,0:T(8,128)(2,1)S(1)} collective-permute-done((bf16[2,32,1024]{2,1,0:T(8,128)(2,1)S(1)}, bf16[2,32,1024]{2,1,0:T(8,128)(2,1)S(1)}, u32[]{:S(2)}, u32[]{:S(2)}) %collective-permute-start.16) | collective-permute-done | bytes 131104 | tf_op jit(solution)/shard_map/ppermute | solution.py:414
  151.6 5.7 %collective-permute-done.17 = bf16[2,32,1024]{2,1,0:T(8,128)(2,1)S(1)} collective-permute-done((bf16[2,32,1024]{2,1,0:T(8,128)(2,1)S(1)}, bf16[2,32,1024]{2,1,0:T(8,128)(2,1)S(1)}, u32[]{:S(2)}, u32[]{:S(2)}) %collective-permute-start.17) | collective-permute-done | bytes 131104 | tf_op jit(solution)/shard_map/ppermute | solution.py:414
  158.2 2.5 %collective-permute-start.13 = (bf16[32,1024]{1,0:T(8,128)(2,1)S(1)}, bf16[32,1024]{1,0:T(8,128)(2,1)S(1)}, u32[]{:S(2)}, u32[]{:S(2)}) collective-permute-start(bf16[32,1024]{1,0:T(8,128)(2,1)S(1)} %get-tuple-element.12), channel_id=1, source_target_pairs={{0,4},{1,5},{2,6},{3,7},{4,0},{5,1},{6,2},{7,3},{8,12},{9,13},{10,... | collective-permute-start | bytes 196616 | tf_op jit(solution)/shard_map/ppermute | solution.py:414
  160.7 2.1 %collective-permute-start.15 = (bf16[32,1024]{1,0:T(8,128)(2,1)S(1)}, bf16[32,1024]{1,0:T(8,128)(2,1)S(1)}, u32[]{:S(2)}, u32[]{:S(2)}) collective-permute-start(bf16[32,1024]{1,0:T(8,128)(2,1)S(1)} %get-tuple-element.13), channel_id=1, source_target_pairs={{0,12},{1,13},{2,14},{3,15},{4,8},{5,9},{6,10},{7,11},{8,4},{9,5},... | collective-permute-start | bytes 196616 | tf_op jit(solution)/shard_map/ppermute | solution.py:414
  163.1 3.7 %collective-permute-done.15 = bf16[32,1024]{1,0:T(8,128)(2,1)S(1)} collective-permute-done((bf16[32,1024]{1,0:T(8,128)(2,1)S(1)}, bf16[32,1024]{1,0:T(8,128)(2,1)S(1)}, u32[]{:S(2)}, u32[]{:S(2)}) %collective-permute-start.15) | collective-permute-done | bytes 65568 | tf_op jit(solution)/shard_map/ppermute | solution.py:414
  166.8 1.8 %collective-permute-done.14 = bf16[32,1024]{1,0:T(8,128)(2,1)S(1)} collective-permute-done((bf16[32,1024]{1,0:T(8,128)(2,1)S(1)}, bf16[32,1024]{1,0:T(8,128)(2,1)S(1)}, u32[]{:S(2)}, u32[]{:S(2)}) %collective-permute-start.14) | collective-permute-done | bytes 65568 | tf_op jit(solution)/shard_map/ppermute | solution.py:414
  (72 shorter events, 23.2 us)
Async XLA Ops:
  1.6 18.7 %copy-start.1 = (bf16[288,2048]{1,0:T(8,128)(2,1)S(1)}, bf16[288,2048]{1,0:T(8,128)(2,1)}, u32[]{:S(2)}) copy-start(bf16[288,2048]{1,0:T(8,128)(2,1)} %w0) | copy-start | bytes 3538948
  1.6 46.2 %copy-start.6 = (s32[2,2]{1,0:T(2,128)S(1)}, s32[2,2]{1,0:T(2,128)}, u32[]{:S(2)}) copy-start(s32[2,2]{1,0:T(2,128)} %grid_ref.1) | copy-start | bytes 52
  20.3 27.6 %collective-permute-start.1 = (bf16[288,2048]{1,0:T(8,128)(2,1)S(1)}, bf16[288,2048]{1,0:T(8,128)(2,1)S(1)}, u32[]{:S(2)}, u32[]{:S(2)}) collective-permute-start(bf16[288,2048]{1,0:T(8,128)(2,1)S(1)} %copy-done.1), channel_id=1, source_target_pairs={{0,2},{1,3},{2,0},{3,1},{4,6},{5,7},{6,4},{7,5},{8,10},{9,11},{10,... | collective-permute-start | bytes 3538952 | tf_op jit(solution)/shard_map/ppermute | solution.py:414
  21.1 49.3 %collective-permute-start = (bf16[288,2048]{1,0:T(8,128)(2,1)S(1)}, bf16[288,2048]{1,0:T(8,128)(2,1)S(1)}, u32[]{:S(2)}, u32[]{:S(2)}) collective-permute-start(bf16[288,2048]{1,0:T(8,128)(2,1)S(1)} %copy-done.1), channel_id=1, source_target_pairs={{0,1},{1,0},{2,3},{3,2},{4,5},{5,4},{6,7},{7,6},{8,9},{9,8},{10,11... | collective-permute-start | bytes 3538952 | tf_op jit(solution)/shard_map/ppermute | solution.py:414
  47.9 22.6 %collective-permute-start.2 = (bf16[288,2048]{1,0:T(8,128)(2,1)S(1)}, bf16[288,2048]{1,0:T(8,128)(2,1)}, u32[]{:S(2)}, u32[]{:S(2)}) collective-permute-start(bf16[288,2048]{1,0:T(8,128)(2,1)S(1)} %collective-permute-done.1.w2), channel_id=1, source_target_pairs={{0,1},{1,0},{2,3},{3,2},{4,5},{5,4},{6,7},{7,6},{8,9},{9,8},{10,11... | collective-permute-start | bytes 3538952 | tf_op jit(solution)/shard_map/ppermute | solution.py:414
  55.1 15.3 %all-to-all-start.1 = ((bf16[16,72,128]{2,1,0:T(8,128)(2,1)}), bf16[16,72,128]{2,1,0:T(8,128)(2,1)}, u32[]{:S(2)}, u32[]{:S(2)}) async-start(bf16[16,72,128]{2,1,0:T(8,128)(2,1)} %copy-done.2), calls=%async_computation.1 | async-start | bytes 589824 | tf_op jit(solution)/shard_map/all_to_all | solution.py:463
  77.8 19.7 %all-to-all-start.2 = ((bf16[4,32,2304]{2,1,0:T(8,128)(2,1)}), bf16[4,32,2304]{2,1,0:T(8,128)(2,1)S(1)}, u32[]{:S(2)}, u32[]{:S(2)}) async-start(bf16[4,32,2304]{2,1,0:T(8,128)(2,1)} %shard_map.111), calls=%async_computation.2 | async-start | bytes 1179648 | tf_op jit(solution)/shard_map/all_to_all | solution.py:488
  98.0 17.7 %collective-permute-start.6 = (bf16[32,2176]{1,0:T(8,128)(2,1)S(1)}, bf16[32,2176]{1,0:T(8,128)(2,1)S(1)}, u32[]{:S(2)}, u32[]{:S(2)}) collective-permute-start(bf16[32,2176]{1,0:T(8,128)(2,1)S(1)} %shard_map.112), channel_id=1, source_target_pairs={{0,2},{1,3},{2,0},{3,1},{4,6},{5,7},{6,4},{7,5},{8,10},{9,11},{10,... | collective-permute-start | bytes 417800 | tf_op jit(solution)/shard_map/ppermute | solution.py:414
  98.9 8.5 %collective-permute-start.5 = (bf16[32,2176]{1,0:T(8,128)(2,1)S(1)}, bf16[32,2176]{1,0:T(8,128)(2,1)S(1)}, u32[]{:S(2)}, u32[]{:S(2)}) collective-permute-start(bf16[32,2176]{1,0:T(8,128)(2,1)S(1)} %shard_map.112), channel_id=1, source_target_pairs={{0,12},{1,13},{2,14},{3,15},{4,8},{5,9},{6,10},{7,11},{8,4},{9,5},... | collective-permute-start | bytes 417800 | tf_op jit(solution)/shard_map/ppermute | solution.py:414
  100.3 11.4 %collective-permute-start.4 = (bf16[32,2176]{1,0:T(8,128)(2,1)S(1)}, bf16[32,2176]{1,0:T(8,128)(2,1)S(1)}, u32[]{:S(2)}, u32[]{:S(2)}) collective-permute-start(bf16[32,2176]{1,0:T(8,128)(2,1)S(1)} %shard_map.112), channel_id=1, source_target_pairs={{0,8},{1,9},{2,10},{3,11},{4,12},{5,13},{6,14},{7,15},{8,0},{9,1},... | collective-permute-start | bytes 417800 | tf_op jit(solution)/shard_map/ppermute | solution.py:414
  100.3 12.0 %collective-permute-start.3 = (bf16[32,2176]{1,0:T(8,128)(2,1)S(1)}, bf16[32,2176]{1,0:T(8,128)(2,1)S(1)}, u32[]{:S(2)}, u32[]{:S(2)}) collective-permute-start(bf16[32,2176]{1,0:T(8,128)(2,1)S(1)} %shard_map.112), channel_id=1, source_target_pairs={{0,4},{1,5},{2,6},{3,7},{4,0},{5,1},{6,2},{7,3},{8,12},{9,13},{10,... | collective-permute-start | bytes 417800 | tf_op jit(solution)/shard_map/ppermute | solution.py:414
  107.3 14.3 %collective-permute-start.9 = (bf16[32,2176]{1,0:T(8,128)(2,1)S(1)}, bf16[32,2176]{1,0:T(8,128)(2,1)S(1)}, u32[]{:S(2)}, u32[]{:S(2)}) collective-permute-start(bf16[32,2176]{1,0:T(8,128)(2,1)S(1)} %collective-permute-done.5), channel_id=1, source_target_pairs={{0,2},{1,3},{2,0},{3,1},{4,6},{5,7},{6,4},{7,5},{8,10},{9,11},{10,... | collective-permute-start | bytes 417800 | tf_op jit(solution)/shard_map/ppermute | solution.py:414
  111.7 9.2 %collective-permute-start.8 = (bf16[32,2176]{1,0:T(8,128)(2,1)S(1)}, bf16[32,2176]{1,0:T(8,128)(2,1)S(1)}, u32[]{:S(2)}, u32[]{:S(2)}) collective-permute-start(bf16[32,2176]{1,0:T(8,128)(2,1)S(1)} %collective-permute-done.4), channel_id=1, source_target_pairs={{0,2},{1,3},{2,0},{3,1},{4,6},{5,7},{6,4},{7,5},{8,10},{9,11},{10,... | collective-permute-start | bytes 417800 | tf_op jit(solution)/shard_map/ppermute | solution.py:414
  112.3 7.9 %collective-permute-start.7 = (bf16[32,2176]{1,0:T(8,128)(2,1)S(1)}, bf16[32,2176]{1,0:T(8,128)(2,1)S(1)}, u32[]{:S(2)}, u32[]{:S(2)}) collective-permute-start(bf16[32,2176]{1,0:T(8,128)(2,1)S(1)} %collective-permute-done.3), channel_id=1, source_target_pairs={{0,2},{1,3},{2,0},{3,1},{4,6},{5,7},{6,4},{7,5},{8,10},{9,11},{10,... | collective-permute-start | bytes 417800 | tf_op jit(solution)/shard_map/ppermute | solution.py:414
  122.3 9.4 %collective-permute-start.10 = (bf16[256,2176]{1,0:T(8,128)(2,1)}, bf16[256,2176]{1,0:T(8,128)(2,1)}, u32[]{:S(2)}, u32[]{:S(2)}) collective-permute-start(bf16[256,2176]{1,0:T(8,128)(2,1)} %constant_dynamic-update-slice_fusion.refs_0_), channel_id=1, source_target_pairs={{0,1},{1,0},{2,3},{3,2},{4,5},{5,4},{6,7},{7,6},{8,9},{9,8},{10,11... | collective-permute-start | bytes 3342344 | tf_op jit(solution)/shard_map/ppermute | solution.py:414
  137.5 6.4 %collective-permute-start.11 = (bf16[8,32,2048]{2,1,0:T(8,128)(2,1)S(1)}, bf16[8,32,2048]{2,1,0:T(8,128)(2,1)S(1)}, u32[]{:S(2)}, u32[]{:S(2)}) collective-permute-start(bf16[8,32,2048]{2,1,0:T(8,128)(2,1)S(1)} %shard_map.114), channel_id=1, source_target_pairs={{0,1},{1,0},{2,3},{3,2},{4,5},{5,4},{6,7},{7,6},{8,9},{9,8},{10,11... | collective-permute-start | bytes 3145736 | tf_op jit(solution)/shard_map/ppermute | solution.py:414
  144.3 7.3 %collective-permute-start.16 = (bf16[2,32,1024]{2,1,0:T(8,128)(2,1)S(1)}, bf16[2,32,1024]{2,1,0:T(8,128)(2,1)S(1)}, u32[]{:S(2)}, u32[]{:S(2)}) collective-permute-start(bf16[2,32,1024]{2,1,0:T(8,128)(2,1)S(1)} %get-tuple-element.9), channel_id=1, source_target_pairs={{0,4},{1,5},{2,6},{3,7},{4,0},{5,1},{6,2},{7,3},{8,12},{9,13},{10,... | collective-permute-start | bytes 393224 | tf_op jit(solution)/shard_map/ppermute | solution.py:414
  144.3 13.0 %collective-permute-start.17 = (bf16[2,32,1024]{2,1,0:T(8,128)(2,1)S(1)}, bf16[2,32,1024]{2,1,0:T(8,128)(2,1)S(1)}, u32[]{:S(2)}, u32[]{:S(2)}) collective-permute-start(bf16[2,32,1024]{2,1,0:T(8,128)(2,1)S(1)} %get-tuple-element.10), channel_id=1, source_target_pairs={{0,8},{1,9},{2,10},{3,11},{4,12},{5,13},{6,14},{7,15},{8,0},{9,1},... | collective-permute-start | bytes 393224 | tf_op jit(solution)/shard_map/ppermute | solution.py:414
  146.6 10.7 %collective-permute-start.18 = (bf16[2,32,1024]{2,1,0:T(8,128)(2,1)S(1)}, bf16[2,32,1024]{2,1,0:T(8,128)(2,1)S(1)}, u32[]{:S(2)}, u32[]{:S(2)}) collective-permute-start(bf16[2,32,1024]{2,1,0:T(8,128)(2,1)S(1)} %get-tuple-element.11), channel_id=1, source_target_pairs={{0,12},{1,13},{2,14},{3,15},{4,8},{5,9},{6,10},{7,11},{8,4},{9,5},... | collective-permute-start | bytes 393224 | tf_op jit(solution)/shard_map/ppermute | solution.py:414
  148.7 9.4 %collective-permute-start.12 = (bf16[4,32,1024]{2,1,0:T(8,128)(2,1)S(1)}, bf16[4,32,1024]{2,1,0:T(8,128)(2,1)S(1)}, u32[]{:S(2)}, u32[]{:S(2)}) collective-permute-start(bf16[4,32,1024]{2,1,0:T(8,128)(2,1)S(1)} %slice_bitcast_fusion), channel_id=1, source_target_pairs={{0,2},{1,3},{2,0},{3,1},{4,6},{5,7},{6,4},{7,5},{8,10},{9,11},{10,... | collective-permute-start | bytes 786440 | tf_op jit(solution)/shard_map/ppermute | solution.py:414
  157.4 5.5 %collective-permute-start.19 = (bf16[32,1024]{1,0:T(8,128)(2,1)S(1)}, bf16[32,1024]{1,0:T(8,128)(2,1)S(1)}, u32[]{:S(2)}, u32[]{:S(2)}) collective-permute-start(bf16[32,1024]{1,0:T(8,128)(2,1)S(1)} %fusion.4), channel_id=1, source_target_pairs={{0,2},{1,3},{2,0},{3,1},{4,6},{5,7},{6,4},{7,5},{8,10},{9,11},{10,... | collective-permute-start | bytes 196616 | tf_op jit(solution)/shard_map/ppermute | solution.py:414
  158.2 4.9 %collective-permute-start.13 = (bf16[32,1024]{1,0:T(8,128)(2,1)S(1)}, bf16[32,1024]{1,0:T(8,128)(2,1)S(1)}, u32[]{:S(2)}, u32[]{:S(2)}) collective-permute-start(bf16[32,1024]{1,0:T(8,128)(2,1)S(1)} %get-tuple-element.12), channel_id=1, source_target_pairs={{0,4},{1,5},{2,6},{3,7},{4,0},{5,1},{6,2},{7,3},{8,12},{9,13},{10,... | collective-permute-start | bytes 196616 | tf_op jit(solution)/shard_map/ppermute | solution.py:414
  160.7 6.1 %collective-permute-start.15 = (bf16[32,1024]{1,0:T(8,128)(2,1)S(1)}, bf16[32,1024]{1,0:T(8,128)(2,1)S(1)}, u32[]{:S(2)}, u32[]{:S(2)}) collective-permute-start(bf16[32,1024]{1,0:T(8,128)(2,1)S(1)} %get-tuple-element.13), channel_id=1, source_target_pairs={{0,12},{1,13},{2,14},{3,15},{4,8},{5,9},{6,10},{7,11},{8,4},{9,5},... | collective-permute-start | bytes 196616 | tf_op jit(solution)/shard_map/ppermute | solution.py:414
  162.9 5.8 %collective-permute-start.14 = (bf16[32,1024]{1,0:T(8,128)(2,1)S(1)}, bf16[32,1024]{1,0:T(8,128)(2,1)S(1)}, u32[]{:S(2)}, u32[]{:S(2)}) collective-permute-start(bf16[32,1024]{1,0:T(8,128)(2,1)S(1)} %get-tuple-element.14), channel_id=1, source_target_pairs={{0,8},{1,9},{2,10},{3,11},{4,12},{5,13},{6,14},{7,15},{8,0},{9,1},... | collective-permute-start | bytes 196616 | tf_op jit(solution)/shard_map/ppermute | solution.py:414
  (7 other events, 15.6 us)

commit v2 on v1

--- a/solution.py
+++ b/solution.py
@@ -220,6 +220,15 @@
 
 def params(mib):
     return pltpu.CompilerParams(vmem_limit_bytes=mib * 2**20)
+
+
+def cost(flops, size, exps=0):
+    return pl.CostEstimate(flops=flops, bytes_accessed=size, transcendentals=exps)
+
+
+def flipped(number, bits):
+    low = (number % 2 + bits % 2) % 2
+    return 2 * ((number // 2 + bits // 2) % 2) + low
 
 
 def pieces(value, count):
@@ -307,9 +316,7 @@
     width = w_out_ref.shape[1]
     copies = []
     for k, source in enumerate((w0, w1, w2, w3)):
-        low = (quarter % 2 + k % 2) % 2
-        high = (quarter // 2 + k // 2) % 2
-        spot = pl.multiple_of((2 * high + low) * depth, depth)
+        spot = pl.multiple_of(flipped(quarter, k) * depth, depth)
         copies.append(pltpu.make_async_copy(source, w_ref.at[pl.ds(spot, depth), :], sems.at[k]))
         copies[-1].start()
     left = lax.broadcasted_iota(jnp.int32, (dim, lanes), 1) < lanes // 2
@@ -325,7 +332,8 @@
     centre = jnp.sum(mixed, axis=1, keepdims=True) / width
     centered = mixed - centre
     square = jnp.sum(centered * centered, axis=1, keepdims=True)
-    gain, bias = gain_ref[position], bias_ref[position]
+    here = pl.ds(pl.multiple_of(position * width, LANES), width)
+    gain, bias = gain_ref[:, here], bias_ref[:, here]
     row = lax.broadcasted_iota(jnp.int32, (16, width), 0)
     extra = jnp.zeros((16, width), F32)
     for k, line in enumerate(pieces(gain, 2) + pieces(bias, 2)):
@@ -345,7 +353,7 @@
     for begin in range(0, out_width, step):
         part = jnp.dot(left_side, w_ref[:, begin : begin + step], preferred_element_type=F32)
         for plane in range(planes):
-            out_ref[plane, :, begin : begin + step] = part[plane * tokens : (plane + 1) * tokens].astype(BF)
+            out_ref[flipped(position, plane), :, begin : begin + step] = part[plane * tokens : (plane + 1) * tokens].astype(BF)
         scale = part[lanes : lanes + 1] + part[lanes + 1 : lanes + 2]
         shift = part[lanes + 2 : lanes + 3] + part[lanes + 3 : lanes + 4]
         for k in range(step // LANES):
@@ -353,16 +361,17 @@
             shared[half + begin // LANES + k] = shift[:, k * LANES : (k + 1) * LANES]
     shared = jnp.concatenate(shared, 0).astype(BF)
     for plane in range(planes):
-        out_ref[plane, :, out_width : out_width + LANES] = shared
-        out_ref[plane, :, out_width + LANES :] = stats[plane * tokens : (plane + 1) * tokens]
-
-
-def route_kernel(x_ref, router_ref, ids_ref, out_ref, *, merge_width, experts):
-    planes, tokens, _ = x_ref.shape
+        out_ref[flipped(position, plane), :, out_width : out_width + LANES] = shared
+        out_ref[flipped(position, plane), :, out_width + LANES :] = stats[plane * tokens : (plane + 1) * tokens]
+
+
+def route_kernel(x0, x1, x2, x3, router_ref, ids_ref, out_ref, *, merge_width, experts):
+    blocks = (x0, x1, x2, x3)
+    planes, tokens = len(blocks), x0.shape[0]
     out_width = out_ref.shape[1] - LANES
     half = tokens // 2
-    stats = [x_ref[p, :, out_width + LANES :].astype(F32) for p in range(planes)]
-    shared = [x_ref[p, :, out_width : out_width + LANES].astype(F32) for p in range(planes)]
+    stats = [blocks[p][:, out_width + LANES :].astype(F32) for p in range(planes)]
+    shared = [blocks[p][:, out_width : out_width + LANES].astype(F32) for p in range(planes)]
     centres = [s[:, 0:1] + s[:, 1:2] + s[:, 2:3] for s in stats]
     squares = [s[:, 3:4] + s[:, 4:5] + s[:, 5:6] for s in stats]
     mean = sum(centres) / planes
@@ -372,7 +381,7 @@
     bias = sum(shared)
     for k in range(out_width // LANES):
         cut = slice(k * LANES, (k + 1) * LANES)
-        total = sum(x_ref[p, :, cut].astype(F32) for p in range(planes))
+        total = sum(blocks[p][:, cut].astype(F32) for p in range(planes))
         total += sum(offsets[p] * shared[p][k : k + 1] for p in range(planes))
         out_ref[:, cut] = (total * inverse + bias[half + k : half + k + 1]).astype(BF)
     logits = jnp.dot(out_ref[:, :out_width], router_ref[...], preferred_element_type=F32)
@@ -388,25 +397,30 @@
     out_ref[:, out_width:] = jnp.where(lane < experts, high, low).astype(BF)
 
 
-def expert_kernel(x_ref, gate_ref, up_ref, down_ref, out_ref, *, experts):
-    blocks, tokens, width = out_ref.shape
+def expert_kernel(*refs, experts):
+    *blocks, gate_ref, up_ref, down_ref, own_ref, other_ref, x_ref = refs
+    tokens, width = own_ref.shape[1:]
+    half = len(blocks) // 2
     expert = lax.axis_index("wide") // 2
-    rows = x_ref.shape[0]
-    inputs = x_ref[:, :width]
-    lane = lax.broadcasted_iota(jnp.int32, (rows, LANES), 1)
-    weight = jnp.where(
-        (lane == expert) | (lane == expert + experts), x_ref[:, width:].astype(F32), 0.0
-    )
-    weight = jnp.sum(weight, axis=1, keepdims=True)
-    gate = jnp.dot(inputs, gate_ref[0], preferred_element_type=F32)
-    up = jnp.dot(inputs, up_ref[0], preferred_element_type=F32)
+    lane = lax.broadcasted_iota(jnp.int32, (tokens, LANES), 1)
+    weights = []
+    for k, block in enumerate(blocks):
+        x_ref[k * tokens : (k + 1) * tokens, :] = block[:, :width]
+        picked = (lane == expert) | (lane == expert + experts)
+        picked = jnp.where(picked, block[:, width:].astype(F32), 0.0)
+        weights.append(jnp.sum(picked, axis=1, keepdims=True))
+    inputs = x_ref[...]
+    turned = (((1,), (1,)), ((), ()))
+    gate = lax.dot_general(inputs, gate_ref[0], turned, preferred_element_type=F32)
+    up = lax.dot_general(inputs, up_ref[0], turned, preferred_element_type=F32)
     hidden = (gate / (1.0 + jnp.exp(-gate)) * up).astype(BF)
     step = 4 * LANES
     for begin in range(0, width, step):
         product = jnp.dot(hidden, down_ref[0, :, begin : begin + step], preferred_element_type=F32)
-        product = (product * weight).astype(BF)
-        for block in range(blocks):
-            out_ref[block, :, begin : begin + step] = product[block * tokens : (block + 1) * tokens]
+        for k in range(len(blocks)):
+            value = (product[k * tokens : (k + 1) * tokens] * weights[k]).astype(BF)
+            out_ref = own_ref if k < half else other_ref
+            out_ref[k % half, :, begin : begin + step] = value
 
 
 def crossed(value, mask):
@@ -451,15 +465,17 @@
     )
     gathered, held = lax.optimization_barrier((gathered, w_merge))
     held_y = crossed(held, 2)
-    held_c = crossed(held, 1)
-    held_yc = crossed(held_y, 1)
     attended = pl.pallas_call(
         attend_kernel,
         out_shape=jax.ShapeDtypeStruct((devices, dim, rows), BF),
         in_specs=[VMEM, SMEM],
         out_specs=VMEM,
         compiler_params=params(48),
+        cost_estimate=cost(2**32, 2**22, 2**21),
     )(gathered, grid)
+    attended, held_y, held = lax.optimization_barrier((attended, held_y, held))
+    held_c = crossed(held, 1)
+    held_yc = crossed(held_y, 1)
     returned = lax.all_to_all(attended, "wide", split_axis=0, concat_axis=0, tiled=True)
     planes = devices // 4
     message = out_width + 2 * LANES
@@ -477,57 +493,46 @@
     )(
         returned,
         w_out,
-        ln_gain.reshape(4, 1, vit_width),
-        ln_bias.reshape(4, 1, vit_width),
+        ln_gain.reshape(1, 4 * vit_width),
+        ln_bias.reshape(1, 4 * vit_width),
         held,
         held_c,
         held_y,
         held_yc,
     )
-    columns = [[q + 4 * i for i in range(planes)] for q in range(4)]
-    summed = lax.all_to_all(
-        partial, "wide", split_axis=0, concat_axis=0, tiled=True, axis_index_groups=columns
-    )
+    along = (4, 8, 12)
+    arrived = [partial[0]] + [crossed(partial[k], mask) for k, mask in enumerate(along, 1)]
     router = jnp.concatenate(
         [w_router, w_router, jnp.zeros((out_width, LANES - 2 * experts), BF)], 1
     )
     routed = pl.pallas_call(
         lambda *refs: route_kernel(*refs, merge_width=4 * vit_width, experts=experts),
         out_shape=jax.ShapeDtypeStruct((tokens, out_width + LANES), BF),
-        in_specs=[VMEM, VMEM, VMEM],
+        in_specs=[VMEM] * 6,
         out_specs=VMEM,
         compiler_params=params(32),
-    )(summed, router, expert_ids)
-    along = (4, 8, 12)
+    )(*arrived, router, expert_ids)
     near = [routed] + [crossed(routed, mask) for mask in along]
     far = [crossed(block, 2) for block in near]
-    own_plane = jnp.concatenate(near + far, 0)
-    other_plane = crossed(own_plane, 1)
-
-    def experts_of(block):
-        return pl.pallas_call(
+    gate_turned, up_turned = jnp.swapaxes(w_gate, 1, 2), jnp.swapaxes(w_up, 1, 2)
+
+    def experts_of(blocks):
+        own, other = pl.pallas_call(
             lambda *refs: expert_kernel(*refs, experts=experts),
-            out_shape=jax.ShapeDtypeStruct((devices // 2, tokens, out_width), BF),
-            in_specs=[VMEM, VMEM, VMEM, VMEM],
-            out_specs=VMEM,
+            out_shape=[jax.ShapeDtypeStruct((planes, tokens, out_width), BF)] * 2,
+            in_specs=[VMEM] * (2 * planes + 3),
+            out_specs=[VMEM, VMEM],
+            scratch_shapes=[pltpu.VMEM((2 * planes * tokens, out_width), BF)],
             compiler_params=params(48),
-        )(block, w_gate, w_up, w_down)
-
-    own_out = experts_of(own_plane)
-    other_out = experts_of(other_plane)
-    total = (own_out.astype(F32) + crossed(other_out, 1).astype(F32)).astype(BF)
-    total = total.reshape(2, planes, tokens, out_width)
-    cut = out_width // 2
-    first, second = total[..., :cut], total[..., cut:]
-    first_y = crossed(first[1], 2)
-    second_z = [crossed(second[:, i], mask) for i, mask in enumerate(along, 1)]
-    first = (first[0].astype(F32) + first_y.astype(F32)).astype(BF)
-    second = second[:, 0].astype(F32) + sum(block.astype(F32) for block in second_z)
-    second_y = crossed(second[1].astype(BF), 2)
-    first_z = [crossed(first[i], mask) for i, mask in enumerate(along, 1)]
-    first = first[0].astype(F32) + sum(block.astype(F32) for block in first_z)
-    second = second[0] + second_y.astype(F32)
-    return jnp.concatenate([first, second], 1).astype(BF)
+            cost_estimate=cost(2**32, 2**24),
+        )(*blocks, *[crossed(block, 1) for block in blocks], gate_turned, up_turned, w_down)
+        total = (own.astype(F32) + crossed(other, 1).astype(F32)).astype(BF)
+        others = [crossed(total[k], mask) for k, mask in enumerate(along, 1)]
+        return total[0].astype(F32) + sum(block.astype(F32) for block in others)
+
+    near_sum = experts_of(near)
+    far_sum = experts_of(far)
+    return (near_sum + crossed(far_sum.astype(BF), 2).astype(F32)).astype(BF)
 
 
 def solution(mesh):

time: 170 us -> 155 us (0.912)
  local copies, waits for them, and re-layouts: 21.3 us -> 10 us
  waiting for transfers between devices: 73.9 us -> 68.3 us
  starting transfers between devices: 28.8 us -> 32.3 us
    all_to_all x1 -> x0, waiting for transfers between devices: 15.2 us -> none  [local(): lax.all_to_all(partial, 'wide', split_axis=0, concat_axis=0, tiled=True,...]
    ppermute x20 -> x30, waiting for transfers between devices: 50.7 us -> 62.3 us  [crossed(): return lax.ppermute(value, 'wide', pairs)]
    unnamed x29 -> x22, local copies, waits for them, and re-layouts: 17.8 us -> 7.12 us
    ppermute x20 -> x30, starting transfers between devices: 20.5 us -> 27.8 us  [crossed(): return lax.ppermute(value, 'wide', pairs)]
    all_to_all x1 -> x0, starting transfers between devices: 3.67 us -> none  [local(): lax.all_to_all(partial, 'wide', split_axis=0, concat_axis=0, tiled=True,...]
    all_to_all x1, waiting for transfers between devices: 7.93 us -> 6.06 us  [local(): lax.all_to_all(attended, 'wide', split_axis=0, concat_axis=0, tiled=True)]
  transfers between devices with their start and end apart: 22 -> 31, of which waited for: 11 -> 12; matrix products, arithmetic and copies ran while one was open for 10% -> 3% of each run, Pallas kernels for 7% -> 11%
where the time goes in v2:
time: 155 us; the launch traced here: 154 us
  waiting for transfers between devices  68.3 us (44%)
  starting transfers between devices  32.3 us (21%)
  Pallas kernels  23.5 us (15%)
  blocking collectives  18.5 us (12%)
  local copies, waits for them, and re-layouts  10 us (6%)
    ppermute x30, waiting for transfers between devices, crossed(): return lax.ppermute(value, 'wide', pairs)  62.3 us
    ppermute x30, starting transfers between devices, crossed(): return lax.ppermute(value, 'wide', pairs)  27.8 us
    all_to_all x1, blocking collectives, local(): lax.all_to_all(packed, 'wide', split_axis=0, concat_axis=0, tiled=True, a...  18.5 us
    pallas_call x2, Pallas kernels, experts_of(): pl.pallas_call(lambda *refs: expert_kernel(*refs, experts=experts), out_s...  10.8 us
    unnamed x22, local copies, waits for them, and re-layouts  7.12 us
    pallas_call x1, Pallas kernels, local(): pl.pallas_call(attend_kernel, out_shape=jax.ShapeDtypeStruct((devices, di...  6.54 us
    all_to_all x1, waiting for transfers between devices, local(): lax.all_to_all(attended, 'wide', split_axis=0, concat_axis=0, tiled=True)  6.06 us
    pallas_call x1, Pallas kernels, local(): pl.pallas_call(merge_kernel, out_shape=jax.ShapeDtypeStruct((planes, toke...  5.12 us
  transfers between devices with their start and end apart: 31, of which 12 were waited for; matrix products, arithmetic and copies ran while one was open for 3% of the time, Pallas kernels for 11%

profile of v2, /device:TPU:0, one launch (start us, length us, event | category | flops | bytes accessed | tf_op | source)
XLA Modules:
  0.0 154.2 jit_solution(14708696948151361233)
XLA Ops:
  1.7 18.5 %all_to_all.10.x_ref = bf16[8,432,128]{2,1,0:T(8,128)(2,1)S(1)} all-to-all(bf16[8,432,128]{2,1,0:T(8,128)(2,1)S(1)} %shard_map.109), channel_id=1, replica_groups={{0,1,2,3,4,5,6,7},{8,9,10,11,12,13,14,15},{16,17,18,19,20,21,22,23},{24..., dimensions={0} | all-to-all | bytes 1769472 | tf_op jit(solution)/shard_map/all_to_all | solution.py:463
  21.1 6.5 %shard_map.110 = bf16[16,72,128]{2,1,0:T(8,128)(2,1)S(1)} custom-call(bf16[8,432,128]{2,1,0:T(8,128)(2,1)S(1)} %all_to_all.10.x_ref, s32[2,2]{1,0:T(2,128)S(1)} %copy-done.7), custom_call_target="tpu_custom_call" | custom-call | flops 4294967296 | bytes 4194304 | tf_op jit(solution)/shard_map/pallas_call | solution.py:468
  28.3 19.5 %collective-permute-done.w2 = bf16[288,2048]{1,0:T(8,128)(2,1)S(1)} collective-permute-done((bf16[288,2048]{1,0:T(8,128)(2,1)S(1)}, bf16[288,2048]{1,0:T(8,128)(2,1)S(1)}, u32[]{:S(2)}, u32[]{:S(2)}) %collective-permute-start) | collective-permute-done | bytes 1179680 | tf_op jit(solution)/shard_map/ppermute | solution.py:428
  48.3 4.6 %all-to-all-start.1 = ((bf16[16,72,128]{2,1,0:T(8,128)(2,1)}), bf16[16,72,128]{2,1,0:T(8,128)(2,1)}, u32[]{:S(2)}, u32[]{:S(2)}) async-start(bf16[16,72,128]{2,1,0:T(8,128)(2,1)} %copy-done.2), calls=%async_computation.1 | async-start | bytes 589824 | tf_op jit(solution)/shard_map/all_to_all | solution.py:479
  55.6 1.8 %copy.12 = bf16[2048,8]{1,0:T(8,128)(2,1)} copy(bf16[2048,8]{0,1:T(8,128)(2,1)} %param.18) | data formatting | bytes 65536 | tf_op args[6]
  57.5 6.1 %all-to-all-done.1.x_ref = bf16[16,72,128]{2,1,0:T(8,128)(2,1)} async-done(((bf16[16,72,128]{2,1,0:T(8,128)(2,1)}), bf16[16,72,128]{2,1,0:T(8,128)(2,1)}, u32[]{:S(2)}, u32[]{:S(2)}) %all-to-all-start.1) | async-done | bytes 294944 | tf_op jit(solution)/shard_map/all_to_all | solution.py:479
  65.0 5.1 %shard_map.111 = bf16[4,32,2304]{2,1,0:T(8,128)(2,1)S(1)} custom-call(bf16[16,72,128]{2,1,0:T(8,128)(2,1)} %all-to-all-done.1.x_ref, bf16[1152,1152]{1,0:T(8,128)(2,1)} %w_out_ref.1, f32[1,4608]{1,0:T(1,128)S(1)} %copy-done.3, f32[1,4608]{1,0:T(1,128)S(1)} %copy-done.4, bf16[288,2048]{1,0:T(8,128)(2,1)S(1)} %copy-done, ...), custom_call_target="tpu_custom_call" | custom-call | tf_op jit(solution)/shard_map/pallas_call | solution.py:482
  71.8 2.8 %collective-permute-start.5 = (bf16[32,2304]{1,0:T(8,128)(2,1)S(1)}, bf16[32,2304]{1,0:T(8,128)(2,1)S(1)}, u32[]{:S(2)}, u32[]{:S(2)}) collective-permute-start(bf16[32,2304]{1,0:T(8,128)(2,1)S(1)} %get-tuple-element.23), channel_id=1, source_target_pairs={{0,12},{1,13},{2,14},{3,15},{4,8},{5,9},{6,10},{7,11},{8,4},{9,5},... | collective-permute-start | bytes 442376 | tf_op jit(solution)/shard_map/ppermute | solution.py:428
  75.0 2.8 %collective-permute-done.3.refs_1_ = bf16[32,2304]{1,0:T(8,128)(2,1)S(1)} collective-permute-done((bf16[32,2304]{1,0:T(8,128)(2,1)S(1)}, bf16[32,2304]{1,0:T(8,128)(2,1)S(1)}, u32[]{:S(2)}, u32[]{:S(2)}) %collective-permute-start.3) | collective-permute-done | bytes 147488 | tf_op jit(solution)/shard_map/ppermute | solution.py:428
  77.8 6.4 %collective-permute-done.4.refs_2_ = bf16[32,2304]{1,0:T(8,128)(2,1)S(1)} collective-permute-done((bf16[32,2304]{1,0:T(8,128)(2,1)S(1)}, bf16[32,2304]{1,0:T(8,128)(2,1)S(1)}, u32[]{:S(2)}, u32[]{:S(2)}) %collective-permute-start.4) | collective-permute-done | bytes 147488 | tf_op jit(solution)/shard_map/ppermute | solution.py:428
  84.8 3.4 %collective-permute-start.6 = (bf16[32,2176]{1,0:T(8,128)(2,1)S(1)}, bf16[32,2176]{1,0:T(8,128)(2,1)S(1)}, u32[]{:S(2)}, u32[]{:S(2)}) collective-permute-start(bf16[32,2176]{1,0:T(8,128)(2,1)S(1)} %shard_map.112.refs_0_), channel_id=1, source_target_pairs={{0,4},{1,5},{2,6},{3,7},{4,0},{5,1},{6,2},{7,3},{8,12},{9,13},{10,... | collective-permute-start | bytes 417800 | tf_op jit(solution)/shard_map/ppermute | solution.py:428
  88.1 2.4 %collective-permute-start.8 = (bf16[32,2176]{1,0:T(8,128)(2,1)S(1)}, bf16[32,2176]{1,0:T(8,128)(2,1)S(1)}, u32[]{:S(2)}, u32[]{:S(2)}) collective-permute-start(bf16[32,2176]{1,0:T(8,128)(2,1)S(1)} %shard_map.112.refs_0_), channel_id=1, source_target_pairs={{0,12},{1,13},{2,14},{3,15},{4,8},{5,9},{6,10},{7,11},{8,4},{9,5},... | collective-permute-start | bytes 417800 | tf_op jit(solution)/shard_map/ppermute | solution.py:428
  92.2 8.4 %collective-permute-done.7.refs_2_ = bf16[32,2176]{1,0:T(8,128)(2,1)S(1)} collective-permute-done((bf16[32,2176]{1,0:T(8,128)(2,1)S(1)}, bf16[32,2176]{1,0:T(8,128)(2,1)S(1)}, u32[]{:S(2)}, u32[]{:S(2)}) %collective-permute-start.7) | collective-permute-done | bytes 139296 | tf_op jit(solution)/shard_map/ppermute | solution.py:428
  104.0 3.0 %collective-permute-done.18.refs_1_ = bf16[32,2176]{1,0:T(8,128)(2,1)S(1)} collective-permute-done((bf16[32,2176]{1,0:T(8,128)(2,1)S(1)}, bf16[32,2176]{1,0:T(8,128)(2,1)S(1)}, u32[]{:S(2)}, u32[]{:S(2)}) %collective-permute-start.18) | collective-permute-done | bytes 139296 | tf_op jit(solution)/shard_map/ppermute | solution.py:428
  107.1 3.0 %collective-permute-done.19.refs_2_ = bf16[32,2176]{1,0:T(8,128)(2,1)S(1)} collective-permute-done((bf16[32,2176]{1,0:T(8,128)(2,1)S(1)}, bf16[32,2176]{1,0:T(8,128)(2,1)S(1)}, u32[]{:S(2)}, u32[]{:S(2)}) %collective-permute-start.19) | collective-permute-done | bytes 139296 | tf_op jit(solution)/shard_map/ppermute | solution.py:428
  110.1 2.6 %collective-permute-done.20.refs_3_ = bf16[32,2176]{1,0:T(8,128)(2,1)S(1)} collective-permute-done((bf16[32,2176]{1,0:T(8,128)(2,1)S(1)}, bf16[32,2176]{1,0:T(8,128)(2,1)S(1)}, u32[]{:S(2)}, u32[]{:S(2)}) %collective-permute-start.20) | collective-permute-done | bytes 139296 | tf_op jit(solution)/shard_map/ppermute | solution.py:428
  112.7 1.8 %copy-done.5 = bf16[1,2048,704]{1,2,0:T(8,128)(2,1)S(1)} copy-done((bf16[1,2048,704]{1,2,0:T(8,128)(2,1)S(1)}, bf16[1,2048,704]{1,2,0:T(8,128)(2,1)}, u32[]{:S(2)}) %copy-start.5) | copy-done | bytes 2883608
  114.5 5.5 %shard_map.113 = (bf16[4,32,2048]{2,1,0:T(8,128)(2,1)S(1)}, bf16[4,32,2048]{2,1,0:T(8,128)(2,1)S(1)}) custom-call(bf16[32,2176]{1,0:T(8,128)(2,1)S(1)} %shard_map.112.refs_0_, bf16[32,2176]{1,0:T(8,128)(2,1)S(1)} %collective-permute-done.6.refs_1_, bf16[32,2176]{1,0:T(8,128)(2,1)S(1)} %collective-permute-done.7.refs_2_, ...), custom_call_target="tpu_custom_call" | custom-call | flops 4294967296 | bytes 16777216 | tf_op jit(solution)/shard_map/pallas_call | solution.py:520
  120.6 5.3 %shard_map.114 = (bf16[4,32,2048]{2,1,0:T(8,128)(2,1)S(1)}, bf16[4,32,2048]{2,1,0:T(8,128)(2,1)S(1)}) custom-call(bf16[32,2176]{1,0:T(8,128)(2,1)S(1)} %collective-permute-done.17.refs_0_, bf16[32,2176]{1,0:T(8,128)(2,1)S(1)} %collective-permute-done.18.refs_1_, bf16[32,2176]{1,0:T(8,128)(2,1)S(1)} %collective-permute-done.19.refs_2_, ...), custom_call_target="tpu_custom_call" | custom-call | flops 4294967296 | bytes 16777216 | tf_op jit(solution)/shard_map/pallas_call | solution.py:520
  130.7 1.8 %collective-permute-start.28 = (bf16[32,2048]{1,0:T(8,128)(2,1)S(1)}, bf16[32,2048]{1,0:T(8,128)(2,1)S(1)}, u32[]{:S(2)}, u32[]{:S(2)}) collective-permute-start(bf16[32,2048]{1,0:T(8,128)(2,1)S(1)} %get-tuple-element.31), channel_id=1, source_target_pairs={{0,12},{1,13},{2,14},{3,15},{4,8},{5,9},{6,10},{7,11},{8,4},{9,5},... | collective-permute-start | bytes 393224 | tf_op jit(solution)/shard_map/ppermute | solution.py:428
  133.2 2.0 %collective-permute-start.15 = (bf16[32,2048]{1,0:T(8,128)(2,1)S(1)}, bf16[32,2048]{1,0:T(8,128)(2,1)S(1)}, u32[]{:S(2)}, u32[]{:S(2)}) collective-permute-start(bf16[32,2048]{1,0:T(8,128)(2,1)S(1)} %get-tuple-element.29), channel_id=1, source_target_pairs={{0,8},{1,9},{2,10},{3,11},{4,12},{5,13},{6,14},{7,15},{8,0},{9,1},... | collective-permute-start | bytes 393224 | tf_op jit(solution)/shard_map/ppermute | solution.py:428
  135.2 3.9 %collective-permute-start.16 = (bf16[32,2048]{1,0:T(8,128)(2,1)S(1)}, bf16[32,2048]{1,0:T(8,128)(2,1)S(1)}, u32[]{:S(2)}, u32[]{:S(2)}) collective-permute-start(bf16[32,2048]{1,0:T(8,128)(2,1)S(1)} %get-tuple-element.28), channel_id=1, source_target_pairs={{0,12},{1,13},{2,14},{3,15},{4,8},{5,9},{6,10},{7,11},{8,4},{9,5},... | collective-permute-start | bytes 393224 | tf_op jit(solution)/shard_map/ppermute | solution.py:428
  139.1 3.5 %collective-permute-done.27 = bf16[32,2048]{1,0:T(8,128)(2,1)S(1)} collective-permute-done((bf16[32,2048]{1,0:T(8,128)(2,1)S(1)}, bf16[32,2048]{1,0:T(8,128)(2,1)S(1)}, u32[]{:S(2)}, u32[]{:S(2)}) %collective-permute-start.27) | collective-permute-done | bytes 131104 | tf_op jit(solution)/shard_map/ppermute | solution.py:428
  143.0 10.5 %collective-permute-done.15 = bf16[32,2048]{1,0:T(8,128)(2,1)S(1)} collective-permute-done((bf16[32,2048]{1,0:T(8,128)(2,1)S(1)}, bf16[32,2048]{1,0:T(8,128)(2,1)S(1)}, u32[]{:S(2)}, u32[]{:S(2)}) %collective-permute-start.15) | collective-permute-done | bytes 131104 | tf_op jit(solution)/shard_map/ppermute | solution.py:428
  (79 shorter events, 23.0 us)
Async XLA Ops:
  20.2 27.6 %collective-permute-start = (bf16[288,2048]{1,0:T(8,128)(2,1)S(1)}, bf16[288,2048]{1,0:T(8,128)(2,1)S(1)}, u32[]{:S(2)}, u32[]{:S(2)}) collective-permute-start(bf16[288,2048]{1,0:T(8,128)(2,1)S(1)} %copy-done), channel_id=1, source_target_pairs={{0,2},{1,3},{2,0},{3,1},{4,6},{5,7},{6,4},{7,5},{8,10},{9,11},{10,... | collective-permute-start | bytes 3538952 | tf_op jit(solution)/shard_map/ppermute | solution.py:428
  47.8 15.7 %collective-permute-start.1 = (bf16[288,2048]{1,0:T(8,128)(2,1)S(1)}, bf16[288,2048]{1,0:T(8,128)(2,1)S(1)}, u32[]{:S(2)}, u32[]{:S(2)}) collective-permute-start(bf16[288,2048]{1,0:T(8,128)(2,1)S(1)} %copy-done), channel_id=1, source_target_pairs={{0,1},{1,0},{2,3},{3,2},{4,5},{5,4},{6,7},{7,6},{8,9},{9,8},{10,11... | collective-permute-start | bytes 3538952 | tf_op jit(solution)/shard_map/ppermute | solution.py:428
  47.8 15.7 %collective-permute-start.2 = (bf16[288,2048]{1,0:T(8,128)(2,1)S(1)}, bf16[288,2048]{1,0:T(8,128)(2,1)}, u32[]{:S(2)}, u32[]{:S(2)}) collective-permute-start(bf16[288,2048]{1,0:T(8,128)(2,1)S(1)} %collective-permute-done.w2), channel_id=1, source_target_pairs={{0,1},{1,0},{2,3},{3,2},{4,5},{5,4},{6,7},{7,6},{8,9},{9,8},{10,11... | collective-permute-start | bytes 3538952 | tf_op jit(solution)/shard_map/ppermute | solution.py:428
  48.3 15.2 %all-to-all-start.1 = ((bf16[16,72,128]{2,1,0:T(8,128)(2,1)}), bf16[16,72,128]{2,1,0:T(8,128)(2,1)}, u32[]{:S(2)}, u32[]{:S(2)}) async-start(bf16[16,72,128]{2,1,0:T(8,128)(2,1)} %copy-done.2), calls=%async_computation.1 | async-start | bytes 589824 | tf_op jit(solution)/shard_map/all_to_all | solution.py:479
  70.4 13.8 %collective-permute-start.4 = (bf16[32,2304]{1,0:T(8,128)(2,1)S(1)}, bf16[32,2304]{1,0:T(8,128)(2,1)S(1)}, u32[]{:S(2)}, u32[]{:S(2)}) collective-permute-start(bf16[32,2304]{1,0:T(8,128)(2,1)S(1)} %get-tuple-element.24), channel_id=1, source_target_pairs={{0,8},{1,9},{2,10},{3,11},{4,12},{5,13},{6,14},{7,15},{8,0},{9,1},... | collective-permute-start | bytes 442376 | tf_op jit(solution)/shard_map/ppermute | solution.py:428
  71.8 12.4 %collective-permute-start.5 = (bf16[32,2304]{1,0:T(8,128)(2,1)S(1)}, bf16[32,2304]{1,0:T(8,128)(2,1)S(1)}, u32[]{:S(2)}, u32[]{:S(2)}) collective-permute-start(bf16[32,2304]{1,0:T(8,128)(2,1)S(1)} %get-tuple-element.23), channel_id=1, source_target_pairs={{0,12},{1,13},{2,14},{3,15},{4,8},{5,9},{6,10},{7,11},{8,4},{9,5},... | collective-permute-start | bytes 442376 | tf_op jit(solution)/shard_map/ppermute | solution.py:428
  88.1 12.5 %collective-permute-start.7 = (bf16[32,2176]{1,0:T(8,128)(2,1)S(1)}, bf16[32,2176]{1,0:T(8,128)(2,1)S(1)}, u32[]{:S(2)}, u32[]{:S(2)}) collective-permute-start(bf16[32,2176]{1,0:T(8,128)(2,1)S(1)} %shard_map.112.refs_0_), channel_id=1, source_target_pairs={{0,8},{1,9},{2,10},{3,11},{4,12},{5,13},{6,14},{7,15},{8,0},{9,1},... | collective-permute-start | bytes 417800 | tf_op jit(solution)/shard_map/ppermute | solution.py:428
  88.1 12.5 %collective-permute-start.8 = (bf16[32,2176]{1,0:T(8,128)(2,1)S(1)}, bf16[32,2176]{1,0:T(8,128)(2,1)S(1)}, u32[]{:S(2)}, u32[]{:S(2)}) collective-permute-start(bf16[32,2176]{1,0:T(8,128)(2,1)S(1)} %shard_map.112.refs_0_), channel_id=1, source_target_pairs={{0,12},{1,13},{2,14},{3,15},{4,8},{5,9},{6,10},{7,11},{8,4},{9,5},... | collective-permute-start | bytes 417800 | tf_op jit(solution)/shard_map/ppermute | solution.py:428
  90.6 10.9 %collective-permute-start.9 = (bf16[32,2176]{1,0:T(8,128)(2,1)S(1)}, bf16[32,2176]{1,0:T(8,128)(2,1)S(1)}, u32[]{:S(2)}, u32[]{:S(2)}) collective-permute-start(bf16[32,2176]{1,0:T(8,128)(2,1)S(1)} %shard_map.112.refs_0_), channel_id=1, source_target_pairs={{0,1},{1,0},{2,3},{3,2},{4,5},{5,4},{6,7},{7,6},{8,9},{9,8},{10,11... | collective-permute-start | bytes 417800 | tf_op jit(solution)/shard_map/ppermute | solution.py:428
  90.6 12.1 %collective-permute-start.17 = (bf16[32,2176]{1,0:T(8,128)(2,1)S(1)}, bf16[32,2176]{1,0:T(8,128)(2,1)S(1)}, u32[]{:S(2)}, u32[]{:S(2)}) collective-permute-start(bf16[32,2176]{1,0:T(8,128)(2,1)S(1)} %shard_map.112.refs_0_), channel_id=1, source_target_pairs={{0,2},{1,3},{2,0},{3,1},{4,6},{5,7},{6,4},{7,5},{8,10},{9,11},{10,... | collective-permute-start | bytes 417800 | tf_op jit(solution)/shard_map/ppermute | solution.py:428
  92.2 11.3 %collective-permute-start.10 = (bf16[32,2176]{1,0:T(8,128)(2,1)S(1)}, bf16[32,2176]{1,0:T(8,128)(2,1)S(1)}, u32[]{:S(2)}, u32[]{:S(2)}) collective-permute-start(bf16[32,2176]{1,0:T(8,128)(2,1)S(1)} %collective-permute-done.6.refs_1_), channel_id=1, source_target_pairs={{0,1},{1,0},{2,3},{3,2},{4,5},{5,4},{6,7},{7,6},{8,9},{9,8},{10,11... | collective-permute-start | bytes 417800 | tf_op jit(solution)/shard_map/ppermute | solution.py:428
  101.5 8.6 %collective-permute-start.19 = (bf16[32,2176]{1,0:T(8,128)(2,1)S(1)}, bf16[32,2176]{1,0:T(8,128)(2,1)S(1)}, u32[]{:S(2)}, u32[]{:S(2)}) collective-permute-start(bf16[32,2176]{1,0:T(8,128)(2,1)S(1)} %collective-permute-done.7.refs_2_), channel_id=1, source_target_pairs={{0,2},{1,3},{2,0},{3,1},{4,6},{5,7},{6,4},{7,5},{8,10},{9,11},{10,... | collective-permute-start | bytes 417800 | tf_op jit(solution)/shard_map/ppermute | solution.py:428
  102.6 10.0 %collective-permute-start.20 = (bf16[32,2176]{1,0:T(8,128)(2,1)S(1)}, bf16[32,2176]{1,0:T(8,128)(2,1)S(1)}, u32[]{:S(2)}, u32[]{:S(2)}) collective-permute-start(bf16[32,2176]{1,0:T(8,128)(2,1)S(1)} %collective-permute-done.8.refs_3_), channel_id=1, source_target_pairs={{0,2},{1,3},{2,0},{3,1},{4,6},{5,7},{6,4},{7,5},{8,10},{9,11},{10,... | collective-permute-start | bytes 417800 | tf_op jit(solution)/shard_map/ppermute | solution.py:428
  103.5 9.2 %collective-permute-start.12 = (bf16[32,2176]{1,0:T(8,128)(2,1)S(1)}, bf16[32,2176]{1,0:T(8,128)(2,1)S(1)}, u32[]{:S(2)}, u32[]{:S(2)}) collective-permute-start(bf16[32,2176]{1,0:T(8,128)(2,1)S(1)} %collective-permute-done.8.refs_3_), channel_id=1, source_target_pairs={{0,1},{1,0},{2,3},{3,2},{4,5},{5,4},{6,7},{7,6},{8,9},{9,8},{10,11... | collective-permute-start | bytes 417800 | tf_op jit(solution)/shard_map/ppermute | solution.py:428
  103.5 17.0 %collective-permute-start.21 = (bf16[32,2176]{1,0:T(8,128)(2,1)S(1)}, bf16[32,2176]{1,0:T(8,128)(2,1)S(1)}, u32[]{:S(2)}, u32[]{:S(2)}) collective-permute-start(bf16[32,2176]{1,0:T(8,128)(2,1)S(1)} %collective-permute-done.17.refs_0_), channel_id=1, source_target_pairs={{0,1},{1,0},{2,3},{3,2},{4,5},{5,4},{6,7},{7,6},{8,9},{9,8},{10,11... | collective-permute-start | bytes 417800 | tf_op jit(solution)/shard_map/ppermute | solution.py:428
  107.1 13.5 %collective-permute-start.22 = (bf16[32,2176]{1,0:T(8,128)(2,1)S(1)}, bf16[32,2176]{1,0:T(8,128)(2,1)S(1)}, u32[]{:S(2)}, u32[]{:S(2)}) collective-permute-start(bf16[32,2176]{1,0:T(8,128)(2,1)S(1)} %collective-permute-done.18.refs_1_), channel_id=1, source_target_pairs={{0,1},{1,0},{2,3},{3,2},{4,5},{5,4},{6,7},{7,6},{8,9},{9,8},{10,11... | collective-permute-start | bytes 417800 | tf_op jit(solution)/shard_map/ppermute | solution.py:428
  110.1 10.5 %collective-permute-start.23 = (bf16[32,2176]{1,0:T(8,128)(2,1)S(1)}, bf16[32,2176]{1,0:T(8,128)(2,1)S(1)}, u32[]{:S(2)}, u32[]{:S(2)}) collective-permute-start(bf16[32,2176]{1,0:T(8,128)(2,1)S(1)} %collective-permute-done.19.refs_2_), channel_id=1, source_target_pairs={{0,1},{1,0},{2,3},{3,2},{4,5},{5,4},{6,7},{7,6},{8,9},{9,8},{10,11... | collective-permute-start | bytes 417800 | tf_op jit(solution)/shard_map/ppermute | solution.py:428
  112.7 7.9 %collective-permute-start.24 = (bf16[32,2176]{1,0:T(8,128)(2,1)S(1)}, bf16[32,2176]{1,0:T(8,128)(2,1)S(1)}, u32[]{:S(2)}, u32[]{:S(2)}) collective-permute-start(bf16[32,2176]{1,0:T(8,128)(2,1)S(1)} %collective-permute-done.20.refs_3_), channel_id=1, source_target_pairs={{0,1},{1,0},{2,3},{3,2},{4,5},{5,4},{6,7},{7,6},{8,9},{9,8},{10,11... | collective-permute-start | bytes 417800 | tf_op jit(solution)/shard_map/ppermute | solution.py:428
  129.6 13.0 %collective-permute-start.27 = (bf16[32,2048]{1,0:T(8,128)(2,1)S(1)}, bf16[32,2048]{1,0:T(8,128)(2,1)S(1)}, u32[]{:S(2)}, u32[]{:S(2)}) collective-permute-start(bf16[32,2048]{1,0:T(8,128)(2,1)S(1)} %get-tuple-element.32), channel_id=1, source_target_pairs={{0,8},{1,9},{2,10},{3,11},{4,12},{5,13},{6,14},{7,15},{8,0},{9,1},... | collective-permute-start | bytes 393224 | tf_op jit(solution)/shard_map/ppermute | solution.py:428
  130.7 11.9 %collective-permute-start.28 = (bf16[32,2048]{1,0:T(8,128)(2,1)S(1)}, bf16[32,2048]{1,0:T(8,128)(2,1)S(1)}, u32[]{:S(2)}, u32[]{:S(2)}) collective-permute-start(bf16[32,2048]{1,0:T(8,128)(2,1)S(1)} %get-tuple-element.31), channel_id=1, source_target_pairs={{0,12},{1,13},{2,14},{3,15},{4,8},{5,9},{6,10},{7,11},{8,4},{9,5},... | collective-permute-start | bytes 393224 | tf_op jit(solution)/shard_map/ppermute | solution.py:428
  132.6 10.4 %collective-permute-start.14 = (bf16[32,2048]{1,0:T(8,128)(2,1)S(1)}, bf16[32,2048]{1,0:T(8,128)(2,1)S(1)}, u32[]{:S(2)}, u32[]{:S(2)}) collective-permute-start(bf16[32,2048]{1,0:T(8,128)(2,1)S(1)} %get-tuple-element.27), channel_id=1, source_target_pairs={{0,4},{1,5},{2,6},{3,7},{4,0},{5,1},{6,2},{7,3},{8,12},{9,13},{10,... | collective-permute-start | bytes 393224 | tf_op jit(solution)/shard_map/ppermute | solution.py:428
  133.2 20.3 %collective-permute-start.15 = (bf16[32,2048]{1,0:T(8,128)(2,1)S(1)}, bf16[32,2048]{1,0:T(8,128)(2,1)S(1)}, u32[]{:S(2)}, u32[]{:S(2)}) collective-permute-start(bf16[32,2048]{1,0:T(8,128)(2,1)S(1)} %get-tuple-element.29), channel_id=1, source_target_pairs={{0,8},{1,9},{2,10},{3,11},{4,12},{5,13},{6,14},{7,15},{8,0},{9,1},... | collective-permute-start | bytes 393224 | tf_op jit(solution)/shard_map/ppermute | solution.py:428
  135.2 18.3 %collective-permute-start.16 = (bf16[32,2048]{1,0:T(8,128)(2,1)S(1)}, bf16[32,2048]{1,0:T(8,128)(2,1)S(1)}, u32[]{:S(2)}, u32[]{:S(2)}) collective-permute-start(bf16[32,2048]{1,0:T(8,128)(2,1)S(1)} %get-tuple-element.28), channel_id=1, source_target_pairs={{0,12},{1,13},{2,14},{3,15},{4,8},{5,9},{6,10},{7,11},{8,4},{9,5},... | collective-permute-start | bytes 393224 | tf_op jit(solution)/shard_map/ppermute | solution.py:428
  142.7 10.8 %collective-permute-start.29 = (bf16[32,2048]{1,0:T(8,128)(2,1)S(1)}, bf16[32,2048]{1,0:T(8,128)(2,1)S(1)}, u32[]{:S(2)}, u32[]{:S(2)}) collective-permute-start(bf16[32,2048]{1,0:T(8,128)(2,1)S(1)} %fusion), channel_id=1, source_target_pairs={{0,2},{1,3},{2,0},{3,1},{4,6},{5,7},{6,4},{7,5},{8,10},{9,11},{10,... | collective-permute-start | bytes 393224 | tf_op jit(solution)/shard_map/ppermute | solution.py:428
  (17 other events, 110.7 us)

commit v3 on v2

--- a/solution.py
+++ b/solution.py
@@ -305,19 +305,21 @@
 
 
 def merge_kernel(
-    x_ref, w_out_ref, gain_ref, bias_ref, w0, w1, w2, w3, out_ref, att_ref, w_ref, sems
+    x_ref, w_out_ref, gain_ref, bias_ref, *refs
 ):
+    *sources, out_ref, att_ref, w_ref, sems = refs
     me = lax.axis_index("wide")
     position, quarter = me // 4, me % 4
     blocks, dim, lanes = x_ref.shape
     pairs = blocks // 2
-    depth = w0.shape[0]
-    out_width = w0.shape[1]
+    early, out_width = sources[0].shape
+    depth = early + sources[4].shape[0]
     width = w_out_ref.shape[1]
     copies = []
-    for k, source in enumerate((w0, w1, w2, w3)):
-        spot = pl.multiple_of(flipped(quarter, k) * depth, depth)
-        copies.append(pltpu.make_async_copy(source, w_ref.at[pl.ds(spot, depth), :], sems.at[k]))
+    for k, source in enumerate(sources):
+        rows = source.shape[0]
+        spot = pl.multiple_of(flipped(quarter, k % 4) * depth + k // 4 * early, 16)
+        copies.append(pltpu.make_async_copy(source, w_ref.at[pl.ds(spot, rows), :], sems.at[k]))
         copies[-1].start()
     left = lax.broadcasted_iota(jnp.int32, (dim, lanes), 1) < lanes // 2
     for pair in range(pairs):
@@ -398,9 +400,8 @@
 
 
 def expert_kernel(*refs, experts):
-    *blocks, gate_ref, up_ref, down_ref, own_ref, other_ref, x_ref = refs
-    tokens, width = own_ref.shape[1:]
-    half = len(blocks) // 2
+    *blocks, g0, g1, u0, u1, d0, d1, out_ref, x_ref = refs
+    tokens, width = out_ref.shape[1:]
     expert = lax.axis_index("wide") // 2
     lane = lax.broadcasted_iota(jnp.int32, (tokens, LANES), 1)
     weights = []
@@ -411,16 +412,18 @@
         weights.append(jnp.sum(picked, axis=1, keepdims=True))
     inputs = x_ref[...]
     turned = (((1,), (1,)), ((), ()))
-    gate = lax.dot_general(inputs, gate_ref[0], turned, preferred_element_type=F32)
-    up = lax.dot_general(inputs, up_ref[0], turned, preferred_element_type=F32)
-    hidden = (gate / (1.0 + jnp.exp(-gate)) * up).astype(BF)
+    hidden = []
+    for gate_ref, up_ref in ((g0, u0), (g1, u1)):
+        gate = lax.dot_general(inputs, gate_ref[0], turned, preferred_element_type=F32)
+        up = lax.dot_general(inputs, up_ref[0], turned, preferred_element_type=F32)
+        hidden.append((gate / (1.0 + jnp.exp(-gate)) * up).astype(BF))
     step = 4 * LANES
     for begin in range(0, width, step):
-        product = jnp.dot(hidden, down_ref[0, :, begin : begin + step], preferred_element_type=F32)
+        cut = slice(begin, begin + step)
+        product = jnp.dot(hidden[0], d0[0, :, cut], preferred_element_type=F32)
+        product += jnp.dot(hidden[1], d1[0, :, cut], preferred_element_type=F32)
         for k in range(len(blocks)):
-            value = (product[k * tokens : (k + 1) * tokens] * weights[k]).astype(BF)
-            out_ref = own_ref if k < half else other_ref
-            out_ref[k % half, :, begin : begin + step] = value
+            out_ref[k, :, cut] = (product[k * tokens : (k + 1) * tokens] * weights[k]).astype(BF)
 
 
 def crossed(value, mask):
@@ -452,6 +455,8 @@
         )
     part = vit_width // peers
     dim = vit_width // HEADS
+    early = w_merge.shape[0] // 3
+    early_y = crossed(w_merge[:early], 2)
     packed = pl.pallas_call(
         pack_kernel,
         out_shape=jax.ShapeDtypeStruct((peers, 3 * part, rows), BF),
@@ -463,8 +468,12 @@
     gathered = lax.all_to_all(
         packed, "wide", split_axis=0, concat_axis=0, tiled=True, axis_index_groups=clips
     )
-    gathered, held = lax.optimization_barrier((gathered, w_merge))
-    held_y = crossed(held, 2)
+    halves = (jnp.swapaxes(w_gate, 1, 2), jnp.swapaxes(w_up, 1, 2), w_down)
+    gathered, early_y, held, *sent = lax.optimization_barrier((gathered, early_y, w_merge, *halves))
+    late = held[early:]
+    late_y = crossed(late, 2)
+    early_c, late_c, early_yc = crossed(held[:early], 1), crossed(late, 1), crossed(early_y, 1)
+    weights = [w for half in zip(halves, [crossed(half, 1) for half in sent]) for w in half]
     attended = pl.pallas_call(
         attend_kernel,
         out_shape=jax.ShapeDtypeStruct((devices, dim, rows), BF),
@@ -473,21 +482,20 @@
         compiler_params=params(48),
         cost_estimate=cost(2**32, 2**22, 2**21),
     )(gathered, grid)
-    attended, held_y, held = lax.optimization_barrier((attended, held_y, held))
-    held_c = crossed(held, 1)
-    held_yc = crossed(held_y, 1)
     returned = lax.all_to_all(attended, "wide", split_axis=0, concat_axis=0, tiled=True)
+    returned, late_y = lax.optimization_barrier((returned, late_y))
+    late_yc = crossed(late_y, 1)
     planes = devices // 4
     message = out_width + 2 * LANES
     partial = pl.pallas_call(
         merge_kernel,
         out_shape=jax.ShapeDtypeStruct((planes, tokens, message), BF),
-        in_specs=[VMEM, VMEM, VMEM, VMEM, HBM, HBM, HBM, HBM],
+        in_specs=[VMEM] * 4 + [HBM] * 8,
         out_specs=VMEM,
         scratch_shapes=[
             pltpu.VMEM((vit_width, rows), BF),
             pltpu.VMEM((vit_width, out_width), BF),
-            pltpu.SemaphoreType.DMA((4,)),
+            pltpu.SemaphoreType.DMA((8,)),
         ],
         compiler_params=params(48),
     )(
@@ -495,10 +503,14 @@
         w_out,
         ln_gain.reshape(1, 4 * vit_width),
         ln_bias.reshape(1, 4 * vit_width),
-        held,
-        held_c,
-        held_y,
-        held_yc,
+        w_merge[:early],
+        early_c,
+        early_y,
+        early_yc,
+        w_merge[early:],
+        late_c,
+        late_y,
+        late_yc,
     )
     along = (4, 8, 12)
     arrived = [partial[0]] + [crossed(partial[k], mask) for k, mask in enumerate(along, 1)]
@@ -514,24 +526,25 @@
     )(*arrived, router, expert_ids)
     near = [routed] + [crossed(routed, mask) for mask in along]
     far = [crossed(block, 2) for block in near]
-    gate_turned, up_turned = jnp.swapaxes(w_gate, 1, 2), jnp.swapaxes(w_up, 1, 2)
 
     def experts_of(blocks):
-        own, other = pl.pallas_call(
+        return pl.pallas_call(
             lambda *refs: expert_kernel(*refs, experts=experts),
-            out_shape=[jax.ShapeDtypeStruct((planes, tokens, out_width), BF)] * 2,
-            in_specs=[VMEM] * (2 * planes + 3),
-            out_specs=[VMEM, VMEM],
-            scratch_shapes=[pltpu.VMEM((2 * planes * tokens, out_width), BF)],
-            compiler_params=params(48),
-            cost_estimate=cost(2**32, 2**24),
-        )(*blocks, *[crossed(block, 1) for block in blocks], gate_turned, up_turned, w_down)
-        total = (own.astype(F32) + crossed(other, 1).astype(F32)).astype(BF)
-        others = [crossed(total[k], mask) for k, mask in enumerate(along, 1)]
-        return total[0].astype(F32) + sum(block.astype(F32) for block in others)
-
-    near_sum = experts_of(near)
-    far_sum = experts_of(far)
+            out_shape=jax.ShapeDtypeStruct((planes, tokens, out_width), BF),
+            in_specs=[VMEM] * (planes + 6),
+            out_specs=VMEM,
+            scratch_shapes=[pltpu.VMEM((planes * tokens, out_width), BF)],
+            compiler_params=params(40),
+            cost_estimate=cost(2**31, 2**24),
+        )(*blocks, *weights)
+
+    def scattered(blocks):
+        others = [crossed(blocks[k], mask) for k, mask in enumerate(along, 1)]
+        return blocks[0].astype(F32) + sum(block.astype(F32) for block in others)
+
+    near_sum = scattered(experts_of(near))
+    far_out, near_sum = lax.optimization_barrier((experts_of(far), near_sum))
+    far_sum = scattered(far_out)
     return (near_sum + crossed(far_sum.astype(BF), 2).astype(F32)).astype(BF)
 
 

time: 155 us -> 156 us (level)
  blocking collectives: 18.5 us -> 0 us
  starting transfers between devices: 32.3 us -> 47.7 us
  waiting for transfers between devices: 68.3 us -> 56.4 us
  Pallas kernels: 23.5 us -> 31.8 us
  local copies, waits for them, and re-layouts: 10 us -> 16.7 us
    all_to_all x1 -> x0, blocking collectives: 18.5 us -> none  [local(): lax.all_to_all(packed, 'wide', split_axis=0, concat_axis=0, tiled=True, a...]
    ppermute x30 -> x26, waiting for transfers between devices: 62.3 us -> 51.6 us  [crossed(): return lax.ppermute(value, 'wide', pairs)]
    ppermute x30 -> x26, starting transfers between devices: 27.8 us -> 36.4 us  [crossed(): return lax.ppermute(value, 'wide', pairs)]
    pallas_call x2, Pallas kernels: 10.8 us -> 17.8 us  [experts_of(): pl.pallas_call(lambda *refs: expert_kernel(*refs, experts=experts), out_s...]
    all_to_all x0 -> x1, starting transfers between devices: none -> 5.26 us  [local(): lax.all_to_all(packed, 'wide', split_axis=0, concat_axis=0, tiled=True, a...]
    unnamed x22 -> x34, local copies, waits for them, and re-layouts: 7.12 us -> 11.8 us
    slice x0 -> x4, local copies, waits for them, and re-layouts: none -> 3.98 us  [the longest x1 1.78 us: local(): held[:early]]
  transfers between devices with their start and end apart: 31 -> 28, of which waited for: 12 -> 16; matrix products, arithmetic and copies ran while one was open for 3% -> 5% of each run, Pallas kernels for 11% -> 20%
where the time goes in v3:
time: 156 us; the launch traced here: 155 us
  waiting for transfers between devices  56.4 us (36%)
  starting transfers between devices  47.7 us (31%)
  Pallas kernels  31.8 us (20%)
  local copies, waits for them, and re-layouts  16.7 us (11%)
  other arithmetic  2.34 us (2%)
    ppermute x26, waiting for transfers between devices, crossed(): return lax.ppermute(value, 'wide', pairs)  51.6 us
    ppermute x26, starting transfers between devices, crossed(): return lax.ppermute(value, 'wide', pairs)  36.4 us
    pallas_call x2, Pallas kernels, experts_of(): pl.pallas_call(lambda *refs: expert_kernel(*refs, experts=experts), out_s...  17.8 us
    unnamed x34, local copies, waits for them, and re-layouts  11.8 us
    pallas_call x1, Pallas kernels, local(): pl.pallas_call(attend_kernel, out_shape=jax.ShapeDtypeStruct((devices, di...  6.52 us
    all_to_all x1, starting transfers between devices, local(): lax.all_to_all(attended, 'wide', split_axis=0, concat_axis=0, tiled=True)  5.98 us
    all_to_all x1, starting transfers between devices, local(): lax.all_to_all(packed, 'wide', split_axis=0, concat_axis=0, tiled=True, a...  5.26 us
    all_to_all x1, waiting for transfers between devices, local(): lax.all_to_all(attended, 'wide', split_axis=0, concat_axis=0, tiled=True)  4.84 us
  transfers between devices with their start and end apart: 28, of which 16 were waited for; matrix products, arithmetic and copies ran while one was open for 5% of the time, Pallas kernels for 20%

profile of v3, /device:TPU:0, one launch (start us, length us, event | category | flops | bytes accessed | tf_op | source)
XLA Modules:
  0.0 155.1 jit_solution(15508029385099887596)
XLA Ops:
  2.5 5.3 %all-to-all-start = ((bf16[8,432,128]{2,1,0:T(8,128)(2,1)}), bf16[8,432,128]{2,1,0:T(8,128)(2,1)S(1)}, u32[]{:S(2)}, u32[]{:S(2)}) async-start(bf16[8,432,128]{2,1,0:T(8,128)(2,1)} %shard_map.109), calls=%async_computation | async-start | bytes 1769472 | tf_op jit(solution)/shard_map/all_to_all | solution.py:468
  7.8 2.1 %collective-permute-start = (bf16[96,2048]{1,0:T(8,128)(2,1)S(1)}, bf16[96,2048]{1,0:T(8,128)(2,1)S(1)}, u32[]{:S(2)}, u32[]{:S(2)}) collective-permute-start(bf16[96,2048]{1,0:T(8,128)(2,1)S(1)} %slice.49.refs_0_), channel_id=1, source_target_pairs={{0,2},{1,3},{2,0},{3,1},{4,6},{5,7},{6,4},{7,5},{8,10},{9,11},{10,... | collective-permute-start | bytes 1179656 | tf_op jit(solution)/shard_map/ppermute | solution.py:431
  9.9 19.0 %collective-permute-done.refs_2_ = bf16[96,2048]{1,0:T(8,128)(2,1)S(1)} collective-permute-done((bf16[96,2048]{1,0:T(8,128)(2,1)S(1)}, bf16[96,2048]{1,0:T(8,128)(2,1)S(1)}, u32[]{:S(2)}, u32[]{:S(2)}) %collective-permute-start) | collective-permute-done | bytes 393248 | tf_op jit(solution)/shard_map/ppermute | solution.py:431
  32.6 6.5 %shard_map.110 = bf16[16,72,128]{2,1,0:T(8,128)(2,1)S(1)} custom-call(bf16[8,432,128]{2,1,0:T(8,128)(2,1)S(1)} %copy-done.4, s32[2,2]{1,0:T(2,128)S(1)} %copy-done.11), custom_call_target="tpu_custom_call" | custom-call | flops 4294967296 | bytes 4194304 | tf_op jit(solution)/shard_map/pallas_call | solution.py:477
  39.9 6.0 %all-to-all-start.1 = ((bf16[16,72,128]{2,1,0:T(8,128)(2,1)}), bf16[16,72,128]{2,1,0:T(8,128)(2,1)}, u32[]{:S(2)}, u32[]{:S(2)}) async-start(bf16[16,72,128]{2,1,0:T(8,128)(2,1)} %copy-done.7), calls=%async_computation.1 | async-start | bytes 589824 | tf_op jit(solution)/shard_map/all_to_all | solution.py:485
  48.8 2.9 %collective-permute-done.1.refs_6_ = bf16[192,2048]{1,0:T(8,128)(2,1)} collective-permute-done((bf16[192,2048]{1,0:T(8,128)(2,1)}, bf16[192,2048]{1,0:T(8,128)(2,1)}, u32[]{:S(2)}, u32[]{:S(2)}) %collective-permute-start.1) | collective-permute-done | bytes 786464 | tf_op jit(solution)/shard_map/ppermute | solution.py:431
  51.7 4.8 %all-to-all-done.1.x_ref = bf16[16,72,128]{2,1,0:T(8,128)(2,1)} async-done(((bf16[16,72,128]{2,1,0:T(8,128)(2,1)}), bf16[16,72,128]{2,1,0:T(8,128)(2,1)}, u32[]{:S(2)}, u32[]{:S(2)}) %all-to-all-start.1) | async-done | bytes 294944 | tf_op jit(solution)/shard_map/all_to_all | solution.py:485
  56.5 3.9 %collective-permute-done.2.refs_1_ = bf16[96,2048]{1,0:T(8,128)(2,1)} collective-permute-done((bf16[96,2048]{1,0:T(8,128)(2,1)}, bf16[96,2048]{1,0:T(8,128)(2,1)}, u32[]{:S(2)}, u32[]{:S(2)}) %collective-permute-start.2) | collective-permute-done | bytes 393248 | tf_op jit(solution)/shard_map/ppermute | solution.py:431
  65.0 4.6 %shard_map.111 = bf16[4,32,2304]{2,1,0:T(8,128)(2,1)S(1)} custom-call(bf16[16,72,128]{2,1,0:T(8,128)(2,1)} %all-to-all-done.1.x_ref, bf16[1152,1152]{1,0:T(8,128)(2,1)} %w_out_ref.1, f32[1,4608]{1,0:T(1,128)S(1)} %reshape.10.gain_ref, f32[1,4608]{1,0:T(1,128)S(1)} %reshape.11.bias_ref, bf16[96,2048]{1,0:T(8,128)(2,1)S(1)} %slice.49.refs_0_, ...), custom_call_target="tpu_custom_call" | custom-call | tf_op jit(solution)/shard_map/pallas_call | solution.py:490
  70.4 3.7 %collective-permute-start.8 = (bf16[32,2304]{1,0:T(8,128)(2,1)S(1)}, bf16[32,2304]{1,0:T(8,128)(2,1)S(1)}, u32[]{:S(2)}, u32[]{:S(2)}) collective-permute-start(bf16[32,2304]{1,0:T(8,128)(2,1)S(1)} %get-tuple-element.25), channel_id=1, source_target_pairs={{0,12},{1,13},{2,14},{3,15},{4,8},{5,9},{6,10},{7,11},{8,4},{9,5},... | collective-permute-start | bytes 442376 | tf_op jit(solution)/shard_map/ppermute | solution.py:431
  75.1 3.7 %collective-permute-done.8.refs_3_ = bf16[32,2304]{1,0:T(8,128)(2,1)S(1)} collective-permute-done((bf16[32,2304]{1,0:T(8,128)(2,1)S(1)}, bf16[32,2304]{1,0:T(8,128)(2,1)S(1)}, u32[]{:S(2)}, u32[]{:S(2)}) %collective-permute-start.8) | collective-permute-done | bytes 147488 | tf_op jit(solution)/shard_map/ppermute | solution.py:431
  79.5 6.4 %collective-permute-start.6 = (bf16[32,2304]{1,0:T(8,128)(2,1)}, bf16[32,2304]{1,0:T(8,128)(2,1)}, u32[]{:S(2)}, u32[]{:S(2)}) collective-permute-start(bf16[32,2304]{1,0:T(8,128)(2,1)} %get-tuple-element.27), channel_id=1, source_target_pairs={{0,4},{1,5},{2,6},{3,7},{4,0},{5,1},{6,2},{7,3},{8,12},{9,13},{10,... | collective-permute-start | bytes 442376 | tf_op jit(solution)/shard_map/ppermute | solution.py:431
  93.5 2.4 %collective-permute-start.14 = (bf16[32,2176]{1,0:T(8,128)(2,1)S(1)}, bf16[32,2176]{1,0:T(8,128)(2,1)S(1)}, u32[]{:S(2)}, u32[]{:S(2)}) collective-permute-start(bf16[32,2176]{1,0:T(8,128)(2,1)S(1)} %shard_map.112.refs_0_), channel_id=1, source_target_pairs={{0,12},{1,13},{2,14},{3,15},{4,8},{5,9},{6,10},{7,11},{8,4},{9,5},... | collective-permute-start | bytes 417800 | tf_op jit(solution)/shard_map/ppermute | solution.py:431
  96.0 6.1 %collective-permute-done.14.refs_3_ = bf16[32,2176]{1,0:T(8,128)(2,1)S(1)} collective-permute-done((bf16[32,2176]{1,0:T(8,128)(2,1)S(1)}, bf16[32,2176]{1,0:T(8,128)(2,1)S(1)}, u32[]{:S(2)}, u32[]{:S(2)}) %collective-permute-start.14) | collective-permute-done | bytes 139296 | tf_op jit(solution)/shard_map/ppermute | solution.py:431
  102.1 4.7 %collective-permute-start.10 = (bf16[32,2176]{1,0:T(8,128)(2,1)S(1)}, bf16[32,2176]{1,0:T(8,128)(2,1)S(1)}, u32[]{:S(2)}, u32[]{:S(2)}) collective-permute-start(bf16[32,2176]{1,0:T(8,128)(2,1)S(1)} %shard_map.112.refs_0_), channel_id=1, source_target_pairs={{0,4},{1,5},{2,6},{3,7},{4,0},{5,1},{6,2},{7,3},{8,12},{9,13},{10,... | collective-permute-start | bytes 417800 | tf_op jit(solution)/shard_map/ppermute | solution.py:431
  115.1 8.9 %shard_map.114 = bf16[4,32,2048]{2,1,0:T(8,128)(2,1)S(1)} custom-call(bf16[32,2176]{1,0:T(8,128)(2,1)S(1)} %shard_map.112.refs_0_, bf16[32,2176]{1,0:T(8,128)(2,1)S(1)} %collective-permute-done.10.refs_1_, bf16[32,2176]{1,0:T(8,128)(2,1)S(1)} %collective-permute-done.12.refs_2_, bf16[32,2176]{1,0:T(8,128)(2,1)S(1)} %collective-permute-done.14.refs_3_, ...), custom_call_target="tpu_custom_call" | custom-call | flops 2147483648 | bytes 16777216 | tf_op jit(solution)/shard_map/pallas_call | solution.py:531
  124.1 2.1 %collective-permute-start.19 = (bf16[32,2048]{1,0:T(8,128)(2,1)S(1)}, bf16[32,2048]{1,0:T(8,128)(2,1)S(1)}, u32[]{:S(2)}, u32[]{:S(2)}) collective-permute-start(bf16[32,2048]{1,0:T(8,128)(2,1)S(1)} %get-tuple-element.32), channel_id=1, source_target_pairs={{0,4},{1,5},{2,6},{3,7},{4,0},{5,1},{6,2},{7,3},{8,12},{9,13},{10,... | collective-permute-start | bytes 393224 | tf_op jit(solution)/shard_map/ppermute | solution.py:431
  126.2 2.5 %collective-permute-start.21 = (bf16[32,2048]{1,0:T(8,128)(2,1)S(1)}, bf16[32,2048]{1,0:T(8,128)(2,1)S(1)}, u32[]{:S(2)}, u32[]{:S(2)}) collective-permute-start(bf16[32,2048]{1,0:T(8,128)(2,1)S(1)} %get-tuple-element.33), channel_id=1, source_target_pairs={{0,12},{1,13},{2,14},{3,15},{4,8},{5,9},{6,10},{7,11},{8,4},{9,5},... | collective-permute-start | bytes 393224 | tf_op jit(solution)/shard_map/ppermute | solution.py:431
  128.7 8.9 %shard_map.113 = bf16[4,32,2048]{2,1,0:T(8,128)(2,1)S(1)} custom-call(bf16[32,2176]{1,0:T(8,128)(2,1)S(1)} %collective-permute-done.9.refs_0_, bf16[32,2176]{1,0:T(8,128)(2,1)S(1)} %collective-permute-done.11.refs_1_, bf16[32,2176]{1,0:T(8,128)(2,1)S(1)} %collective-permute-done.13.refs_2_, bf16[32,2176]{1,0:T(8,128)(2,1)S(1)} %collective-permute-done.15.refs_3_, ...), custom_call_target="tpu_custom_call" | custom-call | flops 2147483648 | bytes 16777216 | tf_op jit(solution)/shard_map/pallas_call | solution.py:531
  137.7 2.0 %collective-permute-start.22 = (bf16[32,2048]{1,0:T(8,128)(2,1)S(1)}, bf16[32,2048]{1,0:T(8,128)(2,1)S(1)}, u32[]{:S(2)}, u32[]{:S(2)}) collective-permute-start(bf16[32,2048]{1,0:T(8,128)(2,1)S(1)} %get-tuple-element.29), channel_id=1, source_target_pairs={{0,4},{1,5},{2,6},{3,7},{4,0},{5,1},{6,2},{7,3},{8,12},{9,13},{10,... | collective-permute-start | bytes 393224 | tf_op jit(solution)/shard_map/ppermute | solution.py:431
  139.7 2.5 %collective-permute-start.24 = (bf16[32,2048]{1,0:T(8,128)(2,1)S(1)}, bf16[32,2048]{1,0:T(8,128)(2,1)S(1)}, u32[]{:S(2)}, u32[]{:S(2)}) collective-permute-start(bf16[32,2048]{1,0:T(8,128)(2,1)S(1)} %get-tuple-element.30), channel_id=1, source_target_pairs={{0,12},{1,13},{2,14},{3,15},{4,8},{5,9},{6,10},{7,11},{8,4},{9,5},... | collective-permute-start | bytes 393224 | tf_op jit(solution)/shard_map/ppermute | solution.py:431
  143.1 3.4 %collective-permute-done.24 = bf16[32,2048]{1,0:T(8,128)(2,1)S(1)} collective-permute-done((bf16[32,2048]{1,0:T(8,128)(2,1)S(1)}, bf16[32,2048]{1,0:T(8,128)(2,1)S(1)}, u32[]{:S(2)}, u32[]{:S(2)}) %collective-permute-start.24) | collective-permute-done | bytes 131104 | tf_op jit(solution)/shard_map/ppermute | solution.py:431
  146.5 2.8 %collective-permute-done.23 = bf16[32,2048]{1,0:T(8,128)(2,1)S(1)} collective-permute-done((bf16[32,2048]{1,0:T(8,128)(2,1)S(1)}, bf16[32,2048]{1,0:T(8,128)(2,1)S(1)}, u32[]{:S(2)}, u32[]{:S(2)}) %collective-permute-start.23) | collective-permute-done | bytes 131104 | tf_op jit(solution)/shard_map/ppermute | solution.py:431
  150.3 4.1 %collective-permute-done.25 = bf16[32,2048]{1,0:T(8,128)(2,1)S(1)} collective-permute-done((bf16[32,2048]{1,0:T(8,128)(2,1)S(1)}, bf16[32,2048]{1,0:T(8,128)(2,1)S(1)}, u32[]{:S(2)}, u32[]{:S(2)}) %collective-permute-start.25) | collective-permute-done | bytes 131104 | tf_op jit(solution)/shard_map/ppermute | solution.py:431
  (87 shorter events, 35.8 us)
Async XLA Ops:
  2.5 26.4 %all-to-all-start = ((bf16[8,432,128]{2,1,0:T(8,128)(2,1)}), bf16[8,432,128]{2,1,0:T(8,128)(2,1)S(1)}, u32[]{:S(2)}, u32[]{:S(2)}) async-start(bf16[8,432,128]{2,1,0:T(8,128)(2,1)} %shard_map.109), calls=%async_computation | async-start | bytes 1769472 | tf_op jit(solution)/shard_map/all_to_all | solution.py:468
  7.8 21.1 %collective-permute-start = (bf16[96,2048]{1,0:T(8,128)(2,1)S(1)}, bf16[96,2048]{1,0:T(8,128)(2,1)S(1)}, u32[]{:S(2)}, u32[]{:S(2)}) collective-permute-start(bf16[96,2048]{1,0:T(8,128)(2,1)S(1)} %slice.49.refs_0_), channel_id=1, source_target_pairs={{0,2},{1,3},{2,0},{3,1},{4,6},{5,7},{6,4},{7,5},{8,10},{9,11},{10,... | collective-permute-start | bytes 1179656 | tf_op jit(solution)/shard_map/ppermute | solution.py:431
  30.9 20.7 %collective-permute-start.1 = (bf16[192,2048]{1,0:T(8,128)(2,1)}, bf16[192,2048]{1,0:T(8,128)(2,1)}, u32[]{:S(2)}, u32[]{:S(2)}) collective-permute-start(bf16[192,2048]{1,0:T(8,128)(2,1)} %slice.50), channel_id=1, source_target_pairs={{0,2},{1,3},{2,0},{3,1},{4,6},{5,7},{6,4},{7,5},{8,10},{9,11},{10,... | collective-permute-start | bytes 2359304 | tf_op jit(solution)/shard_map/ppermute | solution.py:431
  39.9 16.6 %all-to-all-start.1 = ((bf16[16,72,128]{2,1,0:T(8,128)(2,1)}), bf16[16,72,128]{2,1,0:T(8,128)(2,1)}, u32[]{:S(2)}, u32[]{:S(2)}) async-start(bf16[16,72,128]{2,1,0:T(8,128)(2,1)} %copy-done.7), calls=%async_computation.1 | async-start | bytes 589824 | tf_op jit(solution)/shard_map/all_to_all | solution.py:485
  45.9 65.4 %collective-permute-start.16 = (bf16[1,704,2048]{2,1,0:T(8,128)(2,1)S(1)}, bf16[1,704,2048]{2,1,0:T(8,128)(2,1)}, u32[]{:S(2)}, u32[]{:S(2)}) collective-permute-start(bf16[1,704,2048]{2,1,0:T(8,128)(2,1)S(1)} %bitcast.30), channel_id=1, source_target_pairs={{0,1},{1,0},{2,3},{3,2},{4,5},{5,4},{6,7},{7,6},{8,9},{9,8},{10,11... | collective-permute-start | bytes 8650760 | tf_op jit(solution)/shard_map/ppermute | solution.py:431
  46.3 65.6 %collective-permute-start.17 = (bf16[1,704,2048]{2,1,0:T(8,128)(2,1)}, bf16[1,704,2048]{2,1,0:T(8,128)(2,1)}, u32[]{:S(2)}, u32[]{:S(2)}) collective-permute-start(bf16[1,704,2048]{2,1,0:T(8,128)(2,1)} %bitcast.33), channel_id=1, source_target_pairs={{0,1},{1,0},{2,3},{3,2},{4,5},{5,4},{6,7},{7,6},{8,9},{9,8},{10,11... | collective-permute-start | bytes 8650760 | tf_op jit(solution)/shard_map/ppermute | solution.py:431
  46.5 66.9 %collective-permute-start.18 = (bf16[1,704,2048]{2,1,0:T(8,128)(2,1)}, bf16[1,704,2048]{2,1,0:T(8,128)(2,1)}, u32[]{:S(2)}, u32[]{:S(2)}) collective-permute-start(bf16[1,704,2048]{2,1,0:T(8,128)(2,1)} %refs_8_.3), channel_id=1, source_target_pairs={{0,1},{1,0},{2,3},{3,2},{4,5},{5,4},{6,7},{7,6},{8,9},{9,8},{10,11... | collective-permute-start | bytes 8650760 | tf_op jit(solution)/shard_map/ppermute | solution.py:431
  48.6 11.8 %collective-permute-start.2 = (bf16[96,2048]{1,0:T(8,128)(2,1)}, bf16[96,2048]{1,0:T(8,128)(2,1)}, u32[]{:S(2)}, u32[]{:S(2)}) collective-permute-start(bf16[96,2048]{1,0:T(8,128)(2,1)} %slice.51), channel_id=1, source_target_pairs={{0,1},{1,0},{2,3},{3,2},{4,5},{5,4},{6,7},{7,6},{8,9},{9,8},{10,11... | collective-permute-start | bytes 1179656 | tf_op jit(solution)/shard_map/ppermute | solution.py:431
  51.7 9.3 %collective-permute-start.3 = (bf16[96,2048]{1,0:T(8,128)(2,1)}, bf16[96,2048]{1,0:T(8,128)(2,1)}, u32[]{:S(2)}, u32[]{:S(2)}) collective-permute-start(bf16[96,2048]{1,0:T(8,128)(2,1)} %copy-done.5), channel_id=1, source_target_pairs={{0,1},{1,0},{2,3},{3,2},{4,5},{5,4},{6,7},{7,6},{8,9},{9,8},{10,11... | collective-permute-start | bytes 1179656 | tf_op jit(solution)/shard_map/ppermute | solution.py:431
  70.4 8.4 %collective-permute-start.8 = (bf16[32,2304]{1,0:T(8,128)(2,1)S(1)}, bf16[32,2304]{1,0:T(8,128)(2,1)S(1)}, u32[]{:S(2)}, u32[]{:S(2)}) collective-permute-start(bf16[32,2304]{1,0:T(8,128)(2,1)S(1)} %get-tuple-element.25), channel_id=1, source_target_pairs={{0,12},{1,13},{2,14},{3,15},{4,8},{5,9},{6,10},{7,11},{8,4},{9,5},... | collective-permute-start | bytes 442376 | tf_op jit(solution)/shard_map/ppermute | solution.py:431
  75.1 13.7 %collective-permute-start.7 = (bf16[32,2304]{1,0:T(8,128)(2,1)}, bf16[32,2304]{1,0:T(8,128)(2,1)}, u32[]{:S(2)}, u32[]{:S(2)}) collective-permute-start(bf16[32,2304]{1,0:T(8,128)(2,1)} %get-tuple-element.26), channel_id=1, source_target_pairs={{0,8},{1,9},{2,10},{3,11},{4,12},{5,13},{6,14},{7,15},{8,0},{9,1},... | collective-permute-start | bytes 442376 | tf_op jit(solution)/shard_map/ppermute | solution.py:431
  79.5 10.9 %collective-permute-start.6 = (bf16[32,2304]{1,0:T(8,128)(2,1)}, bf16[32,2304]{1,0:T(8,128)(2,1)}, u32[]{:S(2)}, u32[]{:S(2)}) collective-permute-start(bf16[32,2304]{1,0:T(8,128)(2,1)} %get-tuple-element.27), channel_id=1, source_target_pairs={{0,4},{1,5},{2,6},{3,7},{4,0},{5,1},{6,2},{7,3},{8,12},{9,13},{10,... | collective-permute-start | bytes 442376 | tf_op jit(solution)/shard_map/ppermute | solution.py:431
  93.5 8.6 %collective-permute-start.14 = (bf16[32,2176]{1,0:T(8,128)(2,1)S(1)}, bf16[32,2176]{1,0:T(8,128)(2,1)S(1)}, u32[]{:S(2)}, u32[]{:S(2)}) collective-permute-start(bf16[32,2176]{1,0:T(8,128)(2,1)S(1)} %shard_map.112.refs_0_), channel_id=1, source_target_pairs={{0,12},{1,13},{2,14},{3,15},{4,8},{5,9},{6,10},{7,11},{8,4},{9,5},... | collective-permute-start | bytes 417800 | tf_op jit(solution)/shard_map/ppermute | solution.py:431
  95.9 11.9 %collective-permute-start.12 = (bf16[32,2176]{1,0:T(8,128)(2,1)S(1)}, bf16[32,2176]{1,0:T(8,128)(2,1)S(1)}, u32[]{:S(2)}, u32[]{:S(2)}) collective-permute-start(bf16[32,2176]{1,0:T(8,128)(2,1)S(1)} %shard_map.112.refs_0_), channel_id=1, source_target_pairs={{0,8},{1,9},{2,10},{3,11},{4,12},{5,13},{6,14},{7,15},{8,0},{9,1},... | collective-permute-start | bytes 417800 | tf_op jit(solution)/shard_map/ppermute | solution.py:431
  102.1 7.8 %collective-permute-start.10 = (bf16[32,2176]{1,0:T(8,128)(2,1)S(1)}, bf16[32,2176]{1,0:T(8,128)(2,1)S(1)}, u32[]{:S(2)}, u32[]{:S(2)}) collective-permute-start(bf16[32,2176]{1,0:T(8,128)(2,1)S(1)} %shard_map.112.refs_0_), channel_id=1, source_target_pairs={{0,4},{1,5},{2,6},{3,7},{4,0},{5,1},{6,2},{7,3},{8,12},{9,13},{10,... | collective-permute-start | bytes 417800 | tf_op jit(solution)/shard_map/ppermute | solution.py:431
  107.8 18.3 %collective-permute-start.9 = (bf16[32,2176]{1,0:T(8,128)(2,1)S(1)}, bf16[32,2176]{1,0:T(8,128)(2,1)S(1)}, u32[]{:S(2)}, u32[]{:S(2)}) collective-permute-start(bf16[32,2176]{1,0:T(8,128)(2,1)S(1)} %shard_map.112.refs_0_), channel_id=1, source_target_pairs={{0,2},{1,3},{2,0},{3,1},{4,6},{5,7},{6,4},{7,5},{8,10},{9,11},{10,... | collective-permute-start | bytes 417800 | tf_op jit(solution)/shard_map/ppermute | solution.py:431
  109.8 18.8 %collective-permute-start.15 = (bf16[32,2176]{1,0:T(8,128)(2,1)S(1)}, bf16[32,2176]{1,0:T(8,128)(2,1)S(1)}, u32[]{:S(2)}, u32[]{:S(2)}) collective-permute-start(bf16[32,2176]{1,0:T(8,128)(2,1)S(1)} %collective-permute-done.14.refs_3_), channel_id=1, source_target_pairs={{0,2},{1,3},{2,0},{3,1},{4,6},{5,7},{6,4},{7,5},{8,10},{9,11},{10,... | collective-permute-start | bytes 417800 | tf_op jit(solution)/shard_map/ppermute | solution.py:431
  111.3 17.4 %collective-permute-start.13 = (bf16[32,2176]{1,0:T(8,128)(2,1)S(1)}, bf16[32,2176]{1,0:T(8,128)(2,1)S(1)}, u32[]{:S(2)}, u32[]{:S(2)}) collective-permute-start(bf16[32,2176]{1,0:T(8,128)(2,1)S(1)} %collective-permute-done.12.refs_2_), channel_id=1, source_target_pairs={{0,2},{1,3},{2,0},{3,1},{4,6},{5,7},{6,4},{7,5},{8,10},{9,11},{10,... | collective-permute-start | bytes 417800 | tf_op jit(solution)/shard_map/ppermute | solution.py:431
  111.9 16.8 %collective-permute-start.11 = (bf16[32,2176]{1,0:T(8,128)(2,1)S(1)}, bf16[32,2176]{1,0:T(8,128)(2,1)S(1)}, u32[]{:S(2)}, u32[]{:S(2)}) collective-permute-start(bf16[32,2176]{1,0:T(8,128)(2,1)S(1)} %collective-permute-done.10.refs_1_), channel_id=1, source_target_pairs={{0,2},{1,3},{2,0},{3,1},{4,6},{5,7},{6,4},{7,5},{8,10},{9,11},{10,... | collective-permute-start | bytes 417800 | tf_op jit(solution)/shard_map/ppermute | solution.py:431
  124.1 13.5 %collective-permute-start.19 = (bf16[32,2048]{1,0:T(8,128)(2,1)S(1)}, bf16[32,2048]{1,0:T(8,128)(2,1)S(1)}, u32[]{:S(2)}, u32[]{:S(2)}) collective-permute-start(bf16[32,2048]{1,0:T(8,128)(2,1)S(1)} %get-tuple-element.32), channel_id=1, source_target_pairs={{0,4},{1,5},{2,6},{3,7},{4,0},{5,1},{6,2},{7,3},{8,12},{9,13},{10,... | collective-permute-start | bytes 393224 | tf_op jit(solution)/shard_map/ppermute | solution.py:431
  126.2 11.4 %collective-permute-start.21 = (bf16[32,2048]{1,0:T(8,128)(2,1)S(1)}, bf16[32,2048]{1,0:T(8,128)(2,1)S(1)}, u32[]{:S(2)}, u32[]{:S(2)}) collective-permute-start(bf16[32,2048]{1,0:T(8,128)(2,1)S(1)} %get-tuple-element.33), channel_id=1, source_target_pairs={{0,12},{1,13},{2,14},{3,15},{4,8},{5,9},{6,10},{7,11},{8,4},{9,5},... | collective-permute-start | bytes 393224 | tf_op jit(solution)/shard_map/ppermute | solution.py:431
  128.6 9.0 %collective-permute-start.20 = (bf16[32,2048]{1,0:T(8,128)(2,1)S(1)}, bf16[32,2048]{1,0:T(8,128)(2,1)S(1)}, u32[]{:S(2)}, u32[]{:S(2)}) collective-permute-start(bf16[32,2048]{1,0:T(8,128)(2,1)S(1)} %get-tuple-element.34), channel_id=1, source_target_pairs={{0,8},{1,9},{2,10},{3,11},{4,12},{5,13},{6,14},{7,15},{8,0},{9,1},... | collective-permute-start | bytes 393224 | tf_op jit(solution)/shard_map/ppermute | solution.py:431
  139.7 6.8 %collective-permute-start.24 = (bf16[32,2048]{1,0:T(8,128)(2,1)S(1)}, bf16[32,2048]{1,0:T(8,128)(2,1)S(1)}, u32[]{:S(2)}, u32[]{:S(2)}) collective-permute-start(bf16[32,2048]{1,0:T(8,128)(2,1)S(1)} %get-tuple-element.30), channel_id=1, source_target_pairs={{0,12},{1,13},{2,14},{3,15},{4,8},{5,9},{6,10},{7,11},{8,4},{9,5},... | collective-permute-start | bytes 393224 | tf_op jit(solution)/shard_map/ppermute | solution.py:431
  142.2 7.2 %collective-permute-start.23 = (bf16[32,2048]{1,0:T(8,128)(2,1)S(1)}, bf16[32,2048]{1,0:T(8,128)(2,1)S(1)}, u32[]{:S(2)}, u32[]{:S(2)}) collective-permute-start(bf16[32,2048]{1,0:T(8,128)(2,1)S(1)} %get-tuple-element.31), channel_id=1, source_target_pairs={{0,8},{1,9},{2,10},{3,11},{4,12},{5,13},{6,14},{7,15},{8,0},{9,1},... | collective-permute-start | bytes 393224 | tf_op jit(solution)/shard_map/ppermute | solution.py:431
  (20 other events, 134.8 us)

commit v4 on v2

--- a/solution.py
+++ b/solution.py
@@ -212,7 +212,7 @@
 F32 = jnp.float32
 VMEM = pl.BlockSpec(memory_space=pltpu.VMEM)
 SMEM = pl.BlockSpec(memory_space=pltpu.SMEM)
-HBM = pl.BlockSpec(memory_space=pl.ANY)
+HBM = pl.BlockSpec(memory_space=pltpu.HBM)
 LANES = 128
 MASKED = -1e30
 LOG2E = 1.4426950408889634
@@ -397,10 +397,17 @@
     out_ref[:, out_width:] = jnp.where(lane < experts, high, low).astype(BF)
 
 
-def expert_kernel(*refs, experts):
-    *blocks, gate_ref, up_ref, down_ref, own_ref, other_ref, x_ref = refs
+def expert_kernel(*refs, experts, cuts):
+    *blocks, gate_hbm, up_hbm, down_hbm, own_ref, other_ref, x_ref, gate_ref, up_ref, down_ref, sems = refs
     tokens, width = own_ref.shape[1:]
     half = len(blocks) // 2
+    copies = []
+    for k, cut in enumerate(cuts):
+        for kind, source, target in ((0, gate_hbm, gate_ref), (1, up_hbm, up_ref)):
+            copies.append(pltpu.make_async_copy(source.at[0, cut, :], target.at[cut, :], sems.at[2 * k + kind]))
+            copies[-1].start()
+    last = pltpu.make_async_copy(down_hbm.at[0], down_ref, sems.at[2 * len(cuts)])
+    last.start()
     expert = lax.axis_index("wide") // 2
     lane = lax.broadcasted_iota(jnp.int32, (tokens, LANES), 1)
     weights = []
@@ -411,12 +418,18 @@
         weights.append(jnp.sum(picked, axis=1, keepdims=True))
     inputs = x_ref[...]
     turned = (((1,), (1,)), ((), ()))
-    gate = lax.dot_general(inputs, gate_ref[0], turned, preferred_element_type=F32)
-    up = lax.dot_general(inputs, up_ref[0], turned, preferred_element_type=F32)
-    hidden = (gate / (1.0 + jnp.exp(-gate)) * up).astype(BF)
+    hidden = []
+    for k, cut in enumerate(cuts):
+        copies[2 * k].wait()
+        gate = lax.dot_general(inputs, gate_ref[cut, :], turned, preferred_element_type=F32)
+        copies[2 * k + 1].wait()
+        up = lax.dot_general(inputs, up_ref[cut, :], turned, preferred_element_type=F32)
+        hidden.append((gate / (1.0 + jnp.exp(-gate)) * up).astype(BF))
+    hidden = jnp.concatenate(hidden, 1)
+    last.wait()
     step = 4 * LANES
     for begin in range(0, width, step):
-        product = jnp.dot(hidden, down_ref[0, :, begin : begin + step], preferred_element_type=F32)
+        product = jnp.dot(hidden, down_ref[:, begin : begin + step], preferred_element_type=F32)
         for k in range(len(blocks)):
             value = (product[k * tokens : (k + 1) * tokens] * weights[k]).astype(BF)
             out_ref = own_ref if k < half else other_ref
@@ -457,7 +470,7 @@
         out_shape=jax.ShapeDtypeStruct((peers, 3 * part, rows), BF),
         in_specs=[VMEM],
         out_specs=VMEM,
-        compiler_params=params(32),
+        compiler_params=params(8),
     )(qkv)
     clips = [[c * peers + i for i in range(peers)] for c in range(CLIPS)]
     gathered = lax.all_to_all(
@@ -470,13 +483,13 @@
         out_shape=jax.ShapeDtypeStruct((devices, dim, rows), BF),
         in_specs=[VMEM, SMEM],
         out_specs=VMEM,
-        compiler_params=params(48),
+        compiler_params=params(20),
         cost_estimate=cost(2**32, 2**22, 2**21),
     )(gathered, grid)
-    attended, held_y, held = lax.optimization_barrier((attended, held_y, held))
     held_c = crossed(held, 1)
+    returned = lax.all_to_all(attended, "wide", split_axis=0, concat_axis=0, tiled=True)
+    returned, held_y = lax.optimization_barrier((returned, held_y))
     held_yc = crossed(held_y, 1)
-    returned = lax.all_to_all(attended, "wide", split_axis=0, concat_axis=0, tiled=True)
     planes = devices // 4
     message = out_width + 2 * LANES
     partial = pl.pallas_call(
@@ -489,7 +502,7 @@
             pltpu.VMEM((vit_width, out_width), BF),
             pltpu.SemaphoreType.DMA((4,)),
         ],
-        compiler_params=params(48),
+        compiler_params=params(20),
     )(
         returned,
         w_out,
@@ -510,28 +523,45 @@
         out_shape=jax.ShapeDtypeStruct((tokens, out_width + LANES), BF),
         in_specs=[VMEM] * 6,
         out_specs=VMEM,
-        compiler_params=params(32),
+        compiler_params=params(6),
     )(*arrived, router, expert_ids)
     near = [routed] + [crossed(routed, mask) for mask in along]
     far = [crossed(block, 2) for block in near]
     gate_turned, up_turned = jnp.swapaxes(w_gate, 1, 2), jnp.swapaxes(w_up, 1, 2)
 
+    inner = w_down.shape[1]
+    cuts = [slice(k, min(k + 2 * LANES, inner)) for k in range(0, inner, 2 * LANES)]
+
     def experts_of(blocks):
-        own, other = pl.pallas_call(
-            lambda *refs: expert_kernel(*refs, experts=experts),
+        return pl.pallas_call(
+            lambda *refs: expert_kernel(*refs, experts=experts, cuts=cuts),
             out_shape=[jax.ShapeDtypeStruct((planes, tokens, out_width), BF)] * 2,
-            in_specs=[VMEM] * (2 * planes + 3),
+            in_specs=[VMEM] * (2 * planes) + [HBM] * 3,
             out_specs=[VMEM, VMEM],
-            scratch_shapes=[pltpu.VMEM((2 * planes * tokens, out_width), BF)],
-            compiler_params=params(48),
+            scratch_shapes=[
+                pltpu.VMEM((2 * planes * tokens, out_width), BF),
+                pltpu.VMEM((inner, out_width), BF),
+                pltpu.VMEM((inner, out_width), BF),
+                pltpu.VMEM((inner, out_width), BF),
+                pltpu.SemaphoreType.DMA((2 * len(cuts) + 1,)),
+            ],
+            compiler_params=params(32),
             cost_estimate=cost(2**32, 2**24),
         )(*blocks, *[crossed(block, 1) for block in blocks], gate_turned, up_turned, w_down)
-        total = (own.astype(F32) + crossed(other, 1).astype(F32)).astype(BF)
-        others = [crossed(total[k], mask) for k, mask in enumerate(along, 1)]
-        return total[0].astype(F32) + sum(block.astype(F32) for block in others)
-
-    near_sum = experts_of(near)
-    far_sum = experts_of(far)
+
+    def scattered(blocks):
+        others = [crossed(blocks[k], mask) for k, mask in enumerate(along, 1)]
+        return blocks[0].astype(F32) + sum(block.astype(F32) for block in others)
+
+    def paired(own, other):
+        return (own.astype(F32) + crossed(other, 1).astype(F32)).astype(BF)
+
+    near_own, near_other = experts_of(near)
+    *far, near_own, near_other = lax.optimization_barrier((*far, near_own, near_other))
+    far_own, far_other = experts_of(far)
+    near_sum = scattered(paired(near_own, near_other))
+    far_out, near_sum = lax.optimization_barrier((paired(far_own, far_other), near_sum))
+    far_sum = scattered(far_out)
     return (near_sum + crossed(far_sum.astype(BF), 2).astype(F32)).astype(BF)
 
 

time: 155 us -> 144 us (0.929)
  waiting for transfers between devices: 68.3 us -> 58.1 us
  local copies, waits for them, and re-layouts: 10 us -> 7.21 us
    ppermute x30, waiting for transfers between devices: 62.3 us -> 40.6 us  [crossed(): return lax.ppermute(value, 'wide', pairs)]
    all_to_all x1, waiting for transfers between devices: 6.06 us -> 17.4 us  [local(): lax.all_to_all(attended, 'wide', split_axis=0, concat_axis=0, tiled=True)]
    unnamed x22 -> x28, local copies, waits for them, and re-layouts: 7.12 us -> 7 us
  transfers between devices with their start and end apart: 31 -> 31, of which waited for: 12 -> 11; matrix products, arithmetic and copies ran while one was open for 3% -> 1% of each run, Pallas kernels for 11% -> 14%
where the time goes in v4:
time: 144 us; the launch traced here: 143 us
  waiting for transfers between devices  58.1 us (40%)
  starting transfers between devices  33.4 us (23%)
  Pallas kernels  24.4 us (17%)
  blocking collectives  18.5 us (13%)
  local copies, waits for them, and re-layouts  7.21 us (5%)
    ppermute x30, waiting for transfers between devices, crossed(): return lax.ppermute(value, 'wide', pairs)  40.6 us
    ppermute x30, starting transfers between devices, crossed(): return lax.ppermute(value, 'wide', pairs)  28.7 us
    all_to_all x1, blocking collectives, local(): lax.all_to_all(packed, 'wide', split_axis=0, concat_axis=0, tiled=True, a...  18.5 us
    all_to_all x1, waiting for transfers between devices, local(): lax.all_to_all(attended, 'wide', split_axis=0, concat_axis=0, tiled=True)  17.4 us
    pallas_call x2, Pallas kernels, experts_of(): pl.pallas_call(lambda *refs: expert_kernel(*refs, experts=experts, cuts=c...  12.1 us
    pallas_call x1, Pallas kernels, local(): pl.pallas_call(attend_kernel, out_shape=jax.ShapeDtypeStruct((devices, di...  7.24 us
    unnamed x28, local copies, waits for them, and re-layouts  7 us
    all_to_all x1, starting transfers between devices, local(): lax.all_to_all(attended, 'wide', split_axis=0, concat_axis=0, tiled=True)  4.74 us
  transfers between devices with their start and end apart: 31, of which 11 were waited for; matrix products, arithmetic and copies ran while one was open for 1% of the time, Pallas kernels for 14%

profile of v4, /device:TPU:0, one launch (start us, length us, event | category | flops | bytes accessed | tf_op | source)
XLA Modules:
  0.0 143.4 jit_solution(1676994478313860560)
XLA Ops:
  1.6 18.5 %all_to_all.10.x_ref = bf16[8,432,128]{2,1,0:T(8,128)(2,1)S(1)} all-to-all(bf16[8,432,128]{2,1,0:T(8,128)(2,1)S(1)} %shard_map.109), channel_id=1, replica_groups={{0,1,2,3,4,5,6,7},{8,9,10,11,12,13,14,15},{16,17,18,19,20,21,22,23},{24..., dimensions={0} | all-to-all | bytes 1769472 | tf_op jit(solution)/shard_map/all_to_all | solution.py:476
  21.0 7.2 %shard_map.110 = bf16[16,72,128]{2,1,0:T(8,128)(2,1)} custom-call(bf16[8,432,128]{2,1,0:T(8,128)(2,1)S(1)} %all_to_all.10.x_ref, s32[2,2]{1,0:T(2,128)S(1)} %copy-done.8), custom_call_target="tpu_custom_call" | custom-call | flops 4294967296 | bytes 4194304 | tf_op jit(solution)/shard_map/pallas_call | solution.py:481
  28.2 4.7 %all-to-all-start.1 = ((bf16[16,72,128]{2,1,0:T(8,128)(2,1)}), bf16[16,72,128]{2,1,0:T(8,128)(2,1)S(1)}, u32[]{:S(2)}, u32[]{:S(2)}) async-start(bf16[16,72,128]{2,1,0:T(8,128)(2,1)} %shard_map.110), calls=%async_computation.1 | async-start | bytes 589824 | tf_op jit(solution)/shard_map/all_to_all | solution.py:490
  33.4 17.4 %all-to-all-done.1.x_ref = bf16[16,72,128]{2,1,0:T(8,128)(2,1)S(1)} async-done(((bf16[16,72,128]{2,1,0:T(8,128)(2,1)}), bf16[16,72,128]{2,1,0:T(8,128)(2,1)S(1)}, u32[]{:S(2)}, u32[]{:S(2)}) %all-to-all-start.1) | async-done | bytes 294944 | tf_op jit(solution)/shard_map/all_to_all | solution.py:490
  51.4 2.6 %collective-permute-done.2.w3 = bf16[288,2048]{1,0:T(8,128)(2,1)} collective-permute-done((bf16[288,2048]{1,0:T(8,128)(2,1)}, bf16[288,2048]{1,0:T(8,128)(2,1)}, u32[]{:S(2)}, u32[]{:S(2)}) %collective-permute-start.2) | collective-permute-done | bytes 1179680 | tf_op jit(solution)/shard_map/ppermute | solution.py:441
  54.1 4.1 %shard_map.111 = bf16[4,32,2304]{2,1,0:T(8,128)(2,1)S(1)} custom-call(bf16[16,72,128]{2,1,0:T(8,128)(2,1)S(1)} %all-to-all-done.1.x_ref, bf16[1152,1152]{1,0:T(8,128)(2,1)S(1)} %copy-done, f32[1,4608]{1,0:T(1,128)S(1)} %reshape.10.gain_ref, f32[1,4608]{1,0:T(1,128)S(1)} %reshape.11.bias_ref, bf16[288,2048]{1,0:T(8,128)(2,1)} %w0, ...), custom_call_target="tpu_custom_call" | custom-call | tf_op jit(solution)/shard_map/pallas_call | solution.py:495
  59.0 2.6 %collective-permute-start.4 = (bf16[32,2304]{1,0:T(8,128)(2,1)S(1)}, bf16[32,2304]{1,0:T(8,128)(2,1)S(1)}, u32[]{:S(2)}, u32[]{:S(2)}) collective-permute-start(bf16[32,2304]{1,0:T(8,128)(2,1)S(1)} %get-tuple-element.38), channel_id=1, source_target_pairs={{0,8},{1,9},{2,10},{3,11},{4,12},{5,13},{6,14},{7,15},{8,0},{9,1},... | collective-permute-start | bytes 442376 | tf_op jit(solution)/shard_map/ppermute | solution.py:441
  63.1 4.1 %collective-permute-done.3.refs_1_ = bf16[32,2304]{1,0:T(8,128)(2,1)S(1)} collective-permute-done((bf16[32,2304]{1,0:T(8,128)(2,1)S(1)}, bf16[32,2304]{1,0:T(8,128)(2,1)S(1)}, u32[]{:S(2)}, u32[]{:S(2)}) %collective-permute-start.3) | collective-permute-done | bytes 147488 | tf_op jit(solution)/shard_map/ppermute | solution.py:441
  67.1 5.9 %collective-permute-done.4.refs_2_ = bf16[32,2304]{1,0:T(8,128)(2,1)S(1)} collective-permute-done((bf16[32,2304]{1,0:T(8,128)(2,1)S(1)}, bf16[32,2304]{1,0:T(8,128)(2,1)S(1)}, u32[]{:S(2)}, u32[]{:S(2)}) %collective-permute-start.4) | collective-permute-done | bytes 147488 | tf_op jit(solution)/shard_map/ppermute | solution.py:441
  73.5 2.7 %collective-permute-start.7 = (bf16[32,2176]{1,0:T(8,128)(2,1)S(1)}, bf16[32,2176]{1,0:T(8,128)(2,1)S(1)}, u32[]{:S(2)}, u32[]{:S(2)}) collective-permute-start(bf16[32,2176]{1,0:T(8,128)(2,1)S(1)} %shard_map.112.refs_0_), channel_id=1, source_target_pairs={{0,4},{1,5},{2,6},{3,7},{4,0},{5,1},{6,2},{7,3},{8,12},{9,13},{10,... | collective-permute-start | bytes 417800 | tf_op jit(solution)/shard_map/ppermute | solution.py:441
  76.3 1.8 %collective-permute-start.9 = (bf16[32,2176]{1,0:T(8,128)(2,1)S(1)}, bf16[32,2176]{1,0:T(8,128)(2,1)S(1)}, u32[]{:S(2)}, u32[]{:S(2)}) collective-permute-start(bf16[32,2176]{1,0:T(8,128)(2,1)S(1)} %shard_map.112.refs_0_), channel_id=1, source_target_pairs={{0,8},{1,9},{2,10},{3,11},{4,12},{5,13},{6,14},{7,15},{8,0},{9,1},... | collective-permute-start | bytes 417800 | tf_op jit(solution)/shard_map/ppermute | solution.py:441
  79.5 1.6 %collective-permute-done.7.refs_1_ = bf16[32,2176]{1,0:T(8,128)(2,1)S(1)} collective-permute-done((bf16[32,2176]{1,0:T(8,128)(2,1)S(1)}, bf16[32,2176]{1,0:T(8,128)(2,1)S(1)}, u32[]{:S(2)}, u32[]{:S(2)}) %collective-permute-start.7) | collective-permute-done | bytes 139296 | tf_op jit(solution)/shard_map/ppermute | solution.py:441
  81.1 8.4 %collective-permute-done.9.refs_2_ = bf16[32,2176]{1,0:T(8,128)(2,1)S(1)} collective-permute-done((bf16[32,2176]{1,0:T(8,128)(2,1)S(1)}, bf16[32,2176]{1,0:T(8,128)(2,1)S(1)}, u32[]{:S(2)}, u32[]{:S(2)}) %collective-permute-start.9) | collective-permute-done | bytes 139296 | tf_op jit(solution)/shard_map/ppermute | solution.py:441
  94.1 1.8 %copy-done.2 = bf16[1,2048,704]{1,2,0:T(8,128)(2,1)S(1)} copy-done((bf16[1,2048,704]{1,2,0:T(8,128)(2,1)S(1)}, bf16[1,2048,704]{1,2,0:T(8,128)(2,1)}, u32[]{:S(2)}) %copy-start.2) | copy-done | bytes 2883608
  95.9 1.8 %copy-done.4 = bf16[1,2048,704]{1,2,0:T(8,128)(2,1)S(1)} copy-done((bf16[1,2048,704]{1,2,0:T(8,128)(2,1)S(1)}, bf16[1,2048,704]{1,2,0:T(8,128)(2,1)}, u32[]{:S(2)}) %copy-start.4) | copy-done | bytes 2883608
  97.7 1.8 %copy-done.6 = bf16[1,704,2048]{2,1,0:T(8,128)(2,1)S(1)} copy-done((bf16[1,704,2048]{2,1,0:T(8,128)(2,1)S(1)}, bf16[1,704,2048]{2,1,0:T(8,128)(2,1)}, u32[]{:S(2)}) %copy-start.6) | copy-done | bytes 2883608
  99.5 6.1 %shard_map.113 = (bf16[4,32,2048]{2,1,0:T(8,128)(2,1)S(1)}, bf16[4,32,2048]{2,1,0:T(8,128)(2,1)S(1)}) custom-call(bf16[32,2176]{1,0:T(8,128)(2,1)S(1)} %shard_map.112.refs_0_, bf16[32,2176]{1,0:T(8,128)(2,1)S(1)} %collective-permute-done.7.refs_1_, bf16[32,2176]{1,0:T(8,128)(2,1)S(1)} %collective-permute-done.9.refs_2_, ...), custom_call_target="tpu_custom_call" | custom-call | flops 4294967296 | bytes 16777216 | tf_op jit(solution)/shard_map/pallas_call | solution.py:536
  107.8 1.8 %collective-permute-start.23 = (bf16[32,2048]{1,0:T(8,128)(2,1)S(1)}, bf16[32,2048]{1,0:T(8,128)(2,1)S(1)}, u32[]{:S(2)}, u32[]{:S(2)}) collective-permute-start(bf16[32,2048]{1,0:T(8,128)(2,1)S(1)} %get-tuple-element.44), channel_id=1, source_target_pairs={{0,4},{1,5},{2,6},{3,7},{4,0},{5,1},{6,2},{7,3},{8,12},{9,13},{10,... | collective-permute-start | bytes 393224 | tf_op jit(solution)/shard_map/ppermute | solution.py:441
  112.5 6.1 %shard_map.114 = (bf16[4,32,2048]{2,1,0:T(8,128)(2,1)S(1)}, bf16[4,32,2048]{2,1,0:T(8,128)(2,1)S(1)}) custom-call(bf16[32,2176]{1,0:T(8,128)(2,1)S(1)} %collective-permute-done.6.refs_0_, bf16[32,2176]{1,0:T(8,128)(2,1)S(1)} %collective-permute-done.8.refs_1_, bf16[32,2176]{1,0:T(8,128)(2,1)S(1)} %collective-permute-done.10.refs_2_, ...), custom_call_target="tpu_custom_call" | custom-call | flops 4294967296 | bytes 16777216 | tf_op jit(solution)/shard_map/pallas_call | solution.py:536
  118.6 3.9 %collective-permute-done.24 = bf16[32,2048]{1,0:T(8,128)(2,1)S(1)} collective-permute-done((bf16[32,2048]{1,0:T(8,128)(2,1)S(1)}, bf16[32,2048]{1,0:T(8,128)(2,1)S(1)}, u32[]{:S(2)}, u32[]{:S(2)}) %collective-permute-start.24) | collective-permute-done | bytes 131104 | tf_op jit(solution)/shard_map/ppermute | solution.py:441
  122.7 2.4 %collective-permute-start.26 = (bf16[32,2048]{1,0:T(8,128)(2,1)S(1)}, bf16[32,2048]{1,0:T(8,128)(2,1)S(1)}, u32[]{:S(2)}, u32[]{:S(2)}) collective-permute-start(bf16[32,2048]{1,0:T(8,128)(2,1)S(1)} %get-tuple-element.41), channel_id=1, source_target_pairs={{0,4},{1,5},{2,6},{3,7},{4,0},{5,1},{6,2},{7,3},{8,12},{9,13},{10,... | collective-permute-start | bytes 393224 | tf_op jit(solution)/shard_map/ppermute | solution.py:441
  127.8 1.6 %collective-permute-done.26 = bf16[32,2048]{1,0:T(8,128)(2,1)S(1)} collective-permute-done((bf16[32,2048]{1,0:T(8,128)(2,1)S(1)}, bf16[32,2048]{1,0:T(8,128)(2,1)S(1)}, u32[]{:S(2)}, u32[]{:S(2)}) %collective-permute-start.26) | collective-permute-done | bytes 131104 | tf_op jit(solution)/shard_map/ppermute | solution.py:441
  129.5 8.1 %collective-permute-done.27 = bf16[32,2048]{1,0:T(8,128)(2,1)S(1)} collective-permute-done((bf16[32,2048]{1,0:T(8,128)(2,1)S(1)}, bf16[32,2048]{1,0:T(8,128)(2,1)S(1)}, u32[]{:S(2)}, u32[]{:S(2)}) %collective-permute-start.27) | collective-permute-done | bytes 131104 | tf_op jit(solution)/shard_map/ppermute | solution.py:441
  139.0 3.7 %collective-permute-done.29 = bf16[32,2048]{1,0:T(8,128)(2,1)S(1)} collective-permute-done((bf16[32,2048]{1,0:T(8,128)(2,1)S(1)}, bf16[32,2048]{1,0:T(8,128)(2,1)S(1)}, u32[]{:S(2)}, u32[]{:S(2)}) %collective-permute-start.29) | collective-permute-done | bytes 131104 | tf_op jit(solution)/shard_map/ppermute | solution.py:441
  (86 shorter events, 22.4 us)
Async XLA Ops:
  20.1 30.7 %collective-permute-start = (bf16[288,2048]{1,0:T(8,128)(2,1)}, bf16[288,2048]{1,0:T(8,128)(2,1)}, u32[]{:S(2)}, u32[]{:S(2)}) collective-permute-start(bf16[288,2048]{1,0:T(8,128)(2,1)} %w0), channel_id=1, source_target_pairs={{0,2},{1,3},{2,0},{3,1},{4,6},{5,7},{6,4},{7,5},{8,10},{9,11},{10,... | collective-permute-start | bytes 3538952 | tf_op jit(solution)/shard_map/ppermute | solution.py:441
  28.2 22.7 %all-to-all-start.1 = ((bf16[16,72,128]{2,1,0:T(8,128)(2,1)}), bf16[16,72,128]{2,1,0:T(8,128)(2,1)S(1)}, u32[]{:S(2)}, u32[]{:S(2)}) async-start(bf16[16,72,128]{2,1,0:T(8,128)(2,1)} %shard_map.110), calls=%async_computation.1 | async-start | bytes 589824 | tf_op jit(solution)/shard_map/all_to_all | solution.py:490
  33.0 18.5 %collective-permute-start.1 = (bf16[288,2048]{1,0:T(8,128)(2,1)}, bf16[288,2048]{1,0:T(8,128)(2,1)}, u32[]{:S(2)}, u32[]{:S(2)}) collective-permute-start(bf16[288,2048]{1,0:T(8,128)(2,1)} %w0), channel_id=1, source_target_pairs={{0,1},{1,0},{2,3},{3,2},{4,5},{5,4},{6,7},{7,6},{8,9},{9,8},{10,11... | collective-permute-start | bytes 3538952 | tf_op jit(solution)/shard_map/ppermute | solution.py:441
  58.2 8.9 %collective-permute-start.3 = (bf16[32,2304]{1,0:T(8,128)(2,1)S(1)}, bf16[32,2304]{1,0:T(8,128)(2,1)S(1)}, u32[]{:S(2)}, u32[]{:S(2)}) collective-permute-start(bf16[32,2304]{1,0:T(8,128)(2,1)S(1)} %get-tuple-element.39), channel_id=1, source_target_pairs={{0,4},{1,5},{2,6},{3,7},{4,0},{5,1},{6,2},{7,3},{8,12},{9,13},{10,... | collective-permute-start | bytes 442376 | tf_op jit(solution)/shard_map/ppermute | solution.py:441
  59.0 13.9 %collective-permute-start.4 = (bf16[32,2304]{1,0:T(8,128)(2,1)S(1)}, bf16[32,2304]{1,0:T(8,128)(2,1)S(1)}, u32[]{:S(2)}, u32[]{:S(2)}) collective-permute-start(bf16[32,2304]{1,0:T(8,128)(2,1)S(1)} %get-tuple-element.38), channel_id=1, source_target_pairs={{0,8},{1,9},{2,10},{3,11},{4,12},{5,13},{6,14},{7,15},{8,0},{9,1},... | collective-permute-start | bytes 442376 | tf_op jit(solution)/shard_map/ppermute | solution.py:441
  61.6 11.4 %collective-permute-start.5 = (bf16[32,2304]{1,0:T(8,128)(2,1)S(1)}, bf16[32,2304]{1,0:T(8,128)(2,1)S(1)}, u32[]{:S(2)}, u32[]{:S(2)}) collective-permute-start(bf16[32,2304]{1,0:T(8,128)(2,1)S(1)} %get-tuple-element.37), channel_id=1, source_target_pairs={{0,12},{1,13},{2,14},{3,15},{4,8},{5,9},{6,10},{7,11},{8,4},{9,5},... | collective-permute-start | bytes 442376 | tf_op jit(solution)/shard_map/ppermute | solution.py:441
  73.5 7.6 %collective-permute-start.7 = (bf16[32,2176]{1,0:T(8,128)(2,1)S(1)}, bf16[32,2176]{1,0:T(8,128)(2,1)S(1)}, u32[]{:S(2)}, u32[]{:S(2)}) collective-permute-start(bf16[32,2176]{1,0:T(8,128)(2,1)S(1)} %shard_map.112.refs_0_), channel_id=1, source_target_pairs={{0,4},{1,5},{2,6},{3,7},{4,0},{5,1},{6,2},{7,3},{8,12},{9,13},{10,... | collective-permute-start | bytes 417800 | tf_op jit(solution)/shard_map/ppermute | solution.py:441
  76.3 13.2 %collective-permute-start.9 = (bf16[32,2176]{1,0:T(8,128)(2,1)S(1)}, bf16[32,2176]{1,0:T(8,128)(2,1)S(1)}, u32[]{:S(2)}, u32[]{:S(2)}) collective-permute-start(bf16[32,2176]{1,0:T(8,128)(2,1)S(1)} %shard_map.112.refs_0_), channel_id=1, source_target_pairs={{0,8},{1,9},{2,10},{3,11},{4,12},{5,13},{6,14},{7,15},{8,0},{9,1},... | collective-permute-start | bytes 417800 | tf_op jit(solution)/shard_map/ppermute | solution.py:441
  78.1 11.4 %collective-permute-start.11 = (bf16[32,2176]{1,0:T(8,128)(2,1)S(1)}, bf16[32,2176]{1,0:T(8,128)(2,1)S(1)}, u32[]{:S(2)}, u32[]{:S(2)}) collective-permute-start(bf16[32,2176]{1,0:T(8,128)(2,1)S(1)} %shard_map.112.refs_0_), channel_id=1, source_target_pairs={{0,12},{1,13},{2,14},{3,15},{4,8},{5,9},{6,10},{7,11},{8,4},{9,5},... | collective-permute-start | bytes 417800 | tf_op jit(solution)/shard_map/ppermute | solution.py:441
  79.5 11.5 %collective-permute-start.13 = (bf16[32,2176]{1,0:T(8,128)(2,1)S(1)}, bf16[32,2176]{1,0:T(8,128)(2,1)S(1)}, u32[]{:S(2)}, u32[]{:S(2)}) collective-permute-start(bf16[32,2176]{1,0:T(8,128)(2,1)S(1)} %shard_map.112.refs_0_), channel_id=1, source_target_pairs={{0,1},{1,0},{2,3},{3,2},{4,5},{5,4},{6,7},{7,6},{8,9},{9,8},{10,11... | collective-permute-start | bytes 417800 | tf_op jit(solution)/shard_map/ppermute | solution.py:441
  81.1 10.9 %collective-permute-start.14 = (bf16[32,2176]{1,0:T(8,128)(2,1)S(1)}, bf16[32,2176]{1,0:T(8,128)(2,1)S(1)}, u32[]{:S(2)}, u32[]{:S(2)}) collective-permute-start(bf16[32,2176]{1,0:T(8,128)(2,1)S(1)} %collective-permute-done.7.refs_1_), channel_id=1, source_target_pairs={{0,1},{1,0},{2,3},{3,2},{4,5},{5,4},{6,7},{7,6},{8,9},{9,8},{10,11... | collective-permute-start | bytes 417800 | tf_op jit(solution)/shard_map/ppermute | solution.py:441
  90.0 15.6 %collective-permute-start.6 = (bf16[32,2176]{1,0:T(8,128)(2,1)S(1)}, bf16[32,2176]{1,0:T(8,128)(2,1)S(1)}, u32[]{:S(2)}, u32[]{:S(2)}) collective-permute-start(bf16[32,2176]{1,0:T(8,128)(2,1)S(1)} %shard_map.112.refs_0_), channel_id=1, source_target_pairs={{0,2},{1,3},{2,0},{3,1},{4,6},{5,7},{6,4},{7,5},{8,10},{9,11},{10,... | collective-permute-start | bytes 417800 | tf_op jit(solution)/shard_map/ppermute | solution.py:441
  91.0 14.6 %collective-permute-start.10 = (bf16[32,2176]{1,0:T(8,128)(2,1)S(1)}, bf16[32,2176]{1,0:T(8,128)(2,1)S(1)}, u32[]{:S(2)}, u32[]{:S(2)}) collective-permute-start(bf16[32,2176]{1,0:T(8,128)(2,1)S(1)} %collective-permute-done.9.refs_2_), channel_id=1, source_target_pairs={{0,2},{1,3},{2,0},{3,1},{4,6},{5,7},{6,4},{7,5},{8,10},{9,11},{10,... | collective-permute-start | bytes 417800 | tf_op jit(solution)/shard_map/ppermute | solution.py:441
  92.0 13.6 %collective-permute-start.12 = (bf16[32,2176]{1,0:T(8,128)(2,1)S(1)}, bf16[32,2176]{1,0:T(8,128)(2,1)S(1)}, u32[]{:S(2)}, u32[]{:S(2)}) collective-permute-start(bf16[32,2176]{1,0:T(8,128)(2,1)S(1)} %collective-permute-done.11.refs_3_), channel_id=1, source_target_pairs={{0,2},{1,3},{2,0},{3,1},{4,6},{5,7},{6,4},{7,5},{8,10},{9,11},{10,... | collective-permute-start | bytes 417800 | tf_op jit(solution)/shard_map/ppermute | solution.py:441
  93.0 12.6 %collective-permute-start.8 = (bf16[32,2176]{1,0:T(8,128)(2,1)S(1)}, bf16[32,2176]{1,0:T(8,128)(2,1)S(1)}, u32[]{:S(2)}, u32[]{:S(2)}) collective-permute-start(bf16[32,2176]{1,0:T(8,128)(2,1)S(1)} %collective-permute-done.7.refs_1_), channel_id=1, source_target_pairs={{0,2},{1,3},{2,0},{3,1},{4,6},{5,7},{6,4},{7,5},{8,10},{9,11},{10,... | collective-permute-start | bytes 417800 | tf_op jit(solution)/shard_map/ppermute | solution.py:441
  106.3 6.1 %collective-permute-start.19 = (bf16[32,2176]{1,0:T(8,128)(2,1)S(1)}, bf16[32,2176]{1,0:T(8,128)(2,1)S(1)}, u32[]{:S(2)}, u32[]{:S(2)}) collective-permute-start(bf16[32,2176]{1,0:T(8,128)(2,1)S(1)} %collective-permute-done.10.refs_2_), channel_id=1, source_target_pairs={{0,1},{1,0},{2,3},{3,2},{4,5},{5,4},{6,7},{7,6},{8,9},{9,8},{10,11... | collective-permute-start | bytes 417800 | tf_op jit(solution)/shard_map/ppermute | solution.py:441
  106.7 5.7 %collective-permute-start.20 = (bf16[32,2176]{1,0:T(8,128)(2,1)S(1)}, bf16[32,2176]{1,0:T(8,128)(2,1)S(1)}, u32[]{:S(2)}, u32[]{:S(2)}) collective-permute-start(bf16[32,2176]{1,0:T(8,128)(2,1)S(1)} %collective-permute-done.12.refs_3_), channel_id=1, source_target_pairs={{0,1},{1,0},{2,3},{3,2},{4,5},{5,4},{6,7},{7,6},{8,9},{9,8},{10,11... | collective-permute-start | bytes 417800 | tf_op jit(solution)/shard_map/ppermute | solution.py:441
  107.8 10.8 %collective-permute-start.23 = (bf16[32,2048]{1,0:T(8,128)(2,1)S(1)}, bf16[32,2048]{1,0:T(8,128)(2,1)S(1)}, u32[]{:S(2)}, u32[]{:S(2)}) collective-permute-start(bf16[32,2048]{1,0:T(8,128)(2,1)S(1)} %get-tuple-element.44), channel_id=1, source_target_pairs={{0,4},{1,5},{2,6},{3,7},{4,0},{5,1},{6,2},{7,3},{8,12},{9,13},{10,... | collective-permute-start | bytes 393224 | tf_op jit(solution)/shard_map/ppermute | solution.py:441
  109.6 12.9 %collective-permute-start.24 = (bf16[32,2048]{1,0:T(8,128)(2,1)S(1)}, bf16[32,2048]{1,0:T(8,128)(2,1)S(1)}, u32[]{:S(2)}, u32[]{:S(2)}) collective-permute-start(bf16[32,2048]{1,0:T(8,128)(2,1)S(1)} %get-tuple-element.46), channel_id=1, source_target_pairs={{0,8},{1,9},{2,10},{3,11},{4,12},{5,13},{6,14},{7,15},{8,0},{9,1},... | collective-permute-start | bytes 393224 | tf_op jit(solution)/shard_map/ppermute | solution.py:441
  111.0 11.5 %collective-permute-start.25 = (bf16[32,2048]{1,0:T(8,128)(2,1)S(1)}, bf16[32,2048]{1,0:T(8,128)(2,1)S(1)}, u32[]{:S(2)}, u32[]{:S(2)}) collective-permute-start(bf16[32,2048]{1,0:T(8,128)(2,1)S(1)} %get-tuple-element.45), channel_id=1, source_target_pairs={{0,12},{1,13},{2,14},{3,15},{4,8},{5,9},{6,10},{7,11},{8,4},{9,5},... | collective-permute-start | bytes 393224 | tf_op jit(solution)/shard_map/ppermute | solution.py:441
  122.7 6.7 %collective-permute-start.26 = (bf16[32,2048]{1,0:T(8,128)(2,1)S(1)}, bf16[32,2048]{1,0:T(8,128)(2,1)S(1)}, u32[]{:S(2)}, u32[]{:S(2)}) collective-permute-start(bf16[32,2048]{1,0:T(8,128)(2,1)S(1)} %get-tuple-element.41), channel_id=1, source_target_pairs={{0,4},{1,5},{2,6},{3,7},{4,0},{5,1},{6,2},{7,3},{8,12},{9,13},{10,... | collective-permute-start | bytes 393224 | tf_op jit(solution)/shard_map/ppermute | solution.py:441
  125.1 12.5 %collective-permute-start.27 = (bf16[32,2048]{1,0:T(8,128)(2,1)S(1)}, bf16[32,2048]{1,0:T(8,128)(2,1)S(1)}, u32[]{:S(2)}, u32[]{:S(2)}) collective-permute-start(bf16[32,2048]{1,0:T(8,128)(2,1)S(1)} %get-tuple-element.43), channel_id=1, source_target_pairs={{0,8},{1,9},{2,10},{3,11},{4,12},{5,13},{6,14},{7,15},{8,0},{9,1},... | collective-permute-start | bytes 393224 | tf_op jit(solution)/shard_map/ppermute | solution.py:441
  126.4 11.1 %collective-permute-start.28 = (bf16[32,2048]{1,0:T(8,128)(2,1)S(1)}, bf16[32,2048]{1,0:T(8,128)(2,1)S(1)}, u32[]{:S(2)}, u32[]{:S(2)}) collective-permute-start(bf16[32,2048]{1,0:T(8,128)(2,1)S(1)} %get-tuple-element.42), channel_id=1, source_target_pairs={{0,12},{1,13},{2,14},{3,15},{4,8},{5,9},{6,10},{7,11},{8,4},{9,5},... | collective-permute-start | bytes 393224 | tf_op jit(solution)/shard_map/ppermute | solution.py:441
  137.6 5.0 %collective-permute-start.29 = (bf16[32,2048]{1,0:T(8,128)(2,1)S(1)}, bf16[32,2048]{1,0:T(8,128)(2,1)S(1)}, u32[]{:S(2)}, u32[]{:S(2)}) collective-permute-start(bf16[32,2048]{1,0:T(8,128)(2,1)S(1)} %fusion), channel_id=1, source_target_pairs={{0,2},{1,3},{2,0},{3,1},{4,6},{5,7},{6,4},{7,5},{8,10},{9,11},{10,... | collective-permute-start | bytes 393224 | tf_op jit(solution)/shard_map/ppermute | solution.py:441
  (20 other events, 228.5 us)

commit v5 on v4

--- a/solution.py
+++ b/solution.py
@@ -513,8 +513,8 @@
         held_y,
         held_yc,
     )
-    along = (4, 8, 12)
-    arrived = [partial[0]] + [crossed(partial[k], mask) for k, mask in enumerate(along, 1)]
+    along = (8, 12, 4)
+    arrived = [partial[0]] + [crossed(partial[mask // 4], mask) for mask in along]
     router = jnp.concatenate(
         [w_router, w_router, jnp.zeros((out_width, LANES - 2 * experts), BF)], 1
     )
@@ -527,6 +527,7 @@
     )(*arrived, router, expert_ids)
     near = [routed] + [crossed(routed, mask) for mask in along]
     far = [crossed(block, 2) for block in near]
+    *near, far[0] = lax.optimization_barrier((*near, far[0]))
     gate_turned, up_turned = jnp.swapaxes(w_gate, 1, 2), jnp.swapaxes(w_up, 1, 2)
 
     inner = w_down.shape[1]
@@ -545,12 +546,12 @@
                 pltpu.VMEM((inner, out_width), BF),
                 pltpu.SemaphoreType.DMA((2 * len(cuts) + 1,)),
             ],
-            compiler_params=params(32),
+            compiler_params=params(50),
             cost_estimate=cost(2**32, 2**24),
         )(*blocks, *[crossed(block, 1) for block in blocks], gate_turned, up_turned, w_down)
 
     def scattered(blocks):
-        others = [crossed(blocks[k], mask) for k, mask in enumerate(along, 1)]
+        others = [crossed(blocks[1 + along.index(mask)], mask) for mask in along]
         return blocks[0].astype(F32) + sum(block.astype(F32) for block in others)
 
     def paired(own, other):

time: 144 us -> 135 us (0.938)
  local copies, waits for them, and re-layouts: 7.21 us -> 1.75 us
  starting transfers between devices: 33.4 us -> 31.3 us
  waiting for transfers between devices: 58.1 us -> 56.2 us
    unnamed x28 -> x16, local copies, waits for them, and re-layouts: 7 us -> 1.55 us
    ppermute x30, starting transfers between devices: 28.7 us -> 26.6 us  [crossed(): return lax.ppermute(value, 'wide', pairs)]
    ppermute x30, waiting for transfers between devices: 40.6 us -> 38.8 us  [crossed(): return lax.ppermute(value, 'wide', pairs)]
  transfers between devices with their start and end apart: 31 -> 31, of which waited for: 11 -> 12; matrix products, arithmetic and copies ran while one was open for 1% -> 1% of each run, Pallas kernels for 14% -> 15%
where the time goes in v5:
time: 135 us
  waiting for transfers between devices  56.2 us (42%)
  starting transfers between devices  31.3 us (23%)
  Pallas kernels  25.6 us (19%)
  blocking collectives  18.5 us (14%)
  local copies, waits for them, and re-layouts  1.75 us (1%)
  other arithmetic  1.4 us (1%)
    ppermute x30, waiting for transfers between devices, crossed(): return lax.ppermute(value, 'wide', pairs)  38.8 us
    ppermute x30, starting transfers between devices, crossed(): return lax.ppermute(value, 'wide', pairs)  26.6 us
    all_to_all x1, blocking collectives, local(): lax.all_to_all(packed, 'wide', split_axis=0, concat_axis=0, tiled=True, a...  18.5 us
    all_to_all x1, waiting for transfers between devices, local(): lax.all_to_all(attended, 'wide', split_axis=0, concat_axis=0, tiled=True)  17.4 us
    pallas_call x2, Pallas kernels, experts_of(): pl.pallas_call(lambda *refs: expert_kernel(*refs, experts=experts, cuts=c...  13.3 us
    pallas_call x1, Pallas kernels, local(): pl.pallas_call(attend_kernel, out_shape=jax.ShapeDtypeStruct((devices, di...  7.27 us
    all_to_all x1, starting transfers between devices, local(): lax.all_to_all(attended, 'wide', split_axis=0, concat_axis=0, tiled=True)  4.74 us
    pallas_call x1, Pallas kernels, local(): pl.pallas_call(merge_kernel, out_shape=jax.ShapeDtypeStruct((planes, toke...  4.07 us
  transfers between devices with their start and end apart: 31, of which 12 were waited for; matrix products, arithmetic and copies ran while one was open for 1% of the time, Pallas kernels for 15%

profile of v5, /device:TPU:0, one launch (start us, length us, event | category | flops | bytes accessed | tf_op | source)
XLA Modules:
  0.0 135.1 jit_solution(8414346324541919884)
XLA Ops:
  1.6 18.5 %all_to_all.10.x_ref = bf16[8,432,128]{2,1,0:T(8,128)(2,1)S(1)} all-to-all(bf16[8,432,128]{2,1,0:T(8,128)(2,1)S(1)} %shard_map.109), channel_id=1, replica_groups={{0,1,2,3,4,5,6,7},{8,9,10,11,12,13,14,15},{16,17,18,19,20,21,22,23},{24..., dimensions={0} | all-to-all | bytes 1769472 | tf_op jit(solution)/shard_map/all_to_all | solution.py:476
  21.0 7.3 %shard_map.110 = bf16[16,72,128]{2,1,0:T(8,128)(2,1)} custom-call(bf16[8,432,128]{2,1,0:T(8,128)(2,1)S(1)} %all_to_all.10.x_ref, s32[2,2]{1,0:T(2,128)S(1)} %copy-done.2), custom_call_target="tpu_custom_call" | custom-call | flops 4294967296 | bytes 4194304 | tf_op jit(solution)/shard_map/pallas_call | solution.py:481
  28.2 4.7 %all-to-all-start.1 = ((bf16[16,72,128]{2,1,0:T(8,128)(2,1)}), bf16[16,72,128]{2,1,0:T(8,128)(2,1)S(1)}, u32[]{:S(2)}, u32[]{:S(2)}) async-start(bf16[16,72,128]{2,1,0:T(8,128)(2,1)} %shard_map.110), calls=%async_computation.1 | async-start | bytes 589824 | tf_op jit(solution)/shard_map/all_to_all | solution.py:490
  33.5 17.4 %all-to-all-done.1.x_ref = bf16[16,72,128]{2,1,0:T(8,128)(2,1)S(1)} async-done(((bf16[16,72,128]{2,1,0:T(8,128)(2,1)}), bf16[16,72,128]{2,1,0:T(8,128)(2,1)S(1)}, u32[]{:S(2)}, u32[]{:S(2)}) %all-to-all-start.1) | async-done | bytes 294944 | tf_op jit(solution)/shard_map/all_to_all | solution.py:490
  51.4 2.6 %collective-permute-done.2.w3 = bf16[288,2048]{1,0:T(8,128)(2,1)} collective-permute-done((bf16[288,2048]{1,0:T(8,128)(2,1)}, bf16[288,2048]{1,0:T(8,128)(2,1)}, u32[]{:S(2)}, u32[]{:S(2)}) %collective-permute-start.2) | collective-permute-done | bytes 1179680 | tf_op jit(solution)/shard_map/ppermute | solution.py:441
  54.1 4.1 %shard_map.111 = bf16[4,32,2304]{2,1,0:T(8,128)(2,1)S(1)} custom-call(bf16[16,72,128]{2,1,0:T(8,128)(2,1)S(1)} %all-to-all-done.1.x_ref, bf16[1152,1152]{1,0:T(8,128)(2,1)S(1)} %copy-done, f32[1,4608]{1,0:T(1,128)S(1)} %reshape.10.gain_ref, f32[1,4608]{1,0:T(1,128)S(1)} %reshape.11.bias_ref, bf16[288,2048]{1,0:T(8,128)(2,1)} %w0, ...), custom_call_target="tpu_custom_call" | custom-call | tf_op jit(solution)/shard_map/pallas_call | solution.py:495
  58.2 2.7 %collective-permute-start.3 = (bf16[32,2304]{1,0:T(8,128)(2,1)S(1)}, bf16[32,2304]{1,0:T(8,128)(2,1)S(1)}, u32[]{:S(2)}, u32[]{:S(2)}) collective-permute-start(bf16[32,2304]{1,0:T(8,128)(2,1)S(1)} %get-tuple-element.49), channel_id=1, source_target_pairs={{0,8},{1,9},{2,10},{3,11},{4,12},{5,13},{6,14},{7,15},{8,0},{9,1},... | collective-permute-start | bytes 442376 | tf_op jit(solution)/shard_map/ppermute | solution.py:441
  62.2 9.5 %collective-permute-done.3.refs_1_ = bf16[32,2304]{1,0:T(8,128)(2,1)S(1)} collective-permute-done((bf16[32,2304]{1,0:T(8,128)(2,1)S(1)}, bf16[32,2304]{1,0:T(8,128)(2,1)S(1)}, u32[]{:S(2)}, u32[]{:S(2)}) %collective-permute-start.3) | collective-permute-done | bytes 147488 | tf_op jit(solution)/shard_map/ppermute | solution.py:441
  73.3 3.8 %collective-permute-start.6 = (bf16[32,2176]{1,0:T(8,128)(2,1)S(1)}, bf16[32,2176]{1,0:T(8,128)(2,1)S(1)}, u32[]{:S(2)}, u32[]{:S(2)}) collective-permute-start(bf16[32,2176]{1,0:T(8,128)(2,1)S(1)} %shard_map.112.refs_0_), channel_id=1, source_target_pairs={{0,8},{1,9},{2,10},{3,11},{4,12},{5,13},{6,14},{7,15},{8,0},{9,1},... | collective-permute-start | bytes 417800 | tf_op jit(solution)/shard_map/ppermute | solution.py:441
  78.1 1.2 collective-permute-start.9
  79.3 8.3 %collective-permute-done.6.refs_1_ = bf16[32,2176]{1,0:T(8,128)(2,1)S(1)} collective-permute-done((bf16[32,2176]{1,0:T(8,128)(2,1)S(1)}, bf16[32,2176]{1,0:T(8,128)(2,1)S(1)}, u32[]{:S(2)}, u32[]{:S(2)}) %collective-permute-start.6) | collective-permute-done | bytes 139296 | tf_op jit(solution)/shard_map/ppermute | solution.py:441
  88.7 1.2 collective-permute-start.10
  90.7 1.2 collective-permute-start.12
  92.0 6.7 %shard_map.113 = (bf16[4,32,2048]{2,1,0:T(8,128)(2,1)S(1)}, bf16[4,32,2048]{2,1,0:T(8,128)(2,1)S(1)}) custom-call(bf16[32,2176]{1,0:T(8,128)(2,1)S(1)} %shard_map.112.refs_0_, bf16[32,2176]{1,0:T(8,128)(2,1)S(1)} %collective-permute-done.6.refs_1_, bf16[32,2176]{1,0:T(8,128)(2,1)S(1)} %collective-permute-done.7.refs_2_, ...), custom_call_target="tpu_custom_call" | custom-call | flops 4294967296 | bytes 16777216 | tf_op jit(solution)/shard_map/pallas_call | solution.py:537
  98.6 1.7 %collective-permute-done.12.refs_3_ = bf16[32,2176]{1,0:T(8,128)(2,1)S(1)} collective-permute-done((bf16[32,2176]{1,0:T(8,128)(2,1)S(1)}, bf16[32,2176]{1,0:T(8,128)(2,1)S(1)}, u32[]{:S(2)}, u32[]{:S(2)}) %collective-permute-start.12) | collective-permute-done | bytes 139296 | tf_op jit(solution)/shard_map/ppermute | solution.py:441
  102.4 2.2 %collective-permute-start.23 = (bf16[32,2048]{1,0:T(8,128)(2,1)S(1)}, bf16[32,2048]{1,0:T(8,128)(2,1)S(1)}, u32[]{:S(2)}, u32[]{:S(2)}) collective-permute-start(bf16[32,2048]{1,0:T(8,128)(2,1)S(1)} %get-tuple-element.54), channel_id=1, source_target_pairs={{0,8},{1,9},{2,10},{3,11},{4,12},{5,13},{6,14},{7,15},{8,0},{9,1},... | collective-permute-start | bytes 393224 | tf_op jit(solution)/shard_map/ppermute | solution.py:441
  104.6 2.3 %collective-permute-start.24 = (bf16[32,2048]{1,0:T(8,128)(2,1)S(1)}, bf16[32,2048]{1,0:T(8,128)(2,1)S(1)}, u32[]{:S(2)}, u32[]{:S(2)}) collective-permute-start(bf16[32,2048]{1,0:T(8,128)(2,1)S(1)} %get-tuple-element.56), channel_id=1, source_target_pairs={{0,12},{1,13},{2,14},{3,15},{4,8},{5,9},{6,10},{7,11},{8,4},{9,5},... | collective-permute-start | bytes 393224 | tf_op jit(solution)/shard_map/ppermute | solution.py:441
  107.0 6.7 %shard_map.114 = (bf16[4,32,2048]{2,1,0:T(8,128)(2,1)S(1)}, bf16[4,32,2048]{2,1,0:T(8,128)(2,1)S(1)}) custom-call(bf16[32,2176]{1,0:T(8,128)(2,1)S(1)} %collective-permute-done.9.refs_0_, bf16[32,2176]{1,0:T(8,128)(2,1)S(1)} %collective-permute-done.10.refs_1_, bf16[32,2176]{1,0:T(8,128)(2,1)S(1)} %collective-permute-done.11.refs_2_, ...), custom_call_target="tpu_custom_call" | custom-call | flops 4294967296 | bytes 16777216 | tf_op jit(solution)/shard_map/pallas_call | solution.py:537
  113.7 1.6 %collective-permute-done.23 = bf16[32,2048]{1,0:T(8,128)(2,1)S(1)} collective-permute-done((bf16[32,2048]{1,0:T(8,128)(2,1)S(1)}, bf16[32,2048]{1,0:T(8,128)(2,1)S(1)}, u32[]{:S(2)}, u32[]{:S(2)}) %collective-permute-start.23) | collective-permute-done | bytes 131104 | tf_op jit(solution)/shard_map/ppermute | solution.py:441
  116.2 2.5 %collective-permute-start.26 = (bf16[32,2048]{1,0:T(8,128)(2,1)S(1)}, bf16[32,2048]{1,0:T(8,128)(2,1)S(1)}, u32[]{:S(2)}, u32[]{:S(2)}) collective-permute-start(bf16[32,2048]{1,0:T(8,128)(2,1)S(1)} %get-tuple-element.51), channel_id=1, source_target_pairs={{0,8},{1,9},{2,10},{3,11},{4,12},{5,13},{6,14},{7,15},{8,0},{9,1},... | collective-permute-start | bytes 393224 | tf_op jit(solution)/shard_map/ppermute | solution.py:441
  118.7 1.9 %collective-permute-start.27 = (bf16[32,2048]{1,0:T(8,128)(2,1)S(1)}, bf16[32,2048]{1,0:T(8,128)(2,1)S(1)}, u32[]{:S(2)}, u32[]{:S(2)}) collective-permute-start(bf16[32,2048]{1,0:T(8,128)(2,1)S(1)} %get-tuple-element.53), channel_id=1, source_target_pairs={{0,12},{1,13},{2,14},{3,15},{4,8},{5,9},{6,10},{7,11},{8,4},{9,5},... | collective-permute-start | bytes 393224 | tf_op jit(solution)/shard_map/ppermute | solution.py:441
  120.6 8.5 %collective-permute-done.26 = bf16[32,2048]{1,0:T(8,128)(2,1)S(1)} collective-permute-done((bf16[32,2048]{1,0:T(8,128)(2,1)S(1)}, bf16[32,2048]{1,0:T(8,128)(2,1)S(1)}, u32[]{:S(2)}, u32[]{:S(2)}) %collective-permute-start.26) | collective-permute-done | bytes 131104 | tf_op jit(solution)/shard_map/ppermute | solution.py:441
  129.4 1.2 collective-permute-start.29
  130.6 3.8 %collective-permute-done.29 = bf16[32,2048]{1,0:T(8,128)(2,1)S(1)} collective-permute-done((bf16[32,2048]{1,0:T(8,128)(2,1)S(1)}, bf16[32,2048]{1,0:T(8,128)(2,1)S(1)}, u32[]{:S(2)}, u32[]{:S(2)}) %collective-permute-start.29) | collective-permute-done | bytes 131104 | tf_op jit(solution)/shard_map/ppermute | solution.py:441
  (74 shorter events, 13.1 us)
Async XLA Ops:
  20.1 30.7 %collective-permute-start = (bf16[288,2048]{1,0:T(8,128)(2,1)}, bf16[288,2048]{1,0:T(8,128)(2,1)}, u32[]{:S(2)}, u32[]{:S(2)}) collective-permute-start(bf16[288,2048]{1,0:T(8,128)(2,1)} %w0), channel_id=1, source_target_pairs={{0,2},{1,3},{2,0},{3,1},{4,6},{5,7},{6,4},{7,5},{8,10},{9,11},{10,... | collective-permute-start | bytes 3538952 | tf_op jit(solution)/shard_map/ppermute | solution.py:441
  28.2 22.6 %all-to-all-start.1 = ((bf16[16,72,128]{2,1,0:T(8,128)(2,1)}), bf16[16,72,128]{2,1,0:T(8,128)(2,1)S(1)}, u32[]{:S(2)}, u32[]{:S(2)}) async-start(bf16[16,72,128]{2,1,0:T(8,128)(2,1)} %shard_map.110), calls=%async_computation.1 | async-start | bytes 589824 | tf_op jit(solution)/shard_map/all_to_all | solution.py:490
  33.0 18.4 %collective-permute-start.1 = (bf16[288,2048]{1,0:T(8,128)(2,1)}, bf16[288,2048]{1,0:T(8,128)(2,1)}, u32[]{:S(2)}, u32[]{:S(2)}) collective-permute-start(bf16[288,2048]{1,0:T(8,128)(2,1)} %w0), channel_id=1, source_target_pairs={{0,1},{1,0},{2,3},{3,2},{4,5},{5,4},{6,7},{7,6},{8,9},{9,8},{10,11... | collective-permute-start | bytes 3538952 | tf_op jit(solution)/shard_map/ppermute | solution.py:441
  58.2 13.5 %collective-permute-start.3 = (bf16[32,2304]{1,0:T(8,128)(2,1)S(1)}, bf16[32,2304]{1,0:T(8,128)(2,1)S(1)}, u32[]{:S(2)}, u32[]{:S(2)}) collective-permute-start(bf16[32,2304]{1,0:T(8,128)(2,1)S(1)} %get-tuple-element.49), channel_id=1, source_target_pairs={{0,8},{1,9},{2,10},{3,11},{4,12},{5,13},{6,14},{7,15},{8,0},{9,1},... | collective-permute-start | bytes 442376 | tf_op jit(solution)/shard_map/ppermute | solution.py:441
  60.9 10.9 %collective-permute-start.4 = (bf16[32,2304]{1,0:T(8,128)(2,1)S(1)}, bf16[32,2304]{1,0:T(8,128)(2,1)S(1)}, u32[]{:S(2)}, u32[]{:S(2)}) collective-permute-start(bf16[32,2304]{1,0:T(8,128)(2,1)S(1)} %get-tuple-element.48), channel_id=1, source_target_pairs={{0,12},{1,13},{2,14},{3,15},{4,8},{5,9},{6,10},{7,11},{8,4},{9,5},... | collective-permute-start | bytes 442376 | tf_op jit(solution)/shard_map/ppermute | solution.py:441
  61.4 11.4 %collective-permute-start.5 = (bf16[32,2304]{1,0:T(8,128)(2,1)S(1)}, bf16[32,2304]{1,0:T(8,128)(2,1)S(1)}, u32[]{:S(2)}, u32[]{:S(2)}) collective-permute-start(bf16[32,2304]{1,0:T(8,128)(2,1)S(1)} %get-tuple-element.47), channel_id=1, source_target_pairs={{0,4},{1,5},{2,6},{3,7},{4,0},{5,1},{6,2},{7,3},{8,12},{9,13},{10,... | collective-permute-start | bytes 442376 | tf_op jit(solution)/shard_map/ppermute | solution.py:441
  73.3 14.3 %collective-permute-start.6 = (bf16[32,2176]{1,0:T(8,128)(2,1)S(1)}, bf16[32,2176]{1,0:T(8,128)(2,1)S(1)}, u32[]{:S(2)}, u32[]{:S(2)}) collective-permute-start(bf16[32,2176]{1,0:T(8,128)(2,1)S(1)} %shard_map.112.refs_0_), channel_id=1, source_target_pairs={{0,8},{1,9},{2,10},{3,11},{4,12},{5,13},{6,14},{7,15},{8,0},{9,1},... | collective-permute-start | bytes 417800 | tf_op jit(solution)/shard_map/ppermute | solution.py:441
  77.1 10.5 %collective-permute-start.7 = (bf16[32,2176]{1,0:T(8,128)(2,1)S(1)}, bf16[32,2176]{1,0:T(8,128)(2,1)S(1)}, u32[]{:S(2)}, u32[]{:S(2)}) collective-permute-start(bf16[32,2176]{1,0:T(8,128)(2,1)S(1)} %shard_map.112.refs_0_), channel_id=1, source_target_pairs={{0,12},{1,13},{2,14},{3,15},{4,8},{5,9},{6,10},{7,11},{8,4},{9,5},... | collective-permute-start | bytes 417800 | tf_op jit(solution)/shard_map/ppermute | solution.py:441
  78.1 9.5 %collective-permute-start.8 = (bf16[32,2176]{1,0:T(8,128)(2,1)S(1)}, bf16[32,2176]{1,0:T(8,128)(2,1)S(1)}, u32[]{:S(2)}, u32[]{:S(2)}) collective-permute-start(bf16[32,2176]{1,0:T(8,128)(2,1)S(1)} %shard_map.112.refs_0_), channel_id=1, source_target_pairs={{0,4},{1,5},{2,6},{3,7},{4,0},{5,1},{6,2},{7,3},{8,12},{9,13},{10,... | collective-permute-start | bytes 417800 | tf_op jit(solution)/shard_map/ppermute | solution.py:441
  78.1 9.5 %collective-permute-start.9 = (bf16[32,2176]{1,0:T(8,128)(2,1)S(1)}, bf16[32,2176]{1,0:T(8,128)(2,1)S(1)}, u32[]{:S(2)}, u32[]{:S(2)}) collective-permute-start(bf16[32,2176]{1,0:T(8,128)(2,1)S(1)} %shard_map.112.refs_0_), channel_id=1, source_target_pairs={{0,2},{1,3},{2,0},{3,1},{4,6},{5,7},{6,4},{7,5},{8,10},{9,11},{10,... | collective-permute-start | bytes 417800 | tf_op jit(solution)/shard_map/ppermute | solution.py:441
  88.7 9.9 %collective-permute-start.10 = (bf16[32,2176]{1,0:T(8,128)(2,1)S(1)}, bf16[32,2176]{1,0:T(8,128)(2,1)S(1)}, u32[]{:S(2)}, u32[]{:S(2)}) collective-permute-start(bf16[32,2176]{1,0:T(8,128)(2,1)S(1)} %collective-permute-done.6.refs_1_), channel_id=1, source_target_pairs={{0,2},{1,3},{2,0},{3,1},{4,6},{5,7},{6,4},{7,5},{8,10},{9,11},{10,... | collective-permute-start | bytes 417800 | tf_op jit(solution)/shard_map/ppermute | solution.py:441
  89.9 8.7 %collective-permute-start.11 = (bf16[32,2176]{1,0:T(8,128)(2,1)S(1)}, bf16[32,2176]{1,0:T(8,128)(2,1)S(1)}, u32[]{:S(2)}, u32[]{:S(2)}) collective-permute-start(bf16[32,2176]{1,0:T(8,128)(2,1)S(1)} %collective-permute-done.7.refs_2_), channel_id=1, source_target_pairs={{0,2},{1,3},{2,0},{3,1},{4,6},{5,7},{6,4},{7,5},{8,10},{9,11},{10,... | collective-permute-start | bytes 417800 | tf_op jit(solution)/shard_map/ppermute | solution.py:441
  90.7 9.6 %collective-permute-start.12 = (bf16[32,2176]{1,0:T(8,128)(2,1)S(1)}, bf16[32,2176]{1,0:T(8,128)(2,1)S(1)}, u32[]{:S(2)}, u32[]{:S(2)}) collective-permute-start(bf16[32,2176]{1,0:T(8,128)(2,1)S(1)} %collective-permute-done.8.refs_3_), channel_id=1, source_target_pairs={{0,2},{1,3},{2,0},{3,1},{4,6},{5,7},{6,4},{7,5},{8,10},{9,11},{10,... | collective-permute-start | bytes 417800 | tf_op jit(solution)/shard_map/ppermute | solution.py:441
  100.3 4.3 %collective-permute-start.17 = (bf16[32,2176]{1,0:T(8,128)(2,1)S(1)}, bf16[32,2176]{1,0:T(8,128)(2,1)S(1)}, u32[]{:S(2)}, u32[]{:S(2)}) collective-permute-start(bf16[32,2176]{1,0:T(8,128)(2,1)S(1)} %collective-permute-done.9.refs_0_), channel_id=1, source_target_pairs={{0,1},{1,0},{2,3},{3,2},{4,5},{5,4},{6,7},{7,6},{8,9},{9,8},{10,11... | collective-permute-start | bytes 417800 | tf_op jit(solution)/shard_map/ppermute | solution.py:441
  100.9 6.1 %collective-permute-start.18 = (bf16[32,2176]{1,0:T(8,128)(2,1)S(1)}, bf16[32,2176]{1,0:T(8,128)(2,1)S(1)}, u32[]{:S(2)}, u32[]{:S(2)}) collective-permute-start(bf16[32,2176]{1,0:T(8,128)(2,1)S(1)} %collective-permute-done.10.refs_1_), channel_id=1, source_target_pairs={{0,1},{1,0},{2,3},{3,2},{4,5},{5,4},{6,7},{7,6},{8,9},{9,8},{10,11... | collective-permute-start | bytes 417800 | tf_op jit(solution)/shard_map/ppermute | solution.py:441
  100.9 6.1 %collective-permute-start.19 = (bf16[32,2176]{1,0:T(8,128)(2,1)S(1)}, bf16[32,2176]{1,0:T(8,128)(2,1)S(1)}, u32[]{:S(2)}, u32[]{:S(2)}) collective-permute-start(bf16[32,2176]{1,0:T(8,128)(2,1)S(1)} %collective-permute-done.11.refs_2_), channel_id=1, source_target_pairs={{0,1},{1,0},{2,3},{3,2},{4,5},{5,4},{6,7},{7,6},{8,9},{9,8},{10,11... | collective-permute-start | bytes 417800 | tf_op jit(solution)/shard_map/ppermute | solution.py:441
  101.4 5.6 %collective-permute-start.20 = (bf16[32,2176]{1,0:T(8,128)(2,1)S(1)}, bf16[32,2176]{1,0:T(8,128)(2,1)S(1)}, u32[]{:S(2)}, u32[]{:S(2)}) collective-permute-start(bf16[32,2176]{1,0:T(8,128)(2,1)S(1)} %collective-permute-done.12.refs_3_), channel_id=1, source_target_pairs={{0,1},{1,0},{2,3},{3,2},{4,5},{5,4},{6,7},{7,6},{8,9},{9,8},{10,11... | collective-permute-start | bytes 417800 | tf_op jit(solution)/shard_map/ppermute | solution.py:441
  102.4 13.0 %collective-permute-start.23 = (bf16[32,2048]{1,0:T(8,128)(2,1)S(1)}, bf16[32,2048]{1,0:T(8,128)(2,1)S(1)}, u32[]{:S(2)}, u32[]{:S(2)}) collective-permute-start(bf16[32,2048]{1,0:T(8,128)(2,1)S(1)} %get-tuple-element.54), channel_id=1, source_target_pairs={{0,8},{1,9},{2,10},{3,11},{4,12},{5,13},{6,14},{7,15},{8,0},{9,1},... | collective-permute-start | bytes 393224 | tf_op jit(solution)/shard_map/ppermute | solution.py:441
  104.6 10.8 %collective-permute-start.24 = (bf16[32,2048]{1,0:T(8,128)(2,1)S(1)}, bf16[32,2048]{1,0:T(8,128)(2,1)S(1)}, u32[]{:S(2)}, u32[]{:S(2)}) collective-permute-start(bf16[32,2048]{1,0:T(8,128)(2,1)S(1)} %get-tuple-element.56), channel_id=1, source_target_pairs={{0,12},{1,13},{2,14},{3,15},{4,8},{5,9},{6,10},{7,11},{8,4},{9,5},... | collective-permute-start | bytes 393224 | tf_op jit(solution)/shard_map/ppermute | solution.py:441
  107.0 8.9 %collective-permute-start.25 = (bf16[32,2048]{1,0:T(8,128)(2,1)S(1)}, bf16[32,2048]{1,0:T(8,128)(2,1)S(1)}, u32[]{:S(2)}, u32[]{:S(2)}) collective-permute-start(bf16[32,2048]{1,0:T(8,128)(2,1)S(1)} %get-tuple-element.55), channel_id=1, source_target_pairs={{0,4},{1,5},{2,6},{3,7},{4,0},{5,1},{6,2},{7,3},{8,12},{9,13},{10,... | collective-permute-start | bytes 393224 | tf_op jit(solution)/shard_map/ppermute | solution.py:441
  116.2 13.0 %collective-permute-start.26 = (bf16[32,2048]{1,0:T(8,128)(2,1)S(1)}, bf16[32,2048]{1,0:T(8,128)(2,1)S(1)}, u32[]{:S(2)}, u32[]{:S(2)}) collective-permute-start(bf16[32,2048]{1,0:T(8,128)(2,1)S(1)} %get-tuple-element.51), channel_id=1, source_target_pairs={{0,8},{1,9},{2,10},{3,11},{4,12},{5,13},{6,14},{7,15},{8,0},{9,1},... | collective-permute-start | bytes 393224 | tf_op jit(solution)/shard_map/ppermute | solution.py:441
  118.7 10.4 %collective-permute-start.27 = (bf16[32,2048]{1,0:T(8,128)(2,1)S(1)}, bf16[32,2048]{1,0:T(8,128)(2,1)S(1)}, u32[]{:S(2)}, u32[]{:S(2)}) collective-permute-start(bf16[32,2048]{1,0:T(8,128)(2,1)S(1)} %get-tuple-element.53), channel_id=1, source_target_pairs={{0,12},{1,13},{2,14},{3,15},{4,8},{5,9},{6,10},{7,11},{8,4},{9,5},... | collective-permute-start | bytes 393224 | tf_op jit(solution)/shard_map/ppermute | solution.py:441
  120.6 8.7 %collective-permute-start.28 = (bf16[32,2048]{1,0:T(8,128)(2,1)S(1)}, bf16[32,2048]{1,0:T(8,128)(2,1)S(1)}, u32[]{:S(2)}, u32[]{:S(2)}) collective-permute-start(bf16[32,2048]{1,0:T(8,128)(2,1)S(1)} %get-tuple-element.52), channel_id=1, source_target_pairs={{0,4},{1,5},{2,6},{3,7},{4,0},{5,1},{6,2},{7,3},{8,12},{9,13},{10,... | collective-permute-start | bytes 393224 | tf_op jit(solution)/shard_map/ppermute | solution.py:441
  129.4 5.0 %collective-permute-start.29 = (bf16[32,2048]{1,0:T(8,128)(2,1)S(1)}, bf16[32,2048]{1,0:T(8,128)(2,1)S(1)}, u32[]{:S(2)}, u32[]{:S(2)}) collective-permute-start(bf16[32,2048]{1,0:T(8,128)(2,1)S(1)} %fusion), channel_id=1, source_target_pairs={{0,2},{1,3},{2,0},{3,1},{4,6},{5,7},{6,4},{7,5},{8,10},{9,11},{10,... | collective-permute-start | bytes 393224 | tf_op jit(solution)/shard_map/ppermute | solution.py:441
  (14 other events, 177.5 us)

commit v6 on v5

--- a/solution.py
+++ b/solution.py
@@ -562,8 +562,9 @@
     far_own, far_other = experts_of(far)
     near_sum = scattered(paired(near_own, near_other))
     far_out, near_sum = lax.optimization_barrier((paired(far_own, far_other), near_sum))
-    far_sum = scattered(far_out)
-    return (near_sum + crossed(far_sum.astype(BF), 2).astype(F32)).astype(BF)
+    across = [crossed(far_out[k], 2 + mask) for k, mask in enumerate(along, 1)]
+    across.append(crossed(far_out[0], 2))
+    return (near_sum + sum(block.astype(F32) for block in across)).astype(BF)
 
 
 def solution(mesh):

time: 135 us -> 134 us (level)
  waiting for transfers between devices: 56.2 us -> 54 us
    ppermute x30, waiting for transfers between devices: 38.8 us -> 36.6 us  [crossed(): return lax.ppermute(value, 'wide', pairs)]
where the time goes in v6:
time: 134 us
  waiting for transfers between devices  54 us (40%)
  starting transfers between devices  32.2 us (24%)
  Pallas kernels  25.6 us (19%)
  blocking collectives  18.5 us (14%)
  local copies, waits for them, and re-layouts  1.76 us (1%)
  other arithmetic  1.38 us (1%)
    ppermute x30, waiting for transfers between devices, crossed(): return lax.ppermute(value, 'wide', pairs)  36.6 us
    ppermute x30, starting transfers between devices, crossed(): return lax.ppermute(value, 'wide', pairs)  27.5 us
    all_to_all x1, blocking collectives, local(): lax.all_to_all(packed, 'wide', split_axis=0, concat_axis=0, tiled=True, a...  18.5 us
    all_to_all x1, waiting for transfers between devices, local(): lax.all_to_all(attended, 'wide', split_axis=0, concat_axis=0, tiled=True)  17.4 us
    pallas_call x2, Pallas kernels, experts_of(): pl.pallas_call(lambda *refs: expert_kernel(*refs, experts=experts, cuts=c...  13.3 us
    pallas_call x1, Pallas kernels, local(): pl.pallas_call(attend_kernel, out_shape=jax.ShapeDtypeStruct((devices, di...  7.27 us
    all_to_all x1, starting transfers between devices, local(): lax.all_to_all(attended, 'wide', split_axis=0, concat_axis=0, tiled=True)  4.74 us
    pallas_call x1, Pallas kernels, local(): pl.pallas_call(merge_kernel, out_shape=jax.ShapeDtypeStruct((planes, toke...  4.07 us
  transfers between devices with their start and end apart: 31, of which 12 were waited for; matrix products, arithmetic and copies ran while one was open for 1% of the time, Pallas kernels for 15%

profile of v6, /device:TPU:0, one launch (start us, length us, event | category | flops | bytes accessed | tf_op | source)
XLA Modules:
  0.0 133.8 jit_solution(4354084190522396786)
XLA Ops:
  1.6 18.5 %all_to_all.10.x_ref = bf16[8,432,128]{2,1,0:T(8,128)(2,1)S(1)} all-to-all(bf16[8,432,128]{2,1,0:T(8,128)(2,1)S(1)} %shard_map.109), channel_id=1, replica_groups={{0,1,2,3,4,5,6,7},{8,9,10,11,12,13,14,15},{16,17,18,19,20,21,22,23},{24..., dimensions={0} | all-to-all | bytes 1769472 | tf_op jit(solution)/shard_map/all_to_all | solution.py:476
  21.0 7.3 %shard_map.110 = bf16[16,72,128]{2,1,0:T(8,128)(2,1)} custom-call(bf16[8,432,128]{2,1,0:T(8,128)(2,1)S(1)} %all_to_all.10.x_ref, s32[2,2]{1,0:T(2,128)S(1)} %copy-done.2), custom_call_target="tpu_custom_call" | custom-call | flops 4294967296 | bytes 4194304 | tf_op jit(solution)/shard_map/pallas_call | solution.py:481
  28.2 4.7 %all-to-all-start.1 = ((bf16[16,72,128]{2,1,0:T(8,128)(2,1)}), bf16[16,72,128]{2,1,0:T(8,128)(2,1)S(1)}, u32[]{:S(2)}, u32[]{:S(2)}) async-start(bf16[16,72,128]{2,1,0:T(8,128)(2,1)} %shard_map.110), calls=%async_computation.1 | async-start | bytes 589824 | tf_op jit(solution)/shard_map/all_to_all | solution.py:490
  33.5 17.4 %all-to-all-done.1.x_ref = bf16[16,72,128]{2,1,0:T(8,128)(2,1)S(1)} async-done(((bf16[16,72,128]{2,1,0:T(8,128)(2,1)}), bf16[16,72,128]{2,1,0:T(8,128)(2,1)S(1)}, u32[]{:S(2)}, u32[]{:S(2)}) %all-to-all-start.1) | async-done | bytes 294944 | tf_op jit(solution)/shard_map/all_to_all | solution.py:490
  51.4 2.6 %collective-permute-done.2.w3 = bf16[288,2048]{1,0:T(8,128)(2,1)} collective-permute-done((bf16[288,2048]{1,0:T(8,128)(2,1)}, bf16[288,2048]{1,0:T(8,128)(2,1)}, u32[]{:S(2)}, u32[]{:S(2)}) %collective-permute-start.2) | collective-permute-done | bytes 1179680 | tf_op jit(solution)/shard_map/ppermute | solution.py:441
  54.1 4.1 %shard_map.111 = bf16[4,32,2304]{2,1,0:T(8,128)(2,1)S(1)} custom-call(bf16[16,72,128]{2,1,0:T(8,128)(2,1)S(1)} %all-to-all-done.1.x_ref, bf16[1152,1152]{1,0:T(8,128)(2,1)S(1)} %copy-done, f32[1,4608]{1,0:T(1,128)S(1)} %reshape.8.gain_ref, f32[1,4608]{1,0:T(1,128)S(1)} %reshape.9.bias_ref, bf16[288,2048]{1,0:T(8,128)(2,1)} %w0, ...), custom_call_target="tpu_custom_call" | custom-call | tf_op jit(solution)/shard_map/pallas_call | solution.py:495
  58.2 2.7 %collective-permute-start.3 = (bf16[32,2304]{1,0:T(8,128)(2,1)S(1)}, bf16[32,2304]{1,0:T(8,128)(2,1)S(1)}, u32[]{:S(2)}, u32[]{:S(2)}) collective-permute-start(bf16[32,2304]{1,0:T(8,128)(2,1)S(1)} %get-tuple-element.49), channel_id=1, source_target_pairs={{0,8},{1,9},{2,10},{3,11},{4,12},{5,13},{6,14},{7,15},{8,0},{9,1},... | collective-permute-start | bytes 442376 | tf_op jit(solution)/shard_map/ppermute | solution.py:441
  62.2 9.5 %collective-permute-done.3.refs_1_ = bf16[32,2304]{1,0:T(8,128)(2,1)S(1)} collective-permute-done((bf16[32,2304]{1,0:T(8,128)(2,1)S(1)}, bf16[32,2304]{1,0:T(8,128)(2,1)S(1)}, u32[]{:S(2)}, u32[]{:S(2)}) %collective-permute-start.3) | collective-permute-done | bytes 147488 | tf_op jit(solution)/shard_map/ppermute | solution.py:441
  73.3 3.8 %collective-permute-start.6 = (bf16[32,2176]{1,0:T(8,128)(2,1)S(1)}, bf16[32,2176]{1,0:T(8,128)(2,1)S(1)}, u32[]{:S(2)}, u32[]{:S(2)}) collective-permute-start(bf16[32,2176]{1,0:T(8,128)(2,1)S(1)} %shard_map.112.refs_0_), channel_id=1, source_target_pairs={{0,8},{1,9},{2,10},{3,11},{4,12},{5,13},{6,14},{7,15},{8,0},{9,1},... | collective-permute-start | bytes 417800 | tf_op jit(solution)/shard_map/ppermute | solution.py:441
  78.1 1.2 collective-permute-start.9
  79.3 8.3 %collective-permute-done.6.refs_1_ = bf16[32,2176]{1,0:T(8,128)(2,1)S(1)} collective-permute-done((bf16[32,2176]{1,0:T(8,128)(2,1)S(1)}, bf16[32,2176]{1,0:T(8,128)(2,1)S(1)}, u32[]{:S(2)}, u32[]{:S(2)}) %collective-permute-start.6) | collective-permute-done | bytes 139296 | tf_op jit(solution)/shard_map/ppermute | solution.py:441
  88.7 1.2 collective-permute-start.10
  90.7 1.2 collective-permute-start.12
  92.0 6.7 %shard_map.113 = (bf16[4,32,2048]{2,1,0:T(8,128)(2,1)S(1)}, bf16[4,32,2048]{2,1,0:T(8,128)(2,1)S(1)}) custom-call(bf16[32,2176]{1,0:T(8,128)(2,1)S(1)} %shard_map.112.refs_0_, bf16[32,2176]{1,0:T(8,128)(2,1)S(1)} %collective-permute-done.6.refs_1_, bf16[32,2176]{1,0:T(8,128)(2,1)S(1)} %collective-permute-done.7.refs_2_, ...), custom_call_target="tpu_custom_call" | custom-call | flops 4294967296 | bytes 16777216 | tf_op jit(solution)/shard_map/pallas_call | solution.py:537
  98.6 1.7 %collective-permute-done.12.refs_3_ = bf16[32,2176]{1,0:T(8,128)(2,1)S(1)} collective-permute-done((bf16[32,2176]{1,0:T(8,128)(2,1)S(1)}, bf16[32,2176]{1,0:T(8,128)(2,1)S(1)}, u32[]{:S(2)}, u32[]{:S(2)}) %collective-permute-start.12) | collective-permute-done | bytes 139296 | tf_op jit(solution)/shard_map/ppermute | solution.py:441
  102.4 2.2 %collective-permute-start.23 = (bf16[32,2048]{1,0:T(8,128)(2,1)S(1)}, bf16[32,2048]{1,0:T(8,128)(2,1)S(1)}, u32[]{:S(2)}, u32[]{:S(2)}) collective-permute-start(bf16[32,2048]{1,0:T(8,128)(2,1)S(1)} %get-tuple-element.55), channel_id=1, source_target_pairs={{0,8},{1,9},{2,10},{3,11},{4,12},{5,13},{6,14},{7,15},{8,0},{9,1},... | collective-permute-start | bytes 393224 | tf_op jit(solution)/shard_map/ppermute | solution.py:441
  104.6 2.3 %collective-permute-start.24 = (bf16[32,2048]{1,0:T(8,128)(2,1)S(1)}, bf16[32,2048]{1,0:T(8,128)(2,1)S(1)}, u32[]{:S(2)}, u32[]{:S(2)}) collective-permute-start(bf16[32,2048]{1,0:T(8,128)(2,1)S(1)} %get-tuple-element.57), channel_id=1, source_target_pairs={{0,12},{1,13},{2,14},{3,15},{4,8},{5,9},{6,10},{7,11},{8,4},{9,5},... | collective-permute-start | bytes 393224 | tf_op jit(solution)/shard_map/ppermute | solution.py:441
  107.0 6.7 %shard_map.114 = (bf16[4,32,2048]{2,1,0:T(8,128)(2,1)S(1)}, bf16[4,32,2048]{2,1,0:T(8,128)(2,1)S(1)}) custom-call(bf16[32,2176]{1,0:T(8,128)(2,1)S(1)} %collective-permute-done.9.refs_0_, bf16[32,2176]{1,0:T(8,128)(2,1)S(1)} %collective-permute-done.10.refs_1_, bf16[32,2176]{1,0:T(8,128)(2,1)S(1)} %collective-permute-done.11.refs_2_, ...), custom_call_target="tpu_custom_call" | custom-call | flops 4294967296 | bytes 16777216 | tf_op jit(solution)/shard_map/pallas_call | solution.py:537
  113.7 1.6 %collective-permute-done.23 = bf16[32,2048]{1,0:T(8,128)(2,1)S(1)} collective-permute-done((bf16[32,2048]{1,0:T(8,128)(2,1)S(1)}, bf16[32,2048]{1,0:T(8,128)(2,1)S(1)}, u32[]{:S(2)}, u32[]{:S(2)}) %collective-permute-start.23) | collective-permute-done | bytes 131104 | tf_op jit(solution)/shard_map/ppermute | solution.py:441
  116.2 3.1 %collective-permute-start.26 = (bf16[32,2048]{1,0:T(8,128)(2,1)S(1)}, bf16[32,2048]{1,0:T(8,128)(2,1)S(1)}, u32[]{:S(2)}, u32[]{:S(2)}) collective-permute-start(bf16[32,2048]{1,0:T(8,128)(2,1)S(1)} %get-tuple-element.51), channel_id=1, source_target_pairs={{0,10},{1,11},{2,8},{3,9},{4,14},{5,15},{6,12},{7,13},{8,2},{9,3},... | collective-permute-start | bytes 393224 | tf_op jit(solution)/shard_map/ppermute | solution.py:441
  119.2 2.3 %collective-permute-start.27 = (bf16[32,2048]{1,0:T(8,128)(2,1)S(1)}, bf16[32,2048]{1,0:T(8,128)(2,1)S(1)}, u32[]{:S(2)}, u32[]{:S(2)}) collective-permute-start(bf16[32,2048]{1,0:T(8,128)(2,1)S(1)} %get-tuple-element.54), channel_id=1, source_target_pairs={{0,14},{1,15},{2,12},{3,13},{4,10},{5,11},{6,8},{7,9},{8,6},{9,7},... | collective-permute-start | bytes 393224 | tf_op jit(solution)/shard_map/ppermute | solution.py:441
  121.5 1.2 collective-permute-start.29
  122.7 7.4 %collective-permute-done.26 = bf16[32,2048]{1,0:T(8,128)(2,1)S(1)} collective-permute-done((bf16[32,2048]{1,0:T(8,128)(2,1)S(1)}, bf16[32,2048]{1,0:T(8,128)(2,1)S(1)}, u32[]{:S(2)}, u32[]{:S(2)}) %collective-permute-start.26) | collective-permute-done | bytes 131104 | tf_op jit(solution)/shard_map/ppermute | solution.py:441
  130.9 2.1 %collective-permute-done.29 = bf16[32,2048]{1,0:T(8,128)(2,1)S(1)} collective-permute-done((bf16[32,2048]{1,0:T(8,128)(2,1)S(1)}, bf16[32,2048]{1,0:T(8,128)(2,1)S(1)}, u32[]{:S(2)}, u32[]{:S(2)}) %collective-permute-start.29) | collective-permute-done | bytes 131104 | tf_op jit(solution)/shard_map/ppermute | solution.py:441
  (73 shorter events, 13.8 us)
Async XLA Ops:
  20.1 30.7 %collective-permute-start = (bf16[288,2048]{1,0:T(8,128)(2,1)}, bf16[288,2048]{1,0:T(8,128)(2,1)}, u32[]{:S(2)}, u32[]{:S(2)}) collective-permute-start(bf16[288,2048]{1,0:T(8,128)(2,1)} %w0), channel_id=1, source_target_pairs={{0,2},{1,3},{2,0},{3,1},{4,6},{5,7},{6,4},{7,5},{8,10},{9,11},{10,... | collective-permute-start | bytes 3538952 | tf_op jit(solution)/shard_map/ppermute | solution.py:441
  28.2 22.6 %all-to-all-start.1 = ((bf16[16,72,128]{2,1,0:T(8,128)(2,1)}), bf16[16,72,128]{2,1,0:T(8,128)(2,1)S(1)}, u32[]{:S(2)}, u32[]{:S(2)}) async-start(bf16[16,72,128]{2,1,0:T(8,128)(2,1)} %shard_map.110), calls=%async_computation.1 | async-start | bytes 589824 | tf_op jit(solution)/shard_map/all_to_all | solution.py:490
  33.0 18.4 %collective-permute-start.1 = (bf16[288,2048]{1,0:T(8,128)(2,1)}, bf16[288,2048]{1,0:T(8,128)(2,1)}, u32[]{:S(2)}, u32[]{:S(2)}) collective-permute-start(bf16[288,2048]{1,0:T(8,128)(2,1)} %w0), channel_id=1, source_target_pairs={{0,1},{1,0},{2,3},{3,2},{4,5},{5,4},{6,7},{7,6},{8,9},{9,8},{10,11... | collective-permute-start | bytes 3538952 | tf_op jit(solution)/shard_map/ppermute | solution.py:441
  58.2 13.5 %collective-permute-start.3 = (bf16[32,2304]{1,0:T(8,128)(2,1)S(1)}, bf16[32,2304]{1,0:T(8,128)(2,1)S(1)}, u32[]{:S(2)}, u32[]{:S(2)}) collective-permute-start(bf16[32,2304]{1,0:T(8,128)(2,1)S(1)} %get-tuple-element.49), channel_id=1, source_target_pairs={{0,8},{1,9},{2,10},{3,11},{4,12},{5,13},{6,14},{7,15},{8,0},{9,1},... | collective-permute-start | bytes 442376 | tf_op jit(solution)/shard_map/ppermute | solution.py:441
  60.9 10.9 %collective-permute-start.4 = (bf16[32,2304]{1,0:T(8,128)(2,1)S(1)}, bf16[32,2304]{1,0:T(8,128)(2,1)S(1)}, u32[]{:S(2)}, u32[]{:S(2)}) collective-permute-start(bf16[32,2304]{1,0:T(8,128)(2,1)S(1)} %get-tuple-element.48), channel_id=1, source_target_pairs={{0,12},{1,13},{2,14},{3,15},{4,8},{5,9},{6,10},{7,11},{8,4},{9,5},... | collective-permute-start | bytes 442376 | tf_op jit(solution)/shard_map/ppermute | solution.py:441
  61.4 11.4 %collective-permute-start.5 = (bf16[32,2304]{1,0:T(8,128)(2,1)S(1)}, bf16[32,2304]{1,0:T(8,128)(2,1)S(1)}, u32[]{:S(2)}, u32[]{:S(2)}) collective-permute-start(bf16[32,2304]{1,0:T(8,128)(2,1)S(1)} %get-tuple-element.47), channel_id=1, source_target_pairs={{0,4},{1,5},{2,6},{3,7},{4,0},{5,1},{6,2},{7,3},{8,12},{9,13},{10,... | collective-permute-start | bytes 442376 | tf_op jit(solution)/shard_map/ppermute | solution.py:441
  73.3 14.3 %collective-permute-start.6 = (bf16[32,2176]{1,0:T(8,128)(2,1)S(1)}, bf16[32,2176]{1,0:T(8,128)(2,1)S(1)}, u32[]{:S(2)}, u32[]{:S(2)}) collective-permute-start(bf16[32,2176]{1,0:T(8,128)(2,1)S(1)} %shard_map.112.refs_0_), channel_id=1, source_target_pairs={{0,8},{1,9},{2,10},{3,11},{4,12},{5,13},{6,14},{7,15},{8,0},{9,1},... | collective-permute-start | bytes 417800 | tf_op jit(solution)/shard_map/ppermute | solution.py:441
  77.1 10.5 %collective-permute-start.7 = (bf16[32,2176]{1,0:T(8,128)(2,1)S(1)}, bf16[32,2176]{1,0:T(8,128)(2,1)S(1)}, u32[]{:S(2)}, u32[]{:S(2)}) collective-permute-start(bf16[32,2176]{1,0:T(8,128)(2,1)S(1)} %shard_map.112.refs_0_), channel_id=1, source_target_pairs={{0,12},{1,13},{2,14},{3,15},{4,8},{5,9},{6,10},{7,11},{8,4},{9,5},... | collective-permute-start | bytes 417800 | tf_op jit(solution)/shard_map/ppermute | solution.py:441
  78.1 9.5 %collective-permute-start.8 = (bf16[32,2176]{1,0:T(8,128)(2,1)S(1)}, bf16[32,2176]{1,0:T(8,128)(2,1)S(1)}, u32[]{:S(2)}, u32[]{:S(2)}) collective-permute-start(bf16[32,2176]{1,0:T(8,128)(2,1)S(1)} %shard_map.112.refs_0_), channel_id=1, source_target_pairs={{0,4},{1,5},{2,6},{3,7},{4,0},{5,1},{6,2},{7,3},{8,12},{9,13},{10,... | collective-permute-start | bytes 417800 | tf_op jit(solution)/shard_map/ppermute | solution.py:441
  78.1 9.5 %collective-permute-start.9 = (bf16[32,2176]{1,0:T(8,128)(2,1)S(1)}, bf16[32,2176]{1,0:T(8,128)(2,1)S(1)}, u32[]{:S(2)}, u32[]{:S(2)}) collective-permute-start(bf16[32,2176]{1,0:T(8,128)(2,1)S(1)} %shard_map.112.refs_0_), channel_id=1, source_target_pairs={{0,2},{1,3},{2,0},{3,1},{4,6},{5,7},{6,4},{7,5},{8,10},{9,11},{10,... | collective-permute-start | bytes 417800 | tf_op jit(solution)/shard_map/ppermute | solution.py:441
  88.7 9.9 %collective-permute-start.10 = (bf16[32,2176]{1,0:T(8,128)(2,1)S(1)}, bf16[32,2176]{1,0:T(8,128)(2,1)S(1)}, u32[]{:S(2)}, u32[]{:S(2)}) collective-permute-start(bf16[32,2176]{1,0:T(8,128)(2,1)S(1)} %collective-permute-done.6.refs_1_), channel_id=1, source_target_pairs={{0,2},{1,3},{2,0},{3,1},{4,6},{5,7},{6,4},{7,5},{8,10},{9,11},{10,... | collective-permute-start | bytes 417800 | tf_op jit(solution)/shard_map/ppermute | solution.py:441
  89.9 8.7 %collective-permute-start.11 = (bf16[32,2176]{1,0:T(8,128)(2,1)S(1)}, bf16[32,2176]{1,0:T(8,128)(2,1)S(1)}, u32[]{:S(2)}, u32[]{:S(2)}) collective-permute-start(bf16[32,2176]{1,0:T(8,128)(2,1)S(1)} %collective-permute-done.7.refs_2_), channel_id=1, source_target_pairs={{0,2},{1,3},{2,0},{3,1},{4,6},{5,7},{6,4},{7,5},{8,10},{9,11},{10,... | collective-permute-start | bytes 417800 | tf_op jit(solution)/shard_map/ppermute | solution.py:441
  90.7 9.6 %collective-permute-start.12 = (bf16[32,2176]{1,0:T(8,128)(2,1)S(1)}, bf16[32,2176]{1,0:T(8,128)(2,1)S(1)}, u32[]{:S(2)}, u32[]{:S(2)}) collective-permute-start(bf16[32,2176]{1,0:T(8,128)(2,1)S(1)} %collective-permute-done.8.refs_3_), channel_id=1, source_target_pairs={{0,2},{1,3},{2,0},{3,1},{4,6},{5,7},{6,4},{7,5},{8,10},{9,11},{10,... | collective-permute-start | bytes 417800 | tf_op jit(solution)/shard_map/ppermute | solution.py:441
  100.3 4.3 %collective-permute-start.17 = (bf16[32,2176]{1,0:T(8,128)(2,1)S(1)}, bf16[32,2176]{1,0:T(8,128)(2,1)S(1)}, u32[]{:S(2)}, u32[]{:S(2)}) collective-permute-start(bf16[32,2176]{1,0:T(8,128)(2,1)S(1)} %collective-permute-done.9.refs_0_), channel_id=1, source_target_pairs={{0,1},{1,0},{2,3},{3,2},{4,5},{5,4},{6,7},{7,6},{8,9},{9,8},{10,11... | collective-permute-start | bytes 417800 | tf_op jit(solution)/shard_map/ppermute | solution.py:441
  100.9 6.1 %collective-permute-start.18 = (bf16[32,2176]{1,0:T(8,128)(2,1)S(1)}, bf16[32,2176]{1,0:T(8,128)(2,1)S(1)}, u32[]{:S(2)}, u32[]{:S(2)}) collective-permute-start(bf16[32,2176]{1,0:T(8,128)(2,1)S(1)} %collective-permute-done.10.refs_1_), channel_id=1, source_target_pairs={{0,1},{1,0},{2,3},{3,2},{4,5},{5,4},{6,7},{7,6},{8,9},{9,8},{10,11... | collective-permute-start | bytes 417800 | tf_op jit(solution)/shard_map/ppermute | solution.py:441
  100.9 6.1 %collective-permute-start.19 = (bf16[32,2176]{1,0:T(8,128)(2,1)S(1)}, bf16[32,2176]{1,0:T(8,128)(2,1)S(1)}, u32[]{:S(2)}, u32[]{:S(2)}) collective-permute-start(bf16[32,2176]{1,0:T(8,128)(2,1)S(1)} %collective-permute-done.11.refs_2_), channel_id=1, source_target_pairs={{0,1},{1,0},{2,3},{3,2},{4,5},{5,4},{6,7},{7,6},{8,9},{9,8},{10,11... | collective-permute-start | bytes 417800 | tf_op jit(solution)/shard_map/ppermute | solution.py:441
  101.4 5.6 %collective-permute-start.20 = (bf16[32,2176]{1,0:T(8,128)(2,1)S(1)}, bf16[32,2176]{1,0:T(8,128)(2,1)S(1)}, u32[]{:S(2)}, u32[]{:S(2)}) collective-permute-start(bf16[32,2176]{1,0:T(8,128)(2,1)S(1)} %collective-permute-done.12.refs_3_), channel_id=1, source_target_pairs={{0,1},{1,0},{2,3},{3,2},{4,5},{5,4},{6,7},{7,6},{8,9},{9,8},{10,11... | collective-permute-start | bytes 417800 | tf_op jit(solution)/shard_map/ppermute | solution.py:441
  102.4 13.0 %collective-permute-start.23 = (bf16[32,2048]{1,0:T(8,128)(2,1)S(1)}, bf16[32,2048]{1,0:T(8,128)(2,1)S(1)}, u32[]{:S(2)}, u32[]{:S(2)}) collective-permute-start(bf16[32,2048]{1,0:T(8,128)(2,1)S(1)} %get-tuple-element.55), channel_id=1, source_target_pairs={{0,8},{1,9},{2,10},{3,11},{4,12},{5,13},{6,14},{7,15},{8,0},{9,1},... | collective-permute-start | bytes 393224 | tf_op jit(solution)/shard_map/ppermute | solution.py:441
  104.6 10.8 %collective-permute-start.24 = (bf16[32,2048]{1,0:T(8,128)(2,1)S(1)}, bf16[32,2048]{1,0:T(8,128)(2,1)S(1)}, u32[]{:S(2)}, u32[]{:S(2)}) collective-permute-start(bf16[32,2048]{1,0:T(8,128)(2,1)S(1)} %get-tuple-element.57), channel_id=1, source_target_pairs={{0,12},{1,13},{2,14},{3,15},{4,8},{5,9},{6,10},{7,11},{8,4},{9,5},... | collective-permute-start | bytes 393224 | tf_op jit(solution)/shard_map/ppermute | solution.py:441
  107.0 8.9 %collective-permute-start.25 = (bf16[32,2048]{1,0:T(8,128)(2,1)S(1)}, bf16[32,2048]{1,0:T(8,128)(2,1)S(1)}, u32[]{:S(2)}, u32[]{:S(2)}) collective-permute-start(bf16[32,2048]{1,0:T(8,128)(2,1)S(1)} %get-tuple-element.56), channel_id=1, source_target_pairs={{0,4},{1,5},{2,6},{3,7},{4,0},{5,1},{6,2},{7,3},{8,12},{9,13},{10,... | collective-permute-start | bytes 393224 | tf_op jit(solution)/shard_map/ppermute | solution.py:441
  116.2 14.0 %collective-permute-start.26 = (bf16[32,2048]{1,0:T(8,128)(2,1)S(1)}, bf16[32,2048]{1,0:T(8,128)(2,1)S(1)}, u32[]{:S(2)}, u32[]{:S(2)}) collective-permute-start(bf16[32,2048]{1,0:T(8,128)(2,1)S(1)} %get-tuple-element.51), channel_id=1, source_target_pairs={{0,10},{1,11},{2,8},{3,9},{4,14},{5,15},{6,12},{7,13},{8,2},{9,3},... | collective-permute-start | bytes 393224 | tf_op jit(solution)/shard_map/ppermute | solution.py:441
  119.2 10.9 %collective-permute-start.27 = (bf16[32,2048]{1,0:T(8,128)(2,1)S(1)}, bf16[32,2048]{1,0:T(8,128)(2,1)S(1)}, u32[]{:S(2)}, u32[]{:S(2)}) collective-permute-start(bf16[32,2048]{1,0:T(8,128)(2,1)S(1)} %get-tuple-element.54), channel_id=1, source_target_pairs={{0,14},{1,15},{2,12},{3,13},{4,10},{5,11},{6,8},{7,9},{8,6},{9,7},... | collective-permute-start | bytes 393224 | tf_op jit(solution)/shard_map/ppermute | solution.py:441
  121.5 9.4 %collective-permute-start.28 = (bf16[32,2048]{1,0:T(8,128)(2,1)S(1)}, bf16[32,2048]{1,0:T(8,128)(2,1)S(1)}, u32[]{:S(2)}, u32[]{:S(2)}) collective-permute-start(bf16[32,2048]{1,0:T(8,128)(2,1)S(1)} %get-tuple-element.53), channel_id=1, source_target_pairs={{0,6},{1,7},{2,4},{3,5},{4,2},{5,3},{6,0},{7,1},{8,14},{9,15},{10,... | collective-permute-start | bytes 393224 | tf_op jit(solution)/shard_map/ppermute | solution.py:441
  121.5 11.5 %collective-permute-start.29 = (bf16[32,2048]{1,0:T(8,128)(2,1)S(1)}, bf16[32,2048]{1,0:T(8,128)(2,1)S(1)}, u32[]{:S(2)}, u32[]{:S(2)}) collective-permute-start(bf16[32,2048]{1,0:T(8,128)(2,1)S(1)} %get-tuple-element.52), channel_id=1, source_target_pairs={{0,2},{1,3},{2,0},{3,1},{4,6},{5,7},{6,4},{7,5},{8,10},{9,11},{10,... | collective-permute-start | bytes 393224 | tf_op jit(solution)/shard_map/ppermute | solution.py:441
  (14 other events, 177.5 us)

commit v7 on v6

--- a/solution.py
+++ b/solution.py
@@ -240,7 +240,15 @@
     return out
 
 
-def pack_kernel(qkv_ref, out_ref):
+def pack_kernel(qkv_ref, merge_ref, out_ref, common_ref, share_ref, sems):
+    common, share = common_ref.shape[0], share_ref.shape[0]
+    spot = pl.multiple_of(common + share * lax.axis_index("grp"), 16)
+    copies = [
+        pltpu.make_async_copy(merge_ref.at[pl.ds(spot, share), :], share_ref, sems.at[0]),
+        pltpu.make_async_copy(merge_ref.at[pl.ds(0, common), :], common_ref, sems.at[1]),
+    ]
+    for copy in copies:
+        copy.start()
     rows, width = qkv_ref.shape
     tokens = rows // 4
     peers, parts, _ = out_ref.shape
@@ -258,6 +266,8 @@
         ).astype(BF)
         for peer in range(peers):
             out_ref[peer, kind * part : (kind + 1) * part, :] = turned[peer * part : (peer + 1) * part]
+    for copy in copies:
+        copy.wait()
 
 
 def attend_kernel(x_ref, grid_ref, out_ref):
@@ -291,7 +301,7 @@
             own = jnp.concatenate([jnp.where(head_row == head, query, 0.0).astype(BF), ones], 0)
             scores = jnp.dot(keys, own, preferred_element_type=F32)
             highest = jnp.max(scores, axis=0, keepdims=True)
-            weights = jnp.exp2(scores * factor - highest * factor)
+            weights = jnp.exp2((scores - highest) * factor)
             total = jnp.sum(weights, axis=0, keepdims=True)
             value = jnp.dot(values[head], weights.astype(BF), preferred_element_type=F32) / total
             mixed += [value[:, s * lanes : (s + 1) * lanes] for s in range(sides)]
@@ -305,9 +315,10 @@
 
 
 def merge_kernel(
-    x_ref, w_out_ref, gain_ref, bias_ref, w0, w1, w2, w3, out_ref, att_ref, w_ref, sems
+    x_ref, w_out_ref, gain_ref, bias_ref, *refs
 ):
-    me = lax.axis_index("wide")
+    w0, w1, *rest, out_ref, att_ref, w_ref, sems = refs
+    me, group = lax.axis_index("wide"), lax.axis_index("grp")
     position, quarter = me // 4, me % 4
     blocks, dim, lanes = x_ref.shape
     pairs = blocks // 2
@@ -315,9 +326,14 @@
     out_width = w0.shape[1]
     width = w_out_ref.shape[1]
     copies = []
-    for k, source in enumerate((w0, w1, w2, w3)):
-        spot = pl.multiple_of(flipped(quarter, k) * depth, depth)
-        copies.append(pltpu.make_async_copy(source, w_ref.at[pl.ds(spot, depth), :], sems.at[k]))
+    common, share = rest[0].shape[0], rest[1].shape[0]
+    places = [(w0, 0, 0), (w1, 1, 0)]
+    for k in (2, 3):
+        both, mine, theirs = rest[3 * (k - 2) : 3 * (k - 1)]
+        places += [(both, k, 0), (mine, k, common + share * group), (theirs, k, common + share * (1 - group))]
+    for n, (source, k, first) in enumerate(places):
+        spot = pl.multiple_of(flipped(quarter, k) * depth + first, 16)
+        copies.append(pltpu.make_async_copy(source, w_ref.at[pl.ds(spot, source.shape[0]), :], sems.at[n]))
         copies[-1].start()
     left = lax.broadcasted_iota(jnp.int32, (dim, lanes), 1) < lanes // 2
     for pair in range(pairs):
@@ -458,6 +474,8 @@
         and devices == 2 * experts
         and 2 * out_width == tokens * LANES
         and 4 * w_merge.shape[0] == vit_width
+        and lax.axis_size("grp") == 2
+        and w_merge.shape[0] % 32 == 0
     )
     if not suits:
         return general(
@@ -465,19 +483,27 @@
         )
     part = vit_width // peers
     dim = vit_width // HEADS
-    packed = pl.pallas_call(
+    depth = w_merge.shape[0]
+    share = depth // 64 * 16
+    packed, common, shared = pl.pallas_call(
         pack_kernel,
-        out_shape=jax.ShapeDtypeStruct((peers, 3 * part, rows), BF),
-        in_specs=[VMEM],
-        out_specs=VMEM,
-        compiler_params=params(8),
-    )(qkv)
+        out_shape=[
+            jax.ShapeDtypeStruct((peers, 3 * part, rows), BF),
+            jax.ShapeDtypeStruct((depth - 2 * share, out_width), BF),
+            jax.ShapeDtypeStruct((share, out_width), BF),
+        ],
+        in_specs=[VMEM, HBM],
+        out_specs=[VMEM] * 3,
+        scratch_shapes=[pltpu.SemaphoreType.DMA((2,))],
+        compiler_params=params(56),
+    )(qkv, w_merge)
     clips = [[c * peers + i for i in range(peers)] for c in range(CLIPS)]
     gathered = lax.all_to_all(
         packed, "wide", split_axis=0, concat_axis=0, tiled=True, axis_index_groups=clips
     )
-    gathered, held = lax.optimization_barrier((gathered, w_merge))
-    held_y = crossed(held, 2)
+    gathered, common, shared, held = lax.optimization_barrier((gathered, common, shared, w_merge))
+    mine_y = crossed(shared, 2)
+    common_y = crossed(common, 2)
     attended = pl.pallas_call(
         attend_kernel,
         out_shape=jax.ShapeDtypeStruct((devices, dim, rows), BF),
@@ -487,20 +513,23 @@
         cost_estimate=cost(2**32, 2**22, 2**21),
     )(gathered, grid)
     held_c = crossed(held, 1)
+    attended, mine_y = lax.optimization_barrier((attended, mine_y))
+    theirs_y = lax.ppermute(mine_y, "grp", [(0, 1), (1, 0)])
+    mine_yc = crossed(mine_y, 1)
     returned = lax.all_to_all(attended, "wide", split_axis=0, concat_axis=0, tiled=True)
-    returned, held_y = lax.optimization_barrier((returned, held_y))
-    held_yc = crossed(held_y, 1)
+    returned, common_y, theirs_y = lax.optimization_barrier((returned, common_y, theirs_y))
+    common_yc, theirs_yc = crossed(common_y, 1), crossed(theirs_y, 1)
     planes = devices // 4
     message = out_width + 2 * LANES
     partial = pl.pallas_call(
         merge_kernel,
         out_shape=jax.ShapeDtypeStruct((planes, tokens, message), BF),
-        in_specs=[VMEM, VMEM, VMEM, VMEM, HBM, HBM, HBM, HBM],
+        in_specs=[VMEM] * 4 + [pl.BlockSpec(memory_space=pl.ANY)] * 8,
         out_specs=VMEM,
         scratch_shapes=[
             pltpu.VMEM((vit_width, rows), BF),
             pltpu.VMEM((vit_width, out_width), BF),
-            pltpu.SemaphoreType.DMA((4,)),
+            pltpu.SemaphoreType.DMA((8,)),
         ],
         compiler_params=params(20),
     )(
@@ -508,10 +537,14 @@
         w_out,
         ln_gain.reshape(1, 4 * vit_width),
         ln_bias.reshape(1, 4 * vit_width),
-        held,
+        w_merge,
         held_c,
-        held_y,
-        held_yc,
+        common_y,
+        mine_y,
+        theirs_y,
+        common_yc,
+        mine_yc,
+        theirs_yc,
     )
     along = (8, 12, 4)
     arrived = [partial[0]] + [crossed(partial[mask // 4], mask) for mask in along]

time: 134 us -> 133 us (level)
  waiting for transfers between devices: 54 us -> 45.1 us
  local copies, waits for them, and re-layouts: 1.76 us -> 4.73 us
  Pallas kernels: 25.6 us -> 28.1 us
  starting transfers between devices: 32.2 us -> 34.5 us
    all_to_all x1, waiting for transfers between devices: 17.4 us -> 0.2 us  [local(): lax.all_to_all(attended, 'wide', split_axis=0, concat_axis=0, tiled=True)]
    ppermute x0 -> x1, waiting for transfers between devices: none -> 7.04 us  [local(): theirs_y = lax.ppermute(mine_y, 'grp', [(0, 1), (1, 0)])]
    pallas_call x1, Pallas kernels: 0.43 us -> 3.66 us  [local(): pl.pallas_call(pack_kernel, out_shape=[jax.ShapeDtypeStruct((peers, 3 * p...]
    unnamed x16 -> x22, local copies, waits for them, and re-layouts: 1.55 us -> 4.51 us
    ppermute x0 -> x1, starting transfers between devices: none -> 1.49 us  [local(): theirs_y = lax.ppermute(mine_y, 'grp', [(0, 1), (1, 0)])]
    ppermute x30 -> x33, starting transfers between devices: 27.5 us -> 28.8 us  [crossed(): return lax.ppermute(value, 'wide', pairs)]
    ppermute x30 -> x33, waiting for transfers between devices: 36.6 us -> 37.8 us  [crossed(): return lax.ppermute(value, 'wide', pairs)]
  transfers between devices with their start and end apart: 31 -> 35, of which waited for: 12 -> 16; matrix products, arithmetic and copies ran while one was open for 1% -> 1% of each run, Pallas kernels for 15% -> 15%
where the time goes in v7:
time: 133 us
  waiting for transfers between devices  45.1 us (34%)
  starting transfers between devices  34.5 us (26%)
  Pallas kernels  28.1 us (21%)
  blocking collectives  18.7 us (14%)
  local copies, waits for them, and re-layouts  4.73 us (4%)
  other arithmetic  1.38 us (1%)
    ppermute x33, waiting for transfers between devices, crossed(): return lax.ppermute(value, 'wide', pairs)  37.8 us
    ppermute x33, starting transfers between devices, crossed(): return lax.ppermute(value, 'wide', pairs)  28.8 us
    all_to_all x1, blocking collectives, local(): lax.all_to_all(packed, 'wide', split_axis=0, concat_axis=0, tiled=True, a...  18.7 us
    pallas_call x2, Pallas kernels, experts_of(): pl.pallas_call(lambda *refs: expert_kernel(*refs, experts=experts, cuts=c...  13.3 us
    ppermute x1, waiting for transfers between devices, local(): theirs_y = lax.ppermute(mine_y, 'grp', [(0, 1), (1, 0)])  7.04 us
    pallas_call x1, Pallas kernels, local(): pl.pallas_call(attend_kernel, out_shape=jax.ShapeDtypeStruct((devices, di...  6.9 us
    unnamed x22, local copies, waits for them, and re-layouts  4.51 us
    all_to_all x1, starting transfers between devices, local(): lax.all_to_all(attended, 'wide', split_axis=0, concat_axis=0, tiled=True)  4.22 us
  transfers between devices with their start and end apart: 35, of which 16 were waited for; matrix products, arithmetic and copies ran while one was open for 1% of the time, Pallas kernels for 15%

profile of v7, /device:TPU:0, one launch (start us, length us, event | category | flops | bytes accessed | tf_op | source)
XLA Modules:
  0.0 132.8 jit_solution(15397258842074612961)
XLA Ops:
  0.0 3.7 %shard_map.109 = (bf16[8,432,128]{2,1,0:T(8,128)(2,1)}, bf16[160,2048]{1,0:T(8,128)(2,1)}, bf16[64,2048]{1,0:T(8,128)(2,1)}) custom-call(bf16[128,3456]{1,0:T(8,128)(2,1)} %qkv_ref.1, bf16[288,2048]{1,0:T(8,128)(2,1)} %refs_0_.1), custom_call_target="tpu_custom_call" | custom-call | tf_op jit(solution)/shard_map/pallas_call | solution.py:488
  3.7 18.7 %all_to_all.10.x_ref = bf16[8,432,128]{2,1,0:T(8,128)(2,1)S(1)} all-to-all(bf16[8,432,128]{2,1,0:T(8,128)(2,1)} %get-tuple-element.34), channel_id=1, replica_groups={{0,1,2,3,4,5,6,7},{8,9,10,11,12,13,14,15},{16,17,18,19,20,21,22,23},{24..., dimensions={0} | all-to-all | bytes 1769472 | tf_op jit(solution)/shard_map/all_to_all | solution.py:501
  23.3 1.2 collective-permute-start.1
  24.5 6.9 %shard_map.110 = bf16[16,72,128]{2,1,0:T(8,128)(2,1)} custom-call(bf16[8,432,128]{2,1,0:T(8,128)(2,1)S(1)} %all_to_all.10.x_ref, s32[2,2]{1,0:T(2,128)S(1)} %copy-done.4), custom_call_target="tpu_custom_call" | custom-call | flops 4294967296 | bytes 4194304 | tf_op jit(solution)/shard_map/pallas_call | solution.py:507
  32.0 4.2 %all-to-all-start.1 = ((bf16[16,72,128]{2,1,0:T(8,128)(2,1)}), bf16[16,72,128]{2,1,0:T(8,128)(2,1)S(1)}, u32[]{:S(2)}, u32[]{:S(2)}) async-start(bf16[16,72,128]{2,1,0:T(8,128)(2,1)} %shard_map.110), calls=%async_computation.1 | async-start | bytes 589824 | tf_op jit(solution)/shard_map/all_to_all | solution.py:519
  36.7 1.5 %collective-permute-start.2 = (bf16[64,2048]{1,0:T(8,128)(2,1)}, bf16[64,2048]{1,0:T(8,128)(2,1)S(1)}, u32[]{:S(2)}, u32[]{:S(2)}) collective-permute-start(bf16[64,2048]{1,0:T(8,128)(2,1)} %collective-permute-done.refs_3_), channel_id=1, source_target_pairs={{0,16},{16,0},{1,17},{17,1},{2,18},{18,2},{3,19},{19,3},{4,20},{20... | collective-permute-start | bytes 786440 | tf_op jit(solution)/shard_map/ppermute | solution.py:517
  38.2 7.0 %collective-permute-done.2.refs_4_ = bf16[64,2048]{1,0:T(8,128)(2,1)S(1)} collective-permute-done((bf16[64,2048]{1,0:T(8,128)(2,1)}, bf16[64,2048]{1,0:T(8,128)(2,1)S(1)}, u32[]{:S(2)}, u32[]{:S(2)}) %collective-permute-start.2) | collective-permute-done | bytes 262176 | tf_op jit(solution)/shard_map/ppermute | solution.py:517
  46.0 1.5 %collective-permute-done.1.refs_2_ = bf16[160,2048]{1,0:T(8,128)(2,1)S(1)} collective-permute-done((bf16[160,2048]{1,0:T(8,128)(2,1)}, bf16[160,2048]{1,0:T(8,128)(2,1)S(1)}, u32[]{:S(2)}, u32[]{:S(2)}) %collective-permute-start.1) | collective-permute-done | bytes 655392 | tf_op jit(solution)/shard_map/ppermute | solution.py:457
  50.8 1.7 %copy-done.1 = bf16[1152,1152]{1,0:T(8,128)(2,1)S(1)} copy-done((bf16[1152,1152]{1,0:T(8,128)(2,1)S(1)}, bf16[1152,1152]{1,0:T(8,128)(2,1)}, u32[]{:S(2)}) %copy-start.1) | copy-done | bytes 2654232
  53.5 3.7 %shard_map.111 = bf16[4,32,2304]{2,1,0:T(8,128)(2,1)S(1)} custom-call(bf16[16,72,128]{2,1,0:T(8,128)(2,1)S(1)} %all-to-all-done.1.x_ref, bf16[1152,1152]{1,0:T(8,128)(2,1)S(1)} %copy-done.1, f32[1,4608]{1,0:T(1,128)S(1)} %reshape.8.gain_ref, f32[1,4608]{1,0:T(1,128)S(1)} %reshape.9.bias_ref, bf16[288,2048]{1,0:T(8,128)(2,1)S(1)} %copy-done, ...), custom_call_target="tpu_custom_call" | custom-call | tf_op jit(solution)/shard_map/pallas_call | solution.py:524
  57.2 2.7 %collective-permute-start.7 = (bf16[32,2304]{1,0:T(8,128)(2,1)S(1)}, bf16[32,2304]{1,0:T(8,128)(2,1)S(1)}, u32[]{:S(2)}, u32[]{:S(2)}) collective-permute-start(bf16[32,2304]{1,0:T(8,128)(2,1)S(1)} %get-tuple-element.65), channel_id=1, source_target_pairs={{0,8},{1,9},{2,10},{3,11},{4,12},{5,13},{6,14},{7,15},{8,0},{9,1},... | collective-permute-start | bytes 442376 | tf_op jit(solution)/shard_map/ppermute | solution.py:457
  61.2 9.5 %collective-permute-done.7.refs_1_ = bf16[32,2304]{1,0:T(8,128)(2,1)S(1)} collective-permute-done((bf16[32,2304]{1,0:T(8,128)(2,1)S(1)}, bf16[32,2304]{1,0:T(8,128)(2,1)S(1)}, u32[]{:S(2)}, u32[]{:S(2)}) %collective-permute-start.7) | collective-permute-done | bytes 147488 | tf_op jit(solution)/shard_map/ppermute | solution.py:457
  72.4 3.8 %collective-permute-start.10 = (bf16[32,2176]{1,0:T(8,128)(2,1)S(1)}, bf16[32,2176]{1,0:T(8,128)(2,1)S(1)}, u32[]{:S(2)}, u32[]{:S(2)}) collective-permute-start(bf16[32,2176]{1,0:T(8,128)(2,1)S(1)} %shard_map.112.refs_0_), channel_id=1, source_target_pairs={{0,8},{1,9},{2,10},{3,11},{4,12},{5,13},{6,14},{7,15},{8,0},{9,1},... | collective-permute-start | bytes 417800 | tf_op jit(solution)/shard_map/ppermute | solution.py:457
  78.2 8.4 %collective-permute-done.10.refs_1_ = bf16[32,2176]{1,0:T(8,128)(2,1)S(1)} collective-permute-done((bf16[32,2176]{1,0:T(8,128)(2,1)S(1)}, bf16[32,2176]{1,0:T(8,128)(2,1)S(1)}, u32[]{:S(2)}, u32[]{:S(2)}) %collective-permute-start.10) | collective-permute-done | bytes 139296 | tf_op jit(solution)/shard_map/ppermute | solution.py:457
  90.8 6.7 %shard_map.113 = (bf16[4,32,2048]{2,1,0:T(8,128)(2,1)S(1)}, bf16[4,32,2048]{2,1,0:T(8,128)(2,1)S(1)}) custom-call(bf16[32,2176]{1,0:T(8,128)(2,1)S(1)} %shard_map.112.refs_0_, bf16[32,2176]{1,0:T(8,128)(2,1)S(1)} %collective-permute-done.10.refs_1_, bf16[32,2176]{1,0:T(8,128)(2,1)S(1)} %collective-permute-done.11.refs_2_, ...), custom_call_target="tpu_custom_call" | custom-call | flops 4294967296 | bytes 16777216 | tf_op jit(solution)/shard_map/pallas_call | solution.py:570
  97.5 1.8 %collective-permute-done.16.refs_3_ = bf16[32,2176]{1,0:T(8,128)(2,1)S(1)} collective-permute-done((bf16[32,2176]{1,0:T(8,128)(2,1)S(1)}, bf16[32,2176]{1,0:T(8,128)(2,1)S(1)}, u32[]{:S(2)}, u32[]{:S(2)}) %collective-permute-start.16) | collective-permute-done | bytes 139296 | tf_op jit(solution)/shard_map/ppermute | solution.py:457
  101.5 2.2 %collective-permute-start.27 = (bf16[32,2048]{1,0:T(8,128)(2,1)S(1)}, bf16[32,2048]{1,0:T(8,128)(2,1)S(1)}, u32[]{:S(2)}, u32[]{:S(2)}) collective-permute-start(bf16[32,2048]{1,0:T(8,128)(2,1)S(1)} %get-tuple-element.71), channel_id=1, source_target_pairs={{0,8},{1,9},{2,10},{3,11},{4,12},{5,13},{6,14},{7,15},{8,0},{9,1},... | collective-permute-start | bytes 393224 | tf_op jit(solution)/shard_map/ppermute | solution.py:457
  103.7 2.3 %collective-permute-start.28 = (bf16[32,2048]{1,0:T(8,128)(2,1)S(1)}, bf16[32,2048]{1,0:T(8,128)(2,1)S(1)}, u32[]{:S(2)}, u32[]{:S(2)}) collective-permute-start(bf16[32,2048]{1,0:T(8,128)(2,1)S(1)} %get-tuple-element.73), channel_id=1, source_target_pairs={{0,12},{1,13},{2,14},{3,15},{4,8},{5,9},{6,10},{7,11},{8,4},{9,5},... | collective-permute-start | bytes 393224 | tf_op jit(solution)/shard_map/ppermute | solution.py:457
  106.0 6.7 %shard_map.114 = (bf16[4,32,2048]{2,1,0:T(8,128)(2,1)S(1)}, bf16[4,32,2048]{2,1,0:T(8,128)(2,1)S(1)}) custom-call(bf16[32,2176]{1,0:T(8,128)(2,1)S(1)} %collective-permute-done.13.refs_0_, bf16[32,2176]{1,0:T(8,128)(2,1)S(1)} %collective-permute-done.14.refs_1_, bf16[32,2176]{1,0:T(8,128)(2,1)S(1)} %collective-permute-done.15.refs_2_, ...), custom_call_target="tpu_custom_call" | custom-call | flops 4294967296 | bytes 16777216 | tf_op jit(solution)/shard_map/pallas_call | solution.py:570
  112.8 1.6 %collective-permute-done.27 = bf16[32,2048]{1,0:T(8,128)(2,1)S(1)} collective-permute-done((bf16[32,2048]{1,0:T(8,128)(2,1)S(1)}, bf16[32,2048]{1,0:T(8,128)(2,1)S(1)}, u32[]{:S(2)}, u32[]{:S(2)}) %collective-permute-start.27) | collective-permute-done | bytes 131104 | tf_op jit(solution)/shard_map/ppermute | solution.py:457
  115.2 2.9 %collective-permute-start.30 = (bf16[32,2048]{1,0:T(8,128)(2,1)S(1)}, bf16[32,2048]{1,0:T(8,128)(2,1)S(1)}, u32[]{:S(2)}, u32[]{:S(2)}) collective-permute-start(bf16[32,2048]{1,0:T(8,128)(2,1)S(1)} %get-tuple-element.67), channel_id=1, source_target_pairs={{0,10},{1,11},{2,8},{3,9},{4,14},{5,15},{6,12},{7,13},{8,2},{9,3},... | collective-permute-start | bytes 393224 | tf_op jit(solution)/shard_map/ppermute | solution.py:457
  118.1 2.4 %collective-permute-start.31 = (bf16[32,2048]{1,0:T(8,128)(2,1)S(1)}, bf16[32,2048]{1,0:T(8,128)(2,1)S(1)}, u32[]{:S(2)}, u32[]{:S(2)}) collective-permute-start(bf16[32,2048]{1,0:T(8,128)(2,1)S(1)} %get-tuple-element.70), channel_id=1, source_target_pairs={{0,14},{1,15},{2,12},{3,13},{4,10},{5,11},{6,8},{7,9},{8,6},{9,7},... | collective-permute-start | bytes 393224 | tf_op jit(solution)/shard_map/ppermute | solution.py:457
  121.6 7.5 %collective-permute-done.30 = bf16[32,2048]{1,0:T(8,128)(2,1)S(1)} collective-permute-done((bf16[32,2048]{1,0:T(8,128)(2,1)S(1)}, bf16[32,2048]{1,0:T(8,128)(2,1)S(1)}, u32[]{:S(2)}, u32[]{:S(2)}) %collective-permute-start.30) | collective-permute-done | bytes 131104 | tf_op jit(solution)/shard_map/ppermute | solution.py:457
  130.0 2.1 %collective-permute-done.33 = bf16[32,2048]{1,0:T(8,128)(2,1)S(1)} collective-permute-done((bf16[32,2048]{1,0:T(8,128)(2,1)S(1)}, bf16[32,2048]{1,0:T(8,128)(2,1)S(1)}, u32[]{:S(2)}, u32[]{:S(2)}) %collective-permute-start.33) | collective-permute-done | bytes 131104 | tf_op jit(solution)/shard_map/ppermute | solution.py:457
  (87 shorter events, 21.7 us)
Async XLA Ops:
  22.4 9.6 %collective-permute-start = (bf16[64,2048]{1,0:T(8,128)(2,1)}, bf16[64,2048]{1,0:T(8,128)(2,1)}, u32[]{:S(2)}, u32[]{:S(2)}) collective-permute-start(bf16[64,2048]{1,0:T(8,128)(2,1)} %get-tuple-element.38), channel_id=1, source_target_pairs={{0,2},{1,3},{2,0},{3,1},{4,6},{5,7},{6,4},{7,5},{8,10},{9,11},{10,... | collective-permute-start | bytes 786440 | tf_op jit(solution)/shard_map/ppermute | solution.py:457
  23.3 24.1 %collective-permute-start.1 = (bf16[160,2048]{1,0:T(8,128)(2,1)}, bf16[160,2048]{1,0:T(8,128)(2,1)S(1)}, u32[]{:S(2)}, u32[]{:S(2)}) collective-permute-start(bf16[160,2048]{1,0:T(8,128)(2,1)} %get-tuple-element.40), channel_id=1, source_target_pairs={{0,2},{1,3},{2,0},{3,1},{4,6},{5,7},{6,4},{7,5},{8,10},{9,11},{10,... | collective-permute-start | bytes 1966088 | tf_op jit(solution)/shard_map/ppermute | solution.py:457
  32.0 15.6 %all-to-all-start.1 = ((bf16[16,72,128]{2,1,0:T(8,128)(2,1)}), bf16[16,72,128]{2,1,0:T(8,128)(2,1)S(1)}, u32[]{:S(2)}, u32[]{:S(2)}) async-start(bf16[16,72,128]{2,1,0:T(8,128)(2,1)} %shard_map.110), calls=%async_computation.1 | async-start | bytes 589824 | tf_op jit(solution)/shard_map/all_to_all | solution.py:519
  36.3 14.5 %collective-permute-start.3 = (bf16[288,2048]{1,0:T(8,128)(2,1)S(1)}, bf16[288,2048]{1,0:T(8,128)(2,1)S(1)}, u32[]{:S(2)}, u32[]{:S(2)}) collective-permute-start(bf16[288,2048]{1,0:T(8,128)(2,1)S(1)} %copy-done), channel_id=1, source_target_pairs={{0,1},{1,0},{2,3},{3,2},{4,5},{5,4},{6,7},{7,6},{8,9},{9,8},{10,11... | collective-permute-start | bytes 3538952 | tf_op jit(solution)/shard_map/ppermute | solution.py:457
  36.7 8.5 %collective-permute-start.2 = (bf16[64,2048]{1,0:T(8,128)(2,1)}, bf16[64,2048]{1,0:T(8,128)(2,1)S(1)}, u32[]{:S(2)}, u32[]{:S(2)}) collective-permute-start(bf16[64,2048]{1,0:T(8,128)(2,1)} %collective-permute-done.refs_3_), channel_id=1, source_target_pairs={{0,16},{16,0},{1,17},{17,1},{2,18},{18,2},{3,19},{19,3},{4,20},{20... | collective-permute-start | bytes 786440 | tf_op jit(solution)/shard_map/ppermute | solution.py:517
  57.2 13.5 %collective-permute-start.7 = (bf16[32,2304]{1,0:T(8,128)(2,1)S(1)}, bf16[32,2304]{1,0:T(8,128)(2,1)S(1)}, u32[]{:S(2)}, u32[]{:S(2)}) collective-permute-start(bf16[32,2304]{1,0:T(8,128)(2,1)S(1)} %get-tuple-element.65), channel_id=1, source_target_pairs={{0,8},{1,9},{2,10},{3,11},{4,12},{5,13},{6,14},{7,15},{8,0},{9,1},... | collective-permute-start | bytes 442376 | tf_op jit(solution)/shard_map/ppermute | solution.py:457
  59.9 10.9 %collective-permute-start.8 = (bf16[32,2304]{1,0:T(8,128)(2,1)S(1)}, bf16[32,2304]{1,0:T(8,128)(2,1)S(1)}, u32[]{:S(2)}, u32[]{:S(2)}) collective-permute-start(bf16[32,2304]{1,0:T(8,128)(2,1)S(1)} %get-tuple-element.64), channel_id=1, source_target_pairs={{0,12},{1,13},{2,14},{3,15},{4,8},{5,9},{6,10},{7,11},{8,4},{9,5},... | collective-permute-start | bytes 442376 | tf_op jit(solution)/shard_map/ppermute | solution.py:457
  60.4 11.4 %collective-permute-start.9 = (bf16[32,2304]{1,0:T(8,128)(2,1)S(1)}, bf16[32,2304]{1,0:T(8,128)(2,1)S(1)}, u32[]{:S(2)}, u32[]{:S(2)}) collective-permute-start(bf16[32,2304]{1,0:T(8,128)(2,1)S(1)} %get-tuple-element.63), channel_id=1, source_target_pairs={{0,4},{1,5},{2,6},{3,7},{4,0},{5,1},{6,2},{7,3},{8,12},{9,13},{10,... | collective-permute-start | bytes 442376 | tf_op jit(solution)/shard_map/ppermute | solution.py:457
  72.4 14.3 %collective-permute-start.10 = (bf16[32,2176]{1,0:T(8,128)(2,1)S(1)}, bf16[32,2176]{1,0:T(8,128)(2,1)S(1)}, u32[]{:S(2)}, u32[]{:S(2)}) collective-permute-start(bf16[32,2176]{1,0:T(8,128)(2,1)S(1)} %shard_map.112.refs_0_), channel_id=1, source_target_pairs={{0,8},{1,9},{2,10},{3,11},{4,12},{5,13},{6,14},{7,15},{8,0},{9,1},... | collective-permute-start | bytes 417800 | tf_op jit(solution)/shard_map/ppermute | solution.py:457
  76.2 10.5 %collective-permute-start.11 = (bf16[32,2176]{1,0:T(8,128)(2,1)S(1)}, bf16[32,2176]{1,0:T(8,128)(2,1)S(1)}, u32[]{:S(2)}, u32[]{:S(2)}) collective-permute-start(bf16[32,2176]{1,0:T(8,128)(2,1)S(1)} %shard_map.112.refs_0_), channel_id=1, source_target_pairs={{0,12},{1,13},{2,14},{3,15},{4,8},{5,9},{6,10},{7,11},{8,4},{9,5},... | collective-permute-start | bytes 417800 | tf_op jit(solution)/shard_map/ppermute | solution.py:457
  77.2 9.5 %collective-permute-start.12 = (bf16[32,2176]{1,0:T(8,128)(2,1)S(1)}, bf16[32,2176]{1,0:T(8,128)(2,1)S(1)}, u32[]{:S(2)}, u32[]{:S(2)}) collective-permute-start(bf16[32,2176]{1,0:T(8,128)(2,1)S(1)} %shard_map.112.refs_0_), channel_id=1, source_target_pairs={{0,4},{1,5},{2,6},{3,7},{4,0},{5,1},{6,2},{7,3},{8,12},{9,13},{10,... | collective-permute-start | bytes 417800 | tf_op jit(solution)/shard_map/ppermute | solution.py:457
  77.2 9.5 %collective-permute-start.13 = (bf16[32,2176]{1,0:T(8,128)(2,1)S(1)}, bf16[32,2176]{1,0:T(8,128)(2,1)S(1)}, u32[]{:S(2)}, u32[]{:S(2)}) collective-permute-start(bf16[32,2176]{1,0:T(8,128)(2,1)S(1)} %shard_map.112.refs_0_), channel_id=1, source_target_pairs={{0,2},{1,3},{2,0},{3,1},{4,6},{5,7},{6,4},{7,5},{8,10},{9,11},{10,... | collective-permute-start | bytes 417800 | tf_op jit(solution)/shard_map/ppermute | solution.py:457
  87.8 9.8 %collective-permute-start.14 = (bf16[32,2176]{1,0:T(8,128)(2,1)S(1)}, bf16[32,2176]{1,0:T(8,128)(2,1)S(1)}, u32[]{:S(2)}, u32[]{:S(2)}) collective-permute-start(bf16[32,2176]{1,0:T(8,128)(2,1)S(1)} %collective-permute-done.10.refs_1_), channel_id=1, source_target_pairs={{0,2},{1,3},{2,0},{3,1},{4,6},{5,7},{6,4},{7,5},{8,10},{9,11},{10,... | collective-permute-start | bytes 417800 | tf_op jit(solution)/shard_map/ppermute | solution.py:457
  88.8 8.7 %collective-permute-start.15 = (bf16[32,2176]{1,0:T(8,128)(2,1)S(1)}, bf16[32,2176]{1,0:T(8,128)(2,1)S(1)}, u32[]{:S(2)}, u32[]{:S(2)}) collective-permute-start(bf16[32,2176]{1,0:T(8,128)(2,1)S(1)} %collective-permute-done.11.refs_2_), channel_id=1, source_target_pairs={{0,2},{1,3},{2,0},{3,1},{4,6},{5,7},{6,4},{7,5},{8,10},{9,11},{10,... | collective-permute-start | bytes 417800 | tf_op jit(solution)/shard_map/ppermute | solution.py:457
  89.8 9.6 %collective-permute-start.16 = (bf16[32,2176]{1,0:T(8,128)(2,1)S(1)}, bf16[32,2176]{1,0:T(8,128)(2,1)S(1)}, u32[]{:S(2)}, u32[]{:S(2)}) collective-permute-start(bf16[32,2176]{1,0:T(8,128)(2,1)S(1)} %collective-permute-done.12.refs_3_), channel_id=1, source_target_pairs={{0,2},{1,3},{2,0},{3,1},{4,6},{5,7},{6,4},{7,5},{8,10},{9,11},{10,... | collective-permute-start | bytes 417800 | tf_op jit(solution)/shard_map/ppermute | solution.py:457
  99.9 6.1 %collective-permute-start.22 = (bf16[32,2176]{1,0:T(8,128)(2,1)S(1)}, bf16[32,2176]{1,0:T(8,128)(2,1)S(1)}, u32[]{:S(2)}, u32[]{:S(2)}) collective-permute-start(bf16[32,2176]{1,0:T(8,128)(2,1)S(1)} %collective-permute-done.14.refs_1_), channel_id=1, source_target_pairs={{0,1},{1,0},{2,3},{3,2},{4,5},{5,4},{6,7},{7,6},{8,9},{9,8},{10,11... | collective-permute-start | bytes 417800 | tf_op jit(solution)/shard_map/ppermute | solution.py:457
  99.9 6.1 %collective-permute-start.23 = (bf16[32,2176]{1,0:T(8,128)(2,1)S(1)}, bf16[32,2176]{1,0:T(8,128)(2,1)S(1)}, u32[]{:S(2)}, u32[]{:S(2)}) collective-permute-start(bf16[32,2176]{1,0:T(8,128)(2,1)S(1)} %collective-permute-done.15.refs_2_), channel_id=1, source_target_pairs={{0,1},{1,0},{2,3},{3,2},{4,5},{5,4},{6,7},{7,6},{8,9},{9,8},{10,11... | collective-permute-start | bytes 417800 | tf_op jit(solution)/shard_map/ppermute | solution.py:457
  101.5 13.0 %collective-permute-start.27 = (bf16[32,2048]{1,0:T(8,128)(2,1)S(1)}, bf16[32,2048]{1,0:T(8,128)(2,1)S(1)}, u32[]{:S(2)}, u32[]{:S(2)}) collective-permute-start(bf16[32,2048]{1,0:T(8,128)(2,1)S(1)} %get-tuple-element.71), channel_id=1, source_target_pairs={{0,8},{1,9},{2,10},{3,11},{4,12},{5,13},{6,14},{7,15},{8,0},{9,1},... | collective-permute-start | bytes 393224 | tf_op jit(solution)/shard_map/ppermute | solution.py:457
  103.7 10.7 %collective-permute-start.28 = (bf16[32,2048]{1,0:T(8,128)(2,1)S(1)}, bf16[32,2048]{1,0:T(8,128)(2,1)S(1)}, u32[]{:S(2)}, u32[]{:S(2)}) collective-permute-start(bf16[32,2048]{1,0:T(8,128)(2,1)S(1)} %get-tuple-element.73), channel_id=1, source_target_pairs={{0,12},{1,13},{2,14},{3,15},{4,8},{5,9},{6,10},{7,11},{8,4},{9,5},... | collective-permute-start | bytes 393224 | tf_op jit(solution)/shard_map/ppermute | solution.py:457
  106.0 8.9 %collective-permute-start.29 = (bf16[32,2048]{1,0:T(8,128)(2,1)S(1)}, bf16[32,2048]{1,0:T(8,128)(2,1)S(1)}, u32[]{:S(2)}, u32[]{:S(2)}) collective-permute-start(bf16[32,2048]{1,0:T(8,128)(2,1)S(1)} %get-tuple-element.72), channel_id=1, source_target_pairs={{0,4},{1,5},{2,6},{3,7},{4,0},{5,1},{6,2},{7,3},{8,12},{9,13},{10,... | collective-permute-start | bytes 393224 | tf_op jit(solution)/shard_map/ppermute | solution.py:457
  115.2 13.9 %collective-permute-start.30 = (bf16[32,2048]{1,0:T(8,128)(2,1)S(1)}, bf16[32,2048]{1,0:T(8,128)(2,1)S(1)}, u32[]{:S(2)}, u32[]{:S(2)}) collective-permute-start(bf16[32,2048]{1,0:T(8,128)(2,1)S(1)} %get-tuple-element.67), channel_id=1, source_target_pairs={{0,10},{1,11},{2,8},{3,9},{4,14},{5,15},{6,12},{7,13},{8,2},{9,3},... | collective-permute-start | bytes 393224 | tf_op jit(solution)/shard_map/ppermute | solution.py:457
  118.1 11.0 %collective-permute-start.31 = (bf16[32,2048]{1,0:T(8,128)(2,1)S(1)}, bf16[32,2048]{1,0:T(8,128)(2,1)S(1)}, u32[]{:S(2)}, u32[]{:S(2)}) collective-permute-start(bf16[32,2048]{1,0:T(8,128)(2,1)S(1)} %get-tuple-element.70), channel_id=1, source_target_pairs={{0,14},{1,15},{2,12},{3,13},{4,10},{5,11},{6,8},{7,9},{8,6},{9,7},... | collective-permute-start | bytes 393224 | tf_op jit(solution)/shard_map/ppermute | solution.py:457
  120.6 9.4 %collective-permute-start.32 = (bf16[32,2048]{1,0:T(8,128)(2,1)S(1)}, bf16[32,2048]{1,0:T(8,128)(2,1)S(1)}, u32[]{:S(2)}, u32[]{:S(2)}) collective-permute-start(bf16[32,2048]{1,0:T(8,128)(2,1)S(1)} %get-tuple-element.69), channel_id=1, source_target_pairs={{0,6},{1,7},{2,4},{3,5},{4,2},{5,3},{6,0},{7,1},{8,14},{9,15},{10,... | collective-permute-start | bytes 393224 | tf_op jit(solution)/shard_map/ppermute | solution.py:457
  120.6 11.5 %collective-permute-start.33 = (bf16[32,2048]{1,0:T(8,128)(2,1)S(1)}, bf16[32,2048]{1,0:T(8,128)(2,1)S(1)}, u32[]{:S(2)}, u32[]{:S(2)}) collective-permute-start(bf16[32,2048]{1,0:T(8,128)(2,1)S(1)} %get-tuple-element.68), channel_id=1, source_target_pairs={{0,2},{1,3},{2,0},{3,1},{4,6},{5,7},{6,4},{7,5},{8,10},{9,11},{10,... | collective-permute-start | bytes 393224 | tf_op jit(solution)/shard_map/ppermute | solution.py:457
  (21 other events, 174.5 us)

commit v8 on v7

--- a/solution.py
+++ b/solution.py
@@ -240,9 +240,15 @@
     return out
 
 
-def pack_kernel(qkv_ref, merge_ref, out_ref, common_ref, share_ref, sems):
+def pack_kernel(qkv_hbm, merge_ref, out_ref, common_ref, share_ref, qkv_ref, sems):
     common, share = common_ref.shape[0], share_ref.shape[0]
     spot = pl.multiple_of(common + share * lax.axis_index("grp"), 16)
+    third = qkv_hbm.shape[1] // 3
+    loads = []
+    for kind in range(3):
+        cut = slice(kind * third, (kind + 1) * third)
+        loads.append(pltpu.make_async_copy(qkv_hbm.at[:, cut], qkv_ref.at[:, cut], sems.at[2 + kind]))
+        loads[-1].start()
     copies = [
         pltpu.make_async_copy(merge_ref.at[pl.ds(spot, share), :], share_ref, sems.at[0]),
         pltpu.make_async_copy(merge_ref.at[pl.ds(0, common), :], common_ref, sems.at[1]),
@@ -256,8 +262,8 @@
     place = lax.broadcasted_iota(jnp.int32, (rows, rows), 1)
     order = jnp.where(source == 4 * (place % tokens) + place // tokens, 1.0, 0.0).astype(BF)
     part = parts // 3
-    third = width // 3
     for kind in range(3):
+        loads[kind].wait()
         turned = lax.dot_general(
             qkv_ref[:, kind * third : (kind + 1) * third],
             order,
@@ -315,9 +321,9 @@
 
 
 def merge_kernel(
-    x_ref, w_out_ref, gain_ref, bias_ref, *refs
+    x_ref, w_out_hbm, gain_ref, bias_ref, *refs
 ):
-    w0, w1, *rest, out_ref, att_ref, w_ref, sems = refs
+    w0, w1, *rest, out_ref, att_ref, w_ref, w_out_ref, sems = refs
     me, group = lax.axis_index("wide"), lax.axis_index("grp")
     position, quarter = me // 4, me % 4
     blocks, dim, lanes = x_ref.shape
@@ -325,6 +331,8 @@
     depth = w0.shape[0]
     out_width = w0.shape[1]
     width = w_out_ref.shape[1]
+    first_copy = pltpu.make_async_copy(w_out_hbm, w_out_ref, sems.at[8])
+    first_copy.start()
     copies = []
     common, share = rest[0].shape[0], rest[1].shape[0]
     places = [(w0, 0, 0), (w1, 1, 0)]
@@ -341,6 +349,7 @@
         upper = jnp.where(left, first, pltpu.roll(second, lanes // 2, 1))
         lower = jnp.where(left, pltpu.roll(first, lanes // 2, 1), second)
         att_ref[2 * dim * pair : 2 * dim * (pair + 1), :] = jnp.concatenate([upper, lower], 0).astype(BF)
+    first_copy.wait()
     mixed = lax.dot_general(
         att_ref[...], w_out_ref[...], (((0,), (0,)), ((), ())), preferred_element_type=F32
     )
@@ -492,9 +501,9 @@
             jax.ShapeDtypeStruct((depth - 2 * share, out_width), BF),
             jax.ShapeDtypeStruct((share, out_width), BF),
         ],
-        in_specs=[VMEM, HBM],
-        out_specs=[VMEM] * 3,
-        scratch_shapes=[pltpu.SemaphoreType.DMA((2,))],
+        in_specs=[HBM, HBM],
+        out_specs=[VMEM, HBM, HBM],
+        scratch_shapes=[pltpu.VMEM(qkv.shape, BF), pltpu.SemaphoreType.DMA((5,))],
         compiler_params=params(56),
     )(qkv, w_merge)
     clips = [[c * peers + i for i in range(peers)] for c in range(CLIPS)]
@@ -524,14 +533,15 @@
     partial = pl.pallas_call(
         merge_kernel,
         out_shape=jax.ShapeDtypeStruct((planes, tokens, message), BF),
-        in_specs=[VMEM] * 4 + [pl.BlockSpec(memory_space=pl.ANY)] * 8,
+        in_specs=[VMEM, HBM, VMEM, VMEM] + [pl.BlockSpec(memory_space=pl.ANY)] * 8,
         out_specs=VMEM,
         scratch_shapes=[
             pltpu.VMEM((vit_width, rows), BF),
             pltpu.VMEM((vit_width, out_width), BF),
-            pltpu.SemaphoreType.DMA((8,)),
+            pltpu.VMEM((vit_width, vit_width), BF),
+            pltpu.SemaphoreType.DMA((9,)),
         ],
-        compiler_params=params(20),
+        compiler_params=params(50),
     )(
         returned,
         w_out,

time: 133 us -> 156 us (1.17)
  Pallas kernels: 28.1 us -> 54.3 us
  local copies, waits for them, and re-layouts: 4.73 us -> 0.59 us
    pallas_call x1, Pallas kernels: 3.66 us -> 29.9 us  [local(): pl.pallas_call(pack_kernel, out_shape=[jax.ShapeDtypeStruct((peers, 3 * p...]
    unnamed x22 -> x12, local copies, waits for them, and re-layouts: 4.51 us -> 0.38 us
  transfers between devices with their start and end apart: 35 -> 35, of which waited for: 16 -> 16; matrix products, arithmetic and copies ran while one was open for 1% -> 1% of each run, Pallas kernels for 15% -> 13%
where the time goes in v8:
time: 156 us
  Pallas kernels  54.3 us (35%)
  waiting for transfers between devices  45.8 us (29%)
  starting transfers between devices  34.9 us (22%)
  blocking collectives  18.7 us (12%)
    ppermute x33, waiting for transfers between devices, crossed(): return lax.ppermute(value, 'wide', pairs)  38.7 us
    pallas_call x1, Pallas kernels, local(): pl.pallas_call(pack_kernel, out_shape=[jax.ShapeDtypeStruct((peers, 3 * p...  29.9 us
    ppermute x33, starting transfers between devices, crossed(): return lax.ppermute(value, 'wide', pairs)  29.2 us
    all_to_all x1, blocking collectives, local(): lax.all_to_all(packed, 'wide', split_axis=0, concat_axis=0, tiled=True, a...  18.7 us
    pallas_call x2, Pallas kernels, experts_of(): pl.pallas_call(lambda *refs: expert_kernel(*refs, experts=experts, cuts=c...  13.3 us
    pallas_call x1, Pallas kernels, local(): pl.pallas_call(attend_kernel, out_shape=jax.ShapeDtypeStruct((devices, di...  6.89 us
    ppermute x1, waiting for transfers between devices, local(): theirs_y = lax.ppermute(mine_y, 'grp', [(0, 1), (1, 0)])  6.83 us
    all_to_all x1, starting transfers between devices, local(): lax.all_to_all(attended, 'wide', split_axis=0, concat_axis=0, tiled=True)  4.22 us
  transfers between devices with their start and end apart: 35, of which 16 were waited for; matrix products, arithmetic and copies ran while one was open for 1% of the time, Pallas kernels for 13%

profile of v8, /device:TPU:0, one launch (start us, length us, event | category | flops | bytes accessed | tf_op | source)
XLA Modules:
  0.0 155.9 jit_solution(15788304767812641108)
XLA Ops:
  0.0 29.9 %shard_map.109 = (bf16[8,432,128]{2,1,0:T(8,128)(2,1)}, bf16[160,2048]{1,0:T(8,128)(2,1)}, bf16[64,2048]{1,0:T(8,128)(2,1)}) custom-call(bf16[128,3456]{1,0:T(8,128)(2,1)} %qkv_hbm.1, bf16[288,2048]{1,0:T(8,128)(2,1)} %refs_0_.1), custom_call_target="tpu_custom_call" | custom-call | tf_op jit(solution)/shard_map/pallas_call | solution.py:497
  29.9 18.7 %all_to_all.10.x_ref = bf16[8,432,128]{2,1,0:T(8,128)(2,1)S(1)} all-to-all(bf16[8,432,128]{2,1,0:T(8,128)(2,1)} %get-tuple-element.34), channel_id=1, replica_groups={{0,1,2,3,4,5,6,7},{8,9,10,11,12,13,14,15},{16,17,18,19,20,21,22,23},{24..., dimensions={0} | all-to-all | bytes 1769472 | tf_op jit(solution)/shard_map/all_to_all | solution.py:510
  50.7 6.9 %shard_map.110 = bf16[16,72,128]{2,1,0:T(8,128)(2,1)} custom-call(bf16[8,432,128]{2,1,0:T(8,128)(2,1)S(1)} %all_to_all.10.x_ref, s32[2,2]{1,0:T(2,128)S(1)} %copy-done), custom_call_target="tpu_custom_call" | custom-call | flops 4294967296 | bytes 4194304 | tf_op jit(solution)/shard_map/pallas_call | solution.py:516
  58.1 4.2 %all-to-all-start.1 = ((bf16[16,72,128]{2,1,0:T(8,128)(2,1)}), bf16[16,72,128]{2,1,0:T(8,128)(2,1)S(1)}, u32[]{:S(2)}, u32[]{:S(2)}) async-start(bf16[16,72,128]{2,1,0:T(8,128)(2,1)} %shard_map.110), calls=%async_computation.1 | async-start | bytes 589824 | tf_op jit(solution)/shard_map/all_to_all | solution.py:528
  62.8 1.5 collective-permute-start.2
  64.2 6.8 %collective-permute-done.2.refs_4_ = bf16[64,2048]{1,0:T(8,128)(2,1)S(1)} collective-permute-done((bf16[64,2048]{1,0:T(8,128)(2,1)S(1)}, bf16[64,2048]{1,0:T(8,128)(2,1)S(1)}, u32[]{:S(2)}, u32[]{:S(2)}) %collective-permute-start.2) | collective-permute-done | bytes 262176 | tf_op jit(solution)/shard_map/ppermute | solution.py:526
  71.1 2.5 %collective-permute-done.1.refs_2_ = bf16[160,2048]{1,0:T(8,128)(2,1)S(1)} collective-permute-done((bf16[160,2048]{1,0:T(8,128)(2,1)}, bf16[160,2048]{1,0:T(8,128)(2,1)S(1)}, u32[]{:S(2)}, u32[]{:S(2)}) %collective-permute-start.1) | collective-permute-done | bytes 655392 | tf_op jit(solution)/shard_map/ppermute | solution.py:466
  74.8 1.4 collective-permute-done.5.refs_6_
  76.6 3.7 %shard_map.111 = bf16[4,32,2304]{2,1,0:T(8,128)(2,1)S(1)} custom-call(bf16[16,72,128]{2,1,0:T(8,128)(2,1)S(1)} %all-to-all-done.1.x_ref, bf16[1152,1152]{1,0:T(8,128)(2,1)} %w_out_hbm.1, f32[1,4608]{1,0:T(1,128)S(1)} %reshape.8.gain_ref, f32[1,4608]{1,0:T(1,128)S(1)} %reshape.9.bias_ref, bf16[288,2048]{1,0:T(8,128)(2,1)} %refs_0_.1, ...), custom_call_target="tpu_custom_call" | custom-call | tf_op jit(solution)/shard_map/pallas_call | solution.py:533
  80.3 2.7 %collective-permute-start.7 = (bf16[32,2304]{1,0:T(8,128)(2,1)S(1)}, bf16[32,2304]{1,0:T(8,128)(2,1)S(1)}, u32[]{:S(2)}, u32[]{:S(2)}) collective-permute-start(bf16[32,2304]{1,0:T(8,128)(2,1)S(1)} %get-tuple-element.65), channel_id=1, source_target_pairs={{0,8},{1,9},{2,10},{3,11},{4,12},{5,13},{6,14},{7,15},{8,0},{9,1},... | collective-permute-start | bytes 442376 | tf_op jit(solution)/shard_map/ppermute | solution.py:466
  84.3 9.5 %collective-permute-done.7.refs_1_ = bf16[32,2304]{1,0:T(8,128)(2,1)S(1)} collective-permute-done((bf16[32,2304]{1,0:T(8,128)(2,1)S(1)}, bf16[32,2304]{1,0:T(8,128)(2,1)S(1)}, u32[]{:S(2)}, u32[]{:S(2)}) %collective-permute-start.7) | collective-permute-done | bytes 147488 | tf_op jit(solution)/shard_map/ppermute | solution.py:466
  95.5 3.8 %collective-permute-start.10 = (bf16[32,2176]{1,0:T(8,128)(2,1)S(1)}, bf16[32,2176]{1,0:T(8,128)(2,1)S(1)}, u32[]{:S(2)}, u32[]{:S(2)}) collective-permute-start(bf16[32,2176]{1,0:T(8,128)(2,1)S(1)} %shard_map.112.refs_0_), channel_id=1, source_target_pairs={{0,8},{1,9},{2,10},{3,11},{4,12},{5,13},{6,14},{7,15},{8,0},{9,1},... | collective-permute-start | bytes 417800 | tf_op jit(solution)/shard_map/ppermute | solution.py:466
  101.5 8.3 %collective-permute-done.10.refs_1_ = bf16[32,2176]{1,0:T(8,128)(2,1)S(1)} collective-permute-done((bf16[32,2176]{1,0:T(8,128)(2,1)S(1)}, bf16[32,2176]{1,0:T(8,128)(2,1)S(1)}, u32[]{:S(2)}, u32[]{:S(2)}) %collective-permute-start.10) | collective-permute-done | bytes 139296 | tf_op jit(solution)/shard_map/ppermute | solution.py:466
  112.9 1.2 collective-permute-start.16
  114.1 6.7 %shard_map.113 = (bf16[4,32,2048]{2,1,0:T(8,128)(2,1)S(1)}, bf16[4,32,2048]{2,1,0:T(8,128)(2,1)S(1)}) custom-call(bf16[32,2176]{1,0:T(8,128)(2,1)S(1)} %shard_map.112.refs_0_, bf16[32,2176]{1,0:T(8,128)(2,1)S(1)} %collective-permute-done.10.refs_1_, bf16[32,2176]{1,0:T(8,128)(2,1)S(1)} %collective-permute-done.11.refs_2_, ...), custom_call_target="tpu_custom_call" | custom-call | flops 4294967296 | bytes 16777216 | tf_op jit(solution)/shard_map/pallas_call | solution.py:580
  120.8 1.7 %collective-permute-done.16.refs_3_ = bf16[32,2176]{1,0:T(8,128)(2,1)S(1)} collective-permute-done((bf16[32,2176]{1,0:T(8,128)(2,1)S(1)}, bf16[32,2176]{1,0:T(8,128)(2,1)S(1)}, u32[]{:S(2)}, u32[]{:S(2)}) %collective-permute-start.16) | collective-permute-done | bytes 139296 | tf_op jit(solution)/shard_map/ppermute | solution.py:466
  124.5 2.2 %collective-permute-start.27 = (bf16[32,2048]{1,0:T(8,128)(2,1)S(1)}, bf16[32,2048]{1,0:T(8,128)(2,1)S(1)}, u32[]{:S(2)}, u32[]{:S(2)}) collective-permute-start(bf16[32,2048]{1,0:T(8,128)(2,1)S(1)} %get-tuple-element.71), channel_id=1, source_target_pairs={{0,8},{1,9},{2,10},{3,11},{4,12},{5,13},{6,14},{7,15},{8,0},{9,1},... | collective-permute-start | bytes 393224 | tf_op jit(solution)/shard_map/ppermute | solution.py:466
  126.8 2.3 %collective-permute-start.28 = (bf16[32,2048]{1,0:T(8,128)(2,1)S(1)}, bf16[32,2048]{1,0:T(8,128)(2,1)S(1)}, u32[]{:S(2)}, u32[]{:S(2)}) collective-permute-start(bf16[32,2048]{1,0:T(8,128)(2,1)S(1)} %get-tuple-element.73), channel_id=1, source_target_pairs={{0,12},{1,13},{2,14},{3,15},{4,8},{5,9},{6,10},{7,11},{8,4},{9,5},... | collective-permute-start | bytes 393224 | tf_op jit(solution)/shard_map/ppermute | solution.py:466
  129.1 6.7 %shard_map.114 = (bf16[4,32,2048]{2,1,0:T(8,128)(2,1)S(1)}, bf16[4,32,2048]{2,1,0:T(8,128)(2,1)S(1)}) custom-call(bf16[32,2176]{1,0:T(8,128)(2,1)S(1)} %collective-permute-done.13.refs_0_, bf16[32,2176]{1,0:T(8,128)(2,1)S(1)} %collective-permute-done.14.refs_1_, bf16[32,2176]{1,0:T(8,128)(2,1)S(1)} %collective-permute-done.15.refs_2_, ...), custom_call_target="tpu_custom_call" | custom-call | flops 4294967296 | bytes 16777216 | tf_op jit(solution)/shard_map/pallas_call | solution.py:580
  135.9 1.6 %collective-permute-done.27 = bf16[32,2048]{1,0:T(8,128)(2,1)S(1)} collective-permute-done((bf16[32,2048]{1,0:T(8,128)(2,1)S(1)}, bf16[32,2048]{1,0:T(8,128)(2,1)S(1)}, u32[]{:S(2)}, u32[]{:S(2)}) %collective-permute-start.27) | collective-permute-done | bytes 131104 | tf_op jit(solution)/shard_map/ppermute | solution.py:466
  138.3 3.1 %collective-permute-start.30 = (bf16[32,2048]{1,0:T(8,128)(2,1)S(1)}, bf16[32,2048]{1,0:T(8,128)(2,1)S(1)}, u32[]{:S(2)}, u32[]{:S(2)}) collective-permute-start(bf16[32,2048]{1,0:T(8,128)(2,1)S(1)} %get-tuple-element.67), channel_id=1, source_target_pairs={{0,10},{1,11},{2,8},{3,9},{4,14},{5,15},{6,12},{7,13},{8,2},{9,3},... | collective-permute-start | bytes 393224 | tf_op jit(solution)/shard_map/ppermute | solution.py:466
  141.4 2.3 %collective-permute-start.31 = (bf16[32,2048]{1,0:T(8,128)(2,1)S(1)}, bf16[32,2048]{1,0:T(8,128)(2,1)S(1)}, u32[]{:S(2)}, u32[]{:S(2)}) collective-permute-start(bf16[32,2048]{1,0:T(8,128)(2,1)S(1)} %get-tuple-element.70), channel_id=1, source_target_pairs={{0,14},{1,15},{2,12},{3,13},{4,10},{5,11},{6,8},{7,9},{8,6},{9,7},... | collective-permute-start | bytes 393224 | tf_op jit(solution)/shard_map/ppermute | solution.py:466
  144.9 7.4 %collective-permute-done.30 = bf16[32,2048]{1,0:T(8,128)(2,1)S(1)} collective-permute-done((bf16[32,2048]{1,0:T(8,128)(2,1)S(1)}, bf16[32,2048]{1,0:T(8,128)(2,1)S(1)}, u32[]{:S(2)}, u32[]{:S(2)}) %collective-permute-start.30) | collective-permute-done | bytes 131104 | tf_op jit(solution)/shard_map/ppermute | solution.py:466
  153.1 2.1 %collective-permute-done.33 = bf16[32,2048]{1,0:T(8,128)(2,1)S(1)} collective-permute-done((bf16[32,2048]{1,0:T(8,128)(2,1)S(1)}, bf16[32,2048]{1,0:T(8,128)(2,1)S(1)}, u32[]{:S(2)}, u32[]{:S(2)}) %collective-permute-start.33) | collective-permute-done | bytes 131104 | tf_op jit(solution)/shard_map/ppermute | solution.py:466
  (77 shorter events, 18.5 us)
Async XLA Ops:
  48.6 9.4 %collective-permute-start = (bf16[64,2048]{1,0:T(8,128)(2,1)}, bf16[64,2048]{1,0:T(8,128)(2,1)S(1)}, u32[]{:S(2)}, u32[]{:S(2)}) collective-permute-start(bf16[64,2048]{1,0:T(8,128)(2,1)} %get-tuple-element.38), channel_id=1, source_target_pairs={{0,2},{1,3},{2,0},{3,1},{4,6},{5,7},{6,4},{7,5},{8,10},{9,11},{10,... | collective-permute-start | bytes 786440 | tf_op jit(solution)/shard_map/ppermute | solution.py:466
  49.5 24.1 %collective-permute-start.1 = (bf16[160,2048]{1,0:T(8,128)(2,1)}, bf16[160,2048]{1,0:T(8,128)(2,1)S(1)}, u32[]{:S(2)}, u32[]{:S(2)}) collective-permute-start(bf16[160,2048]{1,0:T(8,128)(2,1)} %get-tuple-element.40), channel_id=1, source_target_pairs={{0,2},{1,3},{2,0},{3,1},{4,6},{5,7},{6,4},{7,5},{8,10},{9,11},{10,... | collective-permute-start | bytes 1966088 | tf_op jit(solution)/shard_map/ppermute | solution.py:466
  58.1 15.7 %all-to-all-start.1 = ((bf16[16,72,128]{2,1,0:T(8,128)(2,1)}), bf16[16,72,128]{2,1,0:T(8,128)(2,1)S(1)}, u32[]{:S(2)}, u32[]{:S(2)}) async-start(bf16[16,72,128]{2,1,0:T(8,128)(2,1)} %shard_map.110), calls=%async_computation.1 | async-start | bytes 589824 | tf_op jit(solution)/shard_map/all_to_all | solution.py:528
  62.3 14.3 %collective-permute-start.3 = (bf16[288,2048]{1,0:T(8,128)(2,1)}, bf16[288,2048]{1,0:T(8,128)(2,1)}, u32[]{:S(2)}, u32[]{:S(2)}) collective-permute-start(bf16[288,2048]{1,0:T(8,128)(2,1)} %refs_0_.1), channel_id=1, source_target_pairs={{0,1},{1,0},{2,3},{3,2},{4,5},{5,4},{6,7},{7,6},{8,9},{9,8},{10,11... | collective-permute-start | bytes 3538952 | tf_op jit(solution)/shard_map/ppermute | solution.py:466
  62.8 8.3 %collective-permute-start.2 = (bf16[64,2048]{1,0:T(8,128)(2,1)S(1)}, bf16[64,2048]{1,0:T(8,128)(2,1)S(1)}, u32[]{:S(2)}, u32[]{:S(2)}) collective-permute-start(bf16[64,2048]{1,0:T(8,128)(2,1)S(1)} %collective-permute-done.refs_3_), channel_id=1, source_target_pairs={{0,16},{16,0},{1,17},{17,1},{2,18},{18,2},{3,19},{19,3},{4,20},{20... | collective-permute-start | bytes 786440 | tf_op jit(solution)/shard_map/ppermute | solution.py:526
  80.3 13.5 %collective-permute-start.7 = (bf16[32,2304]{1,0:T(8,128)(2,1)S(1)}, bf16[32,2304]{1,0:T(8,128)(2,1)S(1)}, u32[]{:S(2)}, u32[]{:S(2)}) collective-permute-start(bf16[32,2304]{1,0:T(8,128)(2,1)S(1)} %get-tuple-element.65), channel_id=1, source_target_pairs={{0,8},{1,9},{2,10},{3,11},{4,12},{5,13},{6,14},{7,15},{8,0},{9,1},... | collective-permute-start | bytes 442376 | tf_op jit(solution)/shard_map/ppermute | solution.py:466
  83.0 10.9 %collective-permute-start.8 = (bf16[32,2304]{1,0:T(8,128)(2,1)S(1)}, bf16[32,2304]{1,0:T(8,128)(2,1)S(1)}, u32[]{:S(2)}, u32[]{:S(2)}) collective-permute-start(bf16[32,2304]{1,0:T(8,128)(2,1)S(1)} %get-tuple-element.64), channel_id=1, source_target_pairs={{0,12},{1,13},{2,14},{3,15},{4,8},{5,9},{6,10},{7,11},{8,4},{9,5},... | collective-permute-start | bytes 442376 | tf_op jit(solution)/shard_map/ppermute | solution.py:466
  83.5 11.4 %collective-permute-start.9 = (bf16[32,2304]{1,0:T(8,128)(2,1)S(1)}, bf16[32,2304]{1,0:T(8,128)(2,1)S(1)}, u32[]{:S(2)}, u32[]{:S(2)}) collective-permute-start(bf16[32,2304]{1,0:T(8,128)(2,1)S(1)} %get-tuple-element.63), channel_id=1, source_target_pairs={{0,4},{1,5},{2,6},{3,7},{4,0},{5,1},{6,2},{7,3},{8,12},{9,13},{10,... | collective-permute-start | bytes 442376 | tf_op jit(solution)/shard_map/ppermute | solution.py:466
  95.5 14.3 %collective-permute-start.10 = (bf16[32,2176]{1,0:T(8,128)(2,1)S(1)}, bf16[32,2176]{1,0:T(8,128)(2,1)S(1)}, u32[]{:S(2)}, u32[]{:S(2)}) collective-permute-start(bf16[32,2176]{1,0:T(8,128)(2,1)S(1)} %shard_map.112.refs_0_), channel_id=1, source_target_pairs={{0,8},{1,9},{2,10},{3,11},{4,12},{5,13},{6,14},{7,15},{8,0},{9,1},... | collective-permute-start | bytes 417800 | tf_op jit(solution)/shard_map/ppermute | solution.py:466
  99.2 10.5 %collective-permute-start.11 = (bf16[32,2176]{1,0:T(8,128)(2,1)S(1)}, bf16[32,2176]{1,0:T(8,128)(2,1)S(1)}, u32[]{:S(2)}, u32[]{:S(2)}) collective-permute-start(bf16[32,2176]{1,0:T(8,128)(2,1)S(1)} %shard_map.112.refs_0_), channel_id=1, source_target_pairs={{0,12},{1,13},{2,14},{3,15},{4,8},{5,9},{6,10},{7,11},{8,4},{9,5},... | collective-permute-start | bytes 417800 | tf_op jit(solution)/shard_map/ppermute | solution.py:466
  100.3 9.5 %collective-permute-start.12 = (bf16[32,2176]{1,0:T(8,128)(2,1)S(1)}, bf16[32,2176]{1,0:T(8,128)(2,1)S(1)}, u32[]{:S(2)}, u32[]{:S(2)}) collective-permute-start(bf16[32,2176]{1,0:T(8,128)(2,1)S(1)} %shard_map.112.refs_0_), channel_id=1, source_target_pairs={{0,4},{1,5},{2,6},{3,7},{4,0},{5,1},{6,2},{7,3},{8,12},{9,13},{10,... | collective-permute-start | bytes 417800 | tf_op jit(solution)/shard_map/ppermute | solution.py:466
  100.3 9.5 %collective-permute-start.13 = (bf16[32,2176]{1,0:T(8,128)(2,1)S(1)}, bf16[32,2176]{1,0:T(8,128)(2,1)S(1)}, u32[]{:S(2)}, u32[]{:S(2)}) collective-permute-start(bf16[32,2176]{1,0:T(8,128)(2,1)S(1)} %shard_map.112.refs_0_), channel_id=1, source_target_pairs={{0,2},{1,3},{2,0},{3,1},{4,6},{5,7},{6,4},{7,5},{8,10},{9,11},{10,... | collective-permute-start | bytes 417800 | tf_op jit(solution)/shard_map/ppermute | solution.py:466
  110.8 9.9 %collective-permute-start.14 = (bf16[32,2176]{1,0:T(8,128)(2,1)S(1)}, bf16[32,2176]{1,0:T(8,128)(2,1)S(1)}, u32[]{:S(2)}, u32[]{:S(2)}) collective-permute-start(bf16[32,2176]{1,0:T(8,128)(2,1)S(1)} %collective-permute-done.10.refs_1_), channel_id=1, source_target_pairs={{0,2},{1,3},{2,0},{3,1},{4,6},{5,7},{6,4},{7,5},{8,10},{9,11},{10,... | collective-permute-start | bytes 417800 | tf_op jit(solution)/shard_map/ppermute | solution.py:466
  112.0 8.7 %collective-permute-start.15 = (bf16[32,2176]{1,0:T(8,128)(2,1)S(1)}, bf16[32,2176]{1,0:T(8,128)(2,1)S(1)}, u32[]{:S(2)}, u32[]{:S(2)}) collective-permute-start(bf16[32,2176]{1,0:T(8,128)(2,1)S(1)} %collective-permute-done.11.refs_2_), channel_id=1, source_target_pairs={{0,2},{1,3},{2,0},{3,1},{4,6},{5,7},{6,4},{7,5},{8,10},{9,11},{10,... | collective-permute-start | bytes 417800 | tf_op jit(solution)/shard_map/ppermute | solution.py:466
  112.9 9.6 %collective-permute-start.16 = (bf16[32,2176]{1,0:T(8,128)(2,1)S(1)}, bf16[32,2176]{1,0:T(8,128)(2,1)S(1)}, u32[]{:S(2)}, u32[]{:S(2)}) collective-permute-start(bf16[32,2176]{1,0:T(8,128)(2,1)S(1)} %collective-permute-done.12.refs_3_), channel_id=1, source_target_pairs={{0,2},{1,3},{2,0},{3,1},{4,6},{5,7},{6,4},{7,5},{8,10},{9,11},{10,... | collective-permute-start | bytes 417800 | tf_op jit(solution)/shard_map/ppermute | solution.py:466
  123.0 6.1 %collective-permute-start.22 = (bf16[32,2176]{1,0:T(8,128)(2,1)S(1)}, bf16[32,2176]{1,0:T(8,128)(2,1)S(1)}, u32[]{:S(2)}, u32[]{:S(2)}) collective-permute-start(bf16[32,2176]{1,0:T(8,128)(2,1)S(1)} %collective-permute-done.14.refs_1_), channel_id=1, source_target_pairs={{0,1},{1,0},{2,3},{3,2},{4,5},{5,4},{6,7},{7,6},{8,9},{9,8},{10,11... | collective-permute-start | bytes 417800 | tf_op jit(solution)/shard_map/ppermute | solution.py:466
  123.0 6.1 %collective-permute-start.23 = (bf16[32,2176]{1,0:T(8,128)(2,1)S(1)}, bf16[32,2176]{1,0:T(8,128)(2,1)S(1)}, u32[]{:S(2)}, u32[]{:S(2)}) collective-permute-start(bf16[32,2176]{1,0:T(8,128)(2,1)S(1)} %collective-permute-done.15.refs_2_), channel_id=1, source_target_pairs={{0,1},{1,0},{2,3},{3,2},{4,5},{5,4},{6,7},{7,6},{8,9},{9,8},{10,11... | collective-permute-start | bytes 417800 | tf_op jit(solution)/shard_map/ppermute | solution.py:466
  124.5 13.0 %collective-permute-start.27 = (bf16[32,2048]{1,0:T(8,128)(2,1)S(1)}, bf16[32,2048]{1,0:T(8,128)(2,1)S(1)}, u32[]{:S(2)}, u32[]{:S(2)}) collective-permute-start(bf16[32,2048]{1,0:T(8,128)(2,1)S(1)} %get-tuple-element.71), channel_id=1, source_target_pairs={{0,8},{1,9},{2,10},{3,11},{4,12},{5,13},{6,14},{7,15},{8,0},{9,1},... | collective-permute-start | bytes 393224 | tf_op jit(solution)/shard_map/ppermute | solution.py:466
  126.8 10.7 %collective-permute-start.28 = (bf16[32,2048]{1,0:T(8,128)(2,1)S(1)}, bf16[32,2048]{1,0:T(8,128)(2,1)S(1)}, u32[]{:S(2)}, u32[]{:S(2)}) collective-permute-start(bf16[32,2048]{1,0:T(8,128)(2,1)S(1)} %get-tuple-element.73), channel_id=1, source_target_pairs={{0,12},{1,13},{2,14},{3,15},{4,8},{5,9},{6,10},{7,11},{8,4},{9,5},... | collective-permute-start | bytes 393224 | tf_op jit(solution)/shard_map/ppermute | solution.py:466
  129.1 8.9 %collective-permute-start.29 = (bf16[32,2048]{1,0:T(8,128)(2,1)S(1)}, bf16[32,2048]{1,0:T(8,128)(2,1)S(1)}, u32[]{:S(2)}, u32[]{:S(2)}) collective-permute-start(bf16[32,2048]{1,0:T(8,128)(2,1)S(1)} %get-tuple-element.72), channel_id=1, source_target_pairs={{0,4},{1,5},{2,6},{3,7},{4,0},{5,1},{6,2},{7,3},{8,12},{9,13},{10,... | collective-permute-start | bytes 393224 | tf_op jit(solution)/shard_map/ppermute | solution.py:466
  138.3 14.0 %collective-permute-start.30 = (bf16[32,2048]{1,0:T(8,128)(2,1)S(1)}, bf16[32,2048]{1,0:T(8,128)(2,1)S(1)}, u32[]{:S(2)}, u32[]{:S(2)}) collective-permute-start(bf16[32,2048]{1,0:T(8,128)(2,1)S(1)} %get-tuple-element.67), channel_id=1, source_target_pairs={{0,10},{1,11},{2,8},{3,9},{4,14},{5,15},{6,12},{7,13},{8,2},{9,3},... | collective-permute-start | bytes 393224 | tf_op jit(solution)/shard_map/ppermute | solution.py:466
  141.4 10.9 %collective-permute-start.31 = (bf16[32,2048]{1,0:T(8,128)(2,1)S(1)}, bf16[32,2048]{1,0:T(8,128)(2,1)S(1)}, u32[]{:S(2)}, u32[]{:S(2)}) collective-permute-start(bf16[32,2048]{1,0:T(8,128)(2,1)S(1)} %get-tuple-element.70), channel_id=1, source_target_pairs={{0,14},{1,15},{2,12},{3,13},{4,10},{5,11},{6,8},{7,9},{8,6},{9,7},... | collective-permute-start | bytes 393224 | tf_op jit(solution)/shard_map/ppermute | solution.py:466
  143.7 9.4 %collective-permute-start.32 = (bf16[32,2048]{1,0:T(8,128)(2,1)S(1)}, bf16[32,2048]{1,0:T(8,128)(2,1)S(1)}, u32[]{:S(2)}, u32[]{:S(2)}) collective-permute-start(bf16[32,2048]{1,0:T(8,128)(2,1)S(1)} %get-tuple-element.69), channel_id=1, source_target_pairs={{0,6},{1,7},{2,4},{3,5},{4,2},{5,3},{6,0},{7,1},{8,14},{9,15},{10,... | collective-permute-start | bytes 393224 | tf_op jit(solution)/shard_map/ppermute | solution.py:466
  143.7 11.5 %collective-permute-start.33 = (bf16[32,2048]{1,0:T(8,128)(2,1)S(1)}, bf16[32,2048]{1,0:T(8,128)(2,1)S(1)}, u32[]{:S(2)}, u32[]{:S(2)}) collective-permute-start(bf16[32,2048]{1,0:T(8,128)(2,1)S(1)} %get-tuple-element.68), channel_id=1, source_target_pairs={{0,2},{1,3},{2,0},{3,1},{4,6},{5,7},{6,4},{7,5},{8,10},{9,11},{10,... | collective-permute-start | bytes 393224 | tf_op jit(solution)/shard_map/ppermute | solution.py:466
  (16 other events, 171.8 us)

commit v9 on v8

--- a/solution.py
+++ b/solution.py
@@ -240,21 +240,7 @@
     return out
 
 
-def pack_kernel(qkv_hbm, merge_ref, out_ref, common_ref, share_ref, qkv_ref, sems):
-    common, share = common_ref.shape[0], share_ref.shape[0]
-    spot = pl.multiple_of(common + share * lax.axis_index("grp"), 16)
-    third = qkv_hbm.shape[1] // 3
-    loads = []
-    for kind in range(3):
-        cut = slice(kind * third, (kind + 1) * third)
-        loads.append(pltpu.make_async_copy(qkv_hbm.at[:, cut], qkv_ref.at[:, cut], sems.at[2 + kind]))
-        loads[-1].start()
-    copies = [
-        pltpu.make_async_copy(merge_ref.at[pl.ds(spot, share), :], share_ref, sems.at[0]),
-        pltpu.make_async_copy(merge_ref.at[pl.ds(0, common), :], common_ref, sems.at[1]),
-    ]
-    for copy in copies:
-        copy.start()
+def pack_kernel(qkv_ref, out_ref):
     rows, width = qkv_ref.shape
     tokens = rows // 4
     peers, parts, _ = out_ref.shape
@@ -262,8 +248,8 @@
     place = lax.broadcasted_iota(jnp.int32, (rows, rows), 1)
     order = jnp.where(source == 4 * (place % tokens) + place // tokens, 1.0, 0.0).astype(BF)
     part = parts // 3
+    third = width // 3
     for kind in range(3):
-        loads[kind].wait()
         turned = lax.dot_general(
             qkv_ref[:, kind * third : (kind + 1) * third],
             order,
@@ -272,6 +258,17 @@
         ).astype(BF)
         for peer in range(peers):
             out_ref[peer, kind * part : (kind + 1) * part, :] = turned[peer * part : (peer + 1) * part]
+
+
+def share_kernel(merge_ref, common_ref, share_ref, sems):
+    common, share = common_ref.shape[0], share_ref.shape[0]
+    spot = pl.multiple_of(common + share * lax.axis_index("grp"), 16)
+    copies = [
+        pltpu.make_async_copy(merge_ref.at[pl.ds(spot, share), :], share_ref, sems.at[0]),
+        pltpu.make_async_copy(merge_ref.at[pl.ds(0, common), :], common_ref, sems.at[1]),
+    ]
+    for copy in copies:
+        copy.start()
     for copy in copies:
         copy.wait()
 
@@ -494,18 +491,25 @@
     dim = vit_width // HEADS
     depth = w_merge.shape[0]
     share = depth // 64 * 16
-    packed, common, shared = pl.pallas_call(
+    packed = pl.pallas_call(
         pack_kernel,
+        out_shape=jax.ShapeDtypeStruct((peers, 3 * part, rows), BF),
+        in_specs=[VMEM],
+        out_specs=VMEM,
+        compiler_params=params(8),
+    )(qkv)
+    common, shared = pl.pallas_call(
+        share_kernel,
         out_shape=[
-            jax.ShapeDtypeStruct((peers, 3 * part, rows), BF),
             jax.ShapeDtypeStruct((depth - 2 * share, out_width), BF),
             jax.ShapeDtypeStruct((share, out_width), BF),
         ],
-        in_specs=[HBM, HBM],
-        out_specs=[VMEM, HBM, HBM],
-        scratch_shapes=[pltpu.VMEM(qkv.shape, BF), pltpu.SemaphoreType.DMA((5,))],
-        compiler_params=params(56),
-    )(qkv, w_merge)
+        in_specs=[HBM],
+        out_specs=[VMEM] * 2,
+        scratch_shapes=[pltpu.SemaphoreType.DMA((2,))],
+        compiler_params=params(8),
+        cost_estimate=cost(2**31, 2**24),
+    )(w_merge)
     clips = [[c * peers + i for i in range(peers)] for c in range(CLIPS)]
     gathered = lax.all_to_all(
         packed, "wide", split_axis=0, concat_axis=0, tiled=True, axis_index_groups=clips

time: 156 us -> 128 us (0.82)
  Pallas kernels: 54.3 us -> 26.1 us
  blocking collectives: 18.7 us -> 0 us
  waiting for transfers between devices: 45.8 us -> 55.1 us
  starting transfers between devices: 34.9 us -> 41.4 us
  local copies, waits for them, and re-layouts: 0.59 us -> 3.42 us
    pallas_call x1 -> x2, Pallas kernels: 29.9 us -> 1.64 us  [the longest x1 1.38 us: local(): pl.pallas_call(pack_kernel, out_shape=jax.ShapeDtypeStruct((peers, 3 * pa...]
    all_to_all x1 -> x0, blocking collectives: 18.7 us -> none  [local(): lax.all_to_all(packed, 'wide', split_axis=0, concat_axis=0, tiled=True, a...]
    all_to_all x0 -> x1, waiting for transfers between devices: none -> 11.6 us  [local(): lax.all_to_all(packed, 'wide', split_axis=0, concat_axis=0, tiled=True, a...]
    all_to_all x0 -> x1, starting transfers between devices: none -> 5.25 us  [local(): lax.all_to_all(packed, 'wide', split_axis=0, concat_axis=0, tiled=True, a...]
    unnamed x12 -> x20, local copies, waits for them, and re-layouts: 0.38 us -> 3.2 us
    ppermute x33, waiting for transfers between devices: 38.7 us -> 36.3 us  [crossed(): return lax.ppermute(value, 'wide', pairs)]
  transfers between devices with their start and end apart: 35 -> 36, of which waited for: 16 -> 17; matrix products, arithmetic and copies ran while one was open for 1% -> 1% of each run, Pallas kernels for 13% -> 16%
where the time goes in v9:
time: 128 us
  waiting for transfers between devices  55.1 us (43%)
  starting transfers between devices  41.4 us (32%)
  Pallas kernels  26.1 us (20%)
  local copies, waits for them, and re-layouts  3.42 us (3%)
  other arithmetic  1.38 us (1%)
    ppermute x33, waiting for transfers between devices, crossed(): return lax.ppermute(value, 'wide', pairs)  36.3 us
    ppermute x33, starting transfers between devices, crossed(): return lax.ppermute(value, 'wide', pairs)  29.8 us
    pallas_call x2, Pallas kernels, experts_of(): pl.pallas_call(lambda *refs: expert_kernel(*refs, experts=experts, cuts=c...  13.3 us
    all_to_all x1, waiting for transfers between devices, local(): lax.all_to_all(packed, 'wide', split_axis=0, concat_axis=0, tiled=True, a...  11.6 us
    pallas_call x1, Pallas kernels, local(): pl.pallas_call(attend_kernel, out_shape=jax.ShapeDtypeStruct((devices, di...  6.88 us
    ppermute x1, waiting for transfers between devices, local(): theirs_y = lax.ppermute(mine_y, 'grp', [(0, 1), (1, 0)])  6.83 us
    all_to_all x1, starting transfers between devices, local(): lax.all_to_all(packed, 'wide', split_axis=0, concat_axis=0, tiled=True, a...  5.25 us
    all_to_all x1, starting transfers between devices, local(): lax.all_to_all(attended, 'wide', split_axis=0, concat_axis=0, tiled=True)  4.9 us
  transfers between devices with their start and end apart: 36, of which 17 were waited for; matrix products, arithmetic and copies ran while one was open for 1% of the time, Pallas kernels for 16%

profile of v9, /device:TPU:0, one launch (start us, length us, event | category | flops | bytes accessed | tf_op | source)
XLA Modules:
  0.0 127.7 jit_solution(3074717679201610881)
XLA Ops:
  2.6 5.3 %all-to-all-start = ((bf16[8,432,128]{2,1,0:T(8,128)(2,1)}), bf16[8,432,128]{2,1,0:T(8,128)(2,1)S(1)}, u32[]{:S(2)}, u32[]{:S(2)}) async-start(bf16[8,432,128]{2,1,0:T(8,128)(2,1)} %shard_map.109), calls=%async_computation | async-start | bytes 1769472 | tf_op jit(solution)/shard_map/all_to_all | solution.py:514
  9.0 11.6 %all-to-all-done.x_ref = bf16[8,432,128]{2,1,0:T(8,128)(2,1)S(1)} async-done(((bf16[8,432,128]{2,1,0:T(8,128)(2,1)}), bf16[8,432,128]{2,1,0:T(8,128)(2,1)S(1)}, u32[]{:S(2)}, u32[]{:S(2)}) %all-to-all-start) | async-done | bytes 884768 | tf_op jit(solution)/shard_map/all_to_all | solution.py:514
  20.6 1.5 %collective-permute-start = (bf16[64,2048]{1,0:T(8,128)(2,1)S(1)}, bf16[64,2048]{1,0:T(8,128)(2,1)S(1)}, u32[]{:S(2)}, u32[]{:S(2)}) collective-permute-start(bf16[64,2048]{1,0:T(8,128)(2,1)S(1)} %get-tuple-element.36), channel_id=1, source_target_pairs={{0,2},{1,3},{2,0},{3,1},{4,6},{5,7},{6,4},{7,5},{8,10},{9,11},{10,... | collective-permute-start | bytes 786440 | tf_op jit(solution)/shard_map/ppermute | solution.py:463
  22.6 6.9 %shard_map.111 = bf16[16,72,128]{2,1,0:T(8,128)(2,1)} custom-call(bf16[8,432,128]{2,1,0:T(8,128)(2,1)S(1)} %all-to-all-done.x_ref, s32[2,2]{1,0:T(2,128)S(1)} %copy-done.3), custom_call_target="tpu_custom_call" | custom-call | flops 4294967296 | bytes 4194304 | tf_op jit(solution)/shard_map/pallas_call | solution.py:520
  29.8 4.9 %all-to-all-start.1 = ((bf16[16,72,128]{2,1,0:T(8,128)(2,1)}), bf16[16,72,128]{2,1,0:T(8,128)(2,1)S(1)}, u32[]{:S(2)}, u32[]{:S(2)}) async-start(bf16[16,72,128]{2,1,0:T(8,128)(2,1)} %shard_map.111), calls=%async_computation.1 | async-start | bytes 589824 | tf_op jit(solution)/shard_map/all_to_all | solution.py:532
  35.2 1.5 %collective-permute-start.2 = (bf16[64,2048]{1,0:T(8,128)(2,1)S(1)}, bf16[64,2048]{1,0:T(8,128)(2,1)S(1)}, u32[]{:S(2)}, u32[]{:S(2)}) collective-permute-start(bf16[64,2048]{1,0:T(8,128)(2,1)S(1)} %collective-permute-done.refs_3_), channel_id=1, source_target_pairs={{0,16},{16,0},{1,17},{17,1},{2,18},{18,2},{3,19},{19,3},{4,20},{20... | collective-permute-start | bytes 786440 | tf_op jit(solution)/shard_map/ppermute | solution.py:530
  36.7 6.8 %collective-permute-done.2.refs_4_ = bf16[64,2048]{1,0:T(8,128)(2,1)S(1)} collective-permute-done((bf16[64,2048]{1,0:T(8,128)(2,1)S(1)}, bf16[64,2048]{1,0:T(8,128)(2,1)S(1)}, u32[]{:S(2)}, u32[]{:S(2)}) %collective-permute-start.2) | collective-permute-done | bytes 262176 | tf_op jit(solution)/shard_map/ppermute | solution.py:530
  43.5 1.5 %collective-permute-done.1.refs_2_ = bf16[160,2048]{1,0:T(8,128)(2,1)S(1)} collective-permute-done((bf16[160,2048]{1,0:T(8,128)(2,1)}, bf16[160,2048]{1,0:T(8,128)(2,1)S(1)}, u32[]{:S(2)}, u32[]{:S(2)}) %collective-permute-start.1) | collective-permute-done | bytes 655392 | tf_op jit(solution)/shard_map/ppermute | solution.py:463
  48.5 3.7 %shard_map.112 = bf16[4,32,2304]{2,1,0:T(8,128)(2,1)S(1)} custom-call(bf16[16,72,128]{2,1,0:T(8,128)(2,1)S(1)} %all-to-all-done.1.x_ref, bf16[1152,1152]{1,0:T(8,128)(2,1)} %w_out_hbm.1, f32[1,4608]{1,0:T(1,128)S(1)} %reshape.8.gain_ref, f32[1,4608]{1,0:T(1,128)S(1)} %reshape.9.bias_ref, bf16[288,2048]{1,0:T(8,128)(2,1)} %refs_0_.1, ...), custom_call_target="tpu_custom_call" | custom-call | tf_op jit(solution)/shard_map/pallas_call | solution.py:537
  52.2 2.6 %collective-permute-start.7 = (bf16[32,2304]{1,0:T(8,128)(2,1)S(1)}, bf16[32,2304]{1,0:T(8,128)(2,1)S(1)}, u32[]{:S(2)}, u32[]{:S(2)}) collective-permute-start(bf16[32,2304]{1,0:T(8,128)(2,1)S(1)} %get-tuple-element.63), channel_id=1, source_target_pairs={{0,8},{1,9},{2,10},{3,11},{4,12},{5,13},{6,14},{7,15},{8,0},{9,1},... | collective-permute-start | bytes 442376 | tf_op jit(solution)/shard_map/ppermute | solution.py:463
  56.2 9.4 %collective-permute-done.7.refs_1_ = bf16[32,2304]{1,0:T(8,128)(2,1)S(1)} collective-permute-done((bf16[32,2304]{1,0:T(8,128)(2,1)S(1)}, bf16[32,2304]{1,0:T(8,128)(2,1)S(1)}, u32[]{:S(2)}, u32[]{:S(2)}) %collective-permute-start.7) | collective-permute-done | bytes 147488 | tf_op jit(solution)/shard_map/ppermute | solution.py:463
  67.4 3.7 %collective-permute-start.10 = (bf16[32,2176]{1,0:T(8,128)(2,1)S(1)}, bf16[32,2176]{1,0:T(8,128)(2,1)S(1)}, u32[]{:S(2)}, u32[]{:S(2)}) collective-permute-start(bf16[32,2176]{1,0:T(8,128)(2,1)S(1)} %shard_map.113.refs_0_), channel_id=1, source_target_pairs={{0,8},{1,9},{2,10},{3,11},{4,12},{5,13},{6,14},{7,15},{8,0},{9,1},... | collective-permute-start | bytes 417800 | tf_op jit(solution)/shard_map/ppermute | solution.py:463
  72.1 1.5 %collective-permute-start.13 = (bf16[32,2176]{1,0:T(8,128)(2,1)S(1)}, bf16[32,2176]{1,0:T(8,128)(2,1)S(1)}, u32[]{:S(2)}, u32[]{:S(2)}) collective-permute-start(bf16[32,2176]{1,0:T(8,128)(2,1)S(1)} %shard_map.113.refs_0_), channel_id=1, source_target_pairs={{0,2},{1,3},{2,0},{3,1},{4,6},{5,7},{6,4},{7,5},{8,10},{9,11},{10,... | collective-permute-start | bytes 417800 | tf_op jit(solution)/shard_map/ppermute | solution.py:463
  73.6 8.0 %collective-permute-done.10.refs_1_ = bf16[32,2176]{1,0:T(8,128)(2,1)S(1)} collective-permute-done((bf16[32,2176]{1,0:T(8,128)(2,1)S(1)}, bf16[32,2176]{1,0:T(8,128)(2,1)S(1)}, u32[]{:S(2)}, u32[]{:S(2)}) %collective-permute-start.10) | collective-permute-done | bytes 139296 | tf_op jit(solution)/shard_map/ppermute | solution.py:463
  86.1 6.7 %shard_map.114 = (bf16[4,32,2048]{2,1,0:T(8,128)(2,1)S(1)}, bf16[4,32,2048]{2,1,0:T(8,128)(2,1)S(1)}) custom-call(bf16[32,2176]{1,0:T(8,128)(2,1)S(1)} %shard_map.113.refs_0_, bf16[32,2176]{1,0:T(8,128)(2,1)S(1)} %collective-permute-done.10.refs_1_, bf16[32,2176]{1,0:T(8,128)(2,1)S(1)} %collective-permute-done.11.refs_2_, ...), custom_call_target="tpu_custom_call" | custom-call | flops 4294967296 | bytes 16777216 | tf_op jit(solution)/shard_map/pallas_call | solution.py:584
  92.8 1.5 %collective-permute-done.16.refs_3_ = bf16[32,2176]{1,0:T(8,128)(2,1)S(1)} collective-permute-done((bf16[32,2176]{1,0:T(8,128)(2,1)S(1)}, bf16[32,2176]{1,0:T(8,128)(2,1)S(1)}, u32[]{:S(2)}, u32[]{:S(2)}) %collective-permute-start.16) | collective-permute-done | bytes 139296 | tf_op jit(solution)/shard_map/ppermute | solution.py:463
  96.4 2.3 %collective-permute-start.27 = (bf16[32,2048]{1,0:T(8,128)(2,1)S(1)}, bf16[32,2048]{1,0:T(8,128)(2,1)S(1)}, u32[]{:S(2)}, u32[]{:S(2)}) collective-permute-start(bf16[32,2048]{1,0:T(8,128)(2,1)S(1)} %get-tuple-element.69), channel_id=1, source_target_pairs={{0,8},{1,9},{2,10},{3,11},{4,12},{5,13},{6,14},{7,15},{8,0},{9,1},... | collective-permute-start | bytes 393224 | tf_op jit(solution)/shard_map/ppermute | solution.py:463
  98.7 2.1 %collective-permute-start.28 = (bf16[32,2048]{1,0:T(8,128)(2,1)S(1)}, bf16[32,2048]{1,0:T(8,128)(2,1)S(1)}, u32[]{:S(2)}, u32[]{:S(2)}) collective-permute-start(bf16[32,2048]{1,0:T(8,128)(2,1)S(1)} %get-tuple-element.71), channel_id=1, source_target_pairs={{0,12},{1,13},{2,14},{3,15},{4,8},{5,9},{6,10},{7,11},{8,4},{9,5},... | collective-permute-start | bytes 393224 | tf_op jit(solution)/shard_map/ppermute | solution.py:463
  100.9 6.7 %shard_map.115 = (bf16[4,32,2048]{2,1,0:T(8,128)(2,1)S(1)}, bf16[4,32,2048]{2,1,0:T(8,128)(2,1)S(1)}) custom-call(bf16[32,2176]{1,0:T(8,128)(2,1)S(1)} %collective-permute-done.13.refs_0_, bf16[32,2176]{1,0:T(8,128)(2,1)S(1)} %collective-permute-done.14.refs_1_, bf16[32,2176]{1,0:T(8,128)(2,1)S(1)} %collective-permute-done.15.refs_2_, ...), custom_call_target="tpu_custom_call" | custom-call | flops 4294967296 | bytes 16777216 | tf_op jit(solution)/shard_map/pallas_call | solution.py:584
  107.7 1.7 %collective-permute-done.27 = bf16[32,2048]{1,0:T(8,128)(2,1)S(1)} collective-permute-done((bf16[32,2048]{1,0:T(8,128)(2,1)S(1)}, bf16[32,2048]{1,0:T(8,128)(2,1)S(1)}, u32[]{:S(2)}, u32[]{:S(2)}) %collective-permute-start.27) | collective-permute-done | bytes 131104 | tf_op jit(solution)/shard_map/ppermute | solution.py:463
  110.2 3.4 %collective-permute-start.30 = (bf16[32,2048]{1,0:T(8,128)(2,1)S(1)}, bf16[32,2048]{1,0:T(8,128)(2,1)S(1)}, u32[]{:S(2)}, u32[]{:S(2)}) collective-permute-start(bf16[32,2048]{1,0:T(8,128)(2,1)S(1)} %get-tuple-element.65), channel_id=1, source_target_pairs={{0,10},{1,11},{2,8},{3,9},{4,14},{5,15},{6,12},{7,13},{8,2},{9,3},... | collective-permute-start | bytes 393224 | tf_op jit(solution)/shard_map/ppermute | solution.py:463
  113.6 2.0 %collective-permute-start.31 = (bf16[32,2048]{1,0:T(8,128)(2,1)S(1)}, bf16[32,2048]{1,0:T(8,128)(2,1)S(1)}, u32[]{:S(2)}, u32[]{:S(2)}) collective-permute-start(bf16[32,2048]{1,0:T(8,128)(2,1)S(1)} %get-tuple-element.68), channel_id=1, source_target_pairs={{0,14},{1,15},{2,12},{3,13},{4,10},{5,11},{6,8},{7,9},{8,6},{9,7},... | collective-permute-start | bytes 393224 | tf_op jit(solution)/shard_map/ppermute | solution.py:463
  116.9 7.2 %collective-permute-done.30 = bf16[32,2048]{1,0:T(8,128)(2,1)S(1)} collective-permute-done((bf16[32,2048]{1,0:T(8,128)(2,1)S(1)}, bf16[32,2048]{1,0:T(8,128)(2,1)S(1)}, u32[]{:S(2)}, u32[]{:S(2)}) %collective-permute-start.30) | collective-permute-done | bytes 131104 | tf_op jit(solution)/shard_map/ppermute | solution.py:463
  125.1 1.8 %collective-permute-done.33 = bf16[32,2048]{1,0:T(8,128)(2,1)S(1)} collective-permute-done((bf16[32,2048]{1,0:T(8,128)(2,1)S(1)}, bf16[32,2048]{1,0:T(8,128)(2,1)S(1)}, u32[]{:S(2)}, u32[]{:S(2)}) %collective-permute-start.33) | collective-permute-done | bytes 131104 | tf_op jit(solution)/shard_map/ppermute | solution.py:463
  (87 shorter events, 23.2 us)
Async XLA Ops:
  2.6 18.0 %all-to-all-start = ((bf16[8,432,128]{2,1,0:T(8,128)(2,1)}), bf16[8,432,128]{2,1,0:T(8,128)(2,1)S(1)}, u32[]{:S(2)}, u32[]{:S(2)}) async-start(bf16[8,432,128]{2,1,0:T(8,128)(2,1)} %shard_map.109), calls=%async_computation | async-start | bytes 1769472 | tf_op jit(solution)/shard_map/all_to_all | solution.py:514
  20.6 9.2 %collective-permute-start = (bf16[64,2048]{1,0:T(8,128)(2,1)S(1)}, bf16[64,2048]{1,0:T(8,128)(2,1)S(1)}, u32[]{:S(2)}, u32[]{:S(2)}) collective-permute-start(bf16[64,2048]{1,0:T(8,128)(2,1)S(1)} %get-tuple-element.36), channel_id=1, source_target_pairs={{0,2},{1,3},{2,0},{3,1},{4,6},{5,7},{6,4},{7,5},{8,10},{9,11},{10,... | collective-permute-start | bytes 786440 | tf_op jit(solution)/shard_map/ppermute | solution.py:463
  22.1 23.0 %collective-permute-start.1 = (bf16[160,2048]{1,0:T(8,128)(2,1)}, bf16[160,2048]{1,0:T(8,128)(2,1)S(1)}, u32[]{:S(2)}, u32[]{:S(2)}) collective-permute-start(bf16[160,2048]{1,0:T(8,128)(2,1)} %copy-done.2), channel_id=1, source_target_pairs={{0,2},{1,3},{2,0},{3,1},{4,6},{5,7},{6,4},{7,5},{8,10},{9,11},{10,... | collective-permute-start | bytes 1966088 | tf_op jit(solution)/shard_map/ppermute | solution.py:463
  29.8 15.6 %all-to-all-start.1 = ((bf16[16,72,128]{2,1,0:T(8,128)(2,1)}), bf16[16,72,128]{2,1,0:T(8,128)(2,1)S(1)}, u32[]{:S(2)}, u32[]{:S(2)}) async-start(bf16[16,72,128]{2,1,0:T(8,128)(2,1)} %shard_map.111), calls=%async_computation.1 | async-start | bytes 589824 | tf_op jit(solution)/shard_map/all_to_all | solution.py:532
  34.7 13.7 %collective-permute-start.3 = (bf16[288,2048]{1,0:T(8,128)(2,1)S(1)}, bf16[288,2048]{1,0:T(8,128)(2,1)}, u32[]{:S(2)}, u32[]{:S(2)}) collective-permute-start(bf16[288,2048]{1,0:T(8,128)(2,1)S(1)} %copy-done), channel_id=1, source_target_pairs={{0,1},{1,0},{2,3},{3,2},{4,5},{5,4},{6,7},{7,6},{8,9},{9,8},{10,11... | collective-permute-start | bytes 3538952 | tf_op jit(solution)/shard_map/ppermute | solution.py:463
  35.2 8.3 %collective-permute-start.2 = (bf16[64,2048]{1,0:T(8,128)(2,1)S(1)}, bf16[64,2048]{1,0:T(8,128)(2,1)S(1)}, u32[]{:S(2)}, u32[]{:S(2)}) collective-permute-start(bf16[64,2048]{1,0:T(8,128)(2,1)S(1)} %collective-permute-done.refs_3_), channel_id=1, source_target_pairs={{0,16},{16,0},{1,17},{17,1},{2,18},{18,2},{3,19},{19,3},{4,20},{20... | collective-permute-start | bytes 786440 | tf_op jit(solution)/shard_map/ppermute | solution.py:530
  52.2 13.4 %collective-permute-start.7 = (bf16[32,2304]{1,0:T(8,128)(2,1)S(1)}, bf16[32,2304]{1,0:T(8,128)(2,1)S(1)}, u32[]{:S(2)}, u32[]{:S(2)}) collective-permute-start(bf16[32,2304]{1,0:T(8,128)(2,1)S(1)} %get-tuple-element.63), channel_id=1, source_target_pairs={{0,8},{1,9},{2,10},{3,11},{4,12},{5,13},{6,14},{7,15},{8,0},{9,1},... | collective-permute-start | bytes 442376 | tf_op jit(solution)/shard_map/ppermute | solution.py:463
  54.8 10.7 %collective-permute-start.8 = (bf16[32,2304]{1,0:T(8,128)(2,1)S(1)}, bf16[32,2304]{1,0:T(8,128)(2,1)S(1)}, u32[]{:S(2)}, u32[]{:S(2)}) collective-permute-start(bf16[32,2304]{1,0:T(8,128)(2,1)S(1)} %get-tuple-element.62), channel_id=1, source_target_pairs={{0,12},{1,13},{2,14},{3,15},{4,8},{5,9},{6,10},{7,11},{8,4},{9,5},... | collective-permute-start | bytes 442376 | tf_op jit(solution)/shard_map/ppermute | solution.py:463
  55.1 11.7 %collective-permute-start.9 = (bf16[32,2304]{1,0:T(8,128)(2,1)S(1)}, bf16[32,2304]{1,0:T(8,128)(2,1)S(1)}, u32[]{:S(2)}, u32[]{:S(2)}) collective-permute-start(bf16[32,2304]{1,0:T(8,128)(2,1)S(1)} %get-tuple-element.61), channel_id=1, source_target_pairs={{0,4},{1,5},{2,6},{3,7},{4,0},{5,1},{6,2},{7,3},{8,12},{9,13},{10,... | collective-permute-start | bytes 442376 | tf_op jit(solution)/shard_map/ppermute | solution.py:463
  67.4 14.2 %collective-permute-start.10 = (bf16[32,2176]{1,0:T(8,128)(2,1)S(1)}, bf16[32,2176]{1,0:T(8,128)(2,1)S(1)}, u32[]{:S(2)}, u32[]{:S(2)}) collective-permute-start(bf16[32,2176]{1,0:T(8,128)(2,1)S(1)} %shard_map.113.refs_0_), channel_id=1, source_target_pairs={{0,8},{1,9},{2,10},{3,11},{4,12},{5,13},{6,14},{7,15},{8,0},{9,1},... | collective-permute-start | bytes 417800 | tf_op jit(solution)/shard_map/ppermute | solution.py:463
  71.0 10.6 %collective-permute-start.11 = (bf16[32,2176]{1,0:T(8,128)(2,1)S(1)}, bf16[32,2176]{1,0:T(8,128)(2,1)S(1)}, u32[]{:S(2)}, u32[]{:S(2)}) collective-permute-start(bf16[32,2176]{1,0:T(8,128)(2,1)S(1)} %shard_map.113.refs_0_), channel_id=1, source_target_pairs={{0,12},{1,13},{2,14},{3,15},{4,8},{5,9},{6,10},{7,11},{8,4},{9,5},... | collective-permute-start | bytes 417800 | tf_op jit(solution)/shard_map/ppermute | solution.py:463
  72.1 9.5 %collective-permute-start.12 = (bf16[32,2176]{1,0:T(8,128)(2,1)S(1)}, bf16[32,2176]{1,0:T(8,128)(2,1)S(1)}, u32[]{:S(2)}, u32[]{:S(2)}) collective-permute-start(bf16[32,2176]{1,0:T(8,128)(2,1)S(1)} %shard_map.113.refs_0_), channel_id=1, source_target_pairs={{0,4},{1,5},{2,6},{3,7},{4,0},{5,1},{6,2},{7,3},{8,12},{9,13},{10,... | collective-permute-start | bytes 417800 | tf_op jit(solution)/shard_map/ppermute | solution.py:463
  72.1 9.5 %collective-permute-start.13 = (bf16[32,2176]{1,0:T(8,128)(2,1)S(1)}, bf16[32,2176]{1,0:T(8,128)(2,1)S(1)}, u32[]{:S(2)}, u32[]{:S(2)}) collective-permute-start(bf16[32,2176]{1,0:T(8,128)(2,1)S(1)} %shard_map.113.refs_0_), channel_id=1, source_target_pairs={{0,2},{1,3},{2,0},{3,1},{4,6},{5,7},{6,4},{7,5},{8,10},{9,11},{10,... | collective-permute-start | bytes 417800 | tf_op jit(solution)/shard_map/ppermute | solution.py:463
  82.7 10.1 %collective-permute-start.14 = (bf16[32,2176]{1,0:T(8,128)(2,1)S(1)}, bf16[32,2176]{1,0:T(8,128)(2,1)S(1)}, u32[]{:S(2)}, u32[]{:S(2)}) collective-permute-start(bf16[32,2176]{1,0:T(8,128)(2,1)S(1)} %collective-permute-done.10.refs_1_), channel_id=1, source_target_pairs={{0,2},{1,3},{2,0},{3,1},{4,6},{5,7},{6,4},{7,5},{8,10},{9,11},{10,... | collective-permute-start | bytes 417800 | tf_op jit(solution)/shard_map/ppermute | solution.py:463
  84.1 8.7 %collective-permute-start.15 = (bf16[32,2176]{1,0:T(8,128)(2,1)S(1)}, bf16[32,2176]{1,0:T(8,128)(2,1)S(1)}, u32[]{:S(2)}, u32[]{:S(2)}) collective-permute-start(bf16[32,2176]{1,0:T(8,128)(2,1)S(1)} %collective-permute-done.11.refs_2_), channel_id=1, source_target_pairs={{0,2},{1,3},{2,0},{3,1},{4,6},{5,7},{6,4},{7,5},{8,10},{9,11},{10,... | collective-permute-start | bytes 417800 | tf_op jit(solution)/shard_map/ppermute | solution.py:463
  84.7 9.6 %collective-permute-start.16 = (bf16[32,2176]{1,0:T(8,128)(2,1)S(1)}, bf16[32,2176]{1,0:T(8,128)(2,1)S(1)}, u32[]{:S(2)}, u32[]{:S(2)}) collective-permute-start(bf16[32,2176]{1,0:T(8,128)(2,1)S(1)} %collective-permute-done.12.refs_3_), channel_id=1, source_target_pairs={{0,2},{1,3},{2,0},{3,1},{4,6},{5,7},{6,4},{7,5},{8,10},{9,11},{10,... | collective-permute-start | bytes 417800 | tf_op jit(solution)/shard_map/ppermute | solution.py:463
  94.8 6.1 %collective-permute-start.23 = (bf16[32,2176]{1,0:T(8,128)(2,1)S(1)}, bf16[32,2176]{1,0:T(8,128)(2,1)S(1)}, u32[]{:S(2)}, u32[]{:S(2)}) collective-permute-start(bf16[32,2176]{1,0:T(8,128)(2,1)S(1)} %collective-permute-done.15.refs_2_), channel_id=1, source_target_pairs={{0,1},{1,0},{2,3},{3,2},{4,5},{5,4},{6,7},{7,6},{8,9},{9,8},{10,11... | collective-permute-start | bytes 417800 | tf_op jit(solution)/shard_map/ppermute | solution.py:463
  96.4 13.0 %collective-permute-start.27 = (bf16[32,2048]{1,0:T(8,128)(2,1)S(1)}, bf16[32,2048]{1,0:T(8,128)(2,1)S(1)}, u32[]{:S(2)}, u32[]{:S(2)}) collective-permute-start(bf16[32,2048]{1,0:T(8,128)(2,1)S(1)} %get-tuple-element.69), channel_id=1, source_target_pairs={{0,8},{1,9},{2,10},{3,11},{4,12},{5,13},{6,14},{7,15},{8,0},{9,1},... | collective-permute-start | bytes 393224 | tf_op jit(solution)/shard_map/ppermute | solution.py:463
  98.7 10.6 %collective-permute-start.28 = (bf16[32,2048]{1,0:T(8,128)(2,1)S(1)}, bf16[32,2048]{1,0:T(8,128)(2,1)S(1)}, u32[]{:S(2)}, u32[]{:S(2)}) collective-permute-start(bf16[32,2048]{1,0:T(8,128)(2,1)S(1)} %get-tuple-element.71), channel_id=1, source_target_pairs={{0,12},{1,13},{2,14},{3,15},{4,8},{5,9},{6,10},{7,11},{8,4},{9,5},... | collective-permute-start | bytes 393224 | tf_op jit(solution)/shard_map/ppermute | solution.py:463
  100.9 9.0 %collective-permute-start.29 = (bf16[32,2048]{1,0:T(8,128)(2,1)S(1)}, bf16[32,2048]{1,0:T(8,128)(2,1)S(1)}, u32[]{:S(2)}, u32[]{:S(2)}) collective-permute-start(bf16[32,2048]{1,0:T(8,128)(2,1)S(1)} %get-tuple-element.70), channel_id=1, source_target_pairs={{0,4},{1,5},{2,6},{3,7},{4,0},{5,1},{6,2},{7,3},{8,12},{9,13},{10,... | collective-permute-start | bytes 393224 | tf_op jit(solution)/shard_map/ppermute | solution.py:463
  110.2 14.0 %collective-permute-start.30 = (bf16[32,2048]{1,0:T(8,128)(2,1)S(1)}, bf16[32,2048]{1,0:T(8,128)(2,1)S(1)}, u32[]{:S(2)}, u32[]{:S(2)}) collective-permute-start(bf16[32,2048]{1,0:T(8,128)(2,1)S(1)} %get-tuple-element.65), channel_id=1, source_target_pairs={{0,10},{1,11},{2,8},{3,9},{4,14},{5,15},{6,12},{7,13},{8,2},{9,3},... | collective-permute-start | bytes 393224 | tf_op jit(solution)/shard_map/ppermute | solution.py:463
  113.6 10.6 %collective-permute-start.31 = (bf16[32,2048]{1,0:T(8,128)(2,1)S(1)}, bf16[32,2048]{1,0:T(8,128)(2,1)S(1)}, u32[]{:S(2)}, u32[]{:S(2)}) collective-permute-start(bf16[32,2048]{1,0:T(8,128)(2,1)S(1)} %get-tuple-element.68), channel_id=1, source_target_pairs={{0,14},{1,15},{2,12},{3,13},{4,10},{5,11},{6,8},{7,9},{8,6},{9,7},... | collective-permute-start | bytes 393224 | tf_op jit(solution)/shard_map/ppermute | solution.py:463
  115.5 9.6 %collective-permute-start.32 = (bf16[32,2048]{1,0:T(8,128)(2,1)S(1)}, bf16[32,2048]{1,0:T(8,128)(2,1)S(1)}, u32[]{:S(2)}, u32[]{:S(2)}) collective-permute-start(bf16[32,2048]{1,0:T(8,128)(2,1)S(1)} %get-tuple-element.67), channel_id=1, source_target_pairs={{0,6},{1,7},{2,4},{3,5},{4,2},{5,3},{6,0},{7,1},{8,14},{9,15},{10,... | collective-permute-start | bytes 393224 | tf_op jit(solution)/shard_map/ppermute | solution.py:463
  115.5 11.4 %collective-permute-start.33 = (bf16[32,2048]{1,0:T(8,128)(2,1)S(1)}, bf16[32,2048]{1,0:T(8,128)(2,1)S(1)}, u32[]{:S(2)}, u32[]{:S(2)}) collective-permute-start(bf16[32,2048]{1,0:T(8,128)(2,1)S(1)} %get-tuple-element.66), channel_id=1, source_target_pairs={{0,2},{1,3},{2,0},{3,1},{4,6},{5,7},{6,4},{7,5},{8,10},{9,11},{10,... | collective-permute-start | bytes 393224 | tf_op jit(solution)/shard_map/ppermute | solution.py:463
  (21 other events, 160.2 us)

commit v10 on v9

--- a/solution.py
+++ b/solution.py
@@ -295,19 +295,27 @@
     ones = jnp.where(lax.broadcasted_iota(jnp.int32, (16, sides * lanes), 0) == 0, 1.0, 0.0).astype(BF)
     head_row = lax.broadcasted_iota(jnp.int32, (part, sides * lanes), 0) // dim
     group = lax.broadcasted_iota(jnp.int32, (dim, lanes), 1) // tokens
-    for quarter in range(quarters):
+    def scores_of(item):
+        quarter, head = item // 2, item % 2
         query = jnp.concatenate(
             [x_ref[quarter + quarters * s, :part, :] for s in range(sides)], 1
         ).astype(F32)
-        mixed = []
-        for head in range(2):
-            own = jnp.concatenate([jnp.where(head_row == head, query, 0.0).astype(BF), ones], 0)
-            scores = jnp.dot(keys, own, preferred_element_type=F32)
-            highest = jnp.max(scores, axis=0, keepdims=True)
-            weights = jnp.exp2((scores - highest) * factor)
-            total = jnp.sum(weights, axis=0, keepdims=True)
-            value = jnp.dot(values[head], weights.astype(BF), preferred_element_type=F32) / total
-            mixed += [value[:, s * lanes : (s + 1) * lanes] for s in range(sides)]
+        own = jnp.concatenate([jnp.where(head_row == head, query, 0.0).astype(BF), ones], 0)
+        return jnp.dot(keys, own, preferred_element_type=F32)
+
+    scores = scores_of(0)
+    for item in range(2 * quarters):
+        quarter, head = item // 2, item % 2
+        following = scores_of(item + 1) if item + 1 < 2 * quarters else None
+        highest = jnp.max(scores, axis=0, keepdims=True)
+        weights = jnp.exp2((scores - highest) * factor)
+        total = jnp.sum(weights, axis=0, keepdims=True)
+        value = jnp.dot(values[head], weights.astype(BF), preferred_element_type=F32) / total
+        mixed = [] if head == 0 else mixed
+        mixed += [value[:, s * lanes : (s + 1) * lanes] for s in range(sides)]
+        scores = following
+        if head == 0:
+            continue
         for position in range(4):
             block = mixed[position]
             for g in range(4):
@@ -440,18 +448,30 @@
         weights.append(jnp.sum(picked, axis=1, keepdims=True))
     inputs = x_ref[...]
     turned = (((1,), (1,)), ((), ()))
-    hidden = []
+
+    def gated(gate, up):
+        return (gate / (1.0 + jnp.exp(-gate)) * up).astype(BF)
+
+    hidden, earlier = [], None
     for k, cut in enumerate(cuts):
         copies[2 * k].wait()
         gate = lax.dot_general(inputs, gate_ref[cut, :], turned, preferred_element_type=F32)
         copies[2 * k + 1].wait()
         up = lax.dot_general(inputs, up_ref[cut, :], turned, preferred_element_type=F32)
-        hidden.append((gate / (1.0 + jnp.exp(-gate)) * up).astype(BF))
-    hidden = jnp.concatenate(hidden, 1)
+        if earlier is not None:
+            hidden.append(gated(*earlier))
+        earlier = gate, up
+    hidden = jnp.concatenate(hidden + [gated(*earlier)], 1)
     last.wait()
     step = 4 * LANES
+
+    def product_of(begin):
+        return jnp.dot(hidden, down_ref[:, begin : begin + step], preferred_element_type=F32)
+
+    following = product_of(0)
     for begin in range(0, width, step):
-        product = jnp.dot(hidden, down_ref[:, begin : begin + step], preferred_element_type=F32)
+        product = following
+        following = product_of(begin + step) if begin + step < width else None
         for k in range(len(blocks)):
             value = (product[k * tokens : (k + 1) * tokens] * weights[k]).astype(BF)
             out_ref = own_ref if k < half else other_ref

time: 128 us -> 128 us (level)
  Pallas kernels: 26.1 us -> 24.1 us
  waiting for transfers between devices: 55.1 us -> 57.1 us
    pallas_call x1, Pallas kernels: 6.88 us -> 4.91 us  [local(): pl.pallas_call(attend_kernel, out_shape=jax.ShapeDtypeStruct((devices, di...]
    ppermute x33, waiting for transfers between devices: 36.3 us -> 38.3 us  [crossed(): return lax.ppermute(value, 'wide', pairs)]
  transfers between devices with their start and end apart: 36 -> 36, of which waited for: 17 -> 17; matrix products, arithmetic and copies ran while one was open for 1% -> 1% of each run, Pallas kernels for 16% -> 14%
where the time goes in v10:
time: 128 us
  waiting for transfers between devices  57.1 us (45%)
  starting transfers between devices  41.4 us (32%)
  Pallas kernels  24.1 us (19%)
  local copies, waits for them, and re-layouts  3.42 us (3%)
  other arithmetic  1.38 us (1%)
    ppermute x33, waiting for transfers between devices, crossed(): return lax.ppermute(value, 'wide', pairs)  38.3 us
    ppermute x33, starting transfers between devices, crossed(): return lax.ppermute(value, 'wide', pairs)  29.8 us
    pallas_call x2, Pallas kernels, experts_of(): pl.pallas_call(lambda *refs: expert_kernel(*refs, experts=experts, cuts=c...  13.3 us
    all_to_all x1, waiting for transfers between devices, local(): lax.all_to_all(packed, 'wide', split_axis=0, concat_axis=0, tiled=True, a...  11.6 us
    ppermute x1, waiting for transfers between devices, local(): theirs_y = lax.ppermute(mine_y, 'grp', [(0, 1), (1, 0)])  6.83 us
    all_to_all x1, starting transfers between devices, local(): lax.all_to_all(packed, 'wide', split_axis=0, concat_axis=0, tiled=True, a...  5.25 us
    pallas_call x1, Pallas kernels, local(): pl.pallas_call(attend_kernel, out_shape=jax.ShapeDtypeStruct((devices, di...  4.91 us
    all_to_all x1, starting transfers between devices, local(): lax.all_to_all(attended, 'wide', split_axis=0, concat_axis=0, tiled=True)  4.9 us
  transfers between devices with their start and end apart: 36, of which 17 were waited for; matrix products, arithmetic and copies ran while one was open for 1% of the time, Pallas kernels for 14%

profile of v10, /device:TPU:0, one launch (start us, length us, event | category | flops | bytes accessed | tf_op | source)
XLA Modules:
  0.0 127.7 jit_solution(6174497709703889847)
XLA Ops:
  2.6 5.3 %all-to-all-start = ((bf16[8,432,128]{2,1,0:T(8,128)(2,1)}), bf16[8,432,128]{2,1,0:T(8,128)(2,1)S(1)}, u32[]{:S(2)}, u32[]{:S(2)}) async-start(bf16[8,432,128]{2,1,0:T(8,128)(2,1)} %shard_map.109), calls=%async_computation | async-start | bytes 1769472 | tf_op jit(solution)/shard_map/all_to_all | solution.py:534
  9.0 11.6 %all-to-all-done.x_ref = bf16[8,432,128]{2,1,0:T(8,128)(2,1)S(1)} async-done(((bf16[8,432,128]{2,1,0:T(8,128)(2,1)}), bf16[8,432,128]{2,1,0:T(8,128)(2,1)S(1)}, u32[]{:S(2)}, u32[]{:S(2)}) %all-to-all-start) | async-done | bytes 884768 | tf_op jit(solution)/shard_map/all_to_all | solution.py:534
  22.6 4.9 %shard_map.111 = bf16[16,72,128]{2,1,0:T(8,128)(2,1)} custom-call(bf16[8,432,128]{2,1,0:T(8,128)(2,1)S(1)} %all-to-all-done.x_ref, s32[2,2]{1,0:T(2,128)S(1)} %copy-done.3), custom_call_target="tpu_custom_call" | custom-call | flops 4294967296 | bytes 4194304 | tf_op jit(solution)/shard_map/pallas_call | solution.py:540
  27.6 2.3 %collective-permute-done.refs_3_ = bf16[64,2048]{1,0:T(8,128)(2,1)S(1)} collective-permute-done((bf16[64,2048]{1,0:T(8,128)(2,1)S(1)}, bf16[64,2048]{1,0:T(8,128)(2,1)S(1)}, u32[]{:S(2)}, u32[]{:S(2)}) %collective-permute-start) | collective-permute-done | bytes 262176 | tf_op jit(solution)/shard_map/ppermute | solution.py:483
  29.8 4.9 %all-to-all-start.1 = ((bf16[16,72,128]{2,1,0:T(8,128)(2,1)}), bf16[16,72,128]{2,1,0:T(8,128)(2,1)S(1)}, u32[]{:S(2)}, u32[]{:S(2)}) async-start(bf16[16,72,128]{2,1,0:T(8,128)(2,1)} %shard_map.111), calls=%async_computation.1 | async-start | bytes 589824 | tf_op jit(solution)/shard_map/all_to_all | solution.py:552
  35.2 1.5 %collective-permute-start.2 = (bf16[64,2048]{1,0:T(8,128)(2,1)S(1)}, bf16[64,2048]{1,0:T(8,128)(2,1)S(1)}, u32[]{:S(2)}, u32[]{:S(2)}) collective-permute-start(bf16[64,2048]{1,0:T(8,128)(2,1)S(1)} %collective-permute-done.refs_3_), channel_id=1, source_target_pairs={{0,16},{16,0},{1,17},{17,1},{2,18},{18,2},{3,19},{19,3},{4,20},{20... | collective-permute-start | bytes 786440 | tf_op jit(solution)/shard_map/ppermute | solution.py:550
  36.7 6.8 %collective-permute-done.2.refs_4_ = bf16[64,2048]{1,0:T(8,128)(2,1)S(1)} collective-permute-done((bf16[64,2048]{1,0:T(8,128)(2,1)S(1)}, bf16[64,2048]{1,0:T(8,128)(2,1)S(1)}, u32[]{:S(2)}, u32[]{:S(2)}) %collective-permute-start.2) | collective-permute-done | bytes 262176 | tf_op jit(solution)/shard_map/ppermute | solution.py:550
  43.5 1.5 %collective-permute-done.1.refs_2_ = bf16[160,2048]{1,0:T(8,128)(2,1)S(1)} collective-permute-done((bf16[160,2048]{1,0:T(8,128)(2,1)}, bf16[160,2048]{1,0:T(8,128)(2,1)S(1)}, u32[]{:S(2)}, u32[]{:S(2)}) %collective-permute-start.1) | collective-permute-done | bytes 655392 | tf_op jit(solution)/shard_map/ppermute | solution.py:483
  48.5 3.7 %shard_map.112 = bf16[4,32,2304]{2,1,0:T(8,128)(2,1)S(1)} custom-call(bf16[16,72,128]{2,1,0:T(8,128)(2,1)S(1)} %all-to-all-done.1.x_ref, bf16[1152,1152]{1,0:T(8,128)(2,1)} %w_out_hbm.1, f32[1,4608]{1,0:T(1,128)S(1)} %reshape.8.gain_ref, f32[1,4608]{1,0:T(1,128)S(1)} %reshape.9.bias_ref, bf16[288,2048]{1,0:T(8,128)(2,1)} %refs_0_.1, ...), custom_call_target="tpu_custom_call" | custom-call | tf_op jit(solution)/shard_map/pallas_call | solution.py:557
  52.2 2.6 %collective-permute-start.7 = (bf16[32,2304]{1,0:T(8,128)(2,1)S(1)}, bf16[32,2304]{1,0:T(8,128)(2,1)S(1)}, u32[]{:S(2)}, u32[]{:S(2)}) collective-permute-start(bf16[32,2304]{1,0:T(8,128)(2,1)S(1)} %get-tuple-element.63), channel_id=1, source_target_pairs={{0,8},{1,9},{2,10},{3,11},{4,12},{5,13},{6,14},{7,15},{8,0},{9,1},... | collective-permute-start | bytes 442376 | tf_op jit(solution)/shard_map/ppermute | solution.py:483
  56.2 9.4 %collective-permute-done.7.refs_1_ = bf16[32,2304]{1,0:T(8,128)(2,1)S(1)} collective-permute-done((bf16[32,2304]{1,0:T(8,128)(2,1)S(1)}, bf16[32,2304]{1,0:T(8,128)(2,1)S(1)}, u32[]{:S(2)}, u32[]{:S(2)}) %collective-permute-start.7) | collective-permute-done | bytes 147488 | tf_op jit(solution)/shard_map/ppermute | solution.py:483
  67.4 3.7 %collective-permute-start.10 = (bf16[32,2176]{1,0:T(8,128)(2,1)S(1)}, bf16[32,2176]{1,0:T(8,128)(2,1)S(1)}, u32[]{:S(2)}, u32[]{:S(2)}) collective-permute-start(bf16[32,2176]{1,0:T(8,128)(2,1)S(1)} %shard_map.113.refs_0_), channel_id=1, source_target_pairs={{0,8},{1,9},{2,10},{3,11},{4,12},{5,13},{6,14},{7,15},{8,0},{9,1},... | collective-permute-start | bytes 417800 | tf_op jit(solution)/shard_map/ppermute | solution.py:483
  72.1 1.5 %collective-permute-start.13 = (bf16[32,2176]{1,0:T(8,128)(2,1)S(1)}, bf16[32,2176]{1,0:T(8,128)(2,1)S(1)}, u32[]{:S(2)}, u32[]{:S(2)}) collective-permute-start(bf16[32,2176]{1,0:T(8,128)(2,1)S(1)} %shard_map.113.refs_0_), channel_id=1, source_target_pairs={{0,2},{1,3},{2,0},{3,1},{4,6},{5,7},{6,4},{7,5},{8,10},{9,11},{10,... | collective-permute-start | bytes 417800 | tf_op jit(solution)/shard_map/ppermute | solution.py:483
  73.6 8.0 %collective-permute-done.10.refs_1_ = bf16[32,2176]{1,0:T(8,128)(2,1)S(1)} collective-permute-done((bf16[32,2176]{1,0:T(8,128)(2,1)S(1)}, bf16[32,2176]{1,0:T(8,128)(2,1)S(1)}, u32[]{:S(2)}, u32[]{:S(2)}) %collective-permute-start.10) | collective-permute-done | bytes 139296 | tf_op jit(solution)/shard_map/ppermute | solution.py:483
  86.1 6.7 %shard_map.114 = (bf16[4,32,2048]{2,1,0:T(8,128)(2,1)S(1)}, bf16[4,32,2048]{2,1,0:T(8,128)(2,1)S(1)}) custom-call(bf16[32,2176]{1,0:T(8,128)(2,1)S(1)} %shard_map.113.refs_0_, bf16[32,2176]{1,0:T(8,128)(2,1)S(1)} %collective-permute-done.10.refs_1_, bf16[32,2176]{1,0:T(8,128)(2,1)S(1)} %collective-permute-done.11.refs_2_, ...), custom_call_target="tpu_custom_call" | custom-call | flops 4294967296 | bytes 16777216 | tf_op jit(solution)/shard_map/pallas_call | solution.py:604
  92.8 1.5 %collective-permute-done.16.refs_3_ = bf16[32,2176]{1,0:T(8,128)(2,1)S(1)} collective-permute-done((bf16[32,2176]{1,0:T(8,128)(2,1)S(1)}, bf16[32,2176]{1,0:T(8,128)(2,1)S(1)}, u32[]{:S(2)}, u32[]{:S(2)}) %collective-permute-start.16) | collective-permute-done | bytes 139296 | tf_op jit(solution)/shard_map/ppermute | solution.py:483
  96.4 2.3 %collective-permute-start.27 = (bf16[32,2048]{1,0:T(8,128)(2,1)S(1)}, bf16[32,2048]{1,0:T(8,128)(2,1)S(1)}, u32[]{:S(2)}, u32[]{:S(2)}) collective-permute-start(bf16[32,2048]{1,0:T(8,128)(2,1)S(1)} %get-tuple-element.69), channel_id=1, source_target_pairs={{0,8},{1,9},{2,10},{3,11},{4,12},{5,13},{6,14},{7,15},{8,0},{9,1},... | collective-permute-start | bytes 393224 | tf_op jit(solution)/shard_map/ppermute | solution.py:483
  98.7 2.1 %collective-permute-start.28 = (bf16[32,2048]{1,0:T(8,128)(2,1)S(1)}, bf16[32,2048]{1,0:T(8,128)(2,1)S(1)}, u32[]{:S(2)}, u32[]{:S(2)}) collective-permute-start(bf16[32,2048]{1,0:T(8,128)(2,1)S(1)} %get-tuple-element.71), channel_id=1, source_target_pairs={{0,12},{1,13},{2,14},{3,15},{4,8},{5,9},{6,10},{7,11},{8,4},{9,5},... | collective-permute-start | bytes 393224 | tf_op jit(solution)/shard_map/ppermute | solution.py:483
  100.9 6.7 %shard_map.115 = (bf16[4,32,2048]{2,1,0:T(8,128)(2,1)S(1)}, bf16[4,32,2048]{2,1,0:T(8,128)(2,1)S(1)}) custom-call(bf16[32,2176]{1,0:T(8,128)(2,1)S(1)} %collective-permute-done.13.refs_0_, bf16[32,2176]{1,0:T(8,128)(2,1)S(1)} %collective-permute-done.14.refs_1_, bf16[32,2176]{1,0:T(8,128)(2,1)S(1)} %collective-permute-done.15.refs_2_, ...), custom_call_target="tpu_custom_call" | custom-call | flops 4294967296 | bytes 16777216 | tf_op jit(solution)/shard_map/pallas_call | solution.py:604
  107.7 1.7 %collective-permute-done.27 = bf16[32,2048]{1,0:T(8,128)(2,1)S(1)} collective-permute-done((bf16[32,2048]{1,0:T(8,128)(2,1)S(1)}, bf16[32,2048]{1,0:T(8,128)(2,1)S(1)}, u32[]{:S(2)}, u32[]{:S(2)}) %collective-permute-start.27) | collective-permute-done | bytes 131104 | tf_op jit(solution)/shard_map/ppermute | solution.py:483
  110.2 3.4 %collective-permute-start.30 = (bf16[32,2048]{1,0:T(8,128)(2,1)S(1)}, bf16[32,2048]{1,0:T(8,128)(2,1)S(1)}, u32[]{:S(2)}, u32[]{:S(2)}) collective-permute-start(bf16[32,2048]{1,0:T(8,128)(2,1)S(1)} %get-tuple-element.65), channel_id=1, source_target_pairs={{0,10},{1,11},{2,8},{3,9},{4,14},{5,15},{6,12},{7,13},{8,2},{9,3},... | collective-permute-start | bytes 393224 | tf_op jit(solution)/shard_map/ppermute | solution.py:483
  113.6 2.0 %collective-permute-start.31 = (bf16[32,2048]{1,0:T(8,128)(2,1)S(1)}, bf16[32,2048]{1,0:T(8,128)(2,1)S(1)}, u32[]{:S(2)}, u32[]{:S(2)}) collective-permute-start(bf16[32,2048]{1,0:T(8,128)(2,1)S(1)} %get-tuple-element.68), channel_id=1, source_target_pairs={{0,14},{1,15},{2,12},{3,13},{4,10},{5,11},{6,8},{7,9},{8,6},{9,7},... | collective-permute-start | bytes 393224 | tf_op jit(solution)/shard_map/ppermute | solution.py:483
  116.9 7.3 %collective-permute-done.30 = bf16[32,2048]{1,0:T(8,128)(2,1)S(1)} collective-permute-done((bf16[32,2048]{1,0:T(8,128)(2,1)S(1)}, bf16[32,2048]{1,0:T(8,128)(2,1)S(1)}, u32[]{:S(2)}, u32[]{:S(2)}) %collective-permute-start.30) | collective-permute-done | bytes 131104 | tf_op jit(solution)/shard_map/ppermute | solution.py:483
  125.1 1.8 %collective-permute-done.33 = bf16[32,2048]{1,0:T(8,128)(2,1)S(1)} collective-permute-done((bf16[32,2048]{1,0:T(8,128)(2,1)S(1)}, bf16[32,2048]{1,0:T(8,128)(2,1)S(1)}, u32[]{:S(2)}, u32[]{:S(2)}) %collective-permute-start.33) | collective-permute-done | bytes 131104 | tf_op jit(solution)/shard_map/ppermute | solution.py:483
  (87 shorter events, 24.3 us)
Async XLA Ops:
  2.6 18.0 %all-to-all-start = ((bf16[8,432,128]{2,1,0:T(8,128)(2,1)}), bf16[8,432,128]{2,1,0:T(8,128)(2,1)S(1)}, u32[]{:S(2)}, u32[]{:S(2)}) async-start(bf16[8,432,128]{2,1,0:T(8,128)(2,1)} %shard_map.109), calls=%async_computation | async-start | bytes 1769472 | tf_op jit(solution)/shard_map/all_to_all | solution.py:534
  20.6 9.2 %collective-permute-start = (bf16[64,2048]{1,0:T(8,128)(2,1)S(1)}, bf16[64,2048]{1,0:T(8,128)(2,1)S(1)}, u32[]{:S(2)}, u32[]{:S(2)}) collective-permute-start(bf16[64,2048]{1,0:T(8,128)(2,1)S(1)} %get-tuple-element.36), channel_id=1, source_target_pairs={{0,2},{1,3},{2,0},{3,1},{4,6},{5,7},{6,4},{7,5},{8,10},{9,11},{10,... | collective-permute-start | bytes 786440 | tf_op jit(solution)/shard_map/ppermute | solution.py:483
  22.1 23.0 %collective-permute-start.1 = (bf16[160,2048]{1,0:T(8,128)(2,1)}, bf16[160,2048]{1,0:T(8,128)(2,1)S(1)}, u32[]{:S(2)}, u32[]{:S(2)}) collective-permute-start(bf16[160,2048]{1,0:T(8,128)(2,1)} %copy-done.2), channel_id=1, source_target_pairs={{0,2},{1,3},{2,0},{3,1},{4,6},{5,7},{6,4},{7,5},{8,10},{9,11},{10,... | collective-permute-start | bytes 1966088 | tf_op jit(solution)/shard_map/ppermute | solution.py:483
  29.8 15.6 %all-to-all-start.1 = ((bf16[16,72,128]{2,1,0:T(8,128)(2,1)}), bf16[16,72,128]{2,1,0:T(8,128)(2,1)S(1)}, u32[]{:S(2)}, u32[]{:S(2)}) async-start(bf16[16,72,128]{2,1,0:T(8,128)(2,1)} %shard_map.111), calls=%async_computation.1 | async-start | bytes 589824 | tf_op jit(solution)/shard_map/all_to_all | solution.py:552
  34.7 13.7 %collective-permute-start.3 = (bf16[288,2048]{1,0:T(8,128)(2,1)S(1)}, bf16[288,2048]{1,0:T(8,128)(2,1)}, u32[]{:S(2)}, u32[]{:S(2)}) collective-permute-start(bf16[288,2048]{1,0:T(8,128)(2,1)S(1)} %copy-done), channel_id=1, source_target_pairs={{0,1},{1,0},{2,3},{3,2},{4,5},{5,4},{6,7},{7,6},{8,9},{9,8},{10,11... | collective-permute-start | bytes 3538952 | tf_op jit(solution)/shard_map/ppermute | solution.py:483
  35.2 8.3 %collective-permute-start.2 = (bf16[64,2048]{1,0:T(8,128)(2,1)S(1)}, bf16[64,2048]{1,0:T(8,128)(2,1)S(1)}, u32[]{:S(2)}, u32[]{:S(2)}) collective-permute-start(bf16[64,2048]{1,0:T(8,128)(2,1)S(1)} %collective-permute-done.refs_3_), channel_id=1, source_target_pairs={{0,16},{16,0},{1,17},{17,1},{2,18},{18,2},{3,19},{19,3},{4,20},{20... | collective-permute-start | bytes 786440 | tf_op jit(solution)/shard_map/ppermute | solution.py:550
  52.2 13.4 %collective-permute-start.7 = (bf16[32,2304]{1,0:T(8,128)(2,1)S(1)}, bf16[32,2304]{1,0:T(8,128)(2,1)S(1)}, u32[]{:S(2)}, u32[]{:S(2)}) collective-permute-start(bf16[32,2304]{1,0:T(8,128)(2,1)S(1)} %get-tuple-element.63), channel_id=1, source_target_pairs={{0,8},{1,9},{2,10},{3,11},{4,12},{5,13},{6,14},{7,15},{8,0},{9,1},... | collective-permute-start | bytes 442376 | tf_op jit(solution)/shard_map/ppermute | solution.py:483
  54.8 10.7 %collective-permute-start.8 = (bf16[32,2304]{1,0:T(8,128)(2,1)S(1)}, bf16[32,2304]{1,0:T(8,128)(2,1)S(1)}, u32[]{:S(2)}, u32[]{:S(2)}) collective-permute-start(bf16[32,2304]{1,0:T(8,128)(2,1)S(1)} %get-tuple-element.62), channel_id=1, source_target_pairs={{0,12},{1,13},{2,14},{3,15},{4,8},{5,9},{6,10},{7,11},{8,4},{9,5},... | collective-permute-start | bytes 442376 | tf_op jit(solution)/shard_map/ppermute | solution.py:483
  55.1 11.7 %collective-permute-start.9 = (bf16[32,2304]{1,0:T(8,128)(2,1)S(1)}, bf16[32,2304]{1,0:T(8,128)(2,1)S(1)}, u32[]{:S(2)}, u32[]{:S(2)}) collective-permute-start(bf16[32,2304]{1,0:T(8,128)(2,1)S(1)} %get-tuple-element.61), channel_id=1, source_target_pairs={{0,4},{1,5},{2,6},{3,7},{4,0},{5,1},{6,2},{7,3},{8,12},{9,13},{10,... | collective-permute-start | bytes 442376 | tf_op jit(solution)/shard_map/ppermute | solution.py:483
  67.4 14.2 %collective-permute-start.10 = (bf16[32,2176]{1,0:T(8,128)(2,1)S(1)}, bf16[32,2176]{1,0:T(8,128)(2,1)S(1)}, u32[]{:S(2)}, u32[]{:S(2)}) collective-permute-start(bf16[32,2176]{1,0:T(8,128)(2,1)S(1)} %shard_map.113.refs_0_), channel_id=1, source_target_pairs={{0,8},{1,9},{2,10},{3,11},{4,12},{5,13},{6,14},{7,15},{8,0},{9,1},... | collective-permute-start | bytes 417800 | tf_op jit(solution)/shard_map/ppermute | solution.py:483
  71.0 10.6 %collective-permute-start.11 = (bf16[32,2176]{1,0:T(8,128)(2,1)S(1)}, bf16[32,2176]{1,0:T(8,128)(2,1)S(1)}, u32[]{:S(2)}, u32[]{:S(2)}) collective-permute-start(bf16[32,2176]{1,0:T(8,128)(2,1)S(1)} %shard_map.113.refs_0_), channel_id=1, source_target_pairs={{0,12},{1,13},{2,14},{3,15},{4,8},{5,9},{6,10},{7,11},{8,4},{9,5},... | collective-permute-start | bytes 417800 | tf_op jit(solution)/shard_map/ppermute | solution.py:483
  72.1 9.5 %collective-permute-start.12 = (bf16[32,2176]{1,0:T(8,128)(2,1)S(1)}, bf16[32,2176]{1,0:T(8,128)(2,1)S(1)}, u32[]{:S(2)}, u32[]{:S(2)}) collective-permute-start(bf16[32,2176]{1,0:T(8,128)(2,1)S(1)} %shard_map.113.refs_0_), channel_id=1, source_target_pairs={{0,4},{1,5},{2,6},{3,7},{4,0},{5,1},{6,2},{7,3},{8,12},{9,13},{10,... | collective-permute-start | bytes 417800 | tf_op jit(solution)/shard_map/ppermute | solution.py:483
  72.1 9.5 %collective-permute-start.13 = (bf16[32,2176]{1,0:T(8,128)(2,1)S(1)}, bf16[32,2176]{1,0:T(8,128)(2,1)S(1)}, u32[]{:S(2)}, u32[]{:S(2)}) collective-permute-start(bf16[32,2176]{1,0:T(8,128)(2,1)S(1)} %shard_map.113.refs_0_), channel_id=1, source_target_pairs={{0,2},{1,3},{2,0},{3,1},{4,6},{5,7},{6,4},{7,5},{8,10},{9,11},{10,... | collective-permute-start | bytes 417800 | tf_op jit(solution)/shard_map/ppermute | solution.py:483
  82.7 10.1 %collective-permute-start.14 = (bf16[32,2176]{1,0:T(8,128)(2,1)S(1)}, bf16[32,2176]{1,0:T(8,128)(2,1)S(1)}, u32[]{:S(2)}, u32[]{:S(2)}) collective-permute-start(bf16[32,2176]{1,0:T(8,128)(2,1)S(1)} %collective-permute-done.10.refs_1_), channel_id=1, source_target_pairs={{0,2},{1,3},{2,0},{3,1},{4,6},{5,7},{6,4},{7,5},{8,10},{9,11},{10,... | collective-permute-start | bytes 417800 | tf_op jit(solution)/shard_map/ppermute | solution.py:483
  84.1 8.7 %collective-permute-start.15 = (bf16[32,2176]{1,0:T(8,128)(2,1)S(1)}, bf16[32,2176]{1,0:T(8,128)(2,1)S(1)}, u32[]{:S(2)}, u32[]{:S(2)}) collective-permute-start(bf16[32,2176]{1,0:T(8,128)(2,1)S(1)} %collective-permute-done.11.refs_2_), channel_id=1, source_target_pairs={{0,2},{1,3},{2,0},{3,1},{4,6},{5,7},{6,4},{7,5},{8,10},{9,11},{10,... | collective-permute-start | bytes 417800 | tf_op jit(solution)/shard_map/ppermute | solution.py:483
  84.7 9.6 %collective-permute-start.16 = (bf16[32,2176]{1,0:T(8,128)(2,1)S(1)}, bf16[32,2176]{1,0:T(8,128)(2,1)S(1)}, u32[]{:S(2)}, u32[]{:S(2)}) collective-permute-start(bf16[32,2176]{1,0:T(8,128)(2,1)S(1)} %collective-permute-done.12.refs_3_), channel_id=1, source_target_pairs={{0,2},{1,3},{2,0},{3,1},{4,6},{5,7},{6,4},{7,5},{8,10},{9,11},{10,... | collective-permute-start | bytes 417800 | tf_op jit(solution)/shard_map/ppermute | solution.py:483
  94.8 6.1 %collective-permute-start.23 = (bf16[32,2176]{1,0:T(8,128)(2,1)S(1)}, bf16[32,2176]{1,0:T(8,128)(2,1)S(1)}, u32[]{:S(2)}, u32[]{:S(2)}) collective-permute-start(bf16[32,2176]{1,0:T(8,128)(2,1)S(1)} %collective-permute-done.15.refs_2_), channel_id=1, source_target_pairs={{0,1},{1,0},{2,3},{3,2},{4,5},{5,4},{6,7},{7,6},{8,9},{9,8},{10,11... | collective-permute-start | bytes 417800 | tf_op jit(solution)/shard_map/ppermute | solution.py:483
  96.4 13.0 %collective-permute-start.27 = (bf16[32,2048]{1,0:T(8,128)(2,1)S(1)}, bf16[32,2048]{1,0:T(8,128)(2,1)S(1)}, u32[]{:S(2)}, u32[]{:S(2)}) collective-permute-start(bf16[32,2048]{1,0:T(8,128)(2,1)S(1)} %get-tuple-element.69), channel_id=1, source_target_pairs={{0,8},{1,9},{2,10},{3,11},{4,12},{5,13},{6,14},{7,15},{8,0},{9,1},... | collective-permute-start | bytes 393224 | tf_op jit(solution)/shard_map/ppermute | solution.py:483
  98.7 10.6 %collective-permute-start.28 = (bf16[32,2048]{1,0:T(8,128)(2,1)S(1)}, bf16[32,2048]{1,0:T(8,128)(2,1)S(1)}, u32[]{:S(2)}, u32[]{:S(2)}) collective-permute-start(bf16[32,2048]{1,0:T(8,128)(2,1)S(1)} %get-tuple-element.71), channel_id=1, source_target_pairs={{0,12},{1,13},{2,14},{3,15},{4,8},{5,9},{6,10},{7,11},{8,4},{9,5},... | collective-permute-start | bytes 393224 | tf_op jit(solution)/shard_map/ppermute | solution.py:483
  100.9 9.0 %collective-permute-start.29 = (bf16[32,2048]{1,0:T(8,128)(2,1)S(1)}, bf16[32,2048]{1,0:T(8,128)(2,1)S(1)}, u32[]{:S(2)}, u32[]{:S(2)}) collective-permute-start(bf16[32,2048]{1,0:T(8,128)(2,1)S(1)} %get-tuple-element.70), channel_id=1, source_target_pairs={{0,4},{1,5},{2,6},{3,7},{4,0},{5,1},{6,2},{7,3},{8,12},{9,13},{10,... | collective-permute-start | bytes 393224 | tf_op jit(solution)/shard_map/ppermute | solution.py:483
  110.2 14.0 %collective-permute-start.30 = (bf16[32,2048]{1,0:T(8,128)(2,1)S(1)}, bf16[32,2048]{1,0:T(8,128)(2,1)S(1)}, u32[]{:S(2)}, u32[]{:S(2)}) collective-permute-start(bf16[32,2048]{1,0:T(8,128)(2,1)S(1)} %get-tuple-element.65), channel_id=1, source_target_pairs={{0,10},{1,11},{2,8},{3,9},{4,14},{5,15},{6,12},{7,13},{8,2},{9,3},... | collective-permute-start | bytes 393224 | tf_op jit(solution)/shard_map/ppermute | solution.py:483
  113.6 10.6 %collective-permute-start.31 = (bf16[32,2048]{1,0:T(8,128)(2,1)S(1)}, bf16[32,2048]{1,0:T(8,128)(2,1)S(1)}, u32[]{:S(2)}, u32[]{:S(2)}) collective-permute-start(bf16[32,2048]{1,0:T(8,128)(2,1)S(1)} %get-tuple-element.68), channel_id=1, source_target_pairs={{0,14},{1,15},{2,12},{3,13},{4,10},{5,11},{6,8},{7,9},{8,6},{9,7},... | collective-permute-start | bytes 393224 | tf_op jit(solution)/shard_map/ppermute | solution.py:483
  115.5 9.6 %collective-permute-start.32 = (bf16[32,2048]{1,0:T(8,128)(2,1)S(1)}, bf16[32,2048]{1,0:T(8,128)(2,1)S(1)}, u32[]{:S(2)}, u32[]{:S(2)}) collective-permute-start(bf16[32,2048]{1,0:T(8,128)(2,1)S(1)} %get-tuple-element.67), channel_id=1, source_target_pairs={{0,6},{1,7},{2,4},{3,5},{4,2},{5,3},{6,0},{7,1},{8,14},{9,15},{10,... | collective-permute-start | bytes 393224 | tf_op jit(solution)/shard_map/ppermute | solution.py:483
  115.5 11.4 %collective-permute-start.33 = (bf16[32,2048]{1,0:T(8,128)(2,1)S(1)}, bf16[32,2048]{1,0:T(8,128)(2,1)S(1)}, u32[]{:S(2)}, u32[]{:S(2)}) collective-permute-start(bf16[32,2048]{1,0:T(8,128)(2,1)S(1)} %get-tuple-element.66), channel_id=1, source_target_pairs={{0,2},{1,3},{2,0},{3,1},{4,6},{5,7},{6,4},{7,5},{8,10},{9,11},{10,... | collective-permute-start | bytes 393224 | tf_op jit(solution)/shard_map/ppermute | solution.py:483
  (21 other events, 160.2 us)

commit v11 on v10

--- a/solution.py
+++ b/solution.py
@@ -536,7 +536,6 @@
     )
     gathered, common, shared, held = lax.optimization_barrier((gathered, common, shared, w_merge))
     mine_y = crossed(shared, 2)
-    common_y = crossed(common, 2)
     attended = pl.pallas_call(
         attend_kernel,
         out_shape=jax.ShapeDtypeStruct((devices, dim, rows), BF),
@@ -546,7 +545,8 @@
         cost_estimate=cost(2**32, 2**22, 2**21),
     )(gathered, grid)
     held_c = crossed(held, 1)
-    attended, mine_y = lax.optimization_barrier((attended, mine_y))
+    attended, mine_y, common = lax.optimization_barrier((attended, mine_y, common))
+    common_y = crossed(common, 2)
     theirs_y = lax.ppermute(mine_y, "grp", [(0, 1), (1, 0)])
     mine_yc = crossed(mine_y, 1)
     returned = lax.all_to_all(attended, "wide", split_axis=0, concat_axis=0, tiled=True)

time: 128 us -> 129 us (level)
    all_to_all x1, waiting for transfers between devices: 0.4 us -> 3.97 us  [local(): lax.all_to_all(attended, 'wide', split_axis=0, concat_axis=0, tiled=True)]
    ppermute x33, waiting for transfers between devices: 38.3 us -> 34.8 us  [crossed(): return lax.ppermute(value, 'wide', pairs)]
    ppermute x33, starting transfers between devices: 29.8 us -> 31.6 us  [crossed(): return lax.ppermute(value, 'wide', pairs)]
    unnamed x20 -> x18, local copies, waits for them, and re-layouts: 3.2 us -> 2.38 us
  transfers between devices with their start and end apart: 36 -> 36, of which waited for: 17 -> 16; matrix products, arithmetic and copies ran while one was open for 1% -> 1% of each run, Pallas kernels for 14% -> 14%
where the time goes in v11:
time: 129 us
  waiting for transfers between devices  58 us (45%)
  starting transfers between devices  42.4 us (33%)
  Pallas kernels  24.1 us (19%)
  local copies, waits for them, and re-layouts  2.6 us (2%)
  other arithmetic  1.38 us (1%)
    ppermute x33, waiting for transfers between devices, crossed(): return lax.ppermute(value, 'wide', pairs)  34.8 us
    ppermute x33, starting transfers between devices, crossed(): return lax.ppermute(value, 'wide', pairs)  31.6 us
    pallas_call x2, Pallas kernels, experts_of(): pl.pallas_call(lambda *refs: expert_kernel(*refs, experts=experts, cuts=c...  13.3 us
    all_to_all x1, waiting for transfers between devices, local(): lax.all_to_all(packed, 'wide', split_axis=0, concat_axis=0, tiled=True, a...  12.4 us
    ppermute x1, waiting for transfers between devices, local(): theirs_y = lax.ppermute(mine_y, 'grp', [(0, 1), (1, 0)])  6.83 us
    all_to_all x1, starting transfers between devices, local(): lax.all_to_all(packed, 'wide', split_axis=0, concat_axis=0, tiled=True, a...  5.25 us
    pallas_call x1, Pallas kernels, local(): pl.pallas_call(attend_kernel, out_shape=jax.ShapeDtypeStruct((devices, di...  4.94 us
    all_to_all x1, starting transfers between devices, local(): lax.all_to_all(attended, 'wide', split_axis=0, concat_axis=0, tiled=True)  4.11 us
  transfers between devices with their start and end apart: 36, of which 16 were waited for; matrix products, arithmetic and copies ran while one was open for 1% of the time, Pallas kernels for 14%

profile of v11, /device:TPU:0, one launch (start us, length us, event | category | flops | bytes accessed | tf_op | source)
XLA Modules:
  0.0 128.8 jit_solution(5955255042249064604)
XLA Ops:
  2.6 5.3 %all-to-all-start = ((bf16[8,432,128]{2,1,0:T(8,128)(2,1)}), bf16[8,432,128]{2,1,0:T(8,128)(2,1)S(1)}, u32[]{:S(2)}, u32[]{:S(2)}) async-start(bf16[8,432,128]{2,1,0:T(8,128)(2,1)} %shard_map.109), calls=%async_computation | async-start | bytes 1769472 | tf_op jit(solution)/shard_map/all_to_all | solution.py:534
  8.2 12.4 %all-to-all-done.x_ref = bf16[8,432,128]{2,1,0:T(8,128)(2,1)S(1)} async-done(((bf16[8,432,128]{2,1,0:T(8,128)(2,1)}), bf16[8,432,128]{2,1,0:T(8,128)(2,1)S(1)}, u32[]{:S(2)}, u32[]{:S(2)}) %all-to-all-start) | async-done | bytes 884768 | tf_op jit(solution)/shard_map/all_to_all | solution.py:534
  22.1 4.9 %shard_map.111 = bf16[16,72,128]{2,1,0:T(8,128)(2,1)} custom-call(bf16[8,432,128]{2,1,0:T(8,128)(2,1)S(1)} %all-to-all-done.x_ref, s32[2,2]{1,0:T(2,128)S(1)} %copy-done.2), custom_call_target="tpu_custom_call" | custom-call | flops 4294967296 | bytes 4194304 | tf_op jit(solution)/shard_map/pallas_call | solution.py:539
  29.9 4.1 %all-to-all-start.1 = ((bf16[16,72,128]{2,1,0:T(8,128)(2,1)}), bf16[16,72,128]{2,1,0:T(8,128)(2,1)S(1)}, u32[]{:S(2)}, u32[]{:S(2)}) async-start(bf16[16,72,128]{2,1,0:T(8,128)(2,1)} %shard_map.111), calls=%async_computation.1 | async-start | bytes 589824 | tf_op jit(solution)/shard_map/all_to_all | solution.py:552
  36.0 6.8 %collective-permute-done.2.refs_4_ = bf16[64,2048]{1,0:T(8,128)(2,1)S(1)} collective-permute-done((bf16[64,2048]{1,0:T(8,128)(2,1)S(1)}, bf16[64,2048]{1,0:T(8,128)(2,1)S(1)}, u32[]{:S(2)}, u32[]{:S(2)}) %collective-permute-start.2) | collective-permute-done | bytes 262176 | tf_op jit(solution)/shard_map/ppermute | solution.py:550
  42.8 4.0 %all-to-all-done.1.x_ref = bf16[16,72,128]{2,1,0:T(8,128)(2,1)S(1)} async-done(((bf16[16,72,128]{2,1,0:T(8,128)(2,1)}), bf16[16,72,128]{2,1,0:T(8,128)(2,1)S(1)}, u32[]{:S(2)}, u32[]{:S(2)}) %all-to-all-start.1) | async-done | bytes 294944 | tf_op jit(solution)/shard_map/all_to_all | solution.py:552
  49.8 3.7 %shard_map.112 = bf16[4,32,2304]{2,1,0:T(8,128)(2,1)S(1)} custom-call(bf16[16,72,128]{2,1,0:T(8,128)(2,1)S(1)} %all-to-all-done.1.x_ref, bf16[1152,1152]{1,0:T(8,128)(2,1)} %w_out_hbm.1, f32[1,4608]{1,0:T(1,128)S(1)} %reshape.8.gain_ref, f32[1,4608]{1,0:T(1,128)S(1)} %reshape.9.bias_ref, bf16[288,2048]{1,0:T(8,128)(2,1)} %refs_0_.1, ...), custom_call_target="tpu_custom_call" | custom-call | tf_op jit(solution)/shard_map/pallas_call | solution.py:557
  53.5 2.7 %collective-permute-start.7 = (bf16[32,2304]{1,0:T(8,128)(2,1)S(1)}, bf16[32,2304]{1,0:T(8,128)(2,1)S(1)}, u32[]{:S(2)}, u32[]{:S(2)}) collective-permute-start(bf16[32,2304]{1,0:T(8,128)(2,1)S(1)} %get-tuple-element.65), channel_id=1, source_target_pairs={{0,8},{1,9},{2,10},{3,11},{4,12},{5,13},{6,14},{7,15},{8,0},{9,1},... | collective-permute-start | bytes 442376 | tf_op jit(solution)/shard_map/ppermute | solution.py:483
  57.5 9.0 %collective-permute-done.7.refs_1_ = bf16[32,2304]{1,0:T(8,128)(2,1)S(1)} collective-permute-done((bf16[32,2304]{1,0:T(8,128)(2,1)S(1)}, bf16[32,2304]{1,0:T(8,128)(2,1)S(1)}, u32[]{:S(2)}, u32[]{:S(2)}) %collective-permute-start.7) | collective-permute-done | bytes 147488 | tf_op jit(solution)/shard_map/ppermute | solution.py:483
  68.6 3.4 %collective-permute-start.10 = (bf16[32,2176]{1,0:T(8,128)(2,1)S(1)}, bf16[32,2176]{1,0:T(8,128)(2,1)S(1)}, u32[]{:S(2)}, u32[]{:S(2)}) collective-permute-start(bf16[32,2176]{1,0:T(8,128)(2,1)S(1)} %shard_map.113.refs_0_), channel_id=1, source_target_pairs={{0,8},{1,9},{2,10},{3,11},{4,12},{5,13},{6,14},{7,15},{8,0},{9,1},... | collective-permute-start | bytes 417800 | tf_op jit(solution)/shard_map/ppermute | solution.py:483
  73.2 1.8 %collective-permute-start.13 = (bf16[32,2176]{1,0:T(8,128)(2,1)S(1)}, bf16[32,2176]{1,0:T(8,128)(2,1)S(1)}, u32[]{:S(2)}, u32[]{:S(2)}) collective-permute-start(bf16[32,2176]{1,0:T(8,128)(2,1)S(1)} %shard_map.113.refs_0_), channel_id=1, source_target_pairs={{0,2},{1,3},{2,0},{3,1},{4,6},{5,7},{6,4},{7,5},{8,10},{9,11},{10,... | collective-permute-start | bytes 417800 | tf_op jit(solution)/shard_map/ppermute | solution.py:483
  75.0 7.5 %collective-permute-done.10.refs_1_ = bf16[32,2176]{1,0:T(8,128)(2,1)S(1)} collective-permute-done((bf16[32,2176]{1,0:T(8,128)(2,1)S(1)}, bf16[32,2176]{1,0:T(8,128)(2,1)S(1)}, u32[]{:S(2)}, u32[]{:S(2)}) %collective-permute-start.10) | collective-permute-done | bytes 139296 | tf_op jit(solution)/shard_map/ppermute | solution.py:483
  83.6 1.8 %collective-permute-start.14 = (bf16[32,2176]{1,0:T(8,128)(2,1)S(1)}, bf16[32,2176]{1,0:T(8,128)(2,1)S(1)}, u32[]{:S(2)}, u32[]{:S(2)}) collective-permute-start(bf16[32,2176]{1,0:T(8,128)(2,1)S(1)} %collective-permute-done.10.refs_1_), channel_id=1, source_target_pairs={{0,2},{1,3},{2,0},{3,1},{4,6},{5,7},{6,4},{7,5},{8,10},{9,11},{10,... | collective-permute-start | bytes 417800 | tf_op jit(solution)/shard_map/ppermute | solution.py:483
  85.8 1.7 %collective-permute-start.16 = (bf16[32,2176]{1,0:T(8,128)(2,1)S(1)}, bf16[32,2176]{1,0:T(8,128)(2,1)S(1)}, u32[]{:S(2)}, u32[]{:S(2)}) collective-permute-start(bf16[32,2176]{1,0:T(8,128)(2,1)S(1)} %collective-permute-done.12.refs_3_), channel_id=1, source_target_pairs={{0,2},{1,3},{2,0},{3,1},{4,6},{5,7},{6,4},{7,5},{8,10},{9,11},{10,... | collective-permute-start | bytes 417800 | tf_op jit(solution)/shard_map/ppermute | solution.py:483
  87.5 6.7 %shard_map.114 = (bf16[4,32,2048]{2,1,0:T(8,128)(2,1)S(1)}, bf16[4,32,2048]{2,1,0:T(8,128)(2,1)S(1)}) custom-call(bf16[32,2176]{1,0:T(8,128)(2,1)S(1)} %shard_map.113.refs_0_, bf16[32,2176]{1,0:T(8,128)(2,1)S(1)} %collective-permute-done.10.refs_1_, bf16[32,2176]{1,0:T(8,128)(2,1)S(1)} %collective-permute-done.11.refs_2_, ...), custom_call_target="tpu_custom_call" | custom-call | flops 4294967296 | bytes 16777216 | tf_op jit(solution)/shard_map/pallas_call | solution.py:604
  97.4 2.6 %collective-permute-start.27 = (bf16[32,2048]{1,0:T(8,128)(2,1)S(1)}, bf16[32,2048]{1,0:T(8,128)(2,1)S(1)}, u32[]{:S(2)}, u32[]{:S(2)}) collective-permute-start(bf16[32,2048]{1,0:T(8,128)(2,1)S(1)} %get-tuple-element.71), channel_id=1, source_target_pairs={{0,8},{1,9},{2,10},{3,11},{4,12},{5,13},{6,14},{7,15},{8,0},{9,1},... | collective-permute-start | bytes 393224 | tf_op jit(solution)/shard_map/ppermute | solution.py:483
  100.0 1.9 %collective-permute-start.28 = (bf16[32,2048]{1,0:T(8,128)(2,1)S(1)}, bf16[32,2048]{1,0:T(8,128)(2,1)S(1)}, u32[]{:S(2)}, u32[]{:S(2)}) collective-permute-start(bf16[32,2048]{1,0:T(8,128)(2,1)S(1)} %get-tuple-element.73), channel_id=1, source_target_pairs={{0,12},{1,13},{2,14},{3,15},{4,8},{5,9},{6,10},{7,11},{8,4},{9,5},... | collective-permute-start | bytes 393224 | tf_op jit(solution)/shard_map/ppermute | solution.py:483
  101.9 6.7 %shard_map.115 = (bf16[4,32,2048]{2,1,0:T(8,128)(2,1)S(1)}, bf16[4,32,2048]{2,1,0:T(8,128)(2,1)S(1)}) custom-call(bf16[32,2176]{1,0:T(8,128)(2,1)S(1)} %collective-permute-done.13.refs_0_, bf16[32,2176]{1,0:T(8,128)(2,1)S(1)} %collective-permute-done.14.refs_1_, bf16[32,2176]{1,0:T(8,128)(2,1)S(1)} %collective-permute-done.15.refs_2_, ...), custom_call_target="tpu_custom_call" | custom-call | flops 4294967296 | bytes 16777216 | tf_op jit(solution)/shard_map/pallas_call | solution.py:604
  108.6 1.7 %collective-permute-done.27 = bf16[32,2048]{1,0:T(8,128)(2,1)S(1)} collective-permute-done((bf16[32,2048]{1,0:T(8,128)(2,1)S(1)}, bf16[32,2048]{1,0:T(8,128)(2,1)S(1)}, u32[]{:S(2)}, u32[]{:S(2)}) %collective-permute-start.27) | collective-permute-done | bytes 131104 | tf_op jit(solution)/shard_map/ppermute | solution.py:483
  111.1 3.8 %collective-permute-start.30 = (bf16[32,2048]{1,0:T(8,128)(2,1)S(1)}, bf16[32,2048]{1,0:T(8,128)(2,1)S(1)}, u32[]{:S(2)}, u32[]{:S(2)}) collective-permute-start(bf16[32,2048]{1,0:T(8,128)(2,1)S(1)} %get-tuple-element.67), channel_id=1, source_target_pairs={{0,10},{1,11},{2,8},{3,9},{4,14},{5,15},{6,12},{7,13},{8,2},{9,3},... | collective-permute-start | bytes 393224 | tf_op jit(solution)/shard_map/ppermute | solution.py:483
  114.9 1.6 %collective-permute-start.31 = (bf16[32,2048]{1,0:T(8,128)(2,1)S(1)}, bf16[32,2048]{1,0:T(8,128)(2,1)S(1)}, u32[]{:S(2)}, u32[]{:S(2)}) collective-permute-start(bf16[32,2048]{1,0:T(8,128)(2,1)S(1)} %get-tuple-element.70), channel_id=1, source_target_pairs={{0,14},{1,15},{2,12},{3,13},{4,10},{5,11},{6,8},{7,9},{8,6},{9,7},... | collective-permute-start | bytes 393224 | tf_op jit(solution)/shard_map/ppermute | solution.py:483
  116.8 1.5 %collective-permute-start.33 = (bf16[32,2048]{1,0:T(8,128)(2,1)S(1)}, bf16[32,2048]{1,0:T(8,128)(2,1)S(1)}, u32[]{:S(2)}, u32[]{:S(2)}) collective-permute-start(bf16[32,2048]{1,0:T(8,128)(2,1)S(1)} %get-tuple-element.68), channel_id=1, source_target_pairs={{0,2},{1,3},{2,0},{3,1},{4,6},{5,7},{6,4},{7,5},{8,10},{9,11},{10,... | collective-permute-start | bytes 393224 | tf_op jit(solution)/shard_map/ppermute | solution.py:483
  118.3 6.9 %collective-permute-done.30 = bf16[32,2048]{1,0:T(8,128)(2,1)S(1)} collective-permute-done((bf16[32,2048]{1,0:T(8,128)(2,1)S(1)}, bf16[32,2048]{1,0:T(8,128)(2,1)S(1)}, u32[]{:S(2)}, u32[]{:S(2)}) %collective-permute-start.30) | collective-permute-done | bytes 131104 | tf_op jit(solution)/shard_map/ppermute | solution.py:483
  126.2 1.8 %collective-permute-done.33 = bf16[32,2048]{1,0:T(8,128)(2,1)S(1)} collective-permute-done((bf16[32,2048]{1,0:T(8,128)(2,1)S(1)}, bf16[32,2048]{1,0:T(8,128)(2,1)S(1)}, u32[]{:S(2)}, u32[]{:S(2)}) %collective-permute-start.33) | collective-permute-done | bytes 131104 | tf_op jit(solution)/shard_map/ppermute | solution.py:483
  (85 shorter events, 24.3 us)
Async XLA Ops:
  2.6 18.0 %all-to-all-start = ((bf16[8,432,128]{2,1,0:T(8,128)(2,1)}), bf16[8,432,128]{2,1,0:T(8,128)(2,1)S(1)}, u32[]{:S(2)}, u32[]{:S(2)}) async-start(bf16[8,432,128]{2,1,0:T(8,128)(2,1)} %shard_map.109), calls=%async_computation | async-start | bytes 1769472 | tf_op jit(solution)/shard_map/all_to_all | solution.py:534
  20.6 7.8 %collective-permute-start = (bf16[64,2048]{1,0:T(8,128)(2,1)S(1)}, bf16[64,2048]{1,0:T(8,128)(2,1)S(1)}, u32[]{:S(2)}, u32[]{:S(2)}) collective-permute-start(bf16[64,2048]{1,0:T(8,128)(2,1)S(1)} %get-tuple-element.37), channel_id=1, source_target_pairs={{0,2},{1,3},{2,0},{3,1},{4,6},{5,7},{6,4},{7,5},{8,10},{9,11},{10,... | collective-permute-start | bytes 786440 | tf_op jit(solution)/shard_map/ppermute | solution.py:483
  28.5 18.3 %collective-permute-start.1 = (bf16[160,2048]{1,0:T(8,128)(2,1)S(1)}, bf16[160,2048]{1,0:T(8,128)(2,1)S(1)}, u32[]{:S(2)}, u32[]{:S(2)}) collective-permute-start(bf16[160,2048]{1,0:T(8,128)(2,1)S(1)} %get-tuple-element.40), channel_id=1, source_target_pairs={{0,2},{1,3},{2,0},{3,1},{4,6},{5,7},{6,4},{7,5},{8,10},{9,11},{10,... | collective-permute-start | bytes 1966088 | tf_op jit(solution)/shard_map/ppermute | solution.py:483
  29.9 16.9 %all-to-all-start.1 = ((bf16[16,72,128]{2,1,0:T(8,128)(2,1)}), bf16[16,72,128]{2,1,0:T(8,128)(2,1)S(1)}, u32[]{:S(2)}, u32[]{:S(2)}) async-start(bf16[16,72,128]{2,1,0:T(8,128)(2,1)} %shard_map.111), calls=%async_computation.1 | async-start | bytes 589824 | tf_op jit(solution)/shard_map/all_to_all | solution.py:552
  34.0 15.7 %collective-permute-start.3 = (bf16[288,2048]{1,0:T(8,128)(2,1)S(1)}, bf16[288,2048]{1,0:T(8,128)(2,1)}, u32[]{:S(2)}, u32[]{:S(2)}) collective-permute-start(bf16[288,2048]{1,0:T(8,128)(2,1)S(1)} %copy-done), channel_id=1, source_target_pairs={{0,1},{1,0},{2,3},{3,2},{4,5},{5,4},{6,7},{7,6},{8,9},{9,8},{10,11... | collective-permute-start | bytes 3538952 | tf_op jit(solution)/shard_map/ppermute | solution.py:483
  34.5 8.3 %collective-permute-start.2 = (bf16[64,2048]{1,0:T(8,128)(2,1)S(1)}, bf16[64,2048]{1,0:T(8,128)(2,1)S(1)}, u32[]{:S(2)}, u32[]{:S(2)}) collective-permute-start(bf16[64,2048]{1,0:T(8,128)(2,1)S(1)} %collective-permute-done.refs_3_), channel_id=1, source_target_pairs={{0,16},{16,0},{1,17},{17,1},{2,18},{18,2},{3,19},{19,3},{4,20},{20... | collective-permute-start | bytes 786440 | tf_op jit(solution)/shard_map/ppermute | solution.py:550
  53.5 13.0 %collective-permute-start.7 = (bf16[32,2304]{1,0:T(8,128)(2,1)S(1)}, bf16[32,2304]{1,0:T(8,128)(2,1)S(1)}, u32[]{:S(2)}, u32[]{:S(2)}) collective-permute-start(bf16[32,2304]{1,0:T(8,128)(2,1)S(1)} %get-tuple-element.65), channel_id=1, source_target_pairs={{0,8},{1,9},{2,10},{3,11},{4,12},{5,13},{6,14},{7,15},{8,0},{9,1},... | collective-permute-start | bytes 442376 | tf_op jit(solution)/shard_map/ppermute | solution.py:483
  56.2 10.4 %collective-permute-start.8 = (bf16[32,2304]{1,0:T(8,128)(2,1)S(1)}, bf16[32,2304]{1,0:T(8,128)(2,1)S(1)}, u32[]{:S(2)}, u32[]{:S(2)}) collective-permute-start(bf16[32,2304]{1,0:T(8,128)(2,1)S(1)} %get-tuple-element.64), channel_id=1, source_target_pairs={{0,12},{1,13},{2,14},{3,15},{4,8},{5,9},{6,10},{7,11},{8,4},{9,5},... | collective-permute-start | bytes 442376 | tf_op jit(solution)/shard_map/ppermute | solution.py:483
  56.2 11.8 %collective-permute-start.9 = (bf16[32,2304]{1,0:T(8,128)(2,1)S(1)}, bf16[32,2304]{1,0:T(8,128)(2,1)S(1)}, u32[]{:S(2)}, u32[]{:S(2)}) collective-permute-start(bf16[32,2304]{1,0:T(8,128)(2,1)S(1)} %get-tuple-element.63), channel_id=1, source_target_pairs={{0,4},{1,5},{2,6},{3,7},{4,0},{5,1},{6,2},{7,3},{8,12},{9,13},{10,... | collective-permute-start | bytes 442376 | tf_op jit(solution)/shard_map/ppermute | solution.py:483
  68.6 14.0 %collective-permute-start.10 = (bf16[32,2176]{1,0:T(8,128)(2,1)S(1)}, bf16[32,2176]{1,0:T(8,128)(2,1)S(1)}, u32[]{:S(2)}, u32[]{:S(2)}) collective-permute-start(bf16[32,2176]{1,0:T(8,128)(2,1)S(1)} %shard_map.113.refs_0_), channel_id=1, source_target_pairs={{0,8},{1,9},{2,10},{3,11},{4,12},{5,13},{6,14},{7,15},{8,0},{9,1},... | collective-permute-start | bytes 417800 | tf_op jit(solution)/shard_map/ppermute | solution.py:483
  71.9 10.6 %collective-permute-start.11 = (bf16[32,2176]{1,0:T(8,128)(2,1)S(1)}, bf16[32,2176]{1,0:T(8,128)(2,1)S(1)}, u32[]{:S(2)}, u32[]{:S(2)}) collective-permute-start(bf16[32,2176]{1,0:T(8,128)(2,1)S(1)} %shard_map.113.refs_0_), channel_id=1, source_target_pairs={{0,12},{1,13},{2,14},{3,15},{4,8},{5,9},{6,10},{7,11},{8,4},{9,5},... | collective-permute-start | bytes 417800 | tf_op jit(solution)/shard_map/ppermute | solution.py:483
  73.2 9.4 %collective-permute-start.12 = (bf16[32,2176]{1,0:T(8,128)(2,1)S(1)}, bf16[32,2176]{1,0:T(8,128)(2,1)S(1)}, u32[]{:S(2)}, u32[]{:S(2)}) collective-permute-start(bf16[32,2176]{1,0:T(8,128)(2,1)S(1)} %shard_map.113.refs_0_), channel_id=1, source_target_pairs={{0,4},{1,5},{2,6},{3,7},{4,0},{5,1},{6,2},{7,3},{8,12},{9,13},{10,... | collective-permute-start | bytes 417800 | tf_op jit(solution)/shard_map/ppermute | solution.py:483
  73.2 9.4 %collective-permute-start.13 = (bf16[32,2176]{1,0:T(8,128)(2,1)S(1)}, bf16[32,2176]{1,0:T(8,128)(2,1)S(1)}, u32[]{:S(2)}, u32[]{:S(2)}) collective-permute-start(bf16[32,2176]{1,0:T(8,128)(2,1)S(1)} %shard_map.113.refs_0_), channel_id=1, source_target_pairs={{0,2},{1,3},{2,0},{3,1},{4,6},{5,7},{6,4},{7,5},{8,10},{9,11},{10,... | collective-permute-start | bytes 417800 | tf_op jit(solution)/shard_map/ppermute | solution.py:483
  83.6 10.5 %collective-permute-start.14 = (bf16[32,2176]{1,0:T(8,128)(2,1)S(1)}, bf16[32,2176]{1,0:T(8,128)(2,1)S(1)}, u32[]{:S(2)}, u32[]{:S(2)}) collective-permute-start(bf16[32,2176]{1,0:T(8,128)(2,1)S(1)} %collective-permute-done.10.refs_1_), channel_id=1, source_target_pairs={{0,2},{1,3},{2,0},{3,1},{4,6},{5,7},{6,4},{7,5},{8,10},{9,11},{10,... | collective-permute-start | bytes 417800 | tf_op jit(solution)/shard_map/ppermute | solution.py:483
  85.4 8.7 %collective-permute-start.15 = (bf16[32,2176]{1,0:T(8,128)(2,1)S(1)}, bf16[32,2176]{1,0:T(8,128)(2,1)S(1)}, u32[]{:S(2)}, u32[]{:S(2)}) collective-permute-start(bf16[32,2176]{1,0:T(8,128)(2,1)S(1)} %collective-permute-done.11.refs_2_), channel_id=1, source_target_pairs={{0,2},{1,3},{2,0},{3,1},{4,6},{5,7},{6,4},{7,5},{8,10},{9,11},{10,... | collective-permute-start | bytes 417800 | tf_op jit(solution)/shard_map/ppermute | solution.py:483
  85.8 9.5 %collective-permute-start.16 = (bf16[32,2176]{1,0:T(8,128)(2,1)S(1)}, bf16[32,2176]{1,0:T(8,128)(2,1)S(1)}, u32[]{:S(2)}, u32[]{:S(2)}) collective-permute-start(bf16[32,2176]{1,0:T(8,128)(2,1)S(1)} %collective-permute-done.12.refs_3_), channel_id=1, source_target_pairs={{0,2},{1,3},{2,0},{3,1},{4,6},{5,7},{6,4},{7,5},{8,10},{9,11},{10,... | collective-permute-start | bytes 417800 | tf_op jit(solution)/shard_map/ppermute | solution.py:483
  95.8 6.0 %collective-permute-start.23 = (bf16[32,2176]{1,0:T(8,128)(2,1)S(1)}, bf16[32,2176]{1,0:T(8,128)(2,1)S(1)}, u32[]{:S(2)}, u32[]{:S(2)}) collective-permute-start(bf16[32,2176]{1,0:T(8,128)(2,1)S(1)} %collective-permute-done.15.refs_2_), channel_id=1, source_target_pairs={{0,1},{1,0},{2,3},{3,2},{4,5},{5,4},{6,7},{7,6},{8,9},{9,8},{10,11... | collective-permute-start | bytes 417800 | tf_op jit(solution)/shard_map/ppermute | solution.py:483
  97.4 13.0 %collective-permute-start.27 = (bf16[32,2048]{1,0:T(8,128)(2,1)S(1)}, bf16[32,2048]{1,0:T(8,128)(2,1)S(1)}, u32[]{:S(2)}, u32[]{:S(2)}) collective-permute-start(bf16[32,2048]{1,0:T(8,128)(2,1)S(1)} %get-tuple-element.71), channel_id=1, source_target_pairs={{0,8},{1,9},{2,10},{3,11},{4,12},{5,13},{6,14},{7,15},{8,0},{9,1},... | collective-permute-start | bytes 393224 | tf_op jit(solution)/shard_map/ppermute | solution.py:483
  100.0 10.4 %collective-permute-start.28 = (bf16[32,2048]{1,0:T(8,128)(2,1)S(1)}, bf16[32,2048]{1,0:T(8,128)(2,1)S(1)}, u32[]{:S(2)}, u32[]{:S(2)}) collective-permute-start(bf16[32,2048]{1,0:T(8,128)(2,1)S(1)} %get-tuple-element.73), channel_id=1, source_target_pairs={{0,12},{1,13},{2,14},{3,15},{4,8},{5,9},{6,10},{7,11},{8,4},{9,5},... | collective-permute-start | bytes 393224 | tf_op jit(solution)/shard_map/ppermute | solution.py:483
  101.9 9.0 %collective-permute-start.29 = (bf16[32,2048]{1,0:T(8,128)(2,1)S(1)}, bf16[32,2048]{1,0:T(8,128)(2,1)S(1)}, u32[]{:S(2)}, u32[]{:S(2)}) collective-permute-start(bf16[32,2048]{1,0:T(8,128)(2,1)S(1)} %get-tuple-element.72), channel_id=1, source_target_pairs={{0,4},{1,5},{2,6},{3,7},{4,0},{5,1},{6,2},{7,3},{8,12},{9,13},{10,... | collective-permute-start | bytes 393224 | tf_op jit(solution)/shard_map/ppermute | solution.py:483
  111.1 14.0 %collective-permute-start.30 = (bf16[32,2048]{1,0:T(8,128)(2,1)S(1)}, bf16[32,2048]{1,0:T(8,128)(2,1)S(1)}, u32[]{:S(2)}, u32[]{:S(2)}) collective-permute-start(bf16[32,2048]{1,0:T(8,128)(2,1)S(1)} %get-tuple-element.67), channel_id=1, source_target_pairs={{0,10},{1,11},{2,8},{3,9},{4,14},{5,15},{6,12},{7,13},{8,2},{9,3},... | collective-permute-start | bytes 393224 | tf_op jit(solution)/shard_map/ppermute | solution.py:483
  114.9 10.2 %collective-permute-start.31 = (bf16[32,2048]{1,0:T(8,128)(2,1)S(1)}, bf16[32,2048]{1,0:T(8,128)(2,1)S(1)}, u32[]{:S(2)}, u32[]{:S(2)}) collective-permute-start(bf16[32,2048]{1,0:T(8,128)(2,1)S(1)} %get-tuple-element.70), channel_id=1, source_target_pairs={{0,14},{1,15},{2,12},{3,13},{4,10},{5,11},{6,8},{7,9},{8,6},{9,7},... | collective-permute-start | bytes 393224 | tf_op jit(solution)/shard_map/ppermute | solution.py:483
  116.5 9.7 %collective-permute-start.32 = (bf16[32,2048]{1,0:T(8,128)(2,1)S(1)}, bf16[32,2048]{1,0:T(8,128)(2,1)S(1)}, u32[]{:S(2)}, u32[]{:S(2)}) collective-permute-start(bf16[32,2048]{1,0:T(8,128)(2,1)S(1)} %get-tuple-element.69), channel_id=1, source_target_pairs={{0,6},{1,7},{2,4},{3,5},{4,2},{5,3},{6,0},{7,1},{8,14},{9,15},{10,... | collective-permute-start | bytes 393224 | tf_op jit(solution)/shard_map/ppermute | solution.py:483
  116.8 11.3 %collective-permute-start.33 = (bf16[32,2048]{1,0:T(8,128)(2,1)S(1)}, bf16[32,2048]{1,0:T(8,128)(2,1)S(1)}, u32[]{:S(2)}, u32[]{:S(2)}) collective-permute-start(bf16[32,2048]{1,0:T(8,128)(2,1)S(1)} %get-tuple-element.68), channel_id=1, source_target_pairs={{0,2},{1,3},{2,0},{3,1},{4,6},{5,7},{6,4},{7,5},{8,10},{9,11},{10,... | collective-permute-start | bytes 393224 | tf_op jit(solution)/shard_map/ppermute | solution.py:483
  (20 other events, 164.4 us)

commit v12 on v10

--- a/solution.py
+++ b/solution.py
@@ -430,7 +430,8 @@
 def expert_kernel(*refs, experts, cuts):
     *blocks, gate_hbm, up_hbm, down_hbm, own_ref, other_ref, x_ref, gate_ref, up_ref, down_ref, sems = refs
     tokens, width = own_ref.shape[1:]
-    half = len(blocks) // 2
+    half = own_ref.shape[0]
+    places = [(b, slice(r, r + tokens)) for b in blocks for r in range(0, b.shape[0], tokens)]
     copies = []
     for k, cut in enumerate(cuts):
         for kind, source, target in ((0, gate_hbm, gate_ref), (1, up_hbm, up_ref)):
@@ -441,10 +442,10 @@
     expert = lax.axis_index("wide") // 2
     lane = lax.broadcasted_iota(jnp.int32, (tokens, LANES), 1)
     weights = []
-    for k, block in enumerate(blocks):
-        x_ref[k * tokens : (k + 1) * tokens, :] = block[:, :width]
+    for k, (block, rows) in enumerate(places):
+        x_ref[k * tokens : (k + 1) * tokens, :] = block[rows, :width]
         picked = (lane == expert) | (lane == expert + experts)
-        picked = jnp.where(picked, block[:, width:].astype(F32), 0.0)
+        picked = jnp.where(picked, block[rows, width:].astype(F32), 0.0)
         weights.append(jnp.sum(picked, axis=1, keepdims=True))
     inputs = x_ref[...]
     turned = (((1,), (1,)), ((), ()))
@@ -472,10 +473,17 @@
     for begin in range(0, width, step):
         product = following
         following = product_of(begin + step) if begin + step < width else None
-        for k in range(len(blocks)):
+        for k in range(len(places)):
             value = (product[k * tokens : (k + 1) * tokens] * weights[k]).astype(BF)
             out_ref = own_ref if k < half else other_ref
             out_ref[k % half, :, begin : begin + step] = value
+
+
+def join_kernel(*refs):
+    *blocks, out_ref = refs
+    rows = blocks[0].shape[0]
+    for k, block in enumerate(blocks):
+        out_ref[k * rows : (k + 1) * rows, :] = block[...]
 
 
 def crossed(value, mask):
@@ -592,7 +600,14 @@
         out_specs=VMEM,
         compiler_params=params(6),
     )(*arrived, router, expert_ids)
-    near = [routed] + [crossed(routed, mask) for mask in along]
+    joined = pl.pallas_call(
+        join_kernel,
+        out_shape=jax.ShapeDtypeStruct((len(along) * tokens, out_width + LANES), BF),
+        in_specs=[VMEM] * len(along),
+        out_specs=VMEM,
+        compiler_params=params(6),
+    )(*[crossed(routed, mask) for mask in along])
+    near = [routed, joined]
     far = [crossed(block, 2) for block in near]
     *near, far[0] = lax.optimization_barrier((*near, far[0]))
     gate_turned, up_turned = jnp.swapaxes(w_gate, 1, 2), jnp.swapaxes(w_up, 1, 2)
@@ -604,7 +619,7 @@
         return pl.pallas_call(
             lambda *refs: expert_kernel(*refs, experts=experts, cuts=cuts),
             out_shape=[jax.ShapeDtypeStruct((planes, tokens, out_width), BF)] * 2,
-            in_specs=[VMEM] * (2 * planes) + [HBM] * 3,
+            in_specs=[VMEM] * (2 * len(blocks)) + [HBM] * 3,
             out_specs=[VMEM, VMEM],
             scratch_shapes=[
                 pltpu.VMEM((2 * planes * tokens, out_width), BF),

time: 128 us -> 128 us (level)
  starting transfers between devices: 41.4 us -> 38.5 us
  waiting for transfers between devices: 57.1 us -> 59.6 us
    ppermute x33 -> x27, starting transfers between devices: 29.8 us -> 26.8 us  [crossed(): return lax.ppermute(value, 'wide', pairs)]
    ppermute x33 -> x27, waiting for transfers between devices: 38.3 us -> 40.8 us  [crossed(): return lax.ppermute(value, 'wide', pairs)]
  transfers between devices with their start and end apart: 36 -> 30, of which waited for: 17 -> 18; matrix products, arithmetic and copies ran while one was open for 1% -> 1% of each run, Pallas kernels for 14% -> 15%
where the time goes in v12:
time: 128 us; the launch traced here: 127 us
  waiting for transfers between devices  59.6 us (47%)
  starting transfers between devices  38.5 us (30%)
  Pallas kernels  24.1 us (19%)
  local copies, waits for them, and re-layouts  3.44 us (3%)
  other arithmetic  1.38 us (1%)
    ppermute x27, waiting for transfers between devices, crossed(): return lax.ppermute(value, 'wide', pairs)  40.8 us
    ppermute x27, starting transfers between devices, crossed(): return lax.ppermute(value, 'wide', pairs)  26.8 us
    pallas_call x2, Pallas kernels, experts_of(): pl.pallas_call(lambda *refs: expert_kernel(*refs, experts=experts, cuts=c...  13.3 us
    all_to_all x1, waiting for transfers between devices, local(): lax.all_to_all(packed, 'wide', split_axis=0, concat_axis=0, tiled=True, a...  11.6 us
    ppermute x1, waiting for transfers between devices, local(): theirs_y = lax.ppermute(mine_y, 'grp', [(0, 1), (1, 0)])  6.83 us
    all_to_all x1, starting transfers between devices, local(): lax.all_to_all(packed, 'wide', split_axis=0, concat_axis=0, tiled=True, a...  5.25 us
    pallas_call x1, Pallas kernels, local(): pl.pallas_call(attend_kernel, out_shape=jax.ShapeDtypeStruct((devices, di...  4.92 us
    all_to_all x1, starting transfers between devices, local(): lax.all_to_all(attended, 'wide', split_axis=0, concat_axis=0, tiled=True)  4.9 us
  transfers between devices with their start and end apart: 30, of which 18 were waited for; matrix products, arithmetic and copies ran while one was open for 1% of the time, Pallas kernels for 15%

profile of v12, /device:TPU:0, one launch (start us, length us, event | category | flops | bytes accessed | tf_op | source)
XLA Modules:
  0.0 127.3 jit_solution(2135681194266282193)
XLA Ops:
  2.6 5.3 %all-to-all-start = ((bf16[8,432,128]{2,1,0:T(8,128)(2,1)}), bf16[8,432,128]{2,1,0:T(8,128)(2,1)S(1)}, u32[]{:S(2)}, u32[]{:S(2)}) async-start(bf16[8,432,128]{2,1,0:T(8,128)(2,1)} %shard_map.109), calls=%async_computation | async-start | bytes 1769472 | tf_op jit(solution)/shard_map/all_to_all | solution.py:542
  9.0 11.6 %all-to-all-done.x_ref = bf16[8,432,128]{2,1,0:T(8,128)(2,1)S(1)} async-done(((bf16[8,432,128]{2,1,0:T(8,128)(2,1)}), bf16[8,432,128]{2,1,0:T(8,128)(2,1)S(1)}, u32[]{:S(2)}, u32[]{:S(2)}) %all-to-all-start) | async-done | bytes 884768 | tf_op jit(solution)/shard_map/all_to_all | solution.py:542
  22.6 4.9 %shard_map.111 = bf16[16,72,128]{2,1,0:T(8,128)(2,1)} custom-call(bf16[8,432,128]{2,1,0:T(8,128)(2,1)S(1)} %all-to-all-done.x_ref, s32[2,2]{1,0:T(2,128)S(1)} %copy-done.3), custom_call_target="tpu_custom_call" | custom-call | flops 4294967296 | bytes 4194304 | tf_op jit(solution)/shard_map/pallas_call | solution.py:548
  27.5 2.3 %collective-permute-done.refs_3_ = bf16[64,2048]{1,0:T(8,128)(2,1)S(1)} collective-permute-done((bf16[64,2048]{1,0:T(8,128)(2,1)S(1)}, bf16[64,2048]{1,0:T(8,128)(2,1)S(1)}, u32[]{:S(2)}, u32[]{:S(2)}) %collective-permute-start) | collective-permute-done | bytes 262176 | tf_op jit(solution)/shard_map/ppermute | solution.py:491
  29.8 4.9 %all-to-all-start.1 = ((bf16[16,72,128]{2,1,0:T(8,128)(2,1)}), bf16[16,72,128]{2,1,0:T(8,128)(2,1)S(1)}, u32[]{:S(2)}, u32[]{:S(2)}) async-start(bf16[16,72,128]{2,1,0:T(8,128)(2,1)} %shard_map.111), calls=%async_computation.1 | async-start | bytes 589824 | tf_op jit(solution)/shard_map/all_to_all | solution.py:560
  35.2 1.5 %collective-permute-start.2 = (bf16[64,2048]{1,0:T(8,128)(2,1)S(1)}, bf16[64,2048]{1,0:T(8,128)(2,1)S(1)}, u32[]{:S(2)}, u32[]{:S(2)}) collective-permute-start(bf16[64,2048]{1,0:T(8,128)(2,1)S(1)} %collective-permute-done.refs_3_), channel_id=1, source_target_pairs={{0,16},{16,0},{1,17},{17,1},{2,18},{18,2},{3,19},{19,3},{4,20},{20... | collective-permute-start | bytes 786440 | tf_op jit(solution)/shard_map/ppermute | solution.py:558
  36.7 6.8 %collective-permute-done.2.refs_4_ = bf16[64,2048]{1,0:T(8,128)(2,1)S(1)} collective-permute-done((bf16[64,2048]{1,0:T(8,128)(2,1)S(1)}, bf16[64,2048]{1,0:T(8,128)(2,1)S(1)}, u32[]{:S(2)}, u32[]{:S(2)}) %collective-permute-start.2) | collective-permute-done | bytes 262176 | tf_op jit(solution)/shard_map/ppermute | solution.py:558
  43.5 1.5 %collective-permute-done.1.refs_2_ = bf16[160,2048]{1,0:T(8,128)(2,1)S(1)} collective-permute-done((bf16[160,2048]{1,0:T(8,128)(2,1)}, bf16[160,2048]{1,0:T(8,128)(2,1)S(1)}, u32[]{:S(2)}, u32[]{:S(2)}) %collective-permute-start.1) | collective-permute-done | bytes 655392 | tf_op jit(solution)/shard_map/ppermute | solution.py:491
  48.4 3.7 %shard_map.112 = bf16[4,32,2304]{2,1,0:T(8,128)(2,1)S(1)} custom-call(bf16[16,72,128]{2,1,0:T(8,128)(2,1)S(1)} %all-to-all-done.1.x_ref, bf16[1152,1152]{1,0:T(8,128)(2,1)} %w_out_hbm.1, f32[1,4608]{1,0:T(1,128)S(1)} %reshape.8.gain_ref, f32[1,4608]{1,0:T(1,128)S(1)} %reshape.9.bias_ref, bf16[288,2048]{1,0:T(8,128)(2,1)} %refs_0_.1, ...), custom_call_target="tpu_custom_call" | custom-call | tf_op jit(solution)/shard_map/pallas_call | solution.py:565
  52.2 2.6 %collective-permute-start.7 = (bf16[32,2304]{1,0:T(8,128)(2,1)S(1)}, bf16[32,2304]{1,0:T(8,128)(2,1)S(1)}, u32[]{:S(2)}, u32[]{:S(2)}) collective-permute-start(bf16[32,2304]{1,0:T(8,128)(2,1)S(1)} %get-tuple-element.55), channel_id=1, source_target_pairs={{0,8},{1,9},{2,10},{3,11},{4,12},{5,13},{6,14},{7,15},{8,0},{9,1},... | collective-permute-start | bytes 442376 | tf_op jit(solution)/shard_map/ppermute | solution.py:491
  56.2 9.4 %collective-permute-done.7.refs_1_ = bf16[32,2304]{1,0:T(8,128)(2,1)S(1)} collective-permute-done((bf16[32,2304]{1,0:T(8,128)(2,1)S(1)}, bf16[32,2304]{1,0:T(8,128)(2,1)S(1)}, u32[]{:S(2)}, u32[]{:S(2)}) %collective-permute-start.7) | collective-permute-done | bytes 147488 | tf_op jit(solution)/shard_map/ppermute | solution.py:491
  67.3 3.7 %collective-permute-start.10 = (bf16[32,2176]{1,0:T(8,128)(2,1)S(1)}, bf16[32,2176]{1,0:T(8,128)(2,1)S(1)}, u32[]{:S(2)}, u32[]{:S(2)}) collective-permute-start(bf16[32,2176]{1,0:T(8,128)(2,1)S(1)} %shard_map.113.refs_0_), channel_id=1, source_target_pairs={{0,8},{1,9},{2,10},{3,11},{4,12},{5,13},{6,14},{7,15},{8,0},{9,1},... | collective-permute-start | bytes 417800 | tf_op jit(solution)/shard_map/ppermute | solution.py:491
  72.1 1.5 %collective-permute-start.13 = (bf16[32,2176]{1,0:T(8,128)(2,1)S(1)}, bf16[32,2176]{1,0:T(8,128)(2,1)S(1)}, u32[]{:S(2)}, u32[]{:S(2)}) collective-permute-start(bf16[32,2176]{1,0:T(8,128)(2,1)S(1)} %shard_map.113.refs_0_), channel_id=1, source_target_pairs={{0,2},{1,3},{2,0},{3,1},{4,6},{5,7},{6,4},{7,5},{8,10},{9,11},{10,... | collective-permute-start | bytes 417800 | tf_op jit(solution)/shard_map/ppermute | solution.py:491
  73.6 8.0 %collective-permute-done.10.refs_0_ = bf16[32,2176]{1,0:T(8,128)(2,1)S(1)} collective-permute-done((bf16[32,2176]{1,0:T(8,128)(2,1)S(1)}, bf16[32,2176]{1,0:T(8,128)(2,1)S(1)}, u32[]{:S(2)}, u32[]{:S(2)}) %collective-permute-start.10) | collective-permute-done | bytes 139296 | tf_op jit(solution)/shard_map/ppermute | solution.py:491
  83.7 6.7 %shard_map.115 = (bf16[4,32,2048]{2,1,0:T(8,128)(2,1)S(1)}, bf16[4,32,2048]{2,1,0:T(8,128)(2,1)S(1)}) custom-call(bf16[32,2176]{1,0:T(8,128)(2,1)S(1)} %shard_map.113.refs_0_, bf16[96,2176]{1,0:T(8,128)(2,1)S(1)} %shard_map.114.refs_1_, bf16[32,2176]{1,0:T(8,128)(2,1)S(1)} %collective-permute-done.15.refs_2_, ...), custom_call_target="tpu_custom_call" | custom-call | flops 4294967296 | bytes 16777216 | tf_op jit(solution)/shard_map/pallas_call | solution.py:619
  90.3 3.5 %collective-permute-done.14.refs_1_ = bf16[96,2176]{1,0:T(8,128)(2,1)S(1)} collective-permute-done((bf16[96,2176]{1,0:T(8,128)(2,1)S(1)}, bf16[96,2176]{1,0:T(8,128)(2,1)S(1)}, u32[]{:S(2)}, u32[]{:S(2)}) %collective-permute-start.14) | collective-permute-done | bytes 417824 | tf_op jit(solution)/shard_map/ppermute | solution.py:491
  95.9 2.4 %collective-permute-start.21 = (bf16[32,2048]{1,0:T(8,128)(2,1)S(1)}, bf16[32,2048]{1,0:T(8,128)(2,1)S(1)}, u32[]{:S(2)}, u32[]{:S(2)}) collective-permute-start(bf16[32,2048]{1,0:T(8,128)(2,1)S(1)} %get-tuple-element.61), channel_id=1, source_target_pairs={{0,8},{1,9},{2,10},{3,11},{4,12},{5,13},{6,14},{7,15},{8,0},{9,1},... | collective-permute-start | bytes 393224 | tf_op jit(solution)/shard_map/ppermute | solution.py:491
  98.3 2.1 %collective-permute-start.22 = (bf16[32,2048]{1,0:T(8,128)(2,1)S(1)}, bf16[32,2048]{1,0:T(8,128)(2,1)S(1)}, u32[]{:S(2)}, u32[]{:S(2)}) collective-permute-start(bf16[32,2048]{1,0:T(8,128)(2,1)S(1)} %get-tuple-element.63), channel_id=1, source_target_pairs={{0,12},{1,13},{2,14},{3,15},{4,8},{5,9},{6,10},{7,11},{8,4},{9,5},... | collective-permute-start | bytes 393224 | tf_op jit(solution)/shard_map/ppermute | solution.py:491
  100.5 6.7 %shard_map.116 = (bf16[4,32,2048]{2,1,0:T(8,128)(2,1)S(1)}, bf16[4,32,2048]{2,1,0:T(8,128)(2,1)S(1)}) custom-call(bf16[32,2176]{1,0:T(8,128)(2,1)S(1)} %collective-permute-done.13.refs_0_, bf16[96,2176]{1,0:T(8,128)(2,1)S(1)} %collective-permute-done.14.refs_1_, bf16[32,2176]{1,0:T(8,128)(2,1)S(1)} %collective-permute-done.17.refs_2_, ...), custom_call_target="tpu_custom_call" | custom-call | flops 4294967296 | bytes 16777216 | tf_op jit(solution)/shard_map/pallas_call | solution.py:619
  107.2 1.7 %collective-permute-done.21 = bf16[32,2048]{1,0:T(8,128)(2,1)S(1)} collective-permute-done((bf16[32,2048]{1,0:T(8,128)(2,1)S(1)}, bf16[32,2048]{1,0:T(8,128)(2,1)S(1)}, u32[]{:S(2)}, u32[]{:S(2)}) %collective-permute-start.21) | collective-permute-done | bytes 131104 | tf_op jit(solution)/shard_map/ppermute | solution.py:491
  109.7 3.4 %collective-permute-start.24 = (bf16[32,2048]{1,0:T(8,128)(2,1)S(1)}, bf16[32,2048]{1,0:T(8,128)(2,1)S(1)}, u32[]{:S(2)}, u32[]{:S(2)}) collective-permute-start(bf16[32,2048]{1,0:T(8,128)(2,1)S(1)} %get-tuple-element.57), channel_id=1, source_target_pairs={{0,10},{1,11},{2,8},{3,9},{4,14},{5,15},{6,12},{7,13},{8,2},{9,3},... | collective-permute-start | bytes 393224 | tf_op jit(solution)/shard_map/ppermute | solution.py:491
  113.1 2.0 %collective-permute-start.25 = (bf16[32,2048]{1,0:T(8,128)(2,1)S(1)}, bf16[32,2048]{1,0:T(8,128)(2,1)S(1)}, u32[]{:S(2)}, u32[]{:S(2)}) collective-permute-start(bf16[32,2048]{1,0:T(8,128)(2,1)S(1)} %get-tuple-element.60), channel_id=1, source_target_pairs={{0,14},{1,15},{2,12},{3,13},{4,10},{5,11},{6,8},{7,9},{8,6},{9,7},... | collective-permute-start | bytes 393224 | tf_op jit(solution)/shard_map/ppermute | solution.py:491
  116.4 7.2 %collective-permute-done.24 = bf16[32,2048]{1,0:T(8,128)(2,1)S(1)} collective-permute-done((bf16[32,2048]{1,0:T(8,128)(2,1)S(1)}, bf16[32,2048]{1,0:T(8,128)(2,1)S(1)}, u32[]{:S(2)}, u32[]{:S(2)}) %collective-permute-start.24) | collective-permute-done | bytes 131104 | tf_op jit(solution)/shard_map/ppermute | solution.py:491
  124.7 1.8 %collective-permute-done.27 = bf16[32,2048]{1,0:T(8,128)(2,1)S(1)} collective-permute-done((bf16[32,2048]{1,0:T(8,128)(2,1)S(1)}, bf16[32,2048]{1,0:T(8,128)(2,1)S(1)}, u32[]{:S(2)}, u32[]{:S(2)}) %collective-permute-start.27) | collective-permute-done | bytes 131104 | tf_op jit(solution)/shard_map/ppermute | solution.py:491
  (76 shorter events, 21.9 us)
Async XLA Ops:
  2.6 18.0 %all-to-all-start = ((bf16[8,432,128]{2,1,0:T(8,128)(2,1)}), bf16[8,432,128]{2,1,0:T(8,128)(2,1)S(1)}, u32[]{:S(2)}, u32[]{:S(2)}) async-start(bf16[8,432,128]{2,1,0:T(8,128)(2,1)} %shard_map.109), calls=%async_computation | async-start | bytes 1769472 | tf_op jit(solution)/shard_map/all_to_all | solution.py:542
  20.6 9.2 %collective-permute-start = (bf16[64,2048]{1,0:T(8,128)(2,1)S(1)}, bf16[64,2048]{1,0:T(8,128)(2,1)S(1)}, u32[]{:S(2)}, u32[]{:S(2)}) collective-permute-start(bf16[64,2048]{1,0:T(8,128)(2,1)S(1)} %get-tuple-element.32), channel_id=1, source_target_pairs={{0,2},{1,3},{2,0},{3,1},{4,6},{5,7},{6,4},{7,5},{8,10},{9,11},{10,... | collective-permute-start | bytes 786440 | tf_op jit(solution)/shard_map/ppermute | solution.py:491
  22.1 23.0 %collective-permute-start.1 = (bf16[160,2048]{1,0:T(8,128)(2,1)}, bf16[160,2048]{1,0:T(8,128)(2,1)S(1)}, u32[]{:S(2)}, u32[]{:S(2)}) collective-permute-start(bf16[160,2048]{1,0:T(8,128)(2,1)} %copy-done.2), channel_id=1, source_target_pairs={{0,2},{1,3},{2,0},{3,1},{4,6},{5,7},{6,4},{7,5},{8,10},{9,11},{10,... | collective-permute-start | bytes 1966088 | tf_op jit(solution)/shard_map/ppermute | solution.py:491
  29.8 15.6 %all-to-all-start.1 = ((bf16[16,72,128]{2,1,0:T(8,128)(2,1)}), bf16[16,72,128]{2,1,0:T(8,128)(2,1)S(1)}, u32[]{:S(2)}, u32[]{:S(2)}) async-start(bf16[16,72,128]{2,1,0:T(8,128)(2,1)} %shard_map.111), calls=%async_computation.1 | async-start | bytes 589824 | tf_op jit(solution)/shard_map/all_to_all | solution.py:560
  34.7 13.7 %collective-permute-start.3 = (bf16[288,2048]{1,0:T(8,128)(2,1)S(1)}, bf16[288,2048]{1,0:T(8,128)(2,1)}, u32[]{:S(2)}, u32[]{:S(2)}) collective-permute-start(bf16[288,2048]{1,0:T(8,128)(2,1)S(1)} %copy-done), channel_id=1, source_target_pairs={{0,1},{1,0},{2,3},{3,2},{4,5},{5,4},{6,7},{7,6},{8,9},{9,8},{10,11... | collective-permute-start | bytes 3538952 | tf_op jit(solution)/shard_map/ppermute | solution.py:491
  35.2 8.3 %collective-permute-start.2 = (bf16[64,2048]{1,0:T(8,128)(2,1)S(1)}, bf16[64,2048]{1,0:T(8,128)(2,1)S(1)}, u32[]{:S(2)}, u32[]{:S(2)}) collective-permute-start(bf16[64,2048]{1,0:T(8,128)(2,1)S(1)} %collective-permute-done.refs_3_), channel_id=1, source_target_pairs={{0,16},{16,0},{1,17},{17,1},{2,18},{18,2},{3,19},{19,3},{4,20},{20... | collective-permute-start | bytes 786440 | tf_op jit(solution)/shard_map/ppermute | solution.py:558
  45.5 3.0 %collective-permute-start.4 = (bf16[160,2048]{1,0:T(8,128)(2,1)S(1)}, bf16[160,2048]{1,0:T(8,128)(2,1)S(1)}, u32[]{:S(2)}, u32[]{:S(2)}) collective-permute-start(bf16[160,2048]{1,0:T(8,128)(2,1)S(1)} %collective-permute-done.1.refs_2_), channel_id=1, source_target_pairs={{0,1},{1,0},{2,3},{3,2},{4,5},{5,4},{6,7},{7,6},{8,9},{9,8},{10,11... | collective-permute-start | bytes 1966088 | tf_op jit(solution)/shard_map/ppermute | solution.py:491
  52.2 13.4 %collective-permute-start.7 = (bf16[32,2304]{1,0:T(8,128)(2,1)S(1)}, bf16[32,2304]{1,0:T(8,128)(2,1)S(1)}, u32[]{:S(2)}, u32[]{:S(2)}) collective-permute-start(bf16[32,2304]{1,0:T(8,128)(2,1)S(1)} %get-tuple-element.55), channel_id=1, source_target_pairs={{0,8},{1,9},{2,10},{3,11},{4,12},{5,13},{6,14},{7,15},{8,0},{9,1},... | collective-permute-start | bytes 442376 | tf_op jit(solution)/shard_map/ppermute | solution.py:491
  54.8 10.7 %collective-permute-start.8 = (bf16[32,2304]{1,0:T(8,128)(2,1)S(1)}, bf16[32,2304]{1,0:T(8,128)(2,1)S(1)}, u32[]{:S(2)}, u32[]{:S(2)}) collective-permute-start(bf16[32,2304]{1,0:T(8,128)(2,1)S(1)} %get-tuple-element.54), channel_id=1, source_target_pairs={{0,12},{1,13},{2,14},{3,15},{4,8},{5,9},{6,10},{7,11},{8,4},{9,5},... | collective-permute-start | bytes 442376 | tf_op jit(solution)/shard_map/ppermute | solution.py:491
  55.1 11.7 %collective-permute-start.9 = (bf16[32,2304]{1,0:T(8,128)(2,1)S(1)}, bf16[32,2304]{1,0:T(8,128)(2,1)S(1)}, u32[]{:S(2)}, u32[]{:S(2)}) collective-permute-start(bf16[32,2304]{1,0:T(8,128)(2,1)S(1)} %get-tuple-element.53), channel_id=1, source_target_pairs={{0,4},{1,5},{2,6},{3,7},{4,0},{5,1},{6,2},{7,3},{8,12},{9,13},{10,... | collective-permute-start | bytes 442376 | tf_op jit(solution)/shard_map/ppermute | solution.py:491
  67.3 14.2 %collective-permute-start.10 = (bf16[32,2176]{1,0:T(8,128)(2,1)S(1)}, bf16[32,2176]{1,0:T(8,128)(2,1)S(1)}, u32[]{:S(2)}, u32[]{:S(2)}) collective-permute-start(bf16[32,2176]{1,0:T(8,128)(2,1)S(1)} %shard_map.113.refs_0_), channel_id=1, source_target_pairs={{0,8},{1,9},{2,10},{3,11},{4,12},{5,13},{6,14},{7,15},{8,0},{9,1},... | collective-permute-start | bytes 417800 | tf_op jit(solution)/shard_map/ppermute | solution.py:491
  71.0 10.6 %collective-permute-start.11 = (bf16[32,2176]{1,0:T(8,128)(2,1)S(1)}, bf16[32,2176]{1,0:T(8,128)(2,1)S(1)}, u32[]{:S(2)}, u32[]{:S(2)}) collective-permute-start(bf16[32,2176]{1,0:T(8,128)(2,1)S(1)} %shard_map.113.refs_0_), channel_id=1, source_target_pairs={{0,12},{1,13},{2,14},{3,15},{4,8},{5,9},{6,10},{7,11},{8,4},{9,5},... | collective-permute-start | bytes 417800 | tf_op jit(solution)/shard_map/ppermute | solution.py:491
  72.1 9.5 %collective-permute-start.12 = (bf16[32,2176]{1,0:T(8,128)(2,1)S(1)}, bf16[32,2176]{1,0:T(8,128)(2,1)S(1)}, u32[]{:S(2)}, u32[]{:S(2)}) collective-permute-start(bf16[32,2176]{1,0:T(8,128)(2,1)S(1)} %shard_map.113.refs_0_), channel_id=1, source_target_pairs={{0,4},{1,5},{2,6},{3,7},{4,0},{5,1},{6,2},{7,3},{8,12},{9,13},{10,... | collective-permute-start | bytes 417800 | tf_op jit(solution)/shard_map/ppermute | solution.py:491
  72.1 9.5 %collective-permute-start.13 = (bf16[32,2176]{1,0:T(8,128)(2,1)S(1)}, bf16[32,2176]{1,0:T(8,128)(2,1)S(1)}, u32[]{:S(2)}, u32[]{:S(2)}) collective-permute-start(bf16[32,2176]{1,0:T(8,128)(2,1)S(1)} %shard_map.113.refs_0_), channel_id=1, source_target_pairs={{0,2},{1,3},{2,0},{3,1},{4,6},{5,7},{6,4},{7,5},{8,10},{9,11},{10,... | collective-permute-start | bytes 417800 | tf_op jit(solution)/shard_map/ppermute | solution.py:491
  82.2 11.6 %collective-permute-start.14 = (bf16[96,2176]{1,0:T(8,128)(2,1)S(1)}, bf16[96,2176]{1,0:T(8,128)(2,1)S(1)}, u32[]{:S(2)}, u32[]{:S(2)}) collective-permute-start(bf16[96,2176]{1,0:T(8,128)(2,1)S(1)} %shard_map.114.refs_1_), channel_id=1, source_target_pairs={{0,2},{1,3},{2,0},{3,1},{4,6},{5,7},{6,4},{7,5},{8,10},{9,11},{10,... | collective-permute-start | bytes 1253384 | tf_op jit(solution)/shard_map/ppermute | solution.py:491
  93.8 6.6 %collective-permute-start.18 = (bf16[96,2176]{1,0:T(8,128)(2,1)S(1)}, bf16[96,2176]{1,0:T(8,128)(2,1)S(1)}, u32[]{:S(2)}, u32[]{:S(2)}) collective-permute-start(bf16[96,2176]{1,0:T(8,128)(2,1)S(1)} %collective-permute-done.14.refs_1_), channel_id=1, source_target_pairs={{0,1},{1,0},{2,3},{3,2},{4,5},{5,4},{6,7},{7,6},{8,9},{9,8},{10,11... | collective-permute-start | bytes 1253384 | tf_op jit(solution)/shard_map/ppermute | solution.py:491
  94.4 6.1 %collective-permute-start.17 = (bf16[32,2176]{1,0:T(8,128)(2,1)S(1)}, bf16[32,2176]{1,0:T(8,128)(2,1)S(1)}, u32[]{:S(2)}, u32[]{:S(2)}) collective-permute-start(bf16[32,2176]{1,0:T(8,128)(2,1)S(1)} %collective-permute-done.13.refs_0_), channel_id=1, source_target_pairs={{0,1},{1,0},{2,3},{3,2},{4,5},{5,4},{6,7},{7,6},{8,9},{9,8},{10,11... | collective-permute-start | bytes 417800 | tf_op jit(solution)/shard_map/ppermute | solution.py:491
  95.9 13.0 %collective-permute-start.21 = (bf16[32,2048]{1,0:T(8,128)(2,1)S(1)}, bf16[32,2048]{1,0:T(8,128)(2,1)S(1)}, u32[]{:S(2)}, u32[]{:S(2)}) collective-permute-start(bf16[32,2048]{1,0:T(8,128)(2,1)S(1)} %get-tuple-element.61), channel_id=1, source_target_pairs={{0,8},{1,9},{2,10},{3,11},{4,12},{5,13},{6,14},{7,15},{8,0},{9,1},... | collective-permute-start | bytes 393224 | tf_op jit(solution)/shard_map/ppermute | solution.py:491
  98.3 10.6 %collective-permute-start.22 = (bf16[32,2048]{1,0:T(8,128)(2,1)S(1)}, bf16[32,2048]{1,0:T(8,128)(2,1)S(1)}, u32[]{:S(2)}, u32[]{:S(2)}) collective-permute-start(bf16[32,2048]{1,0:T(8,128)(2,1)S(1)} %get-tuple-element.63), channel_id=1, source_target_pairs={{0,12},{1,13},{2,14},{3,15},{4,8},{5,9},{6,10},{7,11},{8,4},{9,5},... | collective-permute-start | bytes 393224 | tf_op jit(solution)/shard_map/ppermute | solution.py:491
  100.5 8.9 %collective-permute-start.23 = (bf16[32,2048]{1,0:T(8,128)(2,1)S(1)}, bf16[32,2048]{1,0:T(8,128)(2,1)S(1)}, u32[]{:S(2)}, u32[]{:S(2)}) collective-permute-start(bf16[32,2048]{1,0:T(8,128)(2,1)S(1)} %get-tuple-element.62), channel_id=1, source_target_pairs={{0,4},{1,5},{2,6},{3,7},{4,0},{5,1},{6,2},{7,3},{8,12},{9,13},{10,... | collective-permute-start | bytes 393224 | tf_op jit(solution)/shard_map/ppermute | solution.py:491
  109.7 14.0 %collective-permute-start.24 = (bf16[32,2048]{1,0:T(8,128)(2,1)S(1)}, bf16[32,2048]{1,0:T(8,128)(2,1)S(1)}, u32[]{:S(2)}, u32[]{:S(2)}) collective-permute-start(bf16[32,2048]{1,0:T(8,128)(2,1)S(1)} %get-tuple-element.57), channel_id=1, source_target_pairs={{0,10},{1,11},{2,8},{3,9},{4,14},{5,15},{6,12},{7,13},{8,2},{9,3},... | collective-permute-start | bytes 393224 | tf_op jit(solution)/shard_map/ppermute | solution.py:491
  113.1 10.6 %collective-permute-start.25 = (bf16[32,2048]{1,0:T(8,128)(2,1)S(1)}, bf16[32,2048]{1,0:T(8,128)(2,1)S(1)}, u32[]{:S(2)}, u32[]{:S(2)}) collective-permute-start(bf16[32,2048]{1,0:T(8,128)(2,1)S(1)} %get-tuple-element.60), channel_id=1, source_target_pairs={{0,14},{1,15},{2,12},{3,13},{4,10},{5,11},{6,8},{7,9},{8,6},{9,7},... | collective-permute-start | bytes 393224 | tf_op jit(solution)/shard_map/ppermute | solution.py:491
  115.0 9.7 %collective-permute-start.26 = (bf16[32,2048]{1,0:T(8,128)(2,1)S(1)}, bf16[32,2048]{1,0:T(8,128)(2,1)S(1)}, u32[]{:S(2)}, u32[]{:S(2)}) collective-permute-start(bf16[32,2048]{1,0:T(8,128)(2,1)S(1)} %get-tuple-element.59), channel_id=1, source_target_pairs={{0,6},{1,7},{2,4},{3,5},{4,2},{5,3},{6,0},{7,1},{8,14},{9,15},{10,... | collective-permute-start | bytes 393224 | tf_op jit(solution)/shard_map/ppermute | solution.py:491
  115.0 11.5 %collective-permute-start.27 = (bf16[32,2048]{1,0:T(8,128)(2,1)S(1)}, bf16[32,2048]{1,0:T(8,128)(2,1)S(1)}, u32[]{:S(2)}, u32[]{:S(2)}) collective-permute-start(bf16[32,2048]{1,0:T(8,128)(2,1)S(1)} %get-tuple-element.58), channel_id=1, source_target_pairs={{0,2},{1,3},{2,0},{3,1},{4,6},{5,7},{6,4},{7,5},{8,10},{9,11},{10,... | collective-permute-start | bytes 393224 | tf_op jit(solution)/shard_map/ppermute | solution.py:491
  (15 other events, 131.7 us)

commit v13 on v12

--- a/solution.py
+++ b/solution.py
@@ -518,7 +518,7 @@
     part = vit_width // peers
     dim = vit_width // HEADS
     depth = w_merge.shape[0]
-    share = depth // 64 * 16
+    share = depth // 96 * 16
     packed = pl.pallas_call(
         pack_kernel,
         out_shape=jax.ShapeDtypeStruct((peers, 3 * part, rows), BF),

time: 128 us -> 129 us (level)
    all_to_all x1, waiting for transfers between devices: 0.4 us -> 6.15 us  [local(): lax.all_to_all(attended, 'wide', split_axis=0, concat_axis=0, tiled=True)]
    ppermute x27, waiting for transfers between devices: 40.8 us -> 36.9 us  [crossed(): return lax.ppermute(value, 'wide', pairs)]
    ppermute x1, waiting for transfers between devices: 6.83 us -> 5.43 us  [local(): theirs_y = lax.ppermute(mine_y, 'grp', [(0, 1), (1, 0)])]
  transfers between devices with their start and end apart: 30 -> 30, of which waited for: 18 -> 16; matrix products, arithmetic and copies ran while one was open for 1% -> 1% of each run, Pallas kernels for 15% -> 14%
where the time goes in v13:
time: 129 us
  waiting for transfers between devices  59.9 us (46%)
  starting transfers between devices  39.3 us (30%)
  Pallas kernels  24.3 us (19%)
  local copies, waits for them, and re-layouts  3.5 us (3%)
  other arithmetic  1.38 us (1%)
    ppermute x27, waiting for transfers between devices, crossed(): return lax.ppermute(value, 'wide', pairs)  36.9 us
    ppermute x27, starting transfers between devices, crossed(): return lax.ppermute(value, 'wide', pairs)  27.6 us
    pallas_call x2, Pallas kernels, experts_of(): pl.pallas_call(lambda *refs: expert_kernel(*refs, experts=experts, cuts=c...  13.3 us
    all_to_all x1, waiting for transfers between devices, local(): lax.all_to_all(packed, 'wide', split_axis=0, concat_axis=0, tiled=True, a...  11.5 us
    all_to_all x1, waiting for transfers between devices, local(): lax.all_to_all(attended, 'wide', split_axis=0, concat_axis=0, tiled=True)  6.15 us
    ppermute x1, waiting for transfers between devices, local(): theirs_y = lax.ppermute(mine_y, 'grp', [(0, 1), (1, 0)])  5.43 us
    all_to_all x1, starting transfers between devices, local(): lax.all_to_all(packed, 'wide', split_axis=0, concat_axis=0, tiled=True, a...  5.25 us
    pallas_call x1, Pallas kernels, local(): pl.pallas_call(attend_kernel, out_shape=jax.ShapeDtypeStruct((devices, di...  4.92 us
  transfers between devices with their start and end apart: 30, of which 16 were waited for; matrix products, arithmetic and copies ran while one was open for 1% of the time, Pallas kernels for 14%

profile of v13, /device:TPU:0, one launch (start us, length us, event | category | flops | bytes accessed | tf_op | source)
XLA Modules:
  0.0 128.7 jit_solution(3815623976550408997)
XLA Ops:
  2.6 5.3 %all-to-all-start = ((bf16[8,432,128]{2,1,0:T(8,128)(2,1)}), bf16[8,432,128]{2,1,0:T(8,128)(2,1)S(1)}, u32[]{:S(2)}, u32[]{:S(2)}) async-start(bf16[8,432,128]{2,1,0:T(8,128)(2,1)} %shard_map.109), calls=%async_computation | async-start | bytes 1769472 | tf_op jit(solution)/shard_map/all_to_all | solution.py:542
  9.1 11.5 %all-to-all-done.x_ref = bf16[8,432,128]{2,1,0:T(8,128)(2,1)S(1)} async-done(((bf16[8,432,128]{2,1,0:T(8,128)(2,1)}), bf16[8,432,128]{2,1,0:T(8,128)(2,1)S(1)}, u32[]{:S(2)}, u32[]{:S(2)}) %all-to-all-start) | async-done | bytes 884768 | tf_op jit(solution)/shard_map/all_to_all | solution.py:542
  22.6 4.9 %shard_map.111 = bf16[16,72,128]{2,1,0:T(8,128)(2,1)} custom-call(bf16[8,432,128]{2,1,0:T(8,128)(2,1)S(1)} %all-to-all-done.x_ref, s32[2,2]{1,0:T(2,128)S(1)} %copy-done.3), custom_call_target="tpu_custom_call" | custom-call | flops 4294967296 | bytes 4194304 | tf_op jit(solution)/shard_map/pallas_call | solution.py:548
  28.4 4.9 %all-to-all-start.1 = ((bf16[16,72,128]{2,1,0:T(8,128)(2,1)}), bf16[16,72,128]{2,1,0:T(8,128)(2,1)S(1)}, u32[]{:S(2)}, u32[]{:S(2)}) async-start(bf16[16,72,128]{2,1,0:T(8,128)(2,1)} %shard_map.111), calls=%async_computation.1 | async-start | bytes 589824 | tf_op jit(solution)/shard_map/all_to_all | solution.py:560
  35.3 5.4 %collective-permute-done.2.refs_4_ = bf16[48,2048]{1,0:T(8,128)(2,1)S(1)} collective-permute-done((bf16[48,2048]{1,0:T(8,128)(2,1)S(1)}, bf16[48,2048]{1,0:T(8,128)(2,1)S(1)}, u32[]{:S(2)}, u32[]{:S(2)}) %collective-permute-start.2) | collective-permute-done | bytes 196640 | tf_op jit(solution)/shard_map/ppermute | solution.py:558
  40.7 6.2 %all-to-all-done.1.x_ref = bf16[16,72,128]{2,1,0:T(8,128)(2,1)S(1)} async-done(((bf16[16,72,128]{2,1,0:T(8,128)(2,1)}), bf16[16,72,128]{2,1,0:T(8,128)(2,1)S(1)}, u32[]{:S(2)}, u32[]{:S(2)}) %all-to-all-start.1) | async-done | bytes 294944 | tf_op jit(solution)/shard_map/all_to_all | solution.py:560
  49.7 3.8 %shard_map.112 = bf16[4,32,2304]{2,1,0:T(8,128)(2,1)S(1)} custom-call(bf16[16,72,128]{2,1,0:T(8,128)(2,1)S(1)} %all-to-all-done.1.x_ref, bf16[1152,1152]{1,0:T(8,128)(2,1)} %w_out_hbm.1, f32[1,4608]{1,0:T(1,128)S(1)} %reshape.8.gain_ref, f32[1,4608]{1,0:T(1,128)S(1)} %reshape.9.bias_ref, bf16[288,2048]{1,0:T(8,128)(2,1)} %refs_0_.1, ...), custom_call_target="tpu_custom_call" | custom-call | tf_op jit(solution)/shard_map/pallas_call | solution.py:565
  53.6 2.7 %collective-permute-start.7 = (bf16[32,2304]{1,0:T(8,128)(2,1)S(1)}, bf16[32,2304]{1,0:T(8,128)(2,1)S(1)}, u32[]{:S(2)}, u32[]{:S(2)}) collective-permute-start(bf16[32,2304]{1,0:T(8,128)(2,1)S(1)} %get-tuple-element.55), channel_id=1, source_target_pairs={{0,8},{1,9},{2,10},{3,11},{4,12},{5,13},{6,14},{7,15},{8,0},{9,1},... | collective-permute-start | bytes 442376 | tf_op jit(solution)/shard_map/ppermute | solution.py:491
  57.6 9.5 %collective-permute-done.7.refs_1_ = bf16[32,2304]{1,0:T(8,128)(2,1)S(1)} collective-permute-done((bf16[32,2304]{1,0:T(8,128)(2,1)S(1)}, bf16[32,2304]{1,0:T(8,128)(2,1)S(1)}, u32[]{:S(2)}, u32[]{:S(2)}) %collective-permute-start.7) | collective-permute-done | bytes 147488 | tf_op jit(solution)/shard_map/ppermute | solution.py:491
  68.7 3.7 %collective-permute-start.10 = (bf16[32,2176]{1,0:T(8,128)(2,1)S(1)}, bf16[32,2176]{1,0:T(8,128)(2,1)S(1)}, u32[]{:S(2)}, u32[]{:S(2)}) collective-permute-start(bf16[32,2176]{1,0:T(8,128)(2,1)S(1)} %shard_map.113.refs_0_), channel_id=1, source_target_pairs={{0,8},{1,9},{2,10},{3,11},{4,12},{5,13},{6,14},{7,15},{8,0},{9,1},... | collective-permute-start | bytes 417800 | tf_op jit(solution)/shard_map/ppermute | solution.py:491
  73.5 1.8 %collective-permute-start.13 = (bf16[32,2176]{1,0:T(8,128)(2,1)S(1)}, bf16[32,2176]{1,0:T(8,128)(2,1)S(1)}, u32[]{:S(2)}, u32[]{:S(2)}) collective-permute-start(bf16[32,2176]{1,0:T(8,128)(2,1)S(1)} %shard_map.113.refs_0_), channel_id=1, source_target_pairs={{0,2},{1,3},{2,0},{3,1},{4,6},{5,7},{6,4},{7,5},{8,10},{9,11},{10,... | collective-permute-start | bytes 417800 | tf_op jit(solution)/shard_map/ppermute | solution.py:491
  75.3 7.7 %collective-permute-done.10.refs_0_ = bf16[32,2176]{1,0:T(8,128)(2,1)S(1)} collective-permute-done((bf16[32,2176]{1,0:T(8,128)(2,1)S(1)}, bf16[32,2176]{1,0:T(8,128)(2,1)S(1)}, u32[]{:S(2)}, u32[]{:S(2)}) %collective-permute-start.10) | collective-permute-done | bytes 139296 | tf_op jit(solution)/shard_map/ppermute | solution.py:491
  83.6 1.6 %collective-permute-start.14 = (bf16[96,2176]{1,0:T(8,128)(2,1)S(1)}, bf16[96,2176]{1,0:T(8,128)(2,1)S(1)}, u32[]{:S(2)}, u32[]{:S(2)}) collective-permute-start(bf16[96,2176]{1,0:T(8,128)(2,1)S(1)} %shard_map.114.refs_1_), channel_id=1, source_target_pairs={{0,2},{1,3},{2,0},{3,1},{4,6},{5,7},{6,4},{7,5},{8,10},{9,11},{10,... | collective-permute-start | bytes 1253384 | tf_op jit(solution)/shard_map/ppermute | solution.py:491
  85.3 6.7 %shard_map.115 = (bf16[4,32,2048]{2,1,0:T(8,128)(2,1)S(1)}, bf16[4,32,2048]{2,1,0:T(8,128)(2,1)S(1)}) custom-call(bf16[32,2176]{1,0:T(8,128)(2,1)S(1)} %shard_map.113.refs_0_, bf16[96,2176]{1,0:T(8,128)(2,1)S(1)} %shard_map.114.refs_1_, bf16[32,2176]{1,0:T(8,128)(2,1)S(1)} %collective-permute-done.15.refs_2_, ...), custom_call_target="tpu_custom_call" | custom-call | flops 4294967296 | bytes 16777216 | tf_op jit(solution)/shard_map/pallas_call | solution.py:619
  91.9 3.3 %collective-permute-done.14.refs_1_ = bf16[96,2176]{1,0:T(8,128)(2,1)S(1)} collective-permute-done((bf16[96,2176]{1,0:T(8,128)(2,1)S(1)}, bf16[96,2176]{1,0:T(8,128)(2,1)S(1)}, u32[]{:S(2)}, u32[]{:S(2)}) %collective-permute-start.14) | collective-permute-done | bytes 417824 | tf_op jit(solution)/shard_map/ppermute | solution.py:491
  97.3 2.5 %collective-permute-start.21 = (bf16[32,2048]{1,0:T(8,128)(2,1)S(1)}, bf16[32,2048]{1,0:T(8,128)(2,1)S(1)}, u32[]{:S(2)}, u32[]{:S(2)}) collective-permute-start(bf16[32,2048]{1,0:T(8,128)(2,1)S(1)} %get-tuple-element.61), channel_id=1, source_target_pairs={{0,8},{1,9},{2,10},{3,11},{4,12},{5,13},{6,14},{7,15},{8,0},{9,1},... | collective-permute-start | bytes 393224 | tf_op jit(solution)/shard_map/ppermute | solution.py:491
  99.9 2.0 %collective-permute-start.22 = (bf16[32,2048]{1,0:T(8,128)(2,1)S(1)}, bf16[32,2048]{1,0:T(8,128)(2,1)S(1)}, u32[]{:S(2)}, u32[]{:S(2)}) collective-permute-start(bf16[32,2048]{1,0:T(8,128)(2,1)S(1)} %get-tuple-element.63), channel_id=1, source_target_pairs={{0,12},{1,13},{2,14},{3,15},{4,8},{5,9},{6,10},{7,11},{8,4},{9,5},... | collective-permute-start | bytes 393224 | tf_op jit(solution)/shard_map/ppermute | solution.py:491
  101.9 6.7 %shard_map.116 = (bf16[4,32,2048]{2,1,0:T(8,128)(2,1)S(1)}, bf16[4,32,2048]{2,1,0:T(8,128)(2,1)S(1)}) custom-call(bf16[32,2176]{1,0:T(8,128)(2,1)S(1)} %collective-permute-done.13.refs_0_, bf16[96,2176]{1,0:T(8,128)(2,1)S(1)} %collective-permute-done.14.refs_1_, bf16[32,2176]{1,0:T(8,128)(2,1)S(1)} %collective-permute-done.17.refs_2_, ...), custom_call_target="tpu_custom_call" | custom-call | flops 4294967296 | bytes 16777216 | tf_op jit(solution)/shard_map/pallas_call | solution.py:619
  108.6 1.7 %collective-permute-done.21 = bf16[32,2048]{1,0:T(8,128)(2,1)S(1)} collective-permute-done((bf16[32,2048]{1,0:T(8,128)(2,1)S(1)}, bf16[32,2048]{1,0:T(8,128)(2,1)S(1)}, u32[]{:S(2)}, u32[]{:S(2)}) %collective-permute-start.21) | collective-permute-done | bytes 131104 | tf_op jit(solution)/shard_map/ppermute | solution.py:491
  111.1 3.7 %collective-permute-start.24 = (bf16[32,2048]{1,0:T(8,128)(2,1)S(1)}, bf16[32,2048]{1,0:T(8,128)(2,1)S(1)}, u32[]{:S(2)}, u32[]{:S(2)}) collective-permute-start(bf16[32,2048]{1,0:T(8,128)(2,1)S(1)} %get-tuple-element.57), channel_id=1, source_target_pairs={{0,10},{1,11},{2,8},{3,9},{4,14},{5,15},{6,12},{7,13},{8,2},{9,3},... | collective-permute-start | bytes 393224 | tf_op jit(solution)/shard_map/ppermute | solution.py:491
  114.7 1.7 %collective-permute-start.25 = (bf16[32,2048]{1,0:T(8,128)(2,1)S(1)}, bf16[32,2048]{1,0:T(8,128)(2,1)S(1)}, u32[]{:S(2)}, u32[]{:S(2)}) collective-permute-start(bf16[32,2048]{1,0:T(8,128)(2,1)S(1)} %get-tuple-element.60), channel_id=1, source_target_pairs={{0,14},{1,15},{2,12},{3,13},{4,10},{5,11},{6,8},{7,9},{8,6},{9,7},... | collective-permute-start | bytes 393224 | tf_op jit(solution)/shard_map/ppermute | solution.py:491
  116.6 1.5 %collective-permute-start.27 = (bf16[32,2048]{1,0:T(8,128)(2,1)S(1)}, bf16[32,2048]{1,0:T(8,128)(2,1)S(1)}, u32[]{:S(2)}, u32[]{:S(2)}) collective-permute-start(bf16[32,2048]{1,0:T(8,128)(2,1)S(1)} %get-tuple-element.58), channel_id=1, source_target_pairs={{0,2},{1,3},{2,0},{3,1},{4,6},{5,7},{6,4},{7,5},{8,10},{9,11},{10,... | collective-permute-start | bytes 393224 | tf_op jit(solution)/shard_map/ppermute | solution.py:491
  118.1 7.0 %collective-permute-done.24 = bf16[32,2048]{1,0:T(8,128)(2,1)S(1)} collective-permute-done((bf16[32,2048]{1,0:T(8,128)(2,1)S(1)}, bf16[32,2048]{1,0:T(8,128)(2,1)S(1)}, u32[]{:S(2)}, u32[]{:S(2)}) %collective-permute-start.24) | collective-permute-done | bytes 131104 | tf_op jit(solution)/shard_map/ppermute | solution.py:491
  126.1 1.8 %collective-permute-done.27 = bf16[32,2048]{1,0:T(8,128)(2,1)S(1)} collective-permute-done((bf16[32,2048]{1,0:T(8,128)(2,1)S(1)}, bf16[32,2048]{1,0:T(8,128)(2,1)S(1)}, u32[]{:S(2)}, u32[]{:S(2)}) %collective-permute-start.27) | collective-permute-done | bytes 131104 | tf_op jit(solution)/shard_map/ppermute | solution.py:491
  (76 shorter events, 21.1 us)
Async XLA Ops:
  2.6 18.0 %all-to-all-start = ((bf16[8,432,128]{2,1,0:T(8,128)(2,1)}), bf16[8,432,128]{2,1,0:T(8,128)(2,1)S(1)}, u32[]{:S(2)}, u32[]{:S(2)}) async-start(bf16[8,432,128]{2,1,0:T(8,128)(2,1)} %shard_map.109), calls=%async_computation | async-start | bytes 1769472 | tf_op jit(solution)/shard_map/all_to_all | solution.py:542
  20.6 7.8 %collective-permute-start = (bf16[48,2048]{1,0:T(8,128)(2,1)S(1)}, bf16[48,2048]{1,0:T(8,128)(2,1)S(1)}, u32[]{:S(2)}, u32[]{:S(2)}) collective-permute-start(bf16[48,2048]{1,0:T(8,128)(2,1)S(1)} %get-tuple-element.32), channel_id=1, source_target_pairs={{0,2},{1,3},{2,0},{3,1},{4,6},{5,7},{6,4},{7,5},{8,10},{9,11},{10,... | collective-permute-start | bytes 589832 | tf_op jit(solution)/shard_map/ppermute | solution.py:491
  22.1 24.8 %collective-permute-start.1 = (bf16[192,2048]{1,0:T(8,128)(2,1)}, bf16[192,2048]{1,0:T(8,128)(2,1)S(1)}, u32[]{:S(2)}, u32[]{:S(2)}) collective-permute-start(bf16[192,2048]{1,0:T(8,128)(2,1)} %copy-done.2), channel_id=1, source_target_pairs={{0,2},{1,3},{2,0},{3,1},{4,6},{5,7},{6,4},{7,5},{8,10},{9,11},{10,... | collective-permute-start | bytes 2359304 | tf_op jit(solution)/shard_map/ppermute | solution.py:491
  28.4 18.4 %all-to-all-start.1 = ((bf16[16,72,128]{2,1,0:T(8,128)(2,1)}), bf16[16,72,128]{2,1,0:T(8,128)(2,1)S(1)}, u32[]{:S(2)}, u32[]{:S(2)}) async-start(bf16[16,72,128]{2,1,0:T(8,128)(2,1)} %shard_map.111), calls=%async_computation.1 | async-start | bytes 589824 | tf_op jit(solution)/shard_map/all_to_all | solution.py:560
  33.3 16.4 %collective-permute-start.3 = (bf16[288,2048]{1,0:T(8,128)(2,1)S(1)}, bf16[288,2048]{1,0:T(8,128)(2,1)}, u32[]{:S(2)}, u32[]{:S(2)}) collective-permute-start(bf16[288,2048]{1,0:T(8,128)(2,1)S(1)} %copy-done), channel_id=1, source_target_pairs={{0,1},{1,0},{2,3},{3,2},{4,5},{5,4},{6,7},{7,6},{8,9},{9,8},{10,11... | collective-permute-start | bytes 3538952 | tf_op jit(solution)/shard_map/ppermute | solution.py:491
  33.8 6.9 %collective-permute-start.2 = (bf16[48,2048]{1,0:T(8,128)(2,1)S(1)}, bf16[48,2048]{1,0:T(8,128)(2,1)S(1)}, u32[]{:S(2)}, u32[]{:S(2)}) collective-permute-start(bf16[48,2048]{1,0:T(8,128)(2,1)S(1)} %collective-permute-done.refs_3_), channel_id=1, source_target_pairs={{0,16},{16,0},{1,17},{17,1},{2,18},{18,2},{3,19},{19,3},{4,20},{20... | collective-permute-start | bytes 589832 | tf_op jit(solution)/shard_map/ppermute | solution.py:558
  46.9 2.9 %collective-permute-start.4 = (bf16[192,2048]{1,0:T(8,128)(2,1)S(1)}, bf16[192,2048]{1,0:T(8,128)(2,1)}, u32[]{:S(2)}, u32[]{:S(2)}) collective-permute-start(bf16[192,2048]{1,0:T(8,128)(2,1)S(1)} %collective-permute-done.1.refs_2_), channel_id=1, source_target_pairs={{0,1},{1,0},{2,3},{3,2},{4,5},{5,4},{6,7},{7,6},{8,9},{9,8},{10,11... | collective-permute-start | bytes 2359304 | tf_op jit(solution)/shard_map/ppermute | solution.py:491
  53.6 13.4 %collective-permute-start.7 = (bf16[32,2304]{1,0:T(8,128)(2,1)S(1)}, bf16[32,2304]{1,0:T(8,128)(2,1)S(1)}, u32[]{:S(2)}, u32[]{:S(2)}) collective-permute-start(bf16[32,2304]{1,0:T(8,128)(2,1)S(1)} %get-tuple-element.55), channel_id=1, source_target_pairs={{0,8},{1,9},{2,10},{3,11},{4,12},{5,13},{6,14},{7,15},{8,0},{9,1},... | collective-permute-start | bytes 442376 | tf_op jit(solution)/shard_map/ppermute | solution.py:491
  56.2 10.8 %collective-permute-start.8 = (bf16[32,2304]{1,0:T(8,128)(2,1)S(1)}, bf16[32,2304]{1,0:T(8,128)(2,1)S(1)}, u32[]{:S(2)}, u32[]{:S(2)}) collective-permute-start(bf16[32,2304]{1,0:T(8,128)(2,1)S(1)} %get-tuple-element.54), channel_id=1, source_target_pairs={{0,12},{1,13},{2,14},{3,15},{4,8},{5,9},{6,10},{7,11},{8,4},{9,5},... | collective-permute-start | bytes 442376 | tf_op jit(solution)/shard_map/ppermute | solution.py:491
  56.7 11.4 %collective-permute-start.9 = (bf16[32,2304]{1,0:T(8,128)(2,1)S(1)}, bf16[32,2304]{1,0:T(8,128)(2,1)S(1)}, u32[]{:S(2)}, u32[]{:S(2)}) collective-permute-start(bf16[32,2304]{1,0:T(8,128)(2,1)S(1)} %get-tuple-element.53), channel_id=1, source_target_pairs={{0,4},{1,5},{2,6},{3,7},{4,0},{5,1},{6,2},{7,3},{8,12},{9,13},{10,... | collective-permute-start | bytes 442376 | tf_op jit(solution)/shard_map/ppermute | solution.py:491
  68.7 14.3 %collective-permute-start.10 = (bf16[32,2176]{1,0:T(8,128)(2,1)S(1)}, bf16[32,2176]{1,0:T(8,128)(2,1)S(1)}, u32[]{:S(2)}, u32[]{:S(2)}) collective-permute-start(bf16[32,2176]{1,0:T(8,128)(2,1)S(1)} %shard_map.113.refs_0_), channel_id=1, source_target_pairs={{0,8},{1,9},{2,10},{3,11},{4,12},{5,13},{6,14},{7,15},{8,0},{9,1},... | collective-permute-start | bytes 417800 | tf_op jit(solution)/shard_map/ppermute | solution.py:491
  72.4 10.6 %collective-permute-start.11 = (bf16[32,2176]{1,0:T(8,128)(2,1)S(1)}, bf16[32,2176]{1,0:T(8,128)(2,1)S(1)}, u32[]{:S(2)}, u32[]{:S(2)}) collective-permute-start(bf16[32,2176]{1,0:T(8,128)(2,1)S(1)} %shard_map.113.refs_0_), channel_id=1, source_target_pairs={{0,12},{1,13},{2,14},{3,15},{4,8},{5,9},{6,10},{7,11},{8,4},{9,5},... | collective-permute-start | bytes 417800 | tf_op jit(solution)/shard_map/ppermute | solution.py:491
  73.5 9.5 %collective-permute-start.12 = (bf16[32,2176]{1,0:T(8,128)(2,1)S(1)}, bf16[32,2176]{1,0:T(8,128)(2,1)S(1)}, u32[]{:S(2)}, u32[]{:S(2)}) collective-permute-start(bf16[32,2176]{1,0:T(8,128)(2,1)S(1)} %shard_map.113.refs_0_), channel_id=1, source_target_pairs={{0,4},{1,5},{2,6},{3,7},{4,0},{5,1},{6,2},{7,3},{8,12},{9,13},{10,... | collective-permute-start | bytes 417800 | tf_op jit(solution)/shard_map/ppermute | solution.py:491
  73.5 9.5 %collective-permute-start.13 = (bf16[32,2176]{1,0:T(8,128)(2,1)S(1)}, bf16[32,2176]{1,0:T(8,128)(2,1)S(1)}, u32[]{:S(2)}, u32[]{:S(2)}) collective-permute-start(bf16[32,2176]{1,0:T(8,128)(2,1)S(1)} %shard_map.113.refs_0_), channel_id=1, source_target_pairs={{0,2},{1,3},{2,0},{3,1},{4,6},{5,7},{6,4},{7,5},{8,10},{9,11},{10,... | collective-permute-start | bytes 417800 | tf_op jit(solution)/shard_map/ppermute | solution.py:491
  83.6 11.6 %collective-permute-start.14 = (bf16[96,2176]{1,0:T(8,128)(2,1)S(1)}, bf16[96,2176]{1,0:T(8,128)(2,1)S(1)}, u32[]{:S(2)}, u32[]{:S(2)}) collective-permute-start(bf16[96,2176]{1,0:T(8,128)(2,1)S(1)} %shard_map.114.refs_1_), channel_id=1, source_target_pairs={{0,2},{1,3},{2,0},{3,1},{4,6},{5,7},{6,4},{7,5},{8,10},{9,11},{10,... | collective-permute-start | bytes 1253384 | tf_op jit(solution)/shard_map/ppermute | solution.py:491
  95.2 6.6 %collective-permute-start.18 = (bf16[96,2176]{1,0:T(8,128)(2,1)S(1)}, bf16[96,2176]{1,0:T(8,128)(2,1)S(1)}, u32[]{:S(2)}, u32[]{:S(2)}) collective-permute-start(bf16[96,2176]{1,0:T(8,128)(2,1)S(1)} %collective-permute-done.14.refs_1_), channel_id=1, source_target_pairs={{0,1},{1,0},{2,3},{3,2},{4,5},{5,4},{6,7},{7,6},{8,9},{9,8},{10,11... | collective-permute-start | bytes 1253384 | tf_op jit(solution)/shard_map/ppermute | solution.py:491
  95.8 6.1 %collective-permute-start.17 = (bf16[32,2176]{1,0:T(8,128)(2,1)S(1)}, bf16[32,2176]{1,0:T(8,128)(2,1)S(1)}, u32[]{:S(2)}, u32[]{:S(2)}) collective-permute-start(bf16[32,2176]{1,0:T(8,128)(2,1)S(1)} %collective-permute-done.13.refs_0_), channel_id=1, source_target_pairs={{0,1},{1,0},{2,3},{3,2},{4,5},{5,4},{6,7},{7,6},{8,9},{9,8},{10,11... | collective-permute-start | bytes 417800 | tf_op jit(solution)/shard_map/ppermute | solution.py:491
  97.3 13.0 %collective-permute-start.21 = (bf16[32,2048]{1,0:T(8,128)(2,1)S(1)}, bf16[32,2048]{1,0:T(8,128)(2,1)S(1)}, u32[]{:S(2)}, u32[]{:S(2)}) collective-permute-start(bf16[32,2048]{1,0:T(8,128)(2,1)S(1)} %get-tuple-element.61), channel_id=1, source_target_pairs={{0,8},{1,9},{2,10},{3,11},{4,12},{5,13},{6,14},{7,15},{8,0},{9,1},... | collective-permute-start | bytes 393224 | tf_op jit(solution)/shard_map/ppermute | solution.py:491
  99.9 10.4 %collective-permute-start.22 = (bf16[32,2048]{1,0:T(8,128)(2,1)S(1)}, bf16[32,2048]{1,0:T(8,128)(2,1)S(1)}, u32[]{:S(2)}, u32[]{:S(2)}) collective-permute-start(bf16[32,2048]{1,0:T(8,128)(2,1)S(1)} %get-tuple-element.63), channel_id=1, source_target_pairs={{0,12},{1,13},{2,14},{3,15},{4,8},{5,9},{6,10},{7,11},{8,4},{9,5},... | collective-permute-start | bytes 393224 | tf_op jit(solution)/shard_map/ppermute | solution.py:491
  101.9 8.9 %collective-permute-start.23 = (bf16[32,2048]{1,0:T(8,128)(2,1)S(1)}, bf16[32,2048]{1,0:T(8,128)(2,1)S(1)}, u32[]{:S(2)}, u32[]{:S(2)}) collective-permute-start(bf16[32,2048]{1,0:T(8,128)(2,1)S(1)} %get-tuple-element.62), channel_id=1, source_target_pairs={{0,4},{1,5},{2,6},{3,7},{4,0},{5,1},{6,2},{7,3},{8,12},{9,13},{10,... | collective-permute-start | bytes 393224 | tf_op jit(solution)/shard_map/ppermute | solution.py:491
  111.1 14.0 %collective-permute-start.24 = (bf16[32,2048]{1,0:T(8,128)(2,1)S(1)}, bf16[32,2048]{1,0:T(8,128)(2,1)S(1)}, u32[]{:S(2)}, u32[]{:S(2)}) collective-permute-start(bf16[32,2048]{1,0:T(8,128)(2,1)S(1)} %get-tuple-element.57), channel_id=1, source_target_pairs={{0,10},{1,11},{2,8},{3,9},{4,14},{5,15},{6,12},{7,13},{8,2},{9,3},... | collective-permute-start | bytes 393224 | tf_op jit(solution)/shard_map/ppermute | solution.py:491
  114.7 10.3 %collective-permute-start.25 = (bf16[32,2048]{1,0:T(8,128)(2,1)S(1)}, bf16[32,2048]{1,0:T(8,128)(2,1)S(1)}, u32[]{:S(2)}, u32[]{:S(2)}) collective-permute-start(bf16[32,2048]{1,0:T(8,128)(2,1)S(1)} %get-tuple-element.60), channel_id=1, source_target_pairs={{0,14},{1,15},{2,12},{3,13},{4,10},{5,11},{6,8},{7,9},{8,6},{9,7},... | collective-permute-start | bytes 393224 | tf_op jit(solution)/shard_map/ppermute | solution.py:491
  116.4 9.7 %collective-permute-start.26 = (bf16[32,2048]{1,0:T(8,128)(2,1)S(1)}, bf16[32,2048]{1,0:T(8,128)(2,1)S(1)}, u32[]{:S(2)}, u32[]{:S(2)}) collective-permute-start(bf16[32,2048]{1,0:T(8,128)(2,1)S(1)} %get-tuple-element.59), channel_id=1, source_target_pairs={{0,6},{1,7},{2,4},{3,5},{4,2},{5,3},{6,0},{7,1},{8,14},{9,15},{10,... | collective-permute-start | bytes 393224 | tf_op jit(solution)/shard_map/ppermute | solution.py:491
  116.6 11.3 %collective-permute-start.27 = (bf16[32,2048]{1,0:T(8,128)(2,1)S(1)}, bf16[32,2048]{1,0:T(8,128)(2,1)S(1)}, u32[]{:S(2)}, u32[]{:S(2)}) collective-permute-start(bf16[32,2048]{1,0:T(8,128)(2,1)S(1)} %get-tuple-element.58), channel_id=1, source_target_pairs={{0,2},{1,3},{2,0},{3,1},{4,6},{5,7},{6,4},{7,5},{8,10},{9,11},{10,... | collective-permute-start | bytes 393224 | tf_op jit(solution)/shard_map/ppermute | solution.py:491
  (15 other events, 136.2 us)
